TPU v7x, 32 devices: a whole 2x2x4 slice. The times are simulated.
32 devices in a mesh: ens: 2 (over y), cell: 4 (over z), win: 4 (over x, core).
Axes of the slice: x: 2, y: 2, z: 4, core: 2. Of those that a mesh axis runs over, the one named last changes fastest.
Arguments:
- prior_flux: float32 [64, 2048], P(('ens', 'win'), 'cell'), parts along dimension 0, may hold values from -6 to 6
- observed: float32 [8, 512], P(('ens', 'cell')), parts along dimension 0, may hold values from -6 to 6
- obs_weight: float32 [8, 512], P(('ens', 'cell')), parts along dimension 0, may hold values from 1 to 10
- footprint: float32 [4, 4, 4, 16, 4096], P('cell', 'win'), may hold values from -0.1875 to 0.1875
- flux_slot: int32 [4, 4, 4, 16], P('cell', 'win'), may hold values from 0 to 63
- obs_slot: int32 [4, 4, 4, 16], P('cell', 'win'), may hold values from 0 to 7
- slot_count: int32 [4, 4, 4], P('cell', 'win'), may hold values from 1 to 16, as said below
Outputs:
- increment: float32 [64, 2048], P(('ens', 'win'), 'cell'), parts along dimension 0
- departure: float32 [8, 512], P(('ens', 'cell')), parts along dimension 0
There are 2 independent parts, one for each index of `ens`. A program takes and returns all parts, laid end to end along the dimension named above; an argument that names none is the same for every part. Nothing has to cross between parts.
Inputs may be any that keep to these rules, and one draw needn't show every extreme that they name: `slot_count`: some owner receives 16 live slots from every device of a window group, and every device sends 16 live slots to some owner.
All inputs are finite; a program needn't handle non-finite values.
Results may differ from a plain program's by a relative error of at most 0.0001.
Values sent between devices are 32-bit elements; how exact they have to be, the bound alone decides.
No kernel may reach another device: no remote copies, remote signals or barrier semaphores. Data moves between devices by JAX's collectives and lax.ppermute only.
A program may use at most 128 MiB of HBM per device.

v0:
```python
import jax
import jax.numpy as jnp
from jax import lax
from jax.sharding import PartitionSpec as P

CB = 64
OB = 64
CBLK_DEV = 8
WIN_DEV = 8
OBLK_DEV = 8
ITERS = 2


def local(prior_flux, observed, obs_weight, footprint, flux_slot, obs_slot, slot_count):
    owner_count = footprint.shape[2]
    capacity = footprint.shape[3]
    slot_total = owner_count * capacity
    flux_blocks = WIN_DEV * CBLK_DEV
    matrices = footprint.reshape(owner_count, capacity, OB, CB)
    targets = flux_slot.reshape(owner_count, capacity)
    obs_rows = obs_slot.reshape(slot_total)
    live_mask = (
        lax.broadcasted_iota(jnp.int32, (owner_count, capacity), 1)
        < slot_count.reshape(owner_count, 1)
    ).astype(jnp.float32)
    obs_pick = (obs_rows[:, None] == lax.broadcasted_iota(jnp.int32, (1, OBLK_DEV), 1)).astype(
        jnp.float32
    )
    incoming = lax.all_to_all(targets, "cell", split_axis=0, concat_axis=0, tiled=True)
    recv_pick = (
        incoming.reshape(slot_total, 1) == lax.broadcasted_iota(jnp.int32, (1, flux_blocks), 1)
    ).astype(jnp.float32)
    current = prior_flux
    departure = jnp.zeros_like(observed)
    for step in range(ITERS):
        served = jnp.dot(
            recv_pick, current.reshape(flux_blocks, CB), precision=lax.Precision.HIGHEST
        )
        selected = lax.all_to_all(
            served.reshape(owner_count, capacity, CB),
            "cell",
            split_axis=0,
            concat_axis=0,
            tiled=True,
        )
        partial_value = (
            jnp.einsum("ocij,ocj->oci", matrices, selected, precision=lax.Precision.HIGHEST)
            * live_mask[..., None]
        )
        block_sums = jnp.dot(
            obs_pick.T, partial_value.reshape(slot_total, OB), precision=lax.Precision.HIGHEST
        )
        block_sums = block_sums.reshape(1, OBLK_DEV * OB)
        modeled = lax.psum(block_sums, "win")
        departure = obs_weight * (modeled - observed)
        picked = jnp.dot(obs_pick, departure.reshape(OBLK_DEV, OB), precision=lax.Precision.HIGHEST)
        picked = picked.reshape(owner_count, capacity, OB)
        returned = (
            jnp.einsum("ocij,oci->ocj", matrices, picked, precision=lax.Precision.HIGHEST)
            * live_mask[..., None]
        )
        arrived = lax.all_to_all(returned, "cell", split_axis=0, concat_axis=0, tiled=True)
        gradient = jnp.dot(
            recv_pick.T, arrived.reshape(slot_total, CB), precision=lax.Precision.HIGHEST
        )
        gradient = gradient.reshape(WIN_DEV, CBLK_DEV * CB)
        current = current - 0.5 * (current - prior_flux + gradient)
    return (current - prior_flux, departure)


def solution(mesh):
    placed = (
        P(("ens", "win"), "cell"),
        P(("ens", "cell"), None),
        P(("ens", "cell"), None),
        P("cell", "win", None, None, None),
        P("cell", "win", None, None),
        P("cell", "win", None, None),
        P("cell", "win", None),
    )
    return jax.shard_map(
        local,
        mesh=mesh,
        in_specs=placed,
        out_specs=(P(("ens", "win"), "cell"), P(("ens", "cell"), None)),
        check_vma=False,
    )
```

profile of v0, /device:TPU:0, one launch (start us, length us, event | category | flops | bytes accessed | tf_op | source)
XLA Modules:
  0.0 78.5 jit_solution(8392288301899761401)
XLA Ops:
  0.6 6.3 %all-to-all-start = ((s32[4,1,16]{2,1,0:T(1,128)}), s32[4,1,16]{2,1,0:T(1,128)S(1)}, u32[]{:S(2)}, u32[]{:S(2)}) async-start(s32[4,1,16]{2,1,0:T(1,128)} %bitcast.72), calls=%async_computation | async-start | bytes 4096 | tf_op jit(solution)/shard_map/all_to_all | solution.py:29
  7.0 0.8 %reshape.166 = f32[64,64,1]{1,0,2:T(8,128)S(1)} reshape(f32[8,512]{1,0:T(8,128)} %param.7) | data formatting | bytes 32768 | tf_op jit(solution)/shard_map/reshape | solution.py:37
  7.8 4.7 %all-to-all-done = s32[4,1,16]{2,1,0:T(1,128)S(1)} async-done(((s32[4,1,16]{2,1,0:T(1,128)}), s32[4,1,16]{2,1,0:T(1,128)S(1)}, u32[]{:S(2)}, u32[]{:S(2)}) %all-to-all-start) | async-done | bytes 288 | tf_op jit(solution)/shard_map/all_to_all | solution.py:29
  12.6 0.7 reshape.205
  13.3 3.3 %all-to-all-start.1 = ((f32[4,1,1024]{2,1,0:T(1,128)}), f32[4,1,1024]{2,1,0:T(1,128)S(1)}, u32[]{:S(2)}, u32[]{:S(2)}) async-start(f32[4,1,1024]{2,1,0:T(1,128)} %reshape.205), calls=%async_computation.1 | async-start | bytes 32768 | tf_op jit(solution)/shard_map/all_to_all | solution.py:39
  16.6 0.7 fusion.22
  17.3 2.0 %reshape.154 = f32[4,16,64,64]{3,2,1,0:T(8,128)S(1)} reshape(f32[1,1,4,16,4096]{4,3,2,1,0:T(8,128)} %param.10) | data formatting | bytes 2097152 | tf_op jit(solution)/shard_map/reshape | solution.py:19
  19.5 2.7 %all-to-all-done.1 = f32[4,1,1024]{2,1,0:T(1,128)S(1)} async-done(((f32[4,1,1024]{2,1,0:T(1,128)}), f32[4,1,1024]{2,1,0:T(1,128)S(1)}, u32[]{:S(2)}, u32[]{:S(2)}) %all-to-all-start.1) | async-done | bytes 16416 | tf_op jit(solution)/shard_map/all_to_all | solution.py:39
  22.2 0.6 broadcast.88
  22.8 0.7 reduce.13
  23.6 3.4 %fusion.24 = f32[4,16,1,64]{3,2,1,0:T(1,128)S(1)} fusion(f32[4,16,64,1]{2,3,1,0:T(1,128)S(1)} %bitcast.58, f32[4,16,64,64]{3,2,1,0:T(8,128)S(1)} %reshape.154), kind=kOutput, calls=%fused_computation.33 | convolution fusion | flops 3145728 | bytes 1081344 | tf_op jit(solution)/shard_map/ocij,ocj->oci/dot_general | solution.py:47
  27.0 0.3 fusion.1
  27.4 5.7 %psum.14 = f32[1,512]{1,0:T(1,128)S(1)} all-reduce(f32[1,512]{1,0:T(1,128)S(1)} %reshape.156), channel_id=1, replica_groups=mesh['ens'=2,'cell'=4,'win'=4] {'win'}, use_global_device_ids=true, to_apply=%region_0.0 | all-reduce | flops 512 | bytes 4096 | tf_op jit(solution)/shard_map/psum | solution.py:54
  33.4 1.9 %fusion.25 = f32[4,16,1,64]{3,2,1,0:T(1,128)S(1)} fusion(f32[4,16,64,1]{2,3,1,0:T(1,128)S(1)} %bitcast.60, f32[4,16,64,64]{3,2,1,0:T(8,128)S(1)} %reshape.154), kind=kOutput, calls=%fused_computation.34 | convolution fusion | flops 3145728 | bytes 1081344 | tf_op jit(solution)/shard_map/ocij,oci->ocj/dot_general | solution.py:59
  35.3 0.7 reshape.207
  36.0 3.3 %all-to-all-start.2 = ((f32[4,1,1024]{2,1,0:T(1,128)}), f32[4,1,1024]{2,1,0:T(1,128)S(1)}, u32[]{:S(2)}, u32[]{:S(2)}) async-start(f32[4,1,1024]{2,1,0:T(1,128)} %reshape.207), calls=%async_computation.2 | async-start | bytes 32768 | tf_op jit(solution)/shard_map/all_to_all | solution.py:62
  39.3 0.5 broadcast.86
  39.8 0.7 reduce.10
  40.5 4.3 %all-to-all-done.2 = f32[4,1,1024]{2,1,0:T(1,128)S(1)} async-done(((f32[4,1,1024]{2,1,0:T(1,128)}), f32[4,1,1024]{2,1,0:T(1,128)S(1)}, u32[]{:S(2)}, u32[]{:S(2)}) %all-to-all-start.2) | async-done | bytes 16416 | tf_op jit(solution)/shard_map/all_to_all | solution.py:62
  44.9 0.7 reduce.14
  45.7 0.3 fusion.3
  46.4 8.0 %all_to_all.29 = f32[4,1,1024]{2,1,0:T(1,128)S(1)} all-to-all(f32[4,1,1024]{2,1,0:T(1,128)S(1)} %reshape.209), channel_id=1, replica_groups=mesh['ens'=2,'cell'=4,'win'=4] {'cell'}, dimensions={0} | all-to-all | bytes 32768 | tf_op jit(solution)/shard_map/all_to_all | solution.py:39
  54.4 0.7 reduce.15
  55.2 3.4 %fusion.26 = f32[4,16,1,64]{3,2,1,0:T(1,128)S(1)} fusion(f32[4,16,64,1]{2,3,1,0:T(1,128)S(1)} %bitcast.62, f32[4,16,64,64]{3,2,1,0:T(8,128)S(1)} %reshape.154), kind=kOutput, calls=%fused_computation.35 | convolution fusion | flops 3145728 | bytes 1081344 | tf_op jit(solution)/shard_map/ocij,ocj->oci/dot_general | solution.py:47
  59.0 5.7 %psum.15 = f32[1,512]{1,0:T(1,128)S(1)} all-reduce(f32[1,512]{1,0:T(1,128)S(1)} %reshape.162), channel_id=1, replica_groups=mesh['ens'=2,'cell'=4,'win'=4] {'win'}, use_global_device_ids=true, to_apply=%region_1.0 | all-reduce | flops 512 | bytes 4096 | tf_op jit(solution)/shard_map/psum | solution.py:54
  64.7 0.5 broadcast.87
  65.2 1.2 %fusion.23 = (f32[512]{0:T(512)S(1)}, f32[1,512]{1,0:T(1,128)}) fusion(f32[]{:T(128)} %broadcast.87, f32[1,512]{1,0:T(1,128)S(1)} %copy-done.2, f32[1,512]{1,0:T(1,128)S(1)} %psum.15, f32[1,512]{1,0:T(1,128)S(1)} %copy-done.3), kind=kLoop, calls=%fused_computation.32 | loop fusion | flops 1024 | bytes 10244 | tf_op jit(solution)/shard_map/mul | solution.py:55
  66.7 1.9 %fusion.27 = f32[4,16,1,64]{3,2,1,0:T(1,128)S(1)} fusion(f32[4,16,64,1]{2,3,1,0:T(1,128)S(1)} %bitcast.57, f32[4,16,64,64]{3,2,1,0:T(8,128)S(1)} %reshape.154), kind=kOutput, calls=%fused_computation.36 | convolution fusion | flops 3145728 | bytes 1081344 | tf_op jit(solution)/shard_map/ocij,oci->ocj/dot_general | solution.py:59
  68.7 8.0 %all_to_all.30 = f32[4,1,1024]{2,1,0:T(1,128)S(1)} all-to-all(f32[4,1,1024]{2,1,0:T(1,128)S(1)} %reshape.211), channel_id=1, replica_groups=mesh['ens'=2,'cell'=4,'win'=4] {'cell'}, dimensions={0} | all-to-all | bytes 32768 | tf_op jit(solution)/shard_map/all_to_all | solution.py:62
  76.7 0.7 reduce.16
  77.5 0.3 fusion.2
  77.9 0.6 subtract_subtract_fusion
  (34 shorter events, 2.7 us)
Async XLA Ops:
  0.6 18.7 %copy-start.1 = (s32[1,1,4,16]{3,2,1,0:T(4,128)S(1)}, s32[1,1,4,16]{3,2,1,0:T(4,128)}, u32[]{:S(2)}) copy-start(s32[1,1,4,16]{3,2,1,0:T(4,128)} %param.12) | copy-start | bytes 772
  0.6 11.8 %all-to-all-start = ((s32[4,1,16]{2,1,0:T(1,128)}), s32[4,1,16]{2,1,0:T(1,128)S(1)}, u32[]{:S(2)}, u32[]{:S(2)}) async-start(s32[4,1,16]{2,1,0:T(1,128)} %bitcast.72), calls=%async_computation | async-start | bytes 4096 | tf_op jit(solution)/shard_map/all_to_all | solution.py:29
  13.3 8.8 %all-to-all-start.1 = ((f32[4,1,1024]{2,1,0:T(1,128)}), f32[4,1,1024]{2,1,0:T(1,128)S(1)}, u32[]{:S(2)}, u32[]{:S(2)}) async-start(f32[4,1,1024]{2,1,0:T(1,128)} %reshape.205), calls=%async_computation.1 | async-start | bytes 32768 | tf_op jit(solution)/shard_map/all_to_all | solution.py:39
  17.3 15.7 %copy-start.2 = (f32[1,512]{1,0:T(1,128)S(1)}, f32[1,512]{1,0:T(1,128)}, u32[]{:S(2)}) copy-start(f32[1,512]{1,0:T(1,128)} %param.9) | copy-start | bytes 6148
  17.3 15.7 %copy-start.3 = (f32[1,512]{1,0:T(1,128)S(1)}, f32[1,512]{1,0:T(1,128)}, u32[]{:S(2)}) copy-start(f32[1,512]{1,0:T(1,128)} %param.8) | copy-start | bytes 6148
  23.6 22.4 %copy-start = (f32[8,512]{1,0:T(8,128)S(1)}, f32[8,512]{1,0:T(8,128)}, u32[]{:S(2)}) copy-start(f32[8,512]{1,0:T(8,128)} %param.7) | copy-start | bytes 49156
  36.0 8.8 %all-to-all-start.2 = ((f32[4,1,1024]{2,1,0:T(1,128)}), f32[4,1,1024]{2,1,0:T(1,128)S(1)}, u32[]{:S(2)}, u32[]{:S(2)}) async-start(f32[4,1,1024]{2,1,0:T(1,128)} %reshape.207), calls=%async_computation.2 | async-start | bytes 32768 | tf_op jit(solution)/shard_map/all_to_all | solution.py:62
where the time goes:
time: 79.1 us; the launch traced here: 78.5 us
  blocking collectives  27.2 us (34%)
  starting transfers between devices  12.8 us (16%)
  matrix products  12.4 us (16%)
  waiting for transfers between devices  11.7 us (15%)
  local copies, waits for them, and re-layouts  7.07 us (9%)
  other arithmetic  6.5 us (8%)
    psum x2, blocking collectives, local(): modeled = lax.psum(block_sums, 'win')  11.3 us
    all_to_all x1, blocking collectives, local(): lax.all_to_all(served.reshape(owner_count, capacity, CB), 'cell', split_a...  7.96 us
    all_to_all x1, blocking collectives, local(): lax.all_to_all(returned, 'cell', split_axis=0, concat_axis=0, tiled=True)  7.96 us
    dot_general x2, matrix products, local(): jnp.einsum('ocij,ocj->oci', matrices, selected, precision=lax.Precision.H...  6.71 us
    all_to_all x1, starting transfers between devices, local(): lax.all_to_all(targets, 'cell', split_axis=0, concat_axis=0, tiled=True)  6.33 us
    all_to_all x1, waiting for transfers between devices, local(): lax.all_to_all(targets, 'cell', split_axis=0, concat_axis=0, tiled=True)  4.68 us
    all_to_all x1, waiting for transfers between devices, local(): lax.all_to_all(returned, 'cell', split_axis=0, concat_axis=0, tiled=True)  4.32 us
    dot_general x2, matrix products, local(): jnp.einsum('ocij,oci->ocj', matrices, picked, precision=lax.Precision.HIG...  3.73 us
  transfers between devices with their start and end apart: 3, of which 3 were waited for; matrix products, arithmetic and copies ran while one was open for 6% of the time, Pallas kernels for 0%

commit v1 on v0

v1 whole, which is shorter than its diff:
```python
import jax
import jax.numpy as jnp
from jax import lax
from jax.sharding import PartitionSpec as P

CB = 64
OB = 64
CBLK_DEV = 8
WIN_DEV = 8
OBLK_DEV = 8

HI = lax.Precision.HIGHEST


def local(prior_flux, observed, obs_weight, footprint, flux_slot, obs_slot, slot_count):
    owners = footprint.shape[2]
    capacity = footprint.shape[3]
    slots = owners * capacity
    blocks = WIN_DEV * CBLK_DEV
    live = (
        lax.broadcasted_iota(jnp.int32, (owners, capacity), 1)
        < slot_count.reshape(owners, 1)
    ).astype(jnp.float32)
    matrices = footprint.reshape(owners, capacity, OB, CB)
    obs_pick = (
        obs_slot.reshape(slots, 1) == lax.broadcasted_iota(jnp.int32, (1, OBLK_DEV), 1)
    ).astype(jnp.float32) * live.reshape(slots, 1)
    flux_pick = (
        flux_slot.reshape(owners, capacity, 1)
        == lax.broadcasted_iota(jnp.int32, (1, 1, blocks), 2)
    ).astype(jnp.float32)

    def forward(flux):
        selected = jnp.einsum("ocb,obj->ocj", flux_pick, flux, precision=HI)
        value = jnp.einsum("ocij,ocj->oci", matrices, selected, precision=HI)
        sums = jnp.dot(obs_pick.T, value.reshape(slots, OB), precision=HI)
        return lax.psum(sums.reshape(1, OBLK_DEV * OB), "win")

    def adjoint(departure):
        picked = jnp.dot(obs_pick, departure.reshape(OBLK_DEV, OB), precision=HI)
        picked = picked.reshape(owners, capacity, OB)
        returned = jnp.einsum("ocij,oci->ocj", matrices, picked, precision=HI)
        return jnp.einsum("ocb,ocj->obj", flux_pick, returned, precision=HI)

    flux = lax.all_gather(prior_flux.reshape(blocks, CB), "cell")
    model0 = forward(flux)
    departure0 = obs_weight * (model0 - observed)
    adjoint0 = lax.psum(adjoint(departure0), "cell")
    model1 = forward(flux - 0.5 * adjoint0)
    departure1 = obs_weight * (model1 - observed)
    increment = lax.psum_scatter(
        adjoint(-0.25 * departure0 - 0.5 * departure1), "cell", scatter_dimension=0
    )
    return increment.reshape(WIN_DEV, CBLK_DEV * CB), departure1


def solution(mesh):
    placed = (
        P(("ens", "win"), "cell"),
        P(("ens", "cell"), None),
        P(("ens", "cell"), None),
        P("cell", "win", None, None, None),
        P("cell", "win", None, None),
        P("cell", "win", None, None),
        P("cell", "win", None),
    )
    return jax.shard_map(
        local,
        mesh=mesh,
        in_specs=placed,
        out_specs=(P(("ens", "win"), "cell"), P(("ens", "cell"), None)),
        check_vma=False,
    )
```

time: 79.1 us -> 119 us (1.50)
  waiting for transfers between devices: 11.7 us -> 55.4 us
  between operations: 0.77 us -> 14.1 us
  starting transfers between devices: 12.8 us -> 0.08 us
  other arithmetic: 6.5 us -> 2.21 us
  matrix products: 12.4 us -> 14.7 us
  local copies, waits for them, and re-layouts: 7.07 us -> 5.43 us
    psum x0 -> x1, waiting for transfers between devices: none -> 36.1 us  [local(): adjoint0 = lax.psum(adjoint(departure0), 'cell')]
    reduce_scatter x0 -> x1, waiting for transfers between devices: none -> 19.2 us  [local(): lax.psum_scatter(adjoint(-0.25 * departure0 - 0.5 * departure1), 'cell',...]
    all_to_all x2 -> x0, blocking collectives: 15.9 us -> none  [the longest x1 7.96 us: local(): lax.all_to_all(served.reshape(owner_count, capacity, CB), 'cell', split_a...]
    all_gather x0 -> x1, blocking collectives: none -> 15 us  [local(): flux = lax.all_gather(prior_flux.reshape(blocks, CB), 'cell')]
    all_to_all x3 -> x0, starting transfers between devices: 12.8 us -> none  [the longest x1 6.33 us: local(): lax.all_to_all(targets, 'cell', split_axis=0, concat_axis=0, tiled=True)]
    all_to_all x3 -> x0, waiting for transfers between devices: 11.7 us -> none  [the longest x1 4.68 us: local(): lax.all_to_all(targets, 'cell', split_axis=0, concat_axis=0, tiled=True)]
    all_to_all x5 -> x0, other arithmetic: 3.6 us -> none  [the longest x2 1.47 us: local(): lax.all_to_all(returned, 'cell', split_axis=0, concat_axis=0, tiled=True)]
    dot_general x12, matrix products: 12.4 us -> 14.7 us  [the longest x2 6.71 us: forward(): value = jnp.einsum('ocij,ocj->oci', matrices, selected, precision=HI)]
  transfers between devices with their start and end apart: 3 -> 2, of which waited for: 3 -> 2; matrix products, arithmetic and copies ran while one was open for 6% -> 0% of each run, Pallas kernels for 0% -> 0%
where the time goes in v1:
time: 119 us; the launch traced here: 118 us
  waiting for transfers between devices  55.4 us (47%)
  blocking collectives  26.4 us (22%)
  matrix products  14.7 us (12%)
  between operations  14.1 us (12%)
  local copies, waits for them, and re-layouts  5.43 us (5%)
  other arithmetic  2.21 us (2%)
    psum x1, waiting for transfers between devices, local(): adjoint0 = lax.psum(adjoint(departure0), 'cell')  36.1 us
    reduce_scatter x1, waiting for transfers between devices, local(): lax.psum_scatter(adjoint(-0.25 * departure0 - 0.5 * departure1), 'cell',...  19.2 us
    all_gather x1, blocking collectives, local(): flux = lax.all_gather(prior_flux.reshape(blocks, CB), 'cell')  15 us
    psum x2, blocking collectives, forward(): return lax.psum(sums.reshape(1, OBLK_DEV * OB), 'win')  11.3 us
    dot_general x2, matrix products, forward(): value = jnp.einsum('ocij,ocj->oci', matrices, selected, precision=HI)  6.71 us
    dot_general x2, matrix products, adjoint(): returned = jnp.einsum('ocij,oci->ocj', matrices, picked, precision=HI)  3.71 us
  transfers between devices with their start and end apart: 2, of which 2 were waited for; matrix products, arithmetic and copies ran while one was open for 0% of the time, Pallas kernels for 0%

profile of v1, /device:TPU:0, one launch (start us, length us, event | category | flops | bytes accessed | tf_op | source)
XLA Modules:
  0.0 118.3 jit_solution(7783633400833529826)
XLA Ops:
  7.2 0.0 all-reduce.2.cloned.1.call-start
  7.2 0.8 eq.65
  8.0 0.7 fusion.21
  8.7 0.1 reshape.110
  8.8 0.9 compare_select_fusion
  9.7 0.8 all_gather_reshape.3
  10.5 15.0 %all_gather.3 = f32[4,64,64]{2,1,0:T(8,128)S(1)} all-gather(f32[1,64,64]{2,1,0:T(8,128)S(1)} %all_gather_reshape.3), channel_id=1, replica_groups=mesh['ens'=2,'cell'=4,'win'=4] {'cell'}, dimensions={0}, use_global_device_ids=true | all-gather | bytes 81920 | tf_op jit(solution)/shard_map/all_gather | solution.py:45
  25.5 2.0 %reshape.103 = f32[4,16,64,64]{3,2,1,0:T(8,128)S(1)} reshape(f32[1,1,4,16,4096]{4,3,2,1,0:T(8,128)} %param.10) | data formatting | bytes 2097152 | tf_op jit(solution)/shard_map/reshape | solution.py:24
  27.6 0.2 fusion.10
  27.8 3.4 %fusion.26 = f32[4,16,1,64]{3,2,1,0:T(1,128)S(1)} fusion(f32[4,16,64,1]{2,3,1,0:T(1,128)S(1)} %bitcast.54, f32[4,16,64,64]{3,2,1,0:T(8,128)S(1)} %reshape.103), kind=kOutput, calls=%fused_computation.33 | convolution fusion | flops 3145728 | bytes 1081344 | tf_op jit(solution)/shard_map/ocij,ocj->oci/dot_general | solution.py:35
  31.2 0.3 fusion.6
  31.4 0.1 reshape.105
  31.5 5.7 %psum.21 = f32[1,512]{1,0:T(1,128)S(1)} all-reduce(f32[1,512]{1,0:T(1,128)S(1)} %reshape.105), channel_id=1, replica_groups=mesh['ens'=2,'cell'=4,'win'=4] {'win'}, use_global_device_ids=true, to_apply=%region_0.0 | all-reduce | flops 512 | bytes 4096 | tf_op jit(solution)/shard_map/psum | solution.py:37
  37.2 0.1 reshape.113
  37.3 0.2 fusion.27
  37.4 1.9 %fusion.28 = f32[4,16,1,64]{3,2,1,0:T(1,128)S(1)} fusion(f32[4,16,64,1]{2,3,1,0:T(1,128)S(1)} %bitcast.51, f32[4,16,64,64]{3,2,1,0:T(8,128)S(1)} %reshape.103), kind=kOutput, calls=%fused_computation.35 | convolution fusion | flops 3145728 | bytes 1081344 | tf_op jit(solution)/shard_map/ocij,oci->ocj/dot_general | solution.py:42
  39.3 1.0 fusion.9
  40.3 0.0 all-reduce.2.cloned.1.call-update
  40.3 0.0 reduce-scatter.2.cloned.1.call-start
  40.4 36.1 %all-reduce.2.cloned.1.call-done = f32[4,64,64]{2,1,0:T(8,128)} async-done(((f32[4,64,64]{2,1,0:T(8,128)}), f32[4,64,64]{2,1,0:T(8,128)}) %all-reduce.2.cloned.1.call-update) | async-done | bytes 65552 | tf_op jit(solution)/shard_map/psum | solution.py:48
  76.5 1.1 fusion
  77.7 3.4 %fusion.29 = f32[4,16,1,64]{3,2,1,0:T(1,128)S(1)} fusion(f32[4,16,64,1]{2,3,1,0:T(1,128)S(1)} %bitcast.49, f32[4,16,64,64]{3,2,1,0:T(8,128)S(1)} %reshape.103), kind=kOutput, calls=%fused_computation.36 | convolution fusion | flops 3145728 | bytes 1081344 | tf_op jit(solution)/shard_map/ocij,ocj->oci/dot_general | solution.py:35
  81.0 0.3 fusion.4
  81.3 0.1 reshape.108
  81.4 5.7 %psum.23 = f32[1,512]{1,0:T(1,128)S(1)} all-reduce(f32[1,512]{1,0:T(1,128)S(1)} %reshape.108), channel_id=1, replica_groups=mesh['ens'=2,'cell'=4,'win'=4] {'win'}, use_global_device_ids=true, to_apply=%region_2.0 | all-reduce | flops 512 | bytes 4096 | tf_op jit(solution)/shard_map/psum | solution.py:37
  87.0 0.6 subtract_reduce_fusion
  87.6 0.1 reshape.118
  87.7 0.2 fusion.30
  87.9 1.9 %fusion.31 = f32[4,16,1,64]{3,2,1,0:T(1,128)S(1)} fusion(f32[4,16,64,1]{2,3,1,0:T(1,128)S(1)} %bitcast.50, f32[4,16,64,64]{3,2,1,0:T(8,128)S(1)} %reshape.103), kind=kOutput, calls=%fused_computation.38 | convolution fusion | flops 3145728 | bytes 1081344 | tf_op jit(solution)/shard_map/ocij,oci->ocj/dot_general | solution.py:42
  89.7 1.0 fusion.8
  90.7 19.2 %reduce-scatter.2.cloned.1.call-done = f32[1,64,64]{2,1,0:T(8,128)} async-done(((f32[4,64,64]{2,1,0:T(8,128)}), f32[1,64,64]{2,1,0:T(8,128)}) %reduce-scatter.2.cloned.1.call-update) | async-done | bytes 16400 | tf_op jit(solution)/shard_map/reduce_scatter | solution.py:51
  110.0 1.4 %reshape_reduce_scatter.3 = f32[8,512]{1,0:T(8,128)} reshape(f32[1,64,64]{2,1,0:T(8,128)} %reduce-scatter.2.cloned.1.call-done) | data formatting | bytes 32768 | tf_op jit(solution)/shard_map/reshape;reduce_scatter | solution.py:54
  (8 shorter events, 0.0 us)
Async XLA Ops:
  7.2 20.4 %copy-start = (s32[1,1,4,16]{3,2,1,0:T(4,128)S(1)}, s32[1,1,4,16]{3,2,1,0:T(4,128)}, u32[]{:S(2)}) copy-start(s32[1,1,4,16]{3,2,1,0:T(4,128)} %param.11) | copy-start | bytes 772
  7.2 69.3 %all-reduce.2.cloned.1.call-start = ((), (), s32[]{:S(2)}) async-start(), calls=%async_computation.1 | async-start | bytes 262144 | tf_op jit(solution)/shard_map/psum | solution.py:48
  25.5 11.6 %copy-start.1 = (f32[1,512]{1,0:T(1,128)S(1)}, f32[1,512]{1,0:T(1,128)}, u32[]{:S(2)}) copy-start(f32[1,512]{1,0:T(1,128)} %param.9) | copy-start | bytes 6148
  25.5 11.6 %copy-start.2 = (f32[1,512]{1,0:T(1,128)S(1)}, f32[1,512]{1,0:T(1,128)}, u32[]{:S(2)}) copy-start(f32[1,512]{1,0:T(1,128)} %param.8) | copy-start | bytes 6148
  40.3 69.6 %reduce-scatter.2.cloned.1.call-start = ((), (), s32[]{:S(2)}) async-start(), calls=%async_computation.2 | async-start | bytes 163840 | tf_op jit(solution)/shard_map/reduce_scatter | solution.py:51
Sparse Core Ops, SparseCore 0:
  40.5 36.0 all-reduce.1
  90.9 19.0 reduce-scatter.1

commit v2 on v1

v2 whole, which is shorter than its diff:
```python
import jax
import jax.numpy as jnp
from jax import lax
from jax.sharding import PartitionSpec as P

CB = 64
OB = 64
CBLK_DEV = 8
WIN_DEV = 8
OBLK_DEV = 8

HI = lax.Precision.HIGHEST


def others(value, axis, size):
    return [
        lax.ppermute(value, axis, [(i, (i + k) % size) for i in range(size)])
        for k in range(1, size)
    ]


def make_local(cells, wins):
    def local(prior_flux, observed, obs_weight, footprint, flux_slot, obs_slot, slot_count):
        owners = footprint.shape[2]
        capacity = footprint.shape[3]
        slots = owners * capacity
        blocks = WIN_DEV * CBLK_DEV
        me = lax.axis_index("cell")
        live = (
            lax.broadcasted_iota(jnp.int32, (owners, capacity), 1)
            < slot_count.reshape(owners, 1)
        ).astype(jnp.float32)
        matrices = footprint.reshape(owners, capacity, OB, CB)
        obs_pick = (
            obs_slot.reshape(slots, 1) == lax.broadcasted_iota(jnp.int32, (1, OBLK_DEV), 1)
        ).astype(jnp.float32) * live.reshape(slots, 1)
        owner_of = lax.broadcasted_iota(jnp.int32, (owners, capacity), 0)
        my_target = (owner_of * blocks + flux_slot.reshape(owners, capacity)).reshape(slots)

        def forward_part(selected):
            value = jnp.einsum("sij,sj->si", matrices.reshape(slots, OB, CB), selected, precision=HI)
            return jnp.dot(obs_pick.T, value, precision=HI).reshape(1, OBLK_DEV * OB)

        def adjoint(departure):
            picked = jnp.dot(obs_pick, departure.reshape(OBLK_DEV, OB), precision=HI)
            return jnp.einsum("sij,si->sj", matrices.reshape(slots, OB, CB), picked, precision=HI)

        flux_parts = [prior_flux] + others(prior_flux, "cell", cells)
        targets = jnp.concatenate([my_target] + others(my_target, "cell", cells))
        flux = jnp.concatenate([part.reshape(blocks, CB) for part in flux_parts])
        ring_target = (
            lax.rem(me - my_target // blocks + cells, cells) * blocks + my_target % blocks
        )
        pick = (
            ring_target[:, None]
            == lax.broadcasted_iota(jnp.int32, (1, cells * blocks), 1)
        ).astype(jnp.float32)
        selected0 = jnp.dot(pick, flux, precision=HI)
        part0 = forward_part(selected0)
        model0 = lax.psum(part0, "win")
        departure0 = obs_weight * (model0 - observed)
        returned0 = adjoint(departure0)
        all_returned = jnp.concatenate([returned0] + others(returned0, "cell", cells))
        match = (my_target[:, None] == targets[None, :]).astype(jnp.float32)
        selected1 = selected0 - 0.5 * jnp.dot(match, all_returned, precision=HI)
        part1 = forward_part(selected1)
        model1 = sum(others(part1, "win", wins), part1)
        departure1 = obs_weight * (model1 - observed)
        returned1 = adjoint(-0.25 * departure0 - 0.5 * departure1).reshape(owners, capacity, CB)
        pieces = [lax.dynamic_index_in_dim(returned1, me, 0, keepdims=False)]
        for k in range(1, cells):
            piece = lax.dynamic_index_in_dim(returned1, lax.rem(me + k, cells), 0, keepdims=False)
            pieces.append(
                lax.ppermute(piece, "cell", [(i, (i + k) % cells) for i in range(cells)])
            )
        mine = lax.dynamic_index_in_dim(
            targets.reshape(cells, owners, capacity), me, 1, keepdims=False
        ).reshape(cells * capacity) - me * blocks
        scatter = (
            mine[None, :] == lax.broadcasted_iota(jnp.int32, (blocks, 1), 0)
        ).astype(jnp.float32)
        increment = jnp.dot(scatter, jnp.concatenate(pieces), precision=HI)
        return increment.reshape(WIN_DEV, CBLK_DEV * CB), departure1

    return local


def solution(mesh):
    placed = (
        P(("ens", "win"), "cell"),
        P(("ens", "cell"), None),
        P(("ens", "cell"), None),
        P("cell", "win", None, None, None),
        P("cell", "win", None, None),
        P("cell", "win", None, None),
        P("cell", "win", None),
    )
    return jax.shard_map(
        make_local(mesh.shape["cell"], mesh.shape["win"]),
        mesh=mesh,
        in_specs=placed,
        out_specs=(P(("ens", "win"), "cell"), P(("ens", "cell"), None)),
        check_vma=False,
    )
```

time: 119 us -> 56.4 us (0.47)
  waiting for transfers between devices: 55.4 us -> 10.9 us
  blocking collectives: 26.4 us -> 5.66 us
  starting transfers between devices: 0.08 us -> 19.8 us
  between operations: 14.1 us -> 0.75 us
  matrix products: 14.7 us -> 12 us
    psum x1 -> x0, waiting for transfers between devices: 36.1 us -> none  [local(): adjoint0 = lax.psum(adjoint(departure0), 'cell')]
    ppermute x0 -> x15, starting transfers between devices: none -> 19.8 us  [the longest x12 16.6 us: others(): lax.ppermute(value, axis, [(i, (i + k) % size) for i in range(size)])]
    reduce_scatter x1 -> x0, waiting for transfers between devices: 19.2 us -> none  [local(): lax.psum_scatter(adjoint(-0.25 * departure0 - 0.5 * departure1), 'cell',...]
    all_gather x1 -> x0, blocking collectives: 15 us -> none  [local(): flux = lax.all_gather(prior_flux.reshape(blocks, CB), 'cell')]
    ppermute x0 -> x15, waiting for transfers between devices: none -> 10.9 us  [the longest x12 7.82 us: others(): lax.ppermute(value, axis, [(i, (i + k) % size) for i in range(size)])]
    psum x2 -> x1, blocking collectives: 11.3 us -> 5.66 us  [local(): model0 = lax.psum(part0, 'win')]
    dot_general x10 -> x9, matrix products: 14.4 us -> 11.6 us  [the longest x2 6.71 us: forward_part(): jnp.einsum('sij,sj->si', matrices.reshape(slots, OB, CB), selected, preci...]
    reshape x3 -> x8, local copies, waits for them, and re-layouts: 2.18 us -> 2.61 us  [the longest x4 1.01 us: local(): flux = jnp.concatenate([part.reshape(blocks, CB) for part in flux_parts])]
  transfers between devices with their start and end apart: 2 -> 15, of which waited for: 2 -> 8; matrix products, arithmetic and copies ran while one was open for 0% -> 20% of each run, Pallas kernels for 0% -> 0%
where the time goes in v2:
time: 56.4 us; the launch traced here: 56.1 us
  starting transfers between devices  19.8 us (35%)
  matrix products  12 us (21%)
  waiting for transfers between devices  10.9 us (19%)
  blocking collectives  5.66 us (10%)
  local copies, waits for them, and re-layouts  5.45 us (10%)
  other arithmetic  1.53 us (3%)
  between operations  0.75 us (1%)
    ppermute x12, starting transfers between devices, others(): lax.ppermute(value, axis, [(i, (i + k) % size) for i in range(size)])  16.6 us
    ppermute x12, waiting for transfers between devices, others(): lax.ppermute(value, axis, [(i, (i + k) % size) for i in range(size)])  7.82 us
    dot_general x2, matrix products, forward_part(): jnp.einsum('sij,sj->si', matrices.reshape(slots, OB, CB), selected, preci...  6.71 us
    psum x1, blocking collectives, local(): model0 = lax.psum(part0, 'win')  5.66 us
    dot_general x2, matrix products, adjoint(): jnp.einsum('sij,si->sj', matrices.reshape(slots, OB, CB), picked, precisi...  3.71 us
    ppermute x3, starting transfers between devices, local(): lax.ppermute(piece, 'cell', [(i, (i + k) % cells) for i in range(cells)])  3.2 us
    ppermute x3, waiting for transfers between devices, local(): lax.ppermute(piece, 'cell', [(i, (i + k) % cells) for i in range(cells)])  3.07 us
    another operation x1, local copies, waits for them, and re-layouts, adjoint(): matrices.reshape(slots, OB, CB)  2 us
  transfers between devices with their start and end apart: 15, of which 8 were waited for; matrix products, arithmetic and copies ran while one was open for 20% of the time, Pallas kernels for 0%

profile of v2, /device:TPU:0, one launch (start us, length us, event | category | flops | bytes accessed | tf_op | source)
XLA Modules:
  0.0 56.1 jit_solution(12457619019633260017)
XLA Ops:
  0.6 5.1 %collective-permute-start.5 = (f32[8,512]{1,0:T(8,128)}, f32[8,512]{1,0:T(8,128)S(1)}, u32[]{:S(2)}, u32[]{:S(2)}) collective-permute-start(f32[8,512]{1,0:T(8,128)} %param.7), channel_id=1, source_target_pairs={{0,12},{4,0},{8,4},{12,8},{1,13},{5,1},{9,5},{13,9},{2,14},{6,2},{... | collective-permute-start | bytes 49160 | tf_op jit(solution)/shard_map/ppermute | solution.py:17
  5.7 1.0 %collective-permute-start.3 = (f32[8,512]{1,0:T(8,128)}, f32[8,512]{1,0:T(8,128)S(1)}, u32[]{:S(2)}, u32[]{:S(2)}) collective-permute-start(f32[8,512]{1,0:T(8,128)} %param.7), channel_id=1, source_target_pairs={{0,4},{4,8},{8,12},{12,0},{1,5},{5,9},{9,13},{13,1},{2,6},{6,10},{... | collective-permute-start | bytes 49160 | tf_op jit(solution)/shard_map/ppermute | solution.py:17
  6.9 0.8 %reshape.158 = s32[64]{0:T(128)S(1)} reshape(s32[1,1,4,16]{3,2,1,0:T(4,128)} %param.11) | data formatting | bytes 512 | tf_op jit(solution)/shard_map/reshape | solution.py:38
  7.7 2.9 %collective-permute-start.2 = (s32[64]{0:T(128)S(1)}, s32[64]{0:T(128)S(1)}, u32[]{:S(2)}, u32[]{:S(2)}) collective-permute-start(s32[64]{0:T(128)S(1)} %get-tuple-element.5), channel_id=1, source_target_pairs={{0,12},{4,0},{8,4},{12,8},{1,13},{5,1},{9,5},{13,9},{2,14},{6,2},{... | collective-permute-start | bytes 776 | tf_op jit(solution)/shard_map/ppermute | solution.py:17
  10.6 1.1 %collective-permute-start.1 = (s32[64]{0:T(128)S(1)}, s32[64]{0:T(128)S(1)}, u32[]{:S(2)}, u32[]{:S(2)}) collective-permute-start(s32[64]{0:T(128)S(1)} %get-tuple-element.5), channel_id=1, source_target_pairs={{0,8},{4,12},{8,0},{12,4},{1,9},{5,13},{9,1},{13,5},{2,10},{6,14},... | collective-permute-start | bytes 776 | tf_op jit(solution)/shard_map/ppermute | solution.py:17
  11.7 0.7 %fusion.52 = f32[4,16]{1,0:T(4,128)S(1)} fusion(s32[4]{0:T(128)} %bitcast.58), kind=kLoop, calls=%fused_computation.72 | loop fusion | flops 128 | bytes 272 | tf_op jit(solution)/shard_map/convert_element_type | solution.py:32
  12.4 0.8 %reshape.159 = f32[64,64]{1,0:T(8,128)S(1)} reshape(f32[8,512]{1,0:T(8,128)} %param.7) | data formatting | bytes 32768 | tf_op jit(solution)/shard_map/reshape | solution.py:50
  13.2 2.0 %reshape_reshape.2 = f32[64,64,64]{2,1,0:T(8,128)S(1)} reshape(f32[1,1,4,16,4096]{4,3,2,1,0:T(8,128)} %param.10) | data formatting | bytes 2097152 | tf_op jit(solution)/shard_map/reshape;reshape | solution.py:46
  15.9 3.4 %fusion.64 = f32[64,1,64]{2,1,0:T(1,128)S(1)} fusion(f32[64,64,1]{1,2,0:T(1,128)S(1)} %bitcast.48, f32[64,64,64]{2,1,0:T(8,128)S(1)} %reshape_reshape.2), kind=kOutput, calls=%fused_computation.91 | convolution fusion | flops 3145728 | bytes 1081344 | tf_op jit(solution)/shard_map/sij,sj->si/dot_general | solution.py:41
  19.2 0.3 fusion.23
  19.6 5.7 %psum.7 = f32[1,512]{1,0:T(1,128)S(1)} all-reduce(f32[1,512]{1,0:T(1,128)S(1)} %reshape.163), channel_id=1, replica_groups=mesh['ens'=2,'cell'=4,'win'=4] {'win'}, use_global_device_ids=true, to_apply=%region_0.1 | all-reduce | flops 512 | bytes 4096 | tf_op jit(solution)/shard_map/psum | solution.py:60
  25.4 0.2 fusion.21
  25.6 1.9 %fusion.65 = f32[64,1,64]{2,1,0:T(1,128)S(1)} fusion(f32[64,64,1]{1,2,0:T(1,128)S(1)} %bitcast.55, f32[64,64,64]{2,1,0:T(8,128)S(1)} %reshape_reshape.2), kind=kOutput, calls=%fused_computation.92 | convolution fusion | flops 3145728 | bytes 1081344 | tf_op jit(solution)/shard_map/sij,si->sj/dot_general | solution.py:46
  27.4 3.9 %collective-permute-start.8 = (f32[64,64]{1,0:T(8,128)S(1)}, f32[64,64]{1,0:T(8,128)S(1)}, u32[]{:S(2)}, u32[]{:S(2)}) collective-permute-start(f32[64,64]{1,0:T(8,128)S(1)} %bitcast.49), channel_id=1, source_target_pairs={{0,12},{4,0},{8,4},{12,8},{1,13},{5,1},{9,5},{13,9},{2,14},{6,2},{... | collective-permute-start | bytes 49160 | tf_op jit(solution)/shard_map/ppermute | solution.py:17
  31.3 0.6 %collective-permute-start.6 = (f32[64,64]{1,0:T(8,128)S(1)}, f32[64,64]{1,0:T(8,128)S(1)}, u32[]{:S(2)}, u32[]{:S(2)}) collective-permute-start(f32[64,64]{1,0:T(8,128)S(1)} %bitcast.51), channel_id=1, source_target_pairs={{0,4},{4,8},{8,12},{12,0},{1,5},{5,9},{9,13},{13,1},{2,6},{6,10},{... | collective-permute-start | bytes 49160 | tf_op jit(solution)/shard_map/ppermute | solution.py:17
  32.0 0.9 %collective-permute-done.8 = f32[64,64]{1,0:T(8,128)S(1)} collective-permute-done((f32[64,64]{1,0:T(8,128)S(1)}, f32[64,64]{1,0:T(8,128)S(1)}, u32[]{:S(2)}, u32[]{:S(2)}) %collective-permute-start.8) | collective-permute-done | bytes 16416 | tf_op jit(solution)/shard_map/ppermute | solution.py:17
  32.9 3.2 %collective-permute-done.7 = f32[64,64]{1,0:T(8,128)S(1)} collective-permute-done((f32[64,64]{1,0:T(8,128)S(1)}, f32[64,64]{1,0:T(8,128)S(1)}, u32[]{:S(2)}, u32[]{:S(2)}) %collective-permute-start.7) | collective-permute-done | bytes 16416 | tf_op jit(solution)/shard_map/ppermute | solution.py:17
  36.1 0.9 %collective-permute-done.6 = f32[64,64]{1,0:T(8,128)S(1)} collective-permute-done((f32[64,64]{1,0:T(8,128)S(1)}, f32[64,64]{1,0:T(8,128)S(1)}, u32[]{:S(2)}, u32[]{:S(2)}) %collective-permute-start.6) | collective-permute-done | bytes 16416 | tf_op jit(solution)/shard_map/ppermute | solution.py:17
  37.3 3.4 %fusion.66 = f32[64,1,64]{2,1,0:T(1,128)S(1)} fusion(f32[64,64,1]{1,2,0:T(1,128)S(1)} %bitcast.53, f32[64,64,64]{2,1,0:T(8,128)S(1)} %reshape_reshape.2), kind=kOutput, calls=%fused_computation.93 | convolution fusion | flops 3145728 | bytes 1081344 | tf_op jit(solution)/shard_map/sij,sj->si/dot_general | solution.py:41
  40.6 0.3 fusion.19
  41.0 1.8 %collective-permute-start.10 = (f32[1,512]{1,0:T(1,128)S(1)}, f32[1,512]{1,0:T(1,128)S(1)}, u32[]{:S(2)}, u32[]{:S(2)}) collective-permute-start(f32[1,512]{1,0:T(1,128)S(1)} %reshape.165), channel_id=1, source_target_pairs={{0,2},{1,3},{2,0},{3,1},{4,6},{5,7},{6,4},{7,5},{8,10},{9,11},{10,... | collective-permute-start | bytes 6152 | tf_op jit(solution)/shard_map/ppermute | solution.py:17
  43.0 1.7 %collective-permute-done.10 = f32[1,512]{1,0:T(1,128)S(1)} collective-permute-done((f32[1,512]{1,0:T(1,128)S(1)}, f32[1,512]{1,0:T(1,128)S(1)}, u32[]{:S(2)}, u32[]{:S(2)}) %collective-permute-start.10) | collective-permute-done | bytes 2080 | tf_op jit(solution)/shard_map/ppermute | solution.py:17
  44.6 1.2 %collective-permute-done.9 = f32[1,512]{1,0:T(1,128)S(1)} collective-permute-done((f32[1,512]{1,0:T(1,128)S(1)}, f32[1,512]{1,0:T(1,128)S(1)}, u32[]{:S(2)}, u32[]{:S(2)}) %collective-permute-start.9) | collective-permute-done | bytes 2080 | tf_op jit(solution)/shard_map/ppermute | solution.py:17
  45.8 0.6 %subtract_reduce_fusion = (f32[512]{0:T(512)S(1)}, f32[1,512]{1,0:T(1,128)}) fusion(f32[1,512]{1,0:T(1,128)S(1)} %copy-done.1, f32[1,512]{1,0:T(1,128)S(1)} %psum.7, f32[1,512]{1,0:T(1,128)S(1)} %copy-done.2, f32[1,512]{1,0:T(1,128)S(1)} %collective-permute-done.11, f32[1,512]{1,0:T(1,128)S(1)} %collective-permute-done.10, f32[1,512]{1,0:T(1,128)S(1)} %reshape.165, ...), kind=kLoop, calls=%fused_computation.67 | loop fusion | flops 5120 | bytes 18432 | tf_op jit(solution)/shard_map/sub | solution.py:69
  46.5 0.2 fusion.17
  46.7 1.9 %fusion.67 = f32[64,1,64]{2,1,0:T(1,128)S(1)} fusion(f32[64,64,1]{1,2,0:T(1,128)S(1)} %bitcast.54, f32[64,64,64]{2,1,0:T(8,128)S(1)} %reshape_reshape.2), kind=kOutput, calls=%fused_computation.94 | convolution fusion | flops 3145728 | bytes 1081344 | tf_op jit(solution)/shard_map/sij,si->sj/dot_general | solution.py:46
  48.6 0.6 %collective-permute-start.14 = (f32[16,64]{1,0:T(8,128)S(1)}, f32[16,64]{1,0:T(8,128)S(1)}, u32[]{:S(2)}, u32[]{:S(2)}) collective-permute-start(f32[16,64]{1,0:T(8,128)S(1)} %get-tuple-element.7), channel_id=1, source_target_pairs={{0,12},{4,0},{8,4},{12,8},{1,13},{5,1},{9,5},{13,9},{2,14},{6,2},{... | collective-permute-start | bytes 12296 | tf_op jit(solution)/shard_map/ppermute | solution.py:74
  49.2 0.6 %collective-permute-start.13 = (f32[16,64]{1,0:T(8,128)S(1)}, f32[16,64]{1,0:T(8,128)S(1)}, u32[]{:S(2)}, u32[]{:S(2)}) collective-permute-start(f32[16,64]{1,0:T(8,128)S(1)} %get-tuple-element.8), channel_id=1, source_target_pairs={{0,8},{4,12},{8,0},{12,4},{1,9},{5,13},{9,1},{13,5},{2,10},{6,14},... | collective-permute-start | bytes 12296 | tf_op jit(solution)/shard_map/ppermute | solution.py:74
  49.8 1.9 %collective-permute-start.12 = (f32[16,64]{1,0:T(8,128)S(1)}, f32[16,64]{1,0:T(8,128)S(1)}, u32[]{:S(2)}, u32[]{:S(2)}) collective-permute-start(f32[16,64]{1,0:T(8,128)S(1)} %get-tuple-element.9), channel_id=1, source_target_pairs={{0,4},{4,8},{8,12},{12,0},{1,5},{5,9},{9,13},{13,1},{2,6},{6,10},{... | collective-permute-start | bytes 12296 | tf_op jit(solution)/shard_map/ppermute | solution.py:74
  52.3 1.5 %collective-permute-done.13 = f32[16,64]{1,0:T(8,128)S(1)} collective-permute-done((f32[16,64]{1,0:T(8,128)S(1)}, f32[16,64]{1,0:T(8,128)S(1)}, u32[]{:S(2)}, u32[]{:S(2)}) %collective-permute-start.13) | collective-permute-done | bytes 4128 | tf_op jit(solution)/shard_map/ppermute | solution.py:74
  53.7 1.5 %collective-permute-done.12 = f32[16,64]{1,0:T(8,128)S(1)} collective-permute-done((f32[16,64]{1,0:T(8,128)S(1)}, f32[16,64]{1,0:T(8,128)S(1)}, u32[]{:S(2)}, u32[]{:S(2)}) %collective-permute-start.12) | collective-permute-done | bytes 4128 | tf_op jit(solution)/shard_map/ppermute | solution.py:74
  55.4 0.7 %reshape.168 = f32[8,512]{1,0:T(8,128)} reshape(f32[64,64]{1,0:T(8,128)S(1)} %fusion.25) | data formatting | bytes 32768 | tf_op jit(solution)/shard_map/reshape | solution.py:83
  (46 shorter events, 2.3 us)
Async XLA Ops:
  0.6 14.7 %copy-start.3 = (s32[1,1,4,16]{3,2,1,0:T(4,128)S(1)}, s32[1,1,4,16]{3,2,1,0:T(4,128)}, u32[]{:S(2)}) copy-start(s32[1,1,4,16]{3,2,1,0:T(4,128)} %param.12) | copy-start | bytes 772
  0.6 14.8 %collective-permute-start.5 = (f32[8,512]{1,0:T(8,128)}, f32[8,512]{1,0:T(8,128)S(1)}, u32[]{:S(2)}, u32[]{:S(2)}) collective-permute-start(f32[8,512]{1,0:T(8,128)} %param.7), channel_id=1, source_target_pairs={{0,12},{4,0},{8,4},{12,8},{1,13},{5,1},{9,5},{13,9},{2,14},{6,2},{... | collective-permute-start | bytes 49160 | tf_op jit(solution)/shard_map/ppermute | solution.py:17
  5.7 9.8 %collective-permute-start.4 = (f32[8,512]{1,0:T(8,128)}, f32[8,512]{1,0:T(8,128)S(1)}, u32[]{:S(2)}, u32[]{:S(2)}) collective-permute-start(f32[8,512]{1,0:T(8,128)} %param.7), channel_id=1, source_target_pairs={{0,8},{4,12},{8,0},{12,4},{1,9},{5,13},{9,1},{13,5},{2,10},{6,14},... | collective-permute-start | bytes 49160 | tf_op jit(solution)/shard_map/ppermute | solution.py:17
  5.7 9.8 %collective-permute-start.3 = (f32[8,512]{1,0:T(8,128)}, f32[8,512]{1,0:T(8,128)S(1)}, u32[]{:S(2)}, u32[]{:S(2)}) collective-permute-start(f32[8,512]{1,0:T(8,128)} %param.7), channel_id=1, source_target_pairs={{0,4},{4,8},{8,12},{12,0},{1,5},{5,9},{9,13},{13,1},{2,6},{6,10},{... | collective-permute-start | bytes 49160 | tf_op jit(solution)/shard_map/ppermute | solution.py:17
  7.7 23.6 %collective-permute-start.2 = (s32[64]{0:T(128)S(1)}, s32[64]{0:T(128)S(1)}, u32[]{:S(2)}, u32[]{:S(2)}) collective-permute-start(s32[64]{0:T(128)S(1)} %get-tuple-element.5), channel_id=1, source_target_pairs={{0,12},{4,0},{8,4},{12,8},{1,13},{5,1},{9,5},{13,9},{2,14},{6,2},{... | collective-permute-start | bytes 776 | tf_op jit(solution)/shard_map/ppermute | solution.py:17
  10.6 21.4 %collective-permute-start.1 = (s32[64]{0:T(128)S(1)}, s32[64]{0:T(128)S(1)}, u32[]{:S(2)}, u32[]{:S(2)}) collective-permute-start(s32[64]{0:T(128)S(1)} %get-tuple-element.5), channel_id=1, source_target_pairs={{0,8},{4,12},{8,0},{12,4},{1,9},{5,13},{9,1},{13,5},{2,10},{6,14},... | collective-permute-start | bytes 776 | tf_op jit(solution)/shard_map/ppermute | solution.py:17
  15.2 10.0 %copy-start.1 = (f32[1,512]{1,0:T(1,128)S(1)}, f32[1,512]{1,0:T(1,128)}, u32[]{:S(2)}) copy-start(f32[1,512]{1,0:T(1,128)} %param.9) | copy-start | bytes 6148
  15.2 10.0 %copy-start.2 = (f32[1,512]{1,0:T(1,128)S(1)}, f32[1,512]{1,0:T(1,128)}, u32[]{:S(2)}) copy-start(f32[1,512]{1,0:T(1,128)} %param.8) | copy-start | bytes 6148
  15.4 16.6 %collective-permute-start = (s32[64]{0:T(128)S(1)}, s32[64]{0:T(128)S(1)}, u32[]{:S(2)}, u32[]{:S(2)}) collective-permute-start(s32[64]{0:T(128)S(1)} %get-tuple-element.5), channel_id=1, source_target_pairs={{0,4},{4,8},{8,12},{12,0},{1,5},{5,9},{9,13},{13,1},{2,6},{6,10},{... | collective-permute-start | bytes 776 | tf_op jit(solution)/shard_map/ppermute | solution.py:17
  27.4 5.5 %collective-permute-start.8 = (f32[64,64]{1,0:T(8,128)S(1)}, f32[64,64]{1,0:T(8,128)S(1)}, u32[]{:S(2)}, u32[]{:S(2)}) collective-permute-start(f32[64,64]{1,0:T(8,128)S(1)} %bitcast.49), channel_id=1, source_target_pairs={{0,12},{4,0},{8,4},{12,8},{1,13},{5,1},{9,5},{13,9},{2,14},{6,2},{... | collective-permute-start | bytes 49160 | tf_op jit(solution)/shard_map/ppermute | solution.py:17
  31.3 4.8 %collective-permute-start.7 = (f32[64,64]{1,0:T(8,128)S(1)}, f32[64,64]{1,0:T(8,128)S(1)}, u32[]{:S(2)}, u32[]{:S(2)}) collective-permute-start(f32[64,64]{1,0:T(8,128)S(1)} %bitcast.50), channel_id=1, source_target_pairs={{0,8},{4,12},{8,0},{12,4},{1,9},{5,13},{9,1},{13,5},{2,10},{6,14},... | collective-permute-start | bytes 49160 | tf_op jit(solution)/shard_map/ppermute | solution.py:17
  31.3 5.7 %collective-permute-start.6 = (f32[64,64]{1,0:T(8,128)S(1)}, f32[64,64]{1,0:T(8,128)S(1)}, u32[]{:S(2)}, u32[]{:S(2)}) collective-permute-start(f32[64,64]{1,0:T(8,128)S(1)} %bitcast.51), channel_id=1, source_target_pairs={{0,4},{4,8},{8,12},{12,0},{1,5},{5,9},{9,13},{13,1},{2,6},{6,10},{... | collective-permute-start | bytes 49160 | tf_op jit(solution)/shard_map/ppermute | solution.py:17
  37.3 14.5 %copy-start = (s32[1,1,4,16]{3,2,1,0:T(4,128)S(1)}, s32[1,1,4,16]{3,2,1,0:T(4,128)}, u32[]{:S(2)}) copy-start(s32[1,1,4,16]{3,2,1,0:T(4,128)} %param.11) | copy-start | bytes 772
  41.0 2.0 %collective-permute-start.11 = (f32[1,512]{1,0:T(1,128)S(1)}, f32[1,512]{1,0:T(1,128)S(1)}, u32[]{:S(2)}, u32[]{:S(2)}) collective-permute-start(f32[1,512]{1,0:T(1,128)S(1)} %reshape.165), channel_id=1, source_target_pairs={{0,3},{1,0},{2,1},{3,2},{4,7},{5,4},{6,5},{7,6},{8,11},{9,8},{10,9... | collective-permute-start | bytes 6152 | tf_op jit(solution)/shard_map/ppermute | solution.py:17
  41.0 3.6 %collective-permute-start.10 = (f32[1,512]{1,0:T(1,128)S(1)}, f32[1,512]{1,0:T(1,128)S(1)}, u32[]{:S(2)}, u32[]{:S(2)}) collective-permute-start(f32[1,512]{1,0:T(1,128)S(1)} %reshape.165), channel_id=1, source_target_pairs={{0,2},{1,3},{2,0},{3,1},{4,6},{5,7},{6,4},{7,5},{8,10},{9,11},{10,... | collective-permute-start | bytes 6152 | tf_op jit(solution)/shard_map/ppermute | solution.py:17
  42.8 3.0 %collective-permute-start.9 = (f32[1,512]{1,0:T(1,128)S(1)}, f32[1,512]{1,0:T(1,128)S(1)}, u32[]{:S(2)}, u32[]{:S(2)}) collective-permute-start(f32[1,512]{1,0:T(1,128)S(1)} %reshape.165), channel_id=1, source_target_pairs={{0,1},{1,2},{2,3},{3,0},{4,5},{5,6},{6,7},{7,4},{8,9},{9,10},{10,1... | collective-permute-start | bytes 6152 | tf_op jit(solution)/shard_map/ppermute | solution.py:17
  48.6 3.7 %collective-permute-start.14 = (f32[16,64]{1,0:T(8,128)S(1)}, f32[16,64]{1,0:T(8,128)S(1)}, u32[]{:S(2)}, u32[]{:S(2)}) collective-permute-start(f32[16,64]{1,0:T(8,128)S(1)} %get-tuple-element.7), channel_id=1, source_target_pairs={{0,12},{4,0},{8,4},{12,8},{1,13},{5,1},{9,5},{13,9},{2,14},{6,2},{... | collective-permute-start | bytes 12296 | tf_op jit(solution)/shard_map/ppermute | solution.py:74
  49.2 4.5 %collective-permute-start.13 = (f32[16,64]{1,0:T(8,128)S(1)}, f32[16,64]{1,0:T(8,128)S(1)}, u32[]{:S(2)}, u32[]{:S(2)}) collective-permute-start(f32[16,64]{1,0:T(8,128)S(1)} %get-tuple-element.8), channel_id=1, source_target_pairs={{0,8},{4,12},{8,0},{12,4},{1,9},{5,13},{9,1},{13,5},{2,10},{6,14},... | collective-permute-start | bytes 12296 | tf_op jit(solution)/shard_map/ppermute | solution.py:74
  49.8 5.4 %collective-permute-start.12 = (f32[16,64]{1,0:T(8,128)S(1)}, f32[16,64]{1,0:T(8,128)S(1)}, u32[]{:S(2)}, u32[]{:S(2)}) collective-permute-start(f32[16,64]{1,0:T(8,128)S(1)} %get-tuple-element.9), channel_id=1, source_target_pairs={{0,4},{4,8},{8,12},{12,0},{1,5},{5,9},{9,13},{13,1},{2,6},{6,10},{... | collective-permute-start | bytes 12296 | tf_op jit(solution)/shard_map/ppermute | solution.py:74

commit v3 on v1

v3 whole, which is shorter than its diff:
```python
import functools
import jax
import jax.numpy as jnp
from jax import lax
from jax.experimental import pallas as pl
from jax.experimental.pallas import tpu as pltpu
from jax.sharding import PartitionSpec as P

CB = 64
OB = 64
CBLK_DEV = 8
WIN_DEV = 8
OBLK_DEV = 8
BLOCKS = WIN_DEV * CBLK_DEV
LANES = 128
TILES = OB * CB // LANES

F32 = jnp.float32
BF16 = jnp.bfloat16
VMEM = pl.BlockSpec(memory_space=pltpu.VMEM)


def iota(shape, dim):
    return lax.broadcasted_iota(jnp.int32, shape, dim)


def one_hot(where):
    return jnp.where(where, 1.0, 0.0).astype(BF16)


def three(value):
    first = value.astype(BF16)
    rest = value - first.astype(F32)
    second = rest.astype(BF16)
    third = (rest - second.astype(F32)).astype(BF16)
    return [first, second, third]


def pick_rows(pick3, value):
    return jnp.dot(pick3, jnp.concatenate(three(value), axis=0), preferred_element_type=F32)


def swap(value, distance):
    return jnp.take_along_axis(
        value, iota(value.shape, 1) ^ distance, axis=1, mode="promise_in_bounds"
    )


def half_swap(value):
    return pltpu.roll(value, LANES // 2, 1)


def low(shape):
    return iota(shape, 1) < LANES // 2


def tree_sum(parts):
    parts = list(parts)
    while len(parts) > 1:
        parts = [sum(parts[i + 1 : i + 2], parts[i]) for i in range(0, len(parts), 2)]
    return parts[0]


def spread_obs(row):
    out = jnp.zeros((OBLK_DEV, LANES), F32)
    block = iota((OBLK_DEV, LANES), 0)
    lower = low((OBLK_DEV, LANES))
    for t in range(OBLK_DEV // 2):
        tile = jnp.broadcast_to(row[:, LANES * t : LANES * (t + 1)], (OBLK_DEV, LANES))
        turned = half_swap(tile)
        out = jnp.where(block == 2 * t, jnp.where(lower, tile, turned), out)
        out = jnp.where(block == 2 * t + 1, jnp.where(lower, turned, tile), out)
    return out


def forward_tree(h_ref, owner, x, bits, base):
    if bits == 0:
        return h_ref[0, 0, owner, :, LANES * base : LANES * (base + 1)] * x
    a = forward_tree(h_ref, owner, x, bits - 1, base)
    b = forward_tree(h_ref, owner, x, bits - 1, base + 2 ** (bits - 1))
    distance = 2**bits
    clear = (iota(a.shape, 1) & distance) == 0
    return jnp.where(clear, a, b) + swap(jnp.where(clear, b, a), distance)


def for_owners(owners, body):
    lax.fori_loop(0, owners, lambda o, c: (body(o), c)[1], 0, unroll=owners <= 4)


def forward(h_ref, pick_obs, x_scr, value_scr):
    owners, capacity = h_ref.shape[2], h_ref.shape[3]

    def body(o):
        rows = pl.ds(pl.multiple_of(o * capacity, capacity), capacity)
        value_scr[rows, :] = forward_tree(h_ref, o, x_scr[rows, :], 5, 0)

    for_owners(owners, body)
    m = pick_rows(pick_obs, value_scr[...])[:OBLK_DEV]
    m = m + swap(m, 1)
    even = (iota(m.shape, 1) & 1) == 0
    return jnp.where(even == low(m.shape), m, half_swap(m))


def adjoint(h_ref, slot_obs, d, picked_scr, store):
    owners, capacity = h_ref.shape[2], h_ref.shape[3]
    picked_scr[...] = pick_rows(slot_obs, d)

    def body(o):
        rows = pl.ds(pl.multiple_of(o * capacity, capacity), capacity)
        picked = picked_scr[rows, :]
        upper = jnp.where(low(picked.shape), 0, 1)
        total = None
        for t in range(TILES):
            spread = jnp.take_along_axis(picked, upper + 2 * t, axis=1, mode="promise_in_bounds")
            term = h_ref[0, 0, o, :, LANES * t : LANES * (t + 1)] * spread
            total = term if total is None else total + term
        total = total + half_swap(total)
        pair = total[: capacity // 2], total[capacity // 2 :]
        store(o, jnp.where(low(pair[0].shape), *pair))

    for_owners(owners, body)


def prepare(
    fslot_ref, oslot_ref, count_ref, observed_ref, weight_ref,
    pick_flux_ref, target_ref, slot_obs_ref, pick_obs_ref, index_ref, observed_out, weight_out,
):
    me = lax.axis_index("cell")
    owners, capacity = fslot_ref.shape[2:]
    slots = owners * capacity
    eye = iota((capacity, capacity), 0) == iota((capacity, capacity), 1)

    def column(ref):
        return jnp.concatenate(
            [
                jnp.sum(
                    jnp.where(eye, jnp.broadcast_to(ref[0, 0, o : o + 1, :], eye.shape), 0),
                    axis=1,
                    keepdims=True,
                )
                for o in range(owners)
            ],
            axis=0,
        )

    fslot, oslot = column(fslot_ref), column(oslot_ref)
    counts = jnp.concatenate(
        [
            jnp.broadcast_to(count_ref[0, 0:1, o : o + 1], (capacity, 1))
            for o in range(owners)
        ],
        axis=0,
    )
    slot = iota((slots, 1), 0)
    owner = slot // capacity
    live = (slot - owner * capacity) < counts
    oslot = jnp.where(live, oslot, OBLK_DEV)
    target = owner * BLOCKS + fslot
    target_ref[...] = jnp.broadcast_to(target.astype(F32), target_ref.shape)

    depth = owners * BLOCKS // 2
    row = (owner ^ me) * (BLOCKS // 2) + ((fslot & 7) >> 1) * WIN_DEV + (fslot >> 3)
    pick_flux_ref[...] = one_hot(iota((slots, 3 * depth), 1) % depth == row)
    slot_obs_ref[...] = one_hot((iota((slots, 3 * OBLK_DEV), 1) % OBLK_DEV) == oslot)

    eye3 = iota((slots, 3 * slots), 1) % slots == iota((slots, 3 * slots), 0)
    obs_row = jnp.sum(jnp.where(eye3, oslot, 0), axis=0, keepdims=True)
    pick_obs_ref[...] = one_hot(iota((16, 3 * slots), 0) == obs_row) * one_hot(
        iota((16, 3 * slots), 0) < OBLK_DEV
    )

    half = slots // 2
    count = max(1, half // LANES)
    index_ref[...] = jnp.zeros(index_ref.shape, F32)
    for part in range(2):
        for q in range(count):
            r = (iota((slots, LANES), 1) + LANES * q) % half
            at = (r // (capacity // 2)) * capacity + r % (capacity // 2) + part * (capacity // 2)
            index_ref[pl.ds(part * count + q, 1), :] = jnp.sum(
                jnp.where(iota((slots, LANES), 0) == at, target.astype(F32), 0.0),
                axis=0,
                keepdims=True,
            )
    observed_out[...] = spread_obs(observed_ref[...])
    weight_out[...] = spread_obs(weight_ref[...])


def first_model(parts, *refs):
    x_parts = refs[:parts]
    h_ref, pick_flux_ref, target_ref, pick_obs_ref, m_ref, x_ref, value_scr = refs[parts:]
    flux = jnp.concatenate(
        [
            ref[:, LANES * t : LANES * (t + 1)]
            for ref in x_parts
            for t in range(CBLK_DEV // 2)
        ],
        axis=0,
    )
    pair = pick_rows(pick_flux_ref[...], flux)
    odd = (target_ref[...].astype(jnp.int32) & 1) == 1
    x_ref[...] = jnp.where(odd != low(pair.shape), pair, half_swap(pair))
    m_ref[...] = forward(h_ref, pick_obs_ref[...], x_ref, value_scr)


def first_adjoint(parts, *refs):
    m_parts = refs[:parts]
    observed_ref, weight_ref, slot_obs_ref, index_ref, h_ref, message_ref, d_ref, picked_scr = refs[parts:]
    d = weight_ref[...] * (tree_sum([m[...] for m in m_parts]) - observed_ref[...])
    d_ref[...] = d
    rows = h_ref.shape[3] // 2
    half = h_ref.shape[2] * rows

    def store(o, block):
        message_ref[pl.ds(pl.multiple_of(o * rows, rows), rows), :] = block

    adjoint(h_ref, slot_obs_ref[...], d, picked_scr, store)
    message_ref[half:, :] = index_ref[...]


def second_model(parts, *refs):
    messages = refs[:parts]
    target_ref, x_ref, h_ref, pick_obs_ref, m_ref, next_scr, value_scr = refs[parts:]
    slots = target_ref.shape[0]
    half = slots // 2
    count = max(1, half // LANES)
    group = max(1, min(parts, LANES // half))
    total = None
    for first in range(0, parts, group):
        members = messages[first : first + group]
        picks = []
        for part in range(2):
            rows = []
            for q in range(count):
                at = half + part * count + q
                row = members[0][at : at + 1, :]
                for k in range(1, group):
                    row = jnp.where(iota((1, LANES), 1) // half == k, members[k][at : at + 1, :], row)
                rows.append(one_hot(target_ref[...] == row))
            picks.append(jnp.concatenate(rows, axis=1)[:, : group * half])
        pick = jnp.concatenate(picks, axis=0)
        values = jnp.concatenate([ref[:half, :] for ref in members], axis=0)
        found = pick_rows(jnp.concatenate([pick] * 3, axis=1), values)
        total = found if total is None else total + found
    change = jnp.where(low((slots, LANES)), total[:slots], total[slots:])
    next_scr[...] = x_ref[...] - 0.5 * (change + half_swap(change))
    m_ref[...] = forward(h_ref, pick_obs_ref[...], next_scr, value_scr)


def second_adjoint(parts, owners, *refs):
    m_parts = refs[:parts]
    observed_ref, weight_ref, d_ref, slot_obs_ref, h_ref = refs[parts : parts + 5]
    outs = refs[parts + 5 : parts + 5 + owners]
    departure_ref, picked_scr, block_scr = refs[parts + 5 + owners :]
    me = lax.axis_index("cell")
    d = weight_ref[...] * (tree_sum([m[...] for m in m_parts]) - observed_ref[...])
    for t in range(OBLK_DEV // 2):
        departure_ref[:, LANES * t : LANES * (t + 1)] = jnp.where(
            low((1, LANES)), d[2 * t : 2 * t + 1], d[2 * t + 1 : 2 * t + 2]
        )

    def store(o, block):
        block_scr[o] = block

    adjoint(h_ref, slot_obs_ref[...], -0.25 * d_ref[...] - 0.5 * d, picked_scr, store)
    for k in range(owners):
        outs[k][...] = block_scr[me ^ k]


def gather_increment(parts, *refs):
    values, messages, out_ref = refs[:parts], refs[parts : 2 * parts], refs[2 * parts]
    me = lax.axis_index("cell")
    rows = values[0].shape[0]
    half = parts * rows
    count = max(1, half // LANES)
    place = me * rows
    lane = iota((1, LANES), 1)
    row = iota((BLOCKS, LANES), 0)
    block = me * BLOCKS + (row % WIN_DEV) * CBLK_DEV + 2 * ((row // WIN_DEV) % 4) + row // (BLOCKS // 2)
    block = block.astype(F32)
    picks = []
    for part in range(2):
        tiles = []
        for first in range(0, half, LANES):
            index = jnp.zeros((1, LANES), F32)
            for k in range(first // rows, min(parts, (first + LANES) // rows)):
                turned = pltpu.roll(
                    messages[k][half:, :], lax.rem(k * rows - place % LANES + 2 * LANES - first, LANES), 1
                )
                chosen = turned[part * count : part * count + 1]
                for q in range(1, count):
                    chosen = jnp.where(
                        place // LANES == q, turned[part * count + q : part * count + q + 1], chosen
                    )
                index = jnp.where((lane // rows) % parts == k - first // rows, chosen, index)
            tiles.append(one_hot(block == index))
        picks.append(jnp.concatenate(tiles, axis=1))
    pick = jnp.concatenate(picks, axis=0)
    terms = three(jnp.concatenate([ref[...] for ref in values], axis=0))
    if 3 * half <= LANES:
        terms.append(jnp.zeros((LANES - 3 * half, LANES), BF16))
    else:
        pick = jnp.concatenate([pick[:, :half]] * 3, axis=1)
    found = jnp.dot(pick, jnp.concatenate(terms, axis=0), preferred_element_type=F32)
    found = jnp.where(low((BLOCKS, LANES)), found[:BLOCKS], found[BLOCKS:])
    found = found + half_swap(found)
    for t in range(CBLK_DEV // 2):
        even = found[WIN_DEV * t : WIN_DEV * (t + 1)]
        odd = found[BLOCKS // 2 + WIN_DEV * t : BLOCKS // 2 + WIN_DEV * (t + 1)]
        out_ref[:, LANES * t : LANES * (t + 1)] = jnp.where(low(even.shape), even, odd)


def exchange(value, axis, size):
    return [value] + [send(value, axis, size, k) for k in range(size - 1, 0, -1)][::-1]


def send(value, axis, size, k):
    return lax.ppermute(value, axis, [(i, i ^ k) for i in range(size)])


def make_local(cells, wins):
    def local(prior_flux, observed, obs_weight, footprint, flux_slot, obs_slot, slot_count):
        owners, capacity = footprint.shape[2:4]
        slots = owners * capacity
        half = slots // 2
        index_rows = -(-2 * max(1, half // LANES) // 8) * 8
        params = pltpu.CompilerParams(vmem_limit_bytes=4 * footprint.size * 4 + 8 * 2**20)

        def call(body, outs, ins, scratch=()):
            return pl.pallas_call(
                body,
                out_shape=[jax.ShapeDtypeStruct(s, t) for s, t in outs],
                in_specs=[VMEM] * len(ins),
                out_specs=[VMEM] * len(outs),
                scratch_shapes=[pltpu.VMEM(s, F32) for s in scratch],
                compiler_params=params,
            )(*ins)

        obs_tile = ((OBLK_DEV, LANES), F32)
        slot_tile = ((slots, LANES), F32)
        flux_parts = exchange(prior_flux, "cell", cells)
        pick_flux, target, slot_obs, pick_obs, index, observed_t, weight_t = call(
            prepare,
            [
                ((slots, 3 * owners * BLOCKS // 2), BF16),
                slot_tile,
                ((slots, 3 * OBLK_DEV), BF16),
                ((16, 3 * slots), BF16),
                ((index_rows, LANES), F32),
                obs_tile,
                obs_tile,
            ],
            (flux_slot, obs_slot, slot_count, observed, obs_weight),
        )
        m0, x0 = call(
            functools.partial(first_model, cells),
            [obs_tile, slot_tile],
            (*flux_parts, footprint, pick_flux, target, pick_obs),
            [slot_tile[0]],
        )
        message, d0 = call(
            functools.partial(first_adjoint, wins),
            [((half + index_rows, LANES), F32), obs_tile],
            (*exchange(m0, "win", wins), observed_t, weight_t, slot_obs, index, footprint),
            [slot_tile[0]],
        )
        messages = exchange(message, "cell", cells)
        (m1,) = call(
            functools.partial(second_model, cells),
            [obs_tile],
            (*messages, target, x0, footprint, pick_obs),
            [slot_tile[0], slot_tile[0]],
        )
        *blocks, departure = call(
            functools.partial(second_adjoint, wins, owners),
            [((capacity // 2, LANES), F32)] * owners + [((1, OBLK_DEV * OB), F32)],
            (*exchange(m1, "win", wins), observed_t, weight_t, d0, slot_obs, footprint),
            [slot_tile[0], (owners, capacity // 2, LANES)],
        )
        arrived = [send(blocks[k], "cell", cells, k) for k in range(cells - 1, 0, -1)][::-1]
        (increment,) = call(
            functools.partial(gather_increment, cells),
            [((WIN_DEV, CBLK_DEV * CB), F32)],
            (blocks[0], *arrived, *messages),
        )
        return increment, departure

    return local


def solution(mesh):
    placed = (
        P(("ens", "win"), "cell"),
        P(("ens", "cell"), None),
        P(("ens", "cell"), None),
        P("cell", "win", None, None, None),
        P("cell", "win", None, None),
        P("cell", "win", None, None),
        P("cell", "win", None),
    )
    return jax.shard_map(
        make_local(mesh.shape["cell"], mesh.shape["win"]),
        mesh=mesh,
        in_specs=placed,
        out_specs=(P(("ens", "win"), "cell"), P(("ens", "cell"), None)),
        check_vma=False,
    )
```

time: 119 us -> 41.5 us (0.35)
  waiting for transfers between devices: 55.4 us -> 11.4 us
  blocking collectives: 26.4 us -> 0 us
  starting transfers between devices: 0.08 us -> 18.2 us
  matrix products: 14.7 us -> 0 us
  between operations: 14.1 us -> 0.68 us
  Pallas kernels: 0 us -> 5.65 us
  other arithmetic: 2.21 us -> 0 us
    psum x1 -> x0, waiting for transfers between devices: 36.1 us -> none  [local(): adjoint0 = lax.psum(adjoint(departure0), 'cell')]
    reduce_scatter x1 -> x0, waiting for transfers between devices: 19.2 us -> none  [local(): lax.psum_scatter(adjoint(-0.25 * departure0 - 0.5 * departure1), 'cell',...]
    ppermute x0 -> x15, starting transfers between devices: none -> 18.2 us  [send(): return lax.ppermute(value, axis, [(i, i ^ k) for i in range(size)])]
    all_gather x1 -> x0, blocking collectives: 15 us -> none  [local(): flux = lax.all_gather(prior_flux.reshape(blocks, CB), 'cell')]
    dot_general x12 -> x0, matrix products: 14.7 us -> none  [the longest x2 6.71 us: forward(): value = jnp.einsum('ocij,ocj->oci', matrices, selected, precision=HI)]
    ppermute x0 -> x15, waiting for transfers between devices: none -> 11.4 us  [send(): return lax.ppermute(value, axis, [(i, i ^ k) for i in range(size)])]
    psum x2 -> x0, blocking collectives: 11.3 us -> none  [forward(): return lax.psum(sums.reshape(1, OBLK_DEV * OB), 'win')]
    pallas_call x0 -> x6, Pallas kernels: none -> 5.65 us  [call(): pl.pallas_call(body, out_shape=[jax.ShapeDtypeStruct(s, t) for s, t in ou...]
  transfers between devices with their start and end apart: 2 -> 15, of which waited for: 2 -> 9; matrix products, arithmetic and copies ran while one was open for 0% -> 0% of each run, Pallas kernels for 0% -> 1%
where the time goes in v3:
time: 41.5 us; the launch traced here: 41.2 us
  starting transfers between devices  18.2 us (44%)
  waiting for transfers between devices  11.4 us (27%)
  Pallas kernels  5.65 us (14%)
  local copies, waits for them, and re-layouts  5.32 us (13%)
  between operations  0.68 us (2%)
    ppermute x15, starting transfers between devices, send(): return lax.ppermute(value, axis, [(i, i ^ k) for i in range(size)])  18.2 us
    ppermute x15, waiting for transfers between devices, send(): return lax.ppermute(value, axis, [(i, i ^ k) for i in range(size)])  11.4 us
    pallas_call x6, Pallas kernels, call(): pl.pallas_call(body, out_shape=[jax.ShapeDtypeStruct(s, t) for s, t in ou...  5.65 us
    unnamed x16, local copies, waits for them, and re-layouts  5.32 us
  transfers between devices with their start and end apart: 15, of which 9 were waited for; matrix products, arithmetic and copies ran while one was open for 0% of the time, Pallas kernels for 1%

profile of v3, /device:TPU:0, one launch (start us, length us, event | category | flops | bytes accessed | tf_op | source)
XLA Modules:
  0.0 41.2 jit_solution(9915585615358844431)
XLA Ops:
  0.6 4.1 %collective-permute-start.1 = (f32[8,512]{1,0:T(8,128)}, f32[8,512]{1,0:T(8,128)S(1)}, u32[]{:S(2)}, u32[]{:S(2)}) collective-permute-start(f32[8,512]{1,0:T(8,128)} %refs_0_.1), channel_id=1, source_target_pairs={{0,8},{4,12},{8,0},{12,4},{1,9},{5,13},{9,1},{13,5},{2,10},{6,14},... | collective-permute-start | bytes 49160 | tf_op jit(solution)/shard_map/ppermute | solution.py:317
  4.7 1.6 %collective-permute-start = (f32[8,512]{1,0:T(8,128)}, f32[8,512]{1,0:T(8,128)S(1)}, u32[]{:S(2)}, u32[]{:S(2)}) collective-permute-start(f32[8,512]{1,0:T(8,128)} %refs_0_.1), channel_id=1, source_target_pairs={{0,4},{4,0},{8,12},{12,8},{1,5},{5,1},{9,13},{13,9},{2,6},{6,2},{1... | collective-permute-start | bytes 49160 | tf_op jit(solution)/shard_map/ppermute | solution.py:317
  6.3 0.7 %copy-done.3 = s32[1,1,4,16]{3,2,1,0:T(4,128)S(1)} copy-done((s32[1,1,4,16]{3,2,1,0:T(4,128)S(1)}, s32[1,1,4,16]{3,2,1,0:T(4,128)}, u32[]{:S(2)}) %copy-start.3) | copy-done | bytes 280
  7.0 0.7 %copy-done.4 = s32[1,1,4,16]{3,2,1,0:T(4,128)S(1)} copy-done((s32[1,1,4,16]{3,2,1,0:T(4,128)S(1)}, s32[1,1,4,16]{3,2,1,0:T(4,128)}, u32[]{:S(2)}) %copy-start.4) | copy-done | bytes 280
  7.7 0.7 %copy-done.5 = f32[1,512]{1,0:T(1,128)S(1)} copy-done((f32[1,512]{1,0:T(1,128)S(1)}, f32[1,512]{1,0:T(1,128)}, u32[]{:S(2)}) %copy-start.5) | copy-done | bytes 2072
  8.4 0.7 %copy-done.6 = f32[1,512]{1,0:T(1,128)S(1)} copy-done((f32[1,512]{1,0:T(1,128)S(1)}, f32[1,512]{1,0:T(1,128)}, u32[]{:S(2)}) %copy-start.6) | copy-done | bytes 2072
  9.0 0.7 %copy-done.7 = s32[1,1,4]{2,1,0:T(1,128)S(1)} copy-done((s32[1,1,4]{2,1,0:T(1,128)S(1)}, s32[1,1,4]{2,1,0:T(1,128)}, u32[]{:S(2)}) %copy-start.7) | copy-done | bytes 40
  10.0 2.1 %collective-permute-done.2.refs_3_ = f32[8,512]{1,0:T(8,128)S(1)} collective-permute-done((f32[8,512]{1,0:T(8,128)}, f32[8,512]{1,0:T(8,128)S(1)}, u32[]{:S(2)}, u32[]{:S(2)}) %collective-permute-start.2) | collective-permute-done | bytes 16416 | tf_op jit(solution)/shard_map/ppermute | solution.py:317
  12.1 1.2 %copy-done = f32[1,1,4,16,4096]{4,3,2,1,0:T(8,128)S(1)} copy-done((f32[1,1,4,16,4096]{4,3,2,1,0:T(8,128)S(1)}, f32[1,1,4,16,4096]{4,3,2,1,0:T(8,128)}, u32[]{:S(2)}) %copy-start) | copy-done | bytes 1048600
  13.3 0.7 %copy-done.2 = f32[8,512]{1,0:T(8,128)S(1)} copy-done((f32[8,512]{1,0:T(8,128)S(1)}, f32[8,512]{1,0:T(8,128)}, u32[]{:S(2)}) %copy-start.2) | copy-done | bytes 16408
  14.0 1.0 %shard_map.87 = (f32[8,128]{1,0:T(8,128)S(1)}, f32[64,128]{1,0:T(8,128)S(1)}) custom-call(f32[8,512]{1,0:T(8,128)S(1)} %copy-done.2, f32[8,512]{1,0:T(8,128)S(1)} %collective-permute-done.refs_1_, f32[8,512]{1,0:T(8,128)S(1)} %collective-permute-done.1.refs_2_, f32[8,512]{1,0:T(8,128)S(1)} %collective-permute-done.2.refs_3_, ...), custom_call_target="tpu_custom_call" | custom-call | tf_op jit(solution)/shard_map/pallas_call | solution.py:329
  15.0 1.5 %collective-permute-start.4 = (f32[8,128]{1,0:T(8,128)S(1)}, f32[8,128]{1,0:T(8,128)S(1)}, u32[]{:S(2)}, u32[]{:S(2)}) collective-permute-start(f32[8,128]{1,0:T(8,128)S(1)} %get-tuple-element.21.refs_0_), channel_id=1, source_target_pairs={{0,2},{1,3},{2,0},{3,1},{4,6},{5,7},{6,4},{7,5},{8,10},{9,11},{10,... | collective-permute-start | bytes 12296 | tf_op jit(solution)/shard_map/ppermute | solution.py:317
  16.5 0.3 collective-permute-start.3
  16.9 1.2 %collective-permute-done.5.refs_3_ = f32[8,128]{1,0:T(8,128)S(1)} collective-permute-done((f32[8,128]{1,0:T(8,128)S(1)}, f32[8,128]{1,0:T(8,128)S(1)}, u32[]{:S(2)}, u32[]{:S(2)}) %collective-permute-start.5) | collective-permute-done | bytes 4128 | tf_op jit(solution)/shard_map/ppermute | solution.py:317
  18.1 0.6 %collective-permute-done.4.refs_2_ = f32[8,128]{1,0:T(8,128)S(1)} collective-permute-done((f32[8,128]{1,0:T(8,128)S(1)}, f32[8,128]{1,0:T(8,128)S(1)}, u32[]{:S(2)}, u32[]{:S(2)}) %collective-permute-start.4) | collective-permute-done | bytes 4128 | tf_op jit(solution)/shard_map/ppermute | solution.py:317
  18.7 1.0 %shard_map.88 = (f32[40,128]{1,0:T(8,128)S(1)}, f32[8,128]{1,0:T(8,128)S(1)}) custom-call(f32[8,128]{1,0:T(8,128)S(1)} %get-tuple-element.21.refs_0_, f32[8,128]{1,0:T(8,128)S(1)} %collective-permute-done.3.refs_1_, f32[8,128]{1,0:T(8,128)S(1)} %collective-permute-done.4.refs_2_, f32[8,128]{1,0:T(8,128)S(1)} %collective-permute-done.5.refs_3_, ...), custom_call_target="tpu_custom_call" | custom-call | tf_op jit(solution)/shard_map/pallas_call | solution.py:329
  19.7 1.8 %collective-permute-start.8 = (f32[40,128]{1,0:T(8,128)S(1)}, f32[40,128]{1,0:T(8,128)S(1)}, u32[]{:S(2)}, u32[]{:S(2)}) collective-permute-start(f32[40,128]{1,0:T(8,128)S(1)} %get-tuple-element.26.refs_0_.refs_4_), channel_id=1, source_target_pairs={{0,12},{4,8},{8,4},{12,0},{1,13},{5,9},{9,5},{13,1},{2,14},{6,10},... | collective-permute-start | bytes 61448 | tf_op jit(solution)/shard_map/ppermute | solution.py:317
  21.5 2.6 %collective-permute-start.6 = (f32[40,128]{1,0:T(8,128)S(1)}, f32[40,128]{1,0:T(8,128)S(1)}, u32[]{:S(2)}, u32[]{:S(2)}) collective-permute-start(f32[40,128]{1,0:T(8,128)S(1)} %get-tuple-element.26.refs_0_.refs_4_), channel_id=1, source_target_pairs={{0,4},{4,0},{8,12},{12,8},{1,5},{5,1},{9,13},{13,9},{2,6},{6,2},{1... | collective-permute-start | bytes 61448 | tf_op jit(solution)/shard_map/ppermute | solution.py:317
  24.1 1.2 %collective-permute-done.8.refs_3_.refs_7_ = f32[40,128]{1,0:T(8,128)S(1)} collective-permute-done((f32[40,128]{1,0:T(8,128)S(1)}, f32[40,128]{1,0:T(8,128)S(1)}, u32[]{:S(2)}, u32[]{:S(2)}) %collective-permute-start.8) | collective-permute-done | bytes 20512 | tf_op jit(solution)/shard_map/ppermute | solution.py:317
  25.3 0.9 %collective-permute-done.7.refs_2_.refs_6_ = f32[40,128]{1,0:T(8,128)S(1)} collective-permute-done((f32[40,128]{1,0:T(8,128)S(1)}, f32[40,128]{1,0:T(8,128)S(1)}, u32[]{:S(2)}, u32[]{:S(2)}) %collective-permute-start.7) | collective-permute-done | bytes 20512 | tf_op jit(solution)/shard_map/ppermute | solution.py:317
  26.2 1.0 %shard_map.89.refs_0_ = f32[8,128]{1,0:T(8,128)S(1)} custom-call(f32[40,128]{1,0:T(8,128)S(1)} %get-tuple-element.26.refs_0_.refs_4_, f32[40,128]{1,0:T(8,128)S(1)} %collective-permute-done.6.refs_1_.refs_5_, f32[40,128]{1,0:T(8,128)S(1)} %collective-permute-done.7.refs_2_.refs_6_, f32[40,128]{1,0:T(8,128)S(1)} %collective-permute-done.8.refs_3_.refs_7_, ...), custom_call_target="tpu_custom_call" | custom-call | tf_op jit(solution)/shard_map/pallas_call | solution.py:329
  27.2 1.5 %collective-permute-start.10 = (f32[8,128]{1,0:T(8,128)S(1)}, f32[8,128]{1,0:T(8,128)S(1)}, u32[]{:S(2)}, u32[]{:S(2)}) collective-permute-start(f32[8,128]{1,0:T(8,128)S(1)} %shard_map.89.refs_0_), channel_id=1, source_target_pairs={{0,2},{1,3},{2,0},{3,1},{4,6},{5,7},{6,4},{7,5},{8,10},{9,11},{10,... | collective-permute-start | bytes 12296 | tf_op jit(solution)/shard_map/ppermute | solution.py:317
  28.6 0.4 collective-permute-start.9
  29.1 1.2 %collective-permute-done.11.refs_3_ = f32[8,128]{1,0:T(8,128)S(1)} collective-permute-done((f32[8,128]{1,0:T(8,128)S(1)}, f32[8,128]{1,0:T(8,128)S(1)}, u32[]{:S(2)}, u32[]{:S(2)}) %collective-permute-start.11) | collective-permute-done | bytes 4128 | tf_op jit(solution)/shard_map/ppermute | solution.py:317
  30.2 0.6 %collective-permute-done.10.refs_2_ = f32[8,128]{1,0:T(8,128)S(1)} collective-permute-done((f32[8,128]{1,0:T(8,128)S(1)}, f32[8,128]{1,0:T(8,128)S(1)}, u32[]{:S(2)}, u32[]{:S(2)}) %collective-permute-start.10) | collective-permute-done | bytes 4128 | tf_op jit(solution)/shard_map/ppermute | solution.py:317
  30.8 1.5 %shard_map.90 = (f32[8,128]{1,0:T(8,128)S(1)}, f32[8,128]{1,0:T(8,128)S(1)}, f32[8,128]{1,0:T(8,128)S(1)}, f32[8,128]{1,0:T(8,128)S(1)}, f32[1,512]{1,0:T(1,128)}) custom-call(f32[8,128]{1,0:T(8,128)S(1)} %shard_map.89.refs_0_, f32[8,128]{1,0:T(8,128)S(1)} %collective-permute-done.9.refs_1_, f32[8,128]{1,0:T(8,128)S(1)} %collective-permute-done.10.refs_2_, ...), custom_call_target="tpu_custom_call" | custom-call | tf_op jit(solution)/shard_map/pallas_call | solution.py:329
  32.4 1.7 %collective-permute-start.12 = (f32[8,128]{1,0:T(8,128)S(1)}, f32[8,128]{1,0:T(8,128)S(1)}, u32[]{:S(2)}, u32[]{:S(2)}) collective-permute-start(f32[8,128]{1,0:T(8,128)S(1)} %get-tuple-element.30), channel_id=1, source_target_pairs={{0,4},{4,0},{8,12},{12,8},{1,5},{5,1},{9,13},{13,9},{2,6},{6,2},{1... | collective-permute-start | bytes 12296 | tf_op jit(solution)/shard_map/ppermute | solution.py:317
  34.0 0.9 %collective-permute-start.13 = (f32[8,128]{1,0:T(8,128)S(1)}, f32[8,128]{1,0:T(8,128)S(1)}, u32[]{:S(2)}, u32[]{:S(2)}) collective-permute-start(f32[8,128]{1,0:T(8,128)S(1)} %get-tuple-element.31), channel_id=1, source_target_pairs={{0,8},{4,12},{8,0},{12,4},{1,9},{5,13},{9,1},{13,5},{2,10},{6,14},... | collective-permute-start | bytes 12296 | tf_op jit(solution)/shard_map/ppermute | solution.py:317
  34.9 1.8 %collective-permute-start.14 = (f32[8,128]{1,0:T(8,128)S(1)}, f32[8,128]{1,0:T(8,128)S(1)}, u32[]{:S(2)}, u32[]{:S(2)}) collective-permute-start(f32[8,128]{1,0:T(8,128)S(1)} %get-tuple-element.32), channel_id=1, source_target_pairs={{0,12},{4,8},{8,4},{12,0},{1,13},{5,9},{9,5},{13,1},{2,14},{6,10},... | collective-permute-start | bytes 12296 | tf_op jit(solution)/shard_map/ppermute | solution.py:317
  36.7 1.8 %collective-permute-done.13.refs_2_ = f32[8,128]{1,0:T(8,128)S(1)} collective-permute-done((f32[8,128]{1,0:T(8,128)S(1)}, f32[8,128]{1,0:T(8,128)S(1)}, u32[]{:S(2)}, u32[]{:S(2)}) %collective-permute-start.13) | collective-permute-done | bytes 4128 | tf_op jit(solution)/shard_map/ppermute | solution.py:317
  38.5 1.8 %collective-permute-done.14.refs_3_ = f32[8,128]{1,0:T(8,128)S(1)} collective-permute-done((f32[8,128]{1,0:T(8,128)S(1)}, f32[8,128]{1,0:T(8,128)S(1)}, u32[]{:S(2)}, u32[]{:S(2)}) %collective-permute-start.14) | collective-permute-done | bytes 4128 | tf_op jit(solution)/shard_map/ppermute | solution.py:317
  40.3 0.9 %shard_map.91 = f32[8,512]{1,0:T(8,128)} custom-call(f32[8,128]{1,0:T(8,128)S(1)} %get-tuple-element.29.refs_0_, f32[8,128]{1,0:T(8,128)S(1)} %collective-permute-done.12.refs_1_, f32[8,128]{1,0:T(8,128)S(1)} %collective-permute-done.13.refs_2_, f32[8,128]{1,0:T(8,128)S(1)} %collective-permute-done.14.refs_3_, ...), custom_call_target="tpu_custom_call" | custom-call | tf_op jit(solution)/shard_map/pallas_call | solution.py:329
  (20 shorter events, 0.3 us)
Async XLA Ops:
  0.6 9.3 %collective-permute-start.1 = (f32[8,512]{1,0:T(8,128)}, f32[8,512]{1,0:T(8,128)S(1)}, u32[]{:S(2)}, u32[]{:S(2)}) collective-permute-start(f32[8,512]{1,0:T(8,128)} %refs_0_.1), channel_id=1, source_target_pairs={{0,8},{4,12},{8,0},{12,4},{1,9},{5,13},{9,1},{13,5},{2,10},{6,14},... | collective-permute-start | bytes 49160 | tf_op jit(solution)/shard_map/ppermute | solution.py:317
  4.7 5.2 %collective-permute-start = (f32[8,512]{1,0:T(8,128)}, f32[8,512]{1,0:T(8,128)S(1)}, u32[]{:S(2)}, u32[]{:S(2)}) collective-permute-start(f32[8,512]{1,0:T(8,128)} %refs_0_.1), channel_id=1, source_target_pairs={{0,4},{4,0},{8,12},{12,8},{1,5},{5,1},{9,13},{13,9},{2,6},{6,2},{1... | collective-permute-start | bytes 49160 | tf_op jit(solution)/shard_map/ppermute | solution.py:317
  6.3 5.7 %collective-permute-start.2 = (f32[8,512]{1,0:T(8,128)}, f32[8,512]{1,0:T(8,128)S(1)}, u32[]{:S(2)}, u32[]{:S(2)}) collective-permute-start(f32[8,512]{1,0:T(8,128)} %refs_0_.1), channel_id=1, source_target_pairs={{0,12},{4,8},{8,4},{12,0},{1,13},{5,9},{9,5},{13,1},{2,14},{6,10},... | collective-permute-start | bytes 49160 | tf_op jit(solution)/shard_map/ppermute | solution.py:317
  6.3 0.7 %copy-start.3 = (s32[1,1,4,16]{3,2,1,0:T(4,128)S(1)}, s32[1,1,4,16]{3,2,1,0:T(4,128)}, u32[]{:S(2)}) copy-start(s32[1,1,4,16]{3,2,1,0:T(4,128)} %fslot_ref.1) | copy-start | bytes 772
  7.0 0.7 %copy-start.4 = (s32[1,1,4,16]{3,2,1,0:T(4,128)S(1)}, s32[1,1,4,16]{3,2,1,0:T(4,128)}, u32[]{:S(2)}) copy-start(s32[1,1,4,16]{3,2,1,0:T(4,128)} %oslot_ref.1) | copy-start | bytes 772
  7.7 0.7 %copy-start.5 = (f32[1,512]{1,0:T(1,128)S(1)}, f32[1,512]{1,0:T(1,128)}, u32[]{:S(2)}) copy-start(f32[1,512]{1,0:T(1,128)} %observed_ref.1) | copy-start | bytes 6148
  8.4 0.7 %copy-start.6 = (f32[1,512]{1,0:T(1,128)S(1)}, f32[1,512]{1,0:T(1,128)}, u32[]{:S(2)}) copy-start(f32[1,512]{1,0:T(1,128)} %weight_ref.1) | copy-start | bytes 6148
  9.0 0.7 %copy-start.7 = (s32[1,1,4]{2,1,0:T(1,128)S(1)}, s32[1,1,4]{2,1,0:T(1,128)}, u32[]{:S(2)}) copy-start(s32[1,1,4]{2,1,0:T(1,128)} %count_ref.1) | copy-start | bytes 52
  12.1 1.2 %copy-start = (f32[1,1,4,16,4096]{4,3,2,1,0:T(8,128)S(1)}, f32[1,1,4,16,4096]{4,3,2,1,0:T(8,128)}, u32[]{:S(2)}) copy-start(f32[1,1,4,16,4096]{4,3,2,1,0:T(8,128)} %refs_8_.3) | copy-start | bytes 3145732
  13.3 0.7 %copy-start.2 = (f32[8,512]{1,0:T(8,128)S(1)}, f32[8,512]{1,0:T(8,128)}, u32[]{:S(2)}) copy-start(f32[8,512]{1,0:T(8,128)} %refs_0_.1) | copy-start | bytes 49156
  14.0 4.7 %copy-start.1 = (f32[1,1,4,16,4096]{4,3,2,1,0:T(8,128)S(1)}, f32[1,1,4,16,4096]{4,3,2,1,0:T(8,128)}, u32[]{:S(2)}) copy-start(f32[1,1,4,16,4096]{4,3,2,1,0:T(8,128)} %refs_8_.3) | copy-start | bytes 3145732
  15.0 3.0 %collective-permute-start.5 = (f32[8,128]{1,0:T(8,128)S(1)}, f32[8,128]{1,0:T(8,128)S(1)}, u32[]{:S(2)}, u32[]{:S(2)}) collective-permute-start(f32[8,128]{1,0:T(8,128)S(1)} %get-tuple-element.21.refs_0_), channel_id=1, source_target_pairs={{0,3},{1,2},{2,1},{3,0},{4,7},{5,6},{6,5},{7,4},{8,11},{9,10},{10,... | collective-permute-start | bytes 12296 | tf_op jit(solution)/shard_map/ppermute | solution.py:317
  15.0 3.7 %collective-permute-start.4 = (f32[8,128]{1,0:T(8,128)S(1)}, f32[8,128]{1,0:T(8,128)S(1)}, u32[]{:S(2)}, u32[]{:S(2)}) collective-permute-start(f32[8,128]{1,0:T(8,128)S(1)} %get-tuple-element.21.refs_0_), channel_id=1, source_target_pairs={{0,2},{1,3},{2,0},{3,1},{4,6},{5,7},{6,4},{7,5},{8,10},{9,11},{10,... | collective-permute-start | bytes 12296 | tf_op jit(solution)/shard_map/ppermute | solution.py:317
  16.5 2.1 %collective-permute-start.3 = (f32[8,128]{1,0:T(8,128)S(1)}, f32[8,128]{1,0:T(8,128)S(1)}, u32[]{:S(2)}, u32[]{:S(2)}) collective-permute-start(f32[8,128]{1,0:T(8,128)S(1)} %get-tuple-element.21.refs_0_), channel_id=1, source_target_pairs={{0,1},{1,0},{2,3},{3,2},{4,5},{5,4},{6,7},{7,6},{8,9},{9,8},{10,11... | collective-permute-start | bytes 12296 | tf_op jit(solution)/shard_map/ppermute | solution.py:317
  19.7 5.6 %collective-permute-start.8 = (f32[40,128]{1,0:T(8,128)S(1)}, f32[40,128]{1,0:T(8,128)S(1)}, u32[]{:S(2)}, u32[]{:S(2)}) collective-permute-start(f32[40,128]{1,0:T(8,128)S(1)} %get-tuple-element.26.refs_0_.refs_4_), channel_id=1, source_target_pairs={{0,12},{4,8},{8,4},{12,0},{1,13},{5,9},{9,5},{13,1},{2,14},{6,10},... | collective-permute-start | bytes 61448 | tf_op jit(solution)/shard_map/ppermute | solution.py:317
  21.5 4.7 %collective-permute-start.7 = (f32[40,128]{1,0:T(8,128)S(1)}, f32[40,128]{1,0:T(8,128)S(1)}, u32[]{:S(2)}, u32[]{:S(2)}) collective-permute-start(f32[40,128]{1,0:T(8,128)S(1)} %get-tuple-element.26.refs_0_.refs_4_), channel_id=1, source_target_pairs={{0,8},{4,12},{8,0},{12,4},{1,9},{5,13},{9,1},{13,5},{2,10},{6,14},... | collective-permute-start | bytes 61448 | tf_op jit(solution)/shard_map/ppermute | solution.py:317
  21.5 4.7 %collective-permute-start.6 = (f32[40,128]{1,0:T(8,128)S(1)}, f32[40,128]{1,0:T(8,128)S(1)}, u32[]{:S(2)}, u32[]{:S(2)}) collective-permute-start(f32[40,128]{1,0:T(8,128)S(1)} %get-tuple-element.26.refs_0_.refs_4_), channel_id=1, source_target_pairs={{0,4},{4,0},{8,12},{12,8},{1,5},{5,1},{9,13},{13,9},{2,6},{6,2},{1... | collective-permute-start | bytes 61448 | tf_op jit(solution)/shard_map/ppermute | solution.py:317
  27.2 3.1 %collective-permute-start.11 = (f32[8,128]{1,0:T(8,128)S(1)}, f32[8,128]{1,0:T(8,128)S(1)}, u32[]{:S(2)}, u32[]{:S(2)}) collective-permute-start(f32[8,128]{1,0:T(8,128)S(1)} %shard_map.89.refs_0_), channel_id=1, source_target_pairs={{0,3},{1,2},{2,1},{3,0},{4,7},{5,6},{6,5},{7,4},{8,11},{9,10},{10,... | collective-permute-start | bytes 12296 | tf_op jit(solution)/shard_map/ppermute | solution.py:317
  27.2 3.7 %collective-permute-start.10 = (f32[8,128]{1,0:T(8,128)S(1)}, f32[8,128]{1,0:T(8,128)S(1)}, u32[]{:S(2)}, u32[]{:S(2)}) collective-permute-start(f32[8,128]{1,0:T(8,128)S(1)} %shard_map.89.refs_0_), channel_id=1, source_target_pairs={{0,2},{1,3},{2,0},{3,1},{4,6},{5,7},{6,4},{7,5},{8,10},{9,11},{10,... | collective-permute-start | bytes 12296 | tf_op jit(solution)/shard_map/ppermute | solution.py:317
  28.6 2.2 %collective-permute-start.9 = (f32[8,128]{1,0:T(8,128)S(1)}, f32[8,128]{1,0:T(8,128)S(1)}, u32[]{:S(2)}, u32[]{:S(2)}) collective-permute-start(f32[8,128]{1,0:T(8,128)S(1)} %shard_map.89.refs_0_), channel_id=1, source_target_pairs={{0,1},{1,0},{2,3},{3,2},{4,5},{5,4},{6,7},{7,6},{8,9},{9,8},{10,11... | collective-permute-start | bytes 12296 | tf_op jit(solution)/shard_map/ppermute | solution.py:317
  32.4 4.4 %collective-permute-start.12 = (f32[8,128]{1,0:T(8,128)S(1)}, f32[8,128]{1,0:T(8,128)S(1)}, u32[]{:S(2)}, u32[]{:S(2)}) collective-permute-start(f32[8,128]{1,0:T(8,128)S(1)} %get-tuple-element.30), channel_id=1, source_target_pairs={{0,4},{4,0},{8,12},{12,8},{1,5},{5,1},{9,13},{13,9},{2,6},{6,2},{1... | collective-permute-start | bytes 12296 | tf_op jit(solution)/shard_map/ppermute | solution.py:317
  34.0 4.5 %collective-permute-start.13 = (f32[8,128]{1,0:T(8,128)S(1)}, f32[8,128]{1,0:T(8,128)S(1)}, u32[]{:S(2)}, u32[]{:S(2)}) collective-permute-start(f32[8,128]{1,0:T(8,128)S(1)} %get-tuple-element.31), channel_id=1, source_target_pairs={{0,8},{4,12},{8,0},{12,4},{1,9},{5,13},{9,1},{13,5},{2,10},{6,14},... | collective-permute-start | bytes 12296 | tf_op jit(solution)/shard_map/ppermute | solution.py:317
  34.9 5.4 %collective-permute-start.14 = (f32[8,128]{1,0:T(8,128)S(1)}, f32[8,128]{1,0:T(8,128)S(1)}, u32[]{:S(2)}, u32[]{:S(2)}) collective-permute-start(f32[8,128]{1,0:T(8,128)S(1)} %get-tuple-element.32), channel_id=1, source_target_pairs={{0,12},{4,8},{8,4},{12,0},{1,13},{5,9},{9,5},{13,1},{2,14},{6,10},... | collective-permute-start | bytes 12296 | tf_op jit(solution)/shard_map/ppermute | solution.py:317

commit v4 on v3

--- a/solution.py
+++ b/solution.py
@@ -54,11 +54,8 @@
     return iota(shape, 1) < LANES // 2
 
 
-def tree_sum(parts):
-    parts = list(parts)
-    while len(parts) > 1:
-        parts = [sum(parts[i + 1 : i + 2], parts[i]) for i in range(0, len(parts), 2)]
-    return parts[0]
+def entries(refs):
+    return [(ref, i) for ref in refs for i in range(ref.shape[0])]
 
 
 def spread_obs(row):
@@ -122,11 +119,29 @@
 
 
 def prepare(
-    fslot_ref, oslot_ref, count_ref, observed_ref, weight_ref,
-    pick_flux_ref, target_ref, slot_obs_ref, pick_obs_ref, index_ref, observed_out, weight_out,
+    fslot_hbm, oslot_hbm, count_hbm, observed_hbm, weight_hbm, flux_hbm, h_hbm,
+    pick_flux_ref, target_ref, slot_obs_ref, pick_obs_ref, index_ref, observed_out, weight_out, flux_ref, h_ref,
+    fslot_ref, oslot_ref, count_ref, observed_ref, weight_ref, sems, h_sems,
 ):
     me = lax.axis_index("cell")
     owners, capacity = fslot_ref.shape[2:]
+    pairs = (
+        (fslot_hbm, fslot_ref),
+        (oslot_hbm, oslot_ref),
+        (count_hbm, count_ref),
+        (observed_hbm, observed_ref),
+        (weight_hbm, weight_ref),
+        (flux_hbm, flux_ref),
+    )
+    small = [pltpu.make_async_copy(src, dst, sems.at[i]) for i, (src, dst) in enumerate(pairs)]
+    large = [
+        pltpu.make_async_copy(h_hbm.at[:, :, o], h_ref.at[:, :, o], h_sems.at[o])
+        for o in range(owners)
+    ]
+    for copy in small + large:
+        copy.start()
+    for copy in small:
+        copy.wait()
     slots = owners * capacity
     eye = iota((capacity, capacity), 0) == iota((capacity, capacity), 1)
 
@@ -183,15 +198,16 @@
             )
     observed_out[...] = spread_obs(observed_ref[...])
     weight_out[...] = spread_obs(weight_ref[...])
+    for copy in large:
+        copy.wait()
 
 
 def first_model(parts, *refs):
-    x_parts = refs[:parts]
     h_ref, pick_flux_ref, target_ref, pick_obs_ref, m_ref, x_ref, value_scr = refs[parts:]
     flux = jnp.concatenate(
         [
-            ref[:, LANES * t : LANES * (t + 1)]
-            for ref in x_parts
+            ref[i, :, LANES * t : LANES * (t + 1)]
+            for ref, i in entries(refs[:parts])
             for t in range(CBLK_DEV // 2)
         ],
         axis=0,
@@ -202,43 +218,44 @@
     m_ref[...] = forward(h_ref, pick_obs_ref[...], x_ref, value_scr)
 
 
-def first_adjoint(parts, *refs):
-    m_parts = refs[:parts]
-    observed_ref, weight_ref, slot_obs_ref, index_ref, h_ref, message_ref, d_ref, picked_scr = refs[parts:]
-    d = weight_ref[...] * (tree_sum([m[...] for m in m_parts]) - observed_ref[...])
+def first_adjoint(
+    m_ref, other_ref, observed_ref, weight_ref, slot_obs_ref, index_ref, h_ref, message_ref, d_ref, picked_scr
+):
+    d = weight_ref[...] * (m_ref[...] + other_ref[...] - observed_ref[...])
     d_ref[...] = d
     rows = h_ref.shape[3] // 2
     half = h_ref.shape[2] * rows
 
     def store(o, block):
-        message_ref[pl.ds(pl.multiple_of(o * rows, rows), rows), :] = block
+        message_ref[0, pl.ds(pl.multiple_of(o * rows, rows), rows), :] = block
 
     adjoint(h_ref, slot_obs_ref[...], d, picked_scr, store)
-    message_ref[half:, :] = index_ref[...]
+    message_ref[0, half:, :] = index_ref[...]
 
 
 def second_model(parts, *refs):
-    messages = refs[:parts]
+    messages = entries(refs[:parts])
+    cells = len(messages)
     target_ref, x_ref, h_ref, pick_obs_ref, m_ref, next_scr, value_scr = refs[parts:]
     slots = target_ref.shape[0]
     half = slots // 2
     count = max(1, half // LANES)
-    group = max(1, min(parts, LANES // half))
+    group = max(1, min(cells, LANES // half))
     total = None
-    for first in range(0, parts, group):
+    for first in range(0, cells, group):
         members = messages[first : first + group]
         picks = []
         for part in range(2):
             rows = []
             for q in range(count):
                 at = half + part * count + q
-                row = members[0][at : at + 1, :]
-                for k in range(1, group):
-                    row = jnp.where(iota((1, LANES), 1) // half == k, members[k][at : at + 1, :], row)
+                row = jnp.zeros((1, LANES), F32)
+                for k, (ref, i) in enumerate(members):
+                    row = jnp.where(iota((1, LANES), 1) // half % group == k, ref[i, at : at + 1, :], row)
                 rows.append(one_hot(target_ref[...] == row))
             picks.append(jnp.concatenate(rows, axis=1)[:, : group * half])
         pick = jnp.concatenate(picks, axis=0)
-        values = jnp.concatenate([ref[:half, :] for ref in members], axis=0)
+        values = jnp.concatenate([ref[i, :half, :] for ref, i in members], axis=0)
         found = pick_rows(jnp.concatenate([pick] * 3, axis=1), values)
         total = found if total is None else total + found
     change = jnp.where(low((slots, LANES)), total[:slots], total[slots:])
@@ -246,56 +263,63 @@
     m_ref[...] = forward(h_ref, pick_obs_ref[...], next_scr, value_scr)
 
 
-def second_adjoint(parts, owners, *refs):
-    m_parts = refs[:parts]
-    observed_ref, weight_ref, d_ref, slot_obs_ref, h_ref = refs[parts : parts + 5]
-    outs = refs[parts + 5 : parts + 5 + owners]
-    departure_ref, picked_scr, block_scr = refs[parts + 5 + owners :]
+def second_adjoint(
+    m_ref, other_ref, observed_ref, weight_ref, first_ref, slot_obs_ref, h_ref,
+    near_ref, far_ref, d_ref, picked_scr, block_scr,
+):
     me = lax.axis_index("cell")
-    d = weight_ref[...] * (tree_sum([m[...] for m in m_parts]) - observed_ref[...])
-    for t in range(OBLK_DEV // 2):
-        departure_ref[:, LANES * t : LANES * (t + 1)] = jnp.where(
-            low((1, LANES)), d[2 * t : 2 * t + 1], d[2 * t + 1 : 2 * t + 2]
-        )
+    owners = h_ref.shape[2]
+    d = weight_ref[...] * (m_ref[...] + other_ref[...] - observed_ref[...])
+    d_ref[...] = d
 
     def store(o, block):
         block_scr[o] = block
 
-    adjoint(h_ref, slot_obs_ref[...], -0.25 * d_ref[...] - 0.5 * d, picked_scr, store)
-    for k in range(owners):
-        outs[k][...] = block_scr[me ^ k]
-
-
-def gather_increment(parts, *refs):
-    values, messages, out_ref = refs[:parts], refs[parts : 2 * parts], refs[2 * parts]
+    adjoint(h_ref, slot_obs_ref[...], -0.25 * first_ref[...] - 0.5 * d, picked_scr, store)
+    for k in range(owners // 2):
+        near_ref[k] = block_scr[me ^ k]
+        far_ref[k] = block_scr[me ^ (k + owners // 2)]
+
+
+def prepare_increment(parts, rows, *refs):
+    d_ref, pick_ref, departure_ref = refs[parts:]
+    messages = entries(refs[:parts])
+    cells = len(messages)
     me = lax.axis_index("cell")
-    rows = values[0].shape[0]
-    half = parts * rows
+    half = cells * rows
     count = max(1, half // LANES)
     place = me * rows
     lane = iota((1, LANES), 1)
     row = iota((BLOCKS, LANES), 0)
     block = me * BLOCKS + (row % WIN_DEV) * CBLK_DEV + 2 * ((row // WIN_DEV) % 4) + row // (BLOCKS // 2)
     block = block.astype(F32)
-    picks = []
     for part in range(2):
-        tiles = []
         for first in range(0, half, LANES):
             index = jnp.zeros((1, LANES), F32)
-            for k in range(first // rows, min(parts, (first + LANES) // rows)):
+            for k in range(first // rows, min(cells, (first + LANES) // rows)):
+                ref, i = messages[k]
                 turned = pltpu.roll(
-                    messages[k][half:, :], lax.rem(k * rows - place % LANES + 2 * LANES - first, LANES), 1
+                    ref[i, half:, :], lax.rem(k * rows - place % LANES + 2 * LANES - first, LANES), 1
                 )
                 chosen = turned[part * count : part * count + 1]
                 for q in range(1, count):
                     chosen = jnp.where(
                         place // LANES == q, turned[part * count + q : part * count + q + 1], chosen
                     )
-                index = jnp.where((lane // rows) % parts == k - first // rows, chosen, index)
-            tiles.append(one_hot(block == index))
-        picks.append(jnp.concatenate(tiles, axis=1))
-    pick = jnp.concatenate(picks, axis=0)
-    terms = three(jnp.concatenate([ref[...] for ref in values], axis=0))
+                index = jnp.where((lane // rows) % cells == k - first // rows, chosen, index)
+            pick_ref[BLOCKS * part : BLOCKS * (part + 1), first : first + LANES] = one_hot(block == index)
+    for t in range(OBLK_DEV // 2):
+        departure_ref[:, LANES * t : LANES * (t + 1)] = jnp.where(
+            low((1, LANES)), d_ref[2 * t : 2 * t + 1, :], d_ref[2 * t + 1 : 2 * t + 2, :]
+        )
+
+
+def gather_increment(places, *refs):
+    *arrays, pick_ref, out_ref = refs
+    values = jnp.concatenate([arrays[n][i] for n, i in places], axis=0)
+    half = values.shape[0]
+    terms = three(values)
+    pick = pick_ref[...]
     if 3 * half <= LANES:
         terms.append(jnp.zeros((LANES - 3 * half, LANES), BF16))
     else:
@@ -309,12 +333,45 @@
         out_ref[:, LANES * t : LANES * (t + 1)] = jnp.where(low(even.shape), even, odd)
 
 
-def exchange(value, axis, size):
-    return [value] + [send(value, axis, size, k) for k in range(size - 1, 0, -1)][::-1]
-
-
 def send(value, axis, size, k):
     return lax.ppermute(value, axis, [(i, i ^ k) for i in range(size)])
+
+
+def gather_doubling(own, first, axis, size):
+    held, arrived = own, send(first, axis, size, 1)
+    distance = 2
+    while distance < size:
+        held = jnp.concatenate([held, arrived], axis=0)
+        arrived = send(held, axis, size, distance)
+        distance *= 2
+    return held, arrived
+
+
+def sum_doubling(value, axis, size):
+    distance = 1
+    while 2 * distance < size:
+        value = value + send(value, axis, size, distance)
+        distance *= 2
+    return value, send(value, axis, size, distance)
+
+
+def scatter_halving(near, far, axis, size):
+    arrays = [near, far]
+    place = {(0, e): divmod(e, size // 2) for e in range(size)}
+    sources = [0]
+    distance = size // 2
+    out = far
+    while distance:
+        arrays.append(send(out, axis, size, distance))
+        moved = [(s ^ distance, e) for s in sources for e in range(distance)]
+        for n, key in enumerate(moved):
+            place[key] = (len(arrays) - 1, n)
+        sources = sources + [s ^ distance for s in sources]
+        distance //= 2
+        spots = [place[s, e] for s in sources for e in range(distance, 2 * distance)]
+        if distance:
+            out = jnp.concatenate([arrays[n][i : i + 1] for n, i in spots], axis=0)
+    return arrays, [place[e, 0] for e in range(size)]
 
 
 def make_local(cells, wins):
@@ -324,21 +381,33 @@
         half = slots // 2
         index_rows = -(-2 * max(1, half // LANES) // 8) * 8
         params = pltpu.CompilerParams(vmem_limit_bytes=4 * footprint.size * 4 + 8 * 2**20)
-
-        def call(body, outs, ins, scratch=()):
+        hbm = pl.BlockSpec(memory_space=pltpu.HBM)
+
+        def call(body, outs, ins, scratch=(), space=VMEM):
+            if space is hbm:
+                ins = [pltpu.with_memory_space_constraint(value, pltpu.HBM) for value in ins]
+                outs_at = [pltpu.VMEM(s, t) for s, t in outs]
+            else:
+                outs_at = [jax.ShapeDtypeStruct(s, t) for s, t in outs]
             return pl.pallas_call(
                 body,
-                out_shape=[jax.ShapeDtypeStruct(s, t) for s, t in outs],
-                in_specs=[VMEM] * len(ins),
+                out_shape=outs_at,
+                in_specs=[space] * len(ins),
                 out_specs=[VMEM] * len(outs),
-                scratch_shapes=[pltpu.VMEM(s, F32) for s in scratch],
+                scratch_shapes=list(scratch),
                 compiler_params=params,
             )(*ins)
 
+        def like(value):
+            return (value.shape, value.dtype)
+
         obs_tile = ((OBLK_DEV, LANES), F32)
         slot_tile = ((slots, LANES), F32)
-        flux_parts = exchange(prior_flux, "cell", cells)
-        pick_flux, target, slot_obs, pick_obs, index, observed_t, weight_t = call(
+        slot_scratch = pltpu.VMEM(*slot_tile)
+        block_pair = ((owners // 2, capacity // 2, LANES), F32)
+        flux_in = prior_flux[None]
+        small = (flux_slot, obs_slot, slot_count, observed, obs_weight)
+        pick_flux, target, slot_obs, pick_obs, index, observed_t, weight_t, flux, matrices = call(
             prepare,
             [
                 ((slots, 3 * owners * BLOCKS // 2), BF16),
@@ -348,39 +417,53 @@
                 ((index_rows, LANES), F32),
                 obs_tile,
                 obs_tile,
+                like(flux_in),
+                like(footprint),
             ],
-            (flux_slot, obs_slot, slot_count, observed, obs_weight),
-        )
+            (*small, flux_in, footprint),
+            [
+                *(pltpu.VMEM(*like(value)) for value in small),
+                pltpu.SemaphoreType.DMA((len(small) + 1,)),
+                pltpu.SemaphoreType.DMA((owners,)),
+            ],
+            hbm,
+        )
+        fluxes = gather_doubling(flux, flux_in, "cell", cells)
         m0, x0 = call(
-            functools.partial(first_model, cells),
+            functools.partial(first_model, len(fluxes)),
             [obs_tile, slot_tile],
-            (*flux_parts, footprint, pick_flux, target, pick_obs),
-            [slot_tile[0]],
+            (*fluxes, matrices, pick_flux, target, pick_obs),
+            [slot_scratch],
         )
         message, d0 = call(
-            functools.partial(first_adjoint, wins),
-            [((half + index_rows, LANES), F32), obs_tile],
-            (*exchange(m0, "win", wins), observed_t, weight_t, slot_obs, index, footprint),
-            [slot_tile[0]],
-        )
-        messages = exchange(message, "cell", cells)
+            first_adjoint,
+            [((1, half + index_rows, LANES), F32), obs_tile],
+            (*sum_doubling(m0, "win", wins), observed_t, weight_t, slot_obs, index, matrices),
+            [slot_scratch],
+        )
+        messages = gather_doubling(message, message, "cell", cells)
         (m1,) = call(
-            functools.partial(second_model, cells),
+            functools.partial(second_model, len(messages)),
             [obs_tile],
-            (*messages, target, x0, footprint, pick_obs),
-            [slot_tile[0], slot_tile[0]],
-        )
-        *blocks, departure = call(
-            functools.partial(second_adjoint, wins, owners),
-            [((capacity // 2, LANES), F32)] * owners + [((1, OBLK_DEV * OB), F32)],
-            (*exchange(m1, "win", wins), observed_t, weight_t, d0, slot_obs, footprint),
-            [slot_tile[0], (owners, capacity // 2, LANES)],
-        )
-        arrived = [send(blocks[k], "cell", cells, k) for k in range(cells - 1, 0, -1)][::-1]
+            (*messages, target, x0, matrices, pick_obs),
+            [slot_scratch, slot_scratch],
+        )
+        near, far, d1 = call(
+            second_adjoint,
+            [block_pair, block_pair, obs_tile],
+            (*sum_doubling(m1, "win", wins), observed_t, weight_t, d0, slot_obs, matrices),
+            [slot_scratch, pltpu.VMEM((owners, capacity // 2, LANES), F32)],
+        )
+        arrays, places = scatter_halving(near, far, "cell", cells)
+        pick, departure = call(
+            functools.partial(prepare_increment, len(messages), capacity // 2),
+            [((2 * BLOCKS, max(LANES, half)), BF16), ((1, OBLK_DEV * OB), F32)],
+            (*messages, d1),
+        )
         (increment,) = call(
-            functools.partial(gather_increment, cells),
+            functools.partial(gather_increment, places),
             [((WIN_DEV, CBLK_DEV * CB), F32)],
-            (blocks[0], *arrived, *messages),
+            (*arrays, pick),
         )
         return increment, departure
 

time: 41.5 us -> 42.1 us (1.014)
  local copies, waits for them, and re-layouts: 5.32 us -> 0.01 us
  waiting for transfers between devices: 11.4 us -> 15 us
  starting transfers between devices: 18.2 us -> 19.4 us
  Pallas kernels: 5.65 us -> 6.79 us
    unnamed x16 -> x2, local copies, waits for them, and re-layouts: 5.32 us -> 0.01 us
    ppermute x15 -> x10, waiting for transfers between devices: 11.4 us -> 15 us  [send(): return lax.ppermute(value, axis, [(i, i ^ k) for i in range(size)])]
    ppermute x15 -> x10, starting transfers between devices: 18.2 us -> 19.4 us  [send(): return lax.ppermute(value, axis, [(i, i ^ k) for i in range(size)])]
    pallas_call x6 -> x7, Pallas kernels: 5.65 us -> 6.79 us  [call(): pl.pallas_call(body, out_shape=outs_at, in_specs=[space] * len(ins), out_...]
  transfers between devices with their start and end apart: 15 -> 10, of which waited for: 9 -> 10; matrix products, arithmetic and copies ran while one was open for 0% -> 0% of each run, Pallas kernels for 1% -> 5%
where the time goes in v4:
time: 42.1 us; the launch traced here: 41.9 us
  starting transfers between devices  19.4 us (46%)
  waiting for transfers between devices  15 us (36%)
  Pallas kernels  6.79 us (16%)
  between operations  0.67 us (2%)
    ppermute x10, starting transfers between devices, send(): return lax.ppermute(value, axis, [(i, i ^ k) for i in range(size)])  19.4 us
    ppermute x10, waiting for transfers between devices, send(): return lax.ppermute(value, axis, [(i, i ^ k) for i in range(size)])  15 us
    pallas_call x7, Pallas kernels, call(): pl.pallas_call(body, out_shape=outs_at, in_specs=[space] * len(ins), out_...  6.79 us
  transfers between devices with their start and end apart: 10, of which 10 were waited for; matrix products, arithmetic and copies ran while one was open for 0% of the time, Pallas kernels for 5%

profile of v4, /device:TPU:0, one launch (start us, length us, event | category | flops | bytes accessed | tf_op | source)
XLA Modules:
  0.0 41.9 jit_solution(4769766357637864477)
XLA Ops:
  0.6 3.1 %collective-permute-start = (f32[1,8,512]{2,1,0:T(8,128)}, f32[1,8,512]{2,1,0:T(8,128)S(1)}, u32[]{:S(2)}, u32[]{:S(2)}) collective-permute-start(f32[1,8,512]{2,1,0:T(8,128)} %bitcast.1), channel_id=1, source_target_pairs={{0,4},{4,0},{8,12},{12,8},{1,5},{5,1},{9,13},{13,9},{2,6},{6,2},{1... | collective-permute-start | bytes 49160 | tf_op jit(solution)/shard_map/ppermute | solution.py:337
  3.7 1.4 %shard_map.86 = (bf16[64,384]{1,0:T(8,128)(2,1)S(1)}, f32[64,128]{1,0:T(8,128)S(1)}, bf16[64,24]{1,0:T(8,128)(2,1)S(1)}, bf16[16,192]{1,0:T(8,128)(2,1)S(1)}, f3...) custom-call(s32[1,1,4,16]{3,2,1,0:T(4,128)} %fslot_hbm.1, ...), custom_call_target="tpu_custom_call" | custom-call | tf_op jit(solution)/shard_map/pallas_call | solution.py:392
  5.1 0.5 %collective-permute-done = f32[1,8,512]{2,1,0:T(8,128)S(1)} collective-permute-done((f32[1,8,512]{2,1,0:T(8,128)}, f32[1,8,512]{2,1,0:T(8,128)S(1)}, u32[]{:S(2)}, u32[]{:S(2)}) %collective-permute-start) | collective-permute-done | bytes 16416 | tf_op jit(solution)/shard_map/ppermute | solution.py:337
  5.7 3.0 %collective-permute-start.1 = (f32[2,8,512]{2,1,0:T(8,128)S(1)}, f32[2,8,512]{2,1,0:T(8,128)S(1)}, u32[]{:S(2)}, u32[]{:S(2)}) collective-permute-start(f32[2,8,512]{2,1,0:T(8,128)S(1)} %constant_dynamic-update-slice_fusion.refs_0_), channel_id=1, source_target_pairs={{0,8},{4,12},{8,0},{12,4},{1,9},{5,13},{9,1},{13,5},{2,10},{6,14},... | collective-permute-start | bytes 98312 | tf_op jit(solution)/shard_map/ppermute | solution.py:337
  8.7 1.9 %collective-permute-done.1.refs_1_ = f32[2,8,512]{2,1,0:T(8,128)S(1)} collective-permute-done((f32[2,8,512]{2,1,0:T(8,128)S(1)}, f32[2,8,512]{2,1,0:T(8,128)S(1)}, u32[]{:S(2)}, u32[]{:S(2)}) %collective-permute-start.1) | collective-permute-done | bytes 32800 | tf_op jit(solution)/shard_map/ppermute | solution.py:337
  10.6 1.0 %shard_map.87 = (f32[8,128]{1,0:T(8,128)S(1)}, f32[64,128]{1,0:T(8,128)S(1)}) custom-call(f32[2,8,512]{2,1,0:T(8,128)S(1)} %constant_dynamic-update-slice_fusion.refs_0_, f32[2,8,512]{2,1,0:T(8,128)S(1)} %collective-permute-done.1.refs_1_, f32[1,1,4,16,4096]{4,3,2,1,0:T(8,128)S(1)} %get-tuple-element.21.refs_2_.h_ref.refs_4_, ...), custom_call_target="tpu_custom_call" | custom-call | tf_op jit(solution)/shard_map/pallas_call | solution.py:392
  11.6 0.0 collective-permute-start.2
  11.6 1.2 %collective-permute-done.2 = f32[8,128]{1,0:T(8,128)S(1)} collective-permute-done((f32[8,128]{1,0:T(8,128)S(1)}, f32[8,128]{1,0:T(8,128)S(1)}, u32[]{:S(2)}, u32[]{:S(2)}) %collective-permute-start.2) | collective-permute-done | bytes 4128 | tf_op jit(solution)/shard_map/ppermute | solution.py:337
  12.8 1.8 %collective-permute-start.3 = (f32[8,128]{1,0:T(8,128)S(1)}, f32[8,128]{1,0:T(8,128)S(1)}, u32[]{:S(2)}, u32[]{:S(2)}) collective-permute-start(f32[8,128]{1,0:T(8,128)S(1)} %add.6.m_ref), channel_id=1, source_target_pairs={{0,2},{1,3},{2,0},{3,1},{4,6},{5,7},{6,4},{7,5},{8,10},{9,11},{10,... | collective-permute-start | bytes 12296 | tf_op jit(solution)/shard_map/ppermute | solution.py:337
  14.6 1.8 %collective-permute-done.3.other_ref = f32[8,128]{1,0:T(8,128)S(1)} collective-permute-done((f32[8,128]{1,0:T(8,128)S(1)}, f32[8,128]{1,0:T(8,128)S(1)}, u32[]{:S(2)}, u32[]{:S(2)}) %collective-permute-start.3) | collective-permute-done | bytes 4128 | tf_op jit(solution)/shard_map/ppermute | solution.py:337
  16.4 1.0 %shard_map.88 = (f32[1,40,128]{2,1,0:T(8,128)S(1)}, f32[8,128]{1,0:T(8,128)S(1)}) custom-call(f32[8,128]{1,0:T(8,128)S(1)} %add.6.m_ref, f32[8,128]{1,0:T(8,128)S(1)} %collective-permute-done.3.other_ref, f32[8,128]{1,0:T(8,128)S(1)} %get-tuple-element.26.observed_ref, f32[8,128]{1,0:T(8,128)S(1)} %get-tuple-element.27.weight_ref, ...), custom_call_target="tpu_custom_call" | custom-call | tf_op jit(solution)/shard_map/pallas_call | solution.py:392
  17.4 1.9 %collective-permute-start.4 = (f32[1,40,128]{2,1,0:T(8,128)S(1)}, f32[1,40,128]{2,1,0:T(8,128)S(1)}, u32[]{:S(2)}, u32[]{:S(2)}) collective-permute-start(f32[1,40,128]{2,1,0:T(8,128)S(1)} %get-tuple-element.30), channel_id=1, source_target_pairs={{0,4},{4,0},{8,12},{12,8},{1,5},{5,1},{9,13},{13,9},{2,6},{6,2},{1... | collective-permute-start | bytes 61448 | tf_op jit(solution)/shard_map/ppermute | solution.py:337
  19.3 1.9 %collective-permute-done.4 = f32[1,40,128]{2,1,0:T(8,128)S(1)} collective-permute-done((f32[1,40,128]{2,1,0:T(8,128)S(1)}, f32[1,40,128]{2,1,0:T(8,128)S(1)}, u32[]{:S(2)}, u32[]{:S(2)}) %collective-permute-start.4) | collective-permute-done | bytes 20512 | tf_op jit(solution)/shard_map/ppermute | solution.py:337
  21.2 2.9 %collective-permute-start.5 = (f32[2,40,128]{2,1,0:T(8,128)S(1)}, f32[2,40,128]{2,1,0:T(8,128)S(1)}, u32[]{:S(2)}, u32[]{:S(2)}) collective-permute-start(f32[2,40,128]{2,1,0:T(8,128)S(1)} %constant_dynamic-update-slice_fusion.2.refs_0_), channel_id=1, source_target_pairs={{0,8},{4,12},{8,0},{12,4},{1,9},{5,13},{9,1},{13,5},{2,10},{6,14},... | collective-permute-start | bytes 122888 | tf_op jit(solution)/shard_map/ppermute | solution.py:337
  24.1 2.0 %collective-permute-done.5.refs_1_ = f32[2,40,128]{2,1,0:T(8,128)S(1)} collective-permute-done((f32[2,40,128]{2,1,0:T(8,128)S(1)}, f32[2,40,128]{2,1,0:T(8,128)S(1)}, u32[]{:S(2)}, u32[]{:S(2)}) %collective-permute-start.5) | collective-permute-done | bytes 40992 | tf_op jit(solution)/shard_map/ppermute | solution.py:337
  26.1 1.0 %shard_map.89 = f32[8,128]{1,0:T(8,128)S(1)} custom-call(f32[2,40,128]{2,1,0:T(8,128)S(1)} %constant_dynamic-update-slice_fusion.2.refs_0_, f32[2,40,128]{2,1,0:T(8,128)S(1)} %collective-permute-done.5.refs_1_, f32[64,128]{1,0:T(8,128)S(1)} %get-tuple-element.23.refs_4_.refs_2_, f32[64,128]{1,0:T(8,128)S(1)} %get-tuple-element.31.refs_3_, ...), custom_call_target="tpu_custom_call" | custom-call | tf_op jit(solution)/shard_map/pallas_call | solution.py:392
  27.1 0.0 collective-permute-start.6
  27.1 1.2 %collective-permute-done.6 = f32[8,128]{1,0:T(8,128)S(1)} collective-permute-done((f32[8,128]{1,0:T(8,128)S(1)}, f32[8,128]{1,0:T(8,128)S(1)}, u32[]{:S(2)}, u32[]{:S(2)}) %collective-permute-start.6) | collective-permute-done | bytes 4128 | tf_op jit(solution)/shard_map/ppermute | solution.py:337
  28.3 1.8 %collective-permute-start.7 = (f32[8,128]{1,0:T(8,128)S(1)}, f32[8,128]{1,0:T(8,128)S(1)}, u32[]{:S(2)}, u32[]{:S(2)}) collective-permute-start(f32[8,128]{1,0:T(8,128)S(1)} %add.7.m_ref), channel_id=1, source_target_pairs={{0,2},{1,3},{2,0},{3,1},{4,6},{5,7},{6,4},{7,5},{8,10},{9,11},{10,... | collective-permute-start | bytes 12296 | tf_op jit(solution)/shard_map/ppermute | solution.py:337
  30.1 1.8 %collective-permute-done.7.other_ref = f32[8,128]{1,0:T(8,128)S(1)} collective-permute-done((f32[8,128]{1,0:T(8,128)S(1)}, f32[8,128]{1,0:T(8,128)S(1)}, u32[]{:S(2)}, u32[]{:S(2)}) %collective-permute-start.7) | collective-permute-done | bytes 4128 | tf_op jit(solution)/shard_map/ppermute | solution.py:337
  31.9 1.0 %shard_map.90 = (f32[2,8,128]{2,1,0:T(8,128)S(1)}, f32[2,8,128]{2,1,0:T(8,128)S(1)}, f32[8,128]{1,0:T(8,128)S(1)}) custom-call(f32[8,128]{1,0:T(8,128)S(1)} %add.7.m_ref, f32[8,128]{1,0:T(8,128)S(1)} %collective-permute-done.7.other_ref, f32[8,128]{1,0:T(8,128)S(1)} %get-tuple-element.26.observed_ref, f32[8,128]{1,0:T(8,128)S(1)} %get-tuple-element.27.weight_ref, ...), custom_call_target="tpu_custom_call" | custom-call | tf_op jit(solution)/shard_map/pallas_call | solution.py:392
  32.9 2.9 %collective-permute-start.8 = (f32[2,8,128]{2,1,0:T(8,128)S(1)}, f32[2,8,128]{2,1,0:T(8,128)S(1)}, u32[]{:S(2)}, u32[]{:S(2)}) collective-permute-start(f32[2,8,128]{2,1,0:T(8,128)S(1)} %get-tuple-element.34.refs_1_), channel_id=1, source_target_pairs={{0,8},{4,12},{8,0},{12,4},{1,9},{5,13},{9,1},{13,5},{2,10},{6,14},... | collective-permute-start | bytes 24584 | tf_op jit(solution)/shard_map/ppermute | solution.py:337
  35.8 1.6 %collective-permute-done.8.refs_2_ = f32[2,8,128]{2,1,0:T(8,128)S(1)} collective-permute-done((f32[2,8,128]{2,1,0:T(8,128)S(1)}, f32[2,8,128]{2,1,0:T(8,128)S(1)}, u32[]{:S(2)}, u32[]{:S(2)}) %collective-permute-start.8) | collective-permute-done | bytes 8224 | tf_op jit(solution)/shard_map/ppermute | solution.py:337
  37.5 1.9 %collective-permute-start.9 = (f32[2,8,128]{2,1,0:T(8,128)S(1)}, f32[2,8,128]{2,1,0:T(8,128)S(1)}, u32[]{:S(2)}, u32[]{:S(2)}) collective-permute-start(f32[2,8,128]{2,1,0:T(8,128)S(1)} %pad_maximum_fusion), channel_id=1, source_target_pairs={{0,4},{4,0},{8,12},{12,8},{1,5},{5,1},{9,13},{13,9},{2,6},{6,2},{1... | collective-permute-start | bytes 24584 | tf_op jit(solution)/shard_map/ppermute | solution.py:337
  39.4 0.6 %shard_map.91 = (bf16[128,128]{1,0:T(8,128)(2,1)S(1)}, f32[1,512]{1,0:T(1,128)}) custom-call(f32[2,40,128]{2,1,0:T(8,128)S(1)} %constant_dynamic-update-slice_fusion.2.refs_0_, f32[2,40,128]{2,1,0:T(8,128)S(1)} %collective-permute-done.5.refs_1_, f32[8,128]{1,0:T(8,128)S(1)} %get-tuple-element.35.refs_2_), custom_call_target="tpu_custom_call" | custom-call | tf_op jit(solution)/shard_map/pallas_call | solution.py:392
  40.0 1.2 %collective-permute-done.9.refs_3_ = f32[2,8,128]{2,1,0:T(8,128)S(1)} collective-permute-done((f32[2,8,128]{2,1,0:T(8,128)S(1)}, f32[2,8,128]{2,1,0:T(8,128)S(1)}, u32[]{:S(2)}, u32[]{:S(2)}) %collective-permute-start.9) | collective-permute-done | bytes 8224 | tf_op jit(solution)/shard_map/ppermute | solution.py:337
  41.1 0.8 %shard_map.92 = f32[8,512]{1,0:T(8,128)} custom-call(f32[2,8,128]{2,1,0:T(8,128)S(1)} %get-tuple-element.33.refs_0_, f32[2,8,128]{2,1,0:T(8,128)S(1)} %get-tuple-element.34.refs_1_, f32[2,8,128]{2,1,0:T(8,128)S(1)} %collective-permute-done.8.refs_2_, f32[2,8,128]{2,1,0:T(8,128)S(1)} %collective-permute-done.9.refs_3_, ...), custom_call_target="tpu_custom_call" | custom-call | tf_op jit(solution)/shard_map/pallas_call | solution.py:392
  (9 shorter events, 0.0 us)
Async XLA Ops:
  0.6 5.0 %collective-permute-start = (f32[1,8,512]{2,1,0:T(8,128)}, f32[1,8,512]{2,1,0:T(8,128)S(1)}, u32[]{:S(2)}, u32[]{:S(2)}) collective-permute-start(f32[1,8,512]{2,1,0:T(8,128)} %bitcast.1), channel_id=1, source_target_pairs={{0,4},{4,0},{8,12},{12,8},{1,5},{5,1},{9,13},{13,9},{2,6},{6,2},{1... | collective-permute-start | bytes 49160 | tf_op jit(solution)/shard_map/ppermute | solution.py:337
  5.7 4.9 %collective-permute-start.1 = (f32[2,8,512]{2,1,0:T(8,128)S(1)}, f32[2,8,512]{2,1,0:T(8,128)S(1)}, u32[]{:S(2)}, u32[]{:S(2)}) collective-permute-start(f32[2,8,512]{2,1,0:T(8,128)S(1)} %constant_dynamic-update-slice_fusion.refs_0_), channel_id=1, source_target_pairs={{0,8},{4,12},{8,0},{12,4},{1,9},{5,13},{9,1},{13,5},{2,10},{6,14},... | collective-permute-start | bytes 98312 | tf_op jit(solution)/shard_map/ppermute | solution.py:337
  11.6 1.2 %collective-permute-start.2 = (f32[8,128]{1,0:T(8,128)S(1)}, f32[8,128]{1,0:T(8,128)S(1)}, u32[]{:S(2)}, u32[]{:S(2)}) collective-permute-start(f32[8,128]{1,0:T(8,128)S(1)} %get-tuple-element.25), channel_id=1, source_target_pairs={{0,1},{1,0},{2,3},{3,2},{4,5},{5,4},{6,7},{7,6},{8,9},{9,8},{10,11... | collective-permute-start | bytes 12296 | tf_op jit(solution)/shard_map/ppermute | solution.py:337
  12.8 3.6 %collective-permute-start.3 = (f32[8,128]{1,0:T(8,128)S(1)}, f32[8,128]{1,0:T(8,128)S(1)}, u32[]{:S(2)}, u32[]{:S(2)}) collective-permute-start(f32[8,128]{1,0:T(8,128)S(1)} %add.6.m_ref), channel_id=1, source_target_pairs={{0,2},{1,3},{2,0},{3,1},{4,6},{5,7},{6,4},{7,5},{8,10},{9,11},{10,... | collective-permute-start | bytes 12296 | tf_op jit(solution)/shard_map/ppermute | solution.py:337
  17.4 3.8 %collective-permute-start.4 = (f32[1,40,128]{2,1,0:T(8,128)S(1)}, f32[1,40,128]{2,1,0:T(8,128)S(1)}, u32[]{:S(2)}, u32[]{:S(2)}) collective-permute-start(f32[1,40,128]{2,1,0:T(8,128)S(1)} %get-tuple-element.30), channel_id=1, source_target_pairs={{0,4},{4,0},{8,12},{12,8},{1,5},{5,1},{9,13},{13,9},{2,6},{6,2},{1... | collective-permute-start | bytes 61448 | tf_op jit(solution)/shard_map/ppermute | solution.py:337
  21.2 4.9 %collective-permute-start.5 = (f32[2,40,128]{2,1,0:T(8,128)S(1)}, f32[2,40,128]{2,1,0:T(8,128)S(1)}, u32[]{:S(2)}, u32[]{:S(2)}) collective-permute-start(f32[2,40,128]{2,1,0:T(8,128)S(1)} %constant_dynamic-update-slice_fusion.2.refs_0_), channel_id=1, source_target_pairs={{0,8},{4,12},{8,0},{12,4},{1,9},{5,13},{9,1},{13,5},{2,10},{6,14},... | collective-permute-start | bytes 122888 | tf_op jit(solution)/shard_map/ppermute | solution.py:337
  27.1 1.2 %collective-permute-start.6 = (f32[8,128]{1,0:T(8,128)S(1)}, f32[8,128]{1,0:T(8,128)S(1)}, u32[]{:S(2)}, u32[]{:S(2)}) collective-permute-start(f32[8,128]{1,0:T(8,128)S(1)} %shard_map.89), channel_id=1, source_target_pairs={{0,1},{1,0},{2,3},{3,2},{4,5},{5,4},{6,7},{7,6},{8,9},{9,8},{10,11... | collective-permute-start | bytes 12296 | tf_op jit(solution)/shard_map/ppermute | solution.py:337
  28.3 3.6 %collective-permute-start.7 = (f32[8,128]{1,0:T(8,128)S(1)}, f32[8,128]{1,0:T(8,128)S(1)}, u32[]{:S(2)}, u32[]{:S(2)}) collective-permute-start(f32[8,128]{1,0:T(8,128)S(1)} %add.7.m_ref), channel_id=1, source_target_pairs={{0,2},{1,3},{2,0},{3,1},{4,6},{5,7},{6,4},{7,5},{8,10},{9,11},{10,... | collective-permute-start | bytes 12296 | tf_op jit(solution)/shard_map/ppermute | solution.py:337
  32.9 4.6 %collective-permute-start.8 = (f32[2,8,128]{2,1,0:T(8,128)S(1)}, f32[2,8,128]{2,1,0:T(8,128)S(1)}, u32[]{:S(2)}, u32[]{:S(2)}) collective-permute-start(f32[2,8,128]{2,1,0:T(8,128)S(1)} %get-tuple-element.34.refs_1_), channel_id=1, source_target_pairs={{0,8},{4,12},{8,0},{12,4},{1,9},{5,13},{9,1},{13,5},{2,10},{6,14},... | collective-permute-start | bytes 24584 | tf_op jit(solution)/shard_map/ppermute | solution.py:337
  37.5 3.7 %collective-permute-start.9 = (f32[2,8,128]{2,1,0:T(8,128)S(1)}, f32[2,8,128]{2,1,0:T(8,128)S(1)}, u32[]{:S(2)}, u32[]{:S(2)}) collective-permute-start(f32[2,8,128]{2,1,0:T(8,128)S(1)} %pad_maximum_fusion), channel_id=1, source_target_pairs={{0,4},{4,0},{8,12},{12,8},{1,5},{5,1},{9,13},{13,9},{2,6},{6,2},{1... | collective-permute-start | bytes 24584 | tf_op jit(solution)/shard_map/ppermute | solution.py:337

commit v5 on v4

--- a/solution.py
+++ b/solution.py
@@ -54,8 +54,11 @@
     return iota(shape, 1) < LANES // 2
 
 
-def entries(refs):
-    return [(ref, i) for ref in refs for i in range(ref.shape[0])]
+def tree_sum(parts):
+    parts = list(parts)
+    while len(parts) > 1:
+        parts = [sum(parts[i + 1 : i + 2], parts[i]) for i in range(0, len(parts), 2)]
+    return parts[0]
 
 
 def spread_obs(row):
@@ -202,12 +205,13 @@
         copy.wait()
 
 
-def first_model(parts, *refs):
+def first_model(order, *refs):
+    parts = len(order)
     h_ref, pick_flux_ref, target_ref, pick_obs_ref, m_ref, x_ref, value_scr = refs[parts:]
     flux = jnp.concatenate(
         [
-            ref[i, :, LANES * t : LANES * (t + 1)]
-            for ref, i in entries(refs[:parts])
+            ref[:, LANES * t : LANES * (t + 1)]
+            for ref in [refs[order.index(k)] for k in range(parts)]
             for t in range(CBLK_DEV // 2)
         ],
         axis=0,
@@ -218,24 +222,23 @@
     m_ref[...] = forward(h_ref, pick_obs_ref[...], x_ref, value_scr)
 
 
-def first_adjoint(
-    m_ref, other_ref, observed_ref, weight_ref, slot_obs_ref, index_ref, h_ref, message_ref, d_ref, picked_scr
-):
-    d = weight_ref[...] * (m_ref[...] + other_ref[...] - observed_ref[...])
+def first_adjoint(parts, *refs):
+    observed_ref, weight_ref, slot_obs_ref, index_ref, h_ref, message_ref, d_ref, picked_scr = refs[parts:]
+    d = weight_ref[...] * (tree_sum([m[...] for m in refs[:parts]]) - observed_ref[...])
     d_ref[...] = d
     rows = h_ref.shape[3] // 2
     half = h_ref.shape[2] * rows
 
     def store(o, block):
-        message_ref[0, pl.ds(pl.multiple_of(o * rows, rows), rows), :] = block
+        message_ref[pl.ds(pl.multiple_of(o * rows, rows), rows), :] = block
 
     adjoint(h_ref, slot_obs_ref[...], d, picked_scr, store)
-    message_ref[0, half:, :] = index_ref[...]
+    message_ref[half:, :] = index_ref[...]
 
 
 def second_model(parts, *refs):
-    messages = entries(refs[:parts])
-    cells = len(messages)
+    messages = refs[:parts]
+    cells = parts
     target_ref, x_ref, h_ref, pick_obs_ref, m_ref, next_scr, value_scr = refs[parts:]
     slots = target_ref.shape[0]
     half = slots // 2
@@ -250,12 +253,12 @@
             for q in range(count):
                 at = half + part * count + q
                 row = jnp.zeros((1, LANES), F32)
-                for k, (ref, i) in enumerate(members):
-                    row = jnp.where(iota((1, LANES), 1) // half % group == k, ref[i, at : at + 1, :], row)
+                for k, ref in enumerate(members):
+                    row = jnp.where(iota((1, LANES), 1) // half % group == k, ref[at : at + 1, :], row)
                 rows.append(one_hot(target_ref[...] == row))
             picks.append(jnp.concatenate(rows, axis=1)[:, : group * half])
         pick = jnp.concatenate(picks, axis=0)
-        values = jnp.concatenate([ref[i, :half, :] for ref, i in members], axis=0)
+        values = jnp.concatenate([ref[:half, :] for ref in members], axis=0)
         found = pick_rows(jnp.concatenate([pick] * 3, axis=1), values)
         total = found if total is None else total + found
     change = jnp.where(low((slots, LANES)), total[:slots], total[slots:])
@@ -263,28 +266,26 @@
     m_ref[...] = forward(h_ref, pick_obs_ref[...], next_scr, value_scr)
 
 
-def second_adjoint(
-    m_ref, other_ref, observed_ref, weight_ref, first_ref, slot_obs_ref, h_ref,
-    near_ref, far_ref, d_ref, picked_scr, block_scr,
-):
+def second_adjoint(parts, *refs):
+    observed_ref, weight_ref, first_ref, slot_obs_ref, h_ref = refs[parts : parts + 5]
+    *outs, d_ref, picked_scr, block_scr = refs[parts + 5 :]
     me = lax.axis_index("cell")
     owners = h_ref.shape[2]
-    d = weight_ref[...] * (m_ref[...] + other_ref[...] - observed_ref[...])
+    d = weight_ref[...] * (tree_sum([m[...] for m in refs[:parts]]) - observed_ref[...])
     d_ref[...] = d
 
     def store(o, block):
         block_scr[o] = block
 
     adjoint(h_ref, slot_obs_ref[...], -0.25 * first_ref[...] - 0.5 * d, picked_scr, store)
-    for k in range(owners // 2):
-        near_ref[k] = block_scr[me ^ k]
-        far_ref[k] = block_scr[me ^ (k + owners // 2)]
+    for k in range(owners):
+        outs[owners - 1 - k][...] = block_scr[me ^ k]
 
 
 def prepare_increment(parts, rows, *refs):
     d_ref, pick_ref, departure_ref = refs[parts:]
-    messages = entries(refs[:parts])
-    cells = len(messages)
+    messages = refs[:parts]
+    cells = parts
     me = lax.axis_index("cell")
     half = cells * rows
     count = max(1, half // LANES)
@@ -297,9 +298,8 @@
         for first in range(0, half, LANES):
             index = jnp.zeros((1, LANES), F32)
             for k in range(first // rows, min(cells, (first + LANES) // rows)):
-                ref, i = messages[k]
                 turned = pltpu.roll(
-                    ref[i, half:, :], lax.rem(k * rows - place % LANES + 2 * LANES - first, LANES), 1
+                    messages[k][half:, :], lax.rem(k * rows - place % LANES + 2 * LANES - first, LANES), 1
                 )
                 chosen = turned[part * count : part * count + 1]
                 for q in range(1, count):
@@ -314,9 +314,9 @@
         )
 
 
-def gather_increment(places, *refs):
+def gather_increment(*refs):
     *arrays, pick_ref, out_ref = refs
-    values = jnp.concatenate([arrays[n][i] for n, i in places], axis=0)
+    values = jnp.concatenate([ref[...] for ref in arrays[::-1]], axis=0)
     half = values.shape[0]
     terms = three(values)
     pick = pick_ref[...]
@@ -337,41 +337,8 @@
     return lax.ppermute(value, axis, [(i, i ^ k) for i in range(size)])
 
 
-def gather_doubling(own, first, axis, size):
-    held, arrived = own, send(first, axis, size, 1)
-    distance = 2
-    while distance < size:
-        held = jnp.concatenate([held, arrived], axis=0)
-        arrived = send(held, axis, size, distance)
-        distance *= 2
-    return held, arrived
-
-
-def sum_doubling(value, axis, size):
-    distance = 1
-    while 2 * distance < size:
-        value = value + send(value, axis, size, distance)
-        distance *= 2
-    return value, send(value, axis, size, distance)
-
-
-def scatter_halving(near, far, axis, size):
-    arrays = [near, far]
-    place = {(0, e): divmod(e, size // 2) for e in range(size)}
-    sources = [0]
-    distance = size // 2
-    out = far
-    while distance:
-        arrays.append(send(out, axis, size, distance))
-        moved = [(s ^ distance, e) for s in sources for e in range(distance)]
-        for n, key in enumerate(moved):
-            place[key] = (len(arrays) - 1, n)
-        sources = sources + [s ^ distance for s in sources]
-        distance //= 2
-        spots = [place[s, e] for s in sources for e in range(distance, 2 * distance)]
-        if distance:
-            out = jnp.concatenate([arrays[n][i : i + 1] for n, i in spots], axis=0)
-    return arrays, [place[e, 0] for e in range(size)]
+def exchange(own, sent, axis, size):
+    return [own] + [send(sent, axis, size, k) for k in range(size - 1, 0, -1)][::-1]
 
 
 def make_local(cells, wins):
@@ -404,8 +371,6 @@
         obs_tile = ((OBLK_DEV, LANES), F32)
         slot_tile = ((slots, LANES), F32)
         slot_scratch = pltpu.VMEM(*slot_tile)
-        block_pair = ((owners // 2, capacity // 2, LANES), F32)
-        flux_in = prior_flux[None]
         small = (flux_slot, obs_slot, slot_count, observed, obs_weight)
         pick_flux, target, slot_obs, pick_obs, index, observed_t, weight_t, flux, matrices = call(
             prepare,
@@ -417,10 +382,10 @@
                 ((index_rows, LANES), F32),
                 obs_tile,
                 obs_tile,
-                like(flux_in),
+                like(prior_flux),
                 like(footprint),
             ],
-            (*small, flux_in, footprint),
+            (*small, prior_flux, footprint),
             [
                 *(pltpu.VMEM(*like(value)) for value in small),
                 pltpu.SemaphoreType.DMA((len(small) + 1,)),
@@ -428,42 +393,44 @@
             ],
             hbm,
         )
-        fluxes = gather_doubling(flux, flux_in, "cell", cells)
+        order = [0, cells - 1, *range(1, cells - 1)]
+        fluxes = exchange(flux, prior_flux, "cell", cells)
         m0, x0 = call(
-            functools.partial(first_model, len(fluxes)),
+            functools.partial(first_model, order),
             [obs_tile, slot_tile],
-            (*fluxes, matrices, pick_flux, target, pick_obs),
+            (*(fluxes[k] for k in order), matrices, pick_flux, target, pick_obs),
             [slot_scratch],
         )
         message, d0 = call(
-            first_adjoint,
-            [((1, half + index_rows, LANES), F32), obs_tile],
-            (*sum_doubling(m0, "win", wins), observed_t, weight_t, slot_obs, index, matrices),
+            functools.partial(first_adjoint, wins),
+            [((half + index_rows, LANES), F32), obs_tile],
+            (*exchange(m0, m0, "win", wins), observed_t, weight_t, slot_obs, index, matrices),
             [slot_scratch],
         )
-        messages = gather_doubling(message, message, "cell", cells)
+        messages = exchange(message, message, "cell", cells)
         (m1,) = call(
-            functools.partial(second_model, len(messages)),
+            functools.partial(second_model, cells),
             [obs_tile],
             (*messages, target, x0, matrices, pick_obs),
             [slot_scratch, slot_scratch],
         )
-        near, far, d1 = call(
-            second_adjoint,
-            [block_pair, block_pair, obs_tile],
-            (*sum_doubling(m1, "win", wins), observed_t, weight_t, d0, slot_obs, matrices),
+        *blocks, d1 = call(
+            functools.partial(second_adjoint, wins),
+            [((capacity // 2, LANES), F32)] * owners + [obs_tile],
+            (*exchange(m1, m1, "win", wins), observed_t, weight_t, d0, slot_obs, matrices),
             [slot_scratch, pltpu.VMEM((owners, capacity // 2, LANES), F32)],
         )
-        arrays, places = scatter_halving(near, far, "cell", cells)
+        arrays = [send(block, "cell", cells, cells - 1 - i) for i, block in enumerate(blocks[:-1])]
+        arrays = [blocks[-1]] + arrays[::-1]
         pick, departure = call(
-            functools.partial(prepare_increment, len(messages), capacity // 2),
+            functools.partial(prepare_increment, cells, capacity // 2),
             [((2 * BLOCKS, max(LANES, half)), BF16), ((1, OBLK_DEV * OB), F32)],
             (*messages, d1),
         )
         (increment,) = call(
-            functools.partial(gather_increment, places),
+            gather_increment,
             [((WIN_DEV, CBLK_DEV * CB), F32)],
-            (*arrays, pick),
+            (*arrays[::-1], pick),
         )
         return increment, departure
 

time: 42.1 us -> 36.2 us (0.86)
  waiting for transfers between devices: 15 us -> 10.3 us
  starting transfers between devices: 19.4 us -> 18.3 us
    ppermute x10 -> x15, waiting for transfers between devices: 15 us -> 10.3 us  [send(): return lax.ppermute(value, axis, [(i, i ^ k) for i in range(size)])]
    ppermute x10 -> x15, starting transfers between devices: 19.4 us -> 18.3 us  [send(): return lax.ppermute(value, axis, [(i, i ^ k) for i in range(size)])]
  transfers between devices with their start and end apart: 10 -> 15, of which waited for: 10 -> 10; matrix products, arithmetic and copies ran while one was open for 0% -> 0% of each run, Pallas kernels for 5% -> 5%
where the time goes in v5:
time: 36.2 us; the launch traced here: 36 us
  starting transfers between devices  18.3 us (51%)
  waiting for transfers between devices  10.3 us (28%)
  Pallas kernels  6.79 us (19%)
  between operations  0.67 us (2%)
    ppermute x15, starting transfers between devices, send(): return lax.ppermute(value, axis, [(i, i ^ k) for i in range(size)])  18.3 us
    ppermute x15, waiting for transfers between devices, send(): return lax.ppermute(value, axis, [(i, i ^ k) for i in range(size)])  10.3 us
    pallas_call x7, Pallas kernels, call(): pl.pallas_call(body, out_shape=outs_at, in_specs=[space] * len(ins), out_...  6.79 us
  transfers between devices with their start and end apart: 15, of which 10 were waited for; matrix products, arithmetic and copies ran while one was open for 0% of the time, Pallas kernels for 5%

profile of v5, /device:TPU:0, one launch (start us, length us, event | category | flops | bytes accessed | tf_op | source)
XLA Modules:
  0.0 36.0 jit_solution(15787675226020194601)
XLA Ops:
  0.6 5.1 %collective-permute-start = (f32[8,512]{1,0:T(8,128)}, f32[8,512]{1,0:T(8,128)S(1)}, u32[]{:S(2)}, u32[]{:S(2)}) collective-permute-start(f32[8,512]{1,0:T(8,128)} %flux_hbm.1), channel_id=1, source_target_pairs={{0,12},{4,8},{8,4},{12,0},{1,13},{5,9},{9,5},{13,1},{2,14},{6,10},... | collective-permute-start | bytes 49160 | tf_op jit(solution)/shard_map/ppermute | solution.py:337
  5.7 0.0 collective-permute-start.2
  5.8 0.6 %collective-permute-start.1 = (f32[8,512]{1,0:T(8,128)}, f32[8,512]{1,0:T(8,128)S(1)}, u32[]{:S(2)}, u32[]{:S(2)}) collective-permute-start(f32[8,512]{1,0:T(8,128)} %flux_hbm.1), channel_id=1, source_target_pairs={{0,4},{4,0},{8,12},{12,8},{1,5},{5,1},{9,13},{13,9},{2,6},{6,2},{1... | collective-permute-start | bytes 49160 | tf_op jit(solution)/shard_map/ppermute | solution.py:337
  6.4 1.4 %shard_map.86 = (bf16[64,384]{1,0:T(8,128)(2,1)S(1)}, f32[64,128]{1,0:T(8,128)S(1)}, bf16[64,24]{1,0:T(8,128)(2,1)S(1)}, bf16[16,192]{1,0:T(8,128)(2,1)S(1)}, f3...) custom-call(s32[1,1,4,16]{3,2,1,0:T(4,128)} %fslot_hbm.1, ...), custom_call_target="tpu_custom_call" | custom-call | tf_op jit(solution)/shard_map/pallas_call | solution.py:359
  7.8 0.0 collective-permute-done.refs_1_
  7.8 2.8 %collective-permute-done.2.refs_3_ = f32[8,512]{1,0:T(8,128)S(1)} collective-permute-done((f32[8,512]{1,0:T(8,128)}, f32[8,512]{1,0:T(8,128)S(1)}, u32[]{:S(2)}, u32[]{:S(2)}) %collective-permute-start.2) | collective-permute-done | bytes 16416 | tf_op jit(solution)/shard_map/ppermute | solution.py:337
  10.6 1.0 %shard_map.87 = (f32[8,128]{1,0:T(8,128)S(1)}, f32[64,128]{1,0:T(8,128)S(1)}) custom-call(f32[8,512]{1,0:T(8,128)S(1)} %get-tuple-element.22.refs_0_, f32[8,512]{1,0:T(8,128)S(1)} %collective-permute-done.refs_1_, f32[8,512]{1,0:T(8,128)S(1)} %collective-permute-done.1.refs_2_, f32[8,512]{1,0:T(8,128)S(1)} %collective-permute-done.2.refs_3_, ...), custom_call_target="tpu_custom_call" | custom-call | tf_op jit(solution)/shard_map/pallas_call | solution.py:359
  11.6 1.5 %collective-permute-start.4 = (f32[8,128]{1,0:T(8,128)S(1)}, f32[8,128]{1,0:T(8,128)S(1)}, u32[]{:S(2)}, u32[]{:S(2)}) collective-permute-start(f32[8,128]{1,0:T(8,128)S(1)} %get-tuple-element.27.refs_0_), channel_id=1, source_target_pairs={{0,2},{1,3},{2,0},{3,1},{4,6},{5,7},{6,4},{7,5},{8,10},{9,11},{10,... | collective-permute-start | bytes 12296 | tf_op jit(solution)/shard_map/ppermute | solution.py:337
  13.1 0.3 collective-permute-start.3
  13.5 1.2 %collective-permute-done.5.refs_3_ = f32[8,128]{1,0:T(8,128)S(1)} collective-permute-done((f32[8,128]{1,0:T(8,128)S(1)}, f32[8,128]{1,0:T(8,128)S(1)}, u32[]{:S(2)}, u32[]{:S(2)}) %collective-permute-start.5) | collective-permute-done | bytes 4128 | tf_op jit(solution)/shard_map/ppermute | solution.py:337
  14.6 0.6 %collective-permute-done.4.refs_2_ = f32[8,128]{1,0:T(8,128)S(1)} collective-permute-done((f32[8,128]{1,0:T(8,128)S(1)}, f32[8,128]{1,0:T(8,128)S(1)}, u32[]{:S(2)}, u32[]{:S(2)}) %collective-permute-start.4) | collective-permute-done | bytes 4128 | tf_op jit(solution)/shard_map/ppermute | solution.py:337
  15.3 1.0 %shard_map.88 = (f32[40,128]{1,0:T(8,128)S(1)}, f32[8,128]{1,0:T(8,128)S(1)}) custom-call(f32[8,128]{1,0:T(8,128)S(1)} %get-tuple-element.27.refs_0_, f32[8,128]{1,0:T(8,128)S(1)} %collective-permute-done.3.refs_1_, f32[8,128]{1,0:T(8,128)S(1)} %collective-permute-done.4.refs_2_, f32[8,128]{1,0:T(8,128)S(1)} %collective-permute-done.5.refs_3_, ...), custom_call_target="tpu_custom_call" | custom-call | tf_op jit(solution)/shard_map/pallas_call | solution.py:359
  16.3 1.5 %collective-permute-start.8 = (f32[40,128]{1,0:T(8,128)S(1)}, f32[40,128]{1,0:T(8,128)S(1)}, u32[]{:S(2)}, u32[]{:S(2)}) collective-permute-start(f32[40,128]{1,0:T(8,128)S(1)} %get-tuple-element.32.refs_0_), channel_id=1, source_target_pairs={{0,12},{4,8},{8,4},{12,0},{1,13},{5,9},{9,5},{13,1},{2,14},{6,10},... | collective-permute-start | bytes 61448 | tf_op jit(solution)/shard_map/ppermute | solution.py:337
  17.8 0.6 %collective-permute-start.7 = (f32[40,128]{1,0:T(8,128)S(1)}, f32[40,128]{1,0:T(8,128)S(1)}, u32[]{:S(2)}, u32[]{:S(2)}) collective-permute-start(f32[40,128]{1,0:T(8,128)S(1)} %get-tuple-element.32.refs_0_), channel_id=1, source_target_pairs={{0,8},{4,12},{8,0},{12,4},{1,9},{5,13},{9,1},{13,5},{2,10},{6,14},... | collective-permute-start | bytes 61448 | tf_op jit(solution)/shard_map/ppermute | solution.py:337
  18.4 2.3 %collective-permute-start.6 = (f32[40,128]{1,0:T(8,128)S(1)}, f32[40,128]{1,0:T(8,128)S(1)}, u32[]{:S(2)}, u32[]{:S(2)}) collective-permute-start(f32[40,128]{1,0:T(8,128)S(1)} %get-tuple-element.32.refs_0_), channel_id=1, source_target_pairs={{0,4},{4,0},{8,12},{12,8},{1,5},{5,1},{9,13},{13,9},{2,6},{6,2},{1... | collective-permute-start | bytes 61448 | tf_op jit(solution)/shard_map/ppermute | solution.py:337
  20.6 1.3 %collective-permute-done.8.refs_3_ = f32[40,128]{1,0:T(8,128)S(1)} collective-permute-done((f32[40,128]{1,0:T(8,128)S(1)}, f32[40,128]{1,0:T(8,128)S(1)}, u32[]{:S(2)}, u32[]{:S(2)}) %collective-permute-start.8) | collective-permute-done | bytes 20512 | tf_op jit(solution)/shard_map/ppermute | solution.py:337
  21.9 0.5 %collective-permute-done.7.refs_2_ = f32[40,128]{1,0:T(8,128)S(1)} collective-permute-done((f32[40,128]{1,0:T(8,128)S(1)}, f32[40,128]{1,0:T(8,128)S(1)}, u32[]{:S(2)}, u32[]{:S(2)}) %collective-permute-start.7) | collective-permute-done | bytes 20512 | tf_op jit(solution)/shard_map/ppermute | solution.py:337
  22.5 0.2 collective-permute-done.6.refs_1_
  22.6 1.0 %shard_map.89.refs_0_ = f32[8,128]{1,0:T(8,128)S(1)} custom-call(f32[40,128]{1,0:T(8,128)S(1)} %get-tuple-element.32.refs_0_, f32[40,128]{1,0:T(8,128)S(1)} %collective-permute-done.6.refs_1_, f32[40,128]{1,0:T(8,128)S(1)} %collective-permute-done.7.refs_2_, f32[40,128]{1,0:T(8,128)S(1)} %collective-permute-done.8.refs_3_, ...), custom_call_target="tpu_custom_call" | custom-call | tf_op jit(solution)/shard_map/pallas_call | solution.py:359
  23.6 1.5 %collective-permute-start.10 = (f32[8,128]{1,0:T(8,128)S(1)}, f32[8,128]{1,0:T(8,128)S(1)}, u32[]{:S(2)}, u32[]{:S(2)}) collective-permute-start(f32[8,128]{1,0:T(8,128)S(1)} %shard_map.89.refs_0_), channel_id=1, source_target_pairs={{0,2},{1,3},{2,0},{3,1},{4,6},{5,7},{6,4},{7,5},{8,10},{9,11},{10,... | collective-permute-start | bytes 12296 | tf_op jit(solution)/shard_map/ppermute | solution.py:337
  25.2 0.3 collective-permute-start.9
  25.5 1.2 %collective-permute-done.11.refs_3_ = f32[8,128]{1,0:T(8,128)S(1)} collective-permute-done((f32[8,128]{1,0:T(8,128)S(1)}, f32[8,128]{1,0:T(8,128)S(1)}, u32[]{:S(2)}, u32[]{:S(2)}) %collective-permute-start.11) | collective-permute-done | bytes 4128 | tf_op jit(solution)/shard_map/ppermute | solution.py:337
  26.7 0.6 %collective-permute-done.10.refs_2_ = f32[8,128]{1,0:T(8,128)S(1)} collective-permute-done((f32[8,128]{1,0:T(8,128)S(1)}, f32[8,128]{1,0:T(8,128)S(1)}, u32[]{:S(2)}, u32[]{:S(2)}) %collective-permute-start.10) | collective-permute-done | bytes 4128 | tf_op jit(solution)/shard_map/ppermute | solution.py:337
  27.3 1.0 %shard_map.90 = (f32[8,128]{1,0:T(8,128)S(1)}, f32[8,128]{1,0:T(8,128)S(1)}, f32[8,128]{1,0:T(8,128)S(1)}, f32[8,128]{1,0:T(8,128)S(1)}, f32[8,128]{1,0:T(8,128)S(1)}) custom-call(f32[8,128]{1,0:T(8,128)S(1)} %shard_map.89.refs_0_, f32[8,128]{1,0:T(8,128)S(1)} %collective-permute-done.9.refs_1_, f32[8,128]{1,0:T(8,128)S(1)} %collective-permute-done.10.refs_2_, ...), custom_call_target="tpu_custom_call" | custom-call | tf_op jit(solution)/shard_map/pallas_call | solution.py:359
  28.3 2.4 %collective-permute-start.12 = (f32[8,128]{1,0:T(8,128)S(1)}, f32[8,128]{1,0:T(8,128)S(1)}, u32[]{:S(2)}, u32[]{:S(2)}) collective-permute-start(f32[8,128]{1,0:T(8,128)S(1)} %get-tuple-element.35), channel_id=1, source_target_pairs={{0,12},{4,8},{8,4},{12,0},{1,13},{5,9},{9,5},{13,1},{2,14},{6,10},... | collective-permute-start | bytes 12296 | tf_op jit(solution)/shard_map/ppermute | solution.py:337
  30.7 0.9 %collective-permute-start.13 = (f32[8,128]{1,0:T(8,128)S(1)}, f32[8,128]{1,0:T(8,128)S(1)}, u32[]{:S(2)}, u32[]{:S(2)}) collective-permute-start(f32[8,128]{1,0:T(8,128)S(1)} %get-tuple-element.36), channel_id=1, source_target_pairs={{0,8},{4,12},{8,0},{12,4},{1,9},{5,13},{9,1},{13,5},{2,10},{6,14},... | collective-permute-start | bytes 12296 | tf_op jit(solution)/shard_map/ppermute | solution.py:337
  31.6 1.1 %collective-permute-start.14 = (f32[8,128]{1,0:T(8,128)S(1)}, f32[8,128]{1,0:T(8,128)S(1)}, u32[]{:S(2)}, u32[]{:S(2)}) collective-permute-start(f32[8,128]{1,0:T(8,128)S(1)} %get-tuple-element.37), channel_id=1, source_target_pairs={{0,4},{4,0},{8,12},{12,8},{1,5},{5,1},{9,13},{13,9},{2,6},{6,2},{1... | collective-permute-start | bytes 12296 | tf_op jit(solution)/shard_map/ppermute | solution.py:337
  32.7 0.6 %shard_map.91 = (bf16[128,128]{1,0:T(8,128)(2,1)S(1)}, f32[1,512]{1,0:T(1,128)}) custom-call(f32[40,128]{1,0:T(8,128)S(1)} %get-tuple-element.32.refs_0_, f32[40,128]{1,0:T(8,128)S(1)} %collective-permute-done.6.refs_1_, f32[40,128]{1,0:T(8,128)S(1)} %collective-permute-done.7.refs_2_, f32[40,128]{1,0:T(8,128)S(1)} %collective-permute-done.8.refs_3_, ...), custom_call_target="tpu_custom_call" | custom-call | tf_op jit(solution)/shard_map/pallas_call | solution.py:359
  33.3 0.4 %collective-permute-done.12.refs_0_ = f32[8,128]{1,0:T(8,128)S(1)} collective-permute-done((f32[8,128]{1,0:T(8,128)S(1)}, f32[8,128]{1,0:T(8,128)S(1)}, u32[]{:S(2)}, u32[]{:S(2)}) %collective-permute-start.12) | collective-permute-done | bytes 4128 | tf_op jit(solution)/shard_map/ppermute | solution.py:337
  33.7 1.5 %collective-permute-done.13.refs_1_ = f32[8,128]{1,0:T(8,128)S(1)} collective-permute-done((f32[8,128]{1,0:T(8,128)S(1)}, f32[8,128]{1,0:T(8,128)S(1)}, u32[]{:S(2)}, u32[]{:S(2)}) %collective-permute-start.13) | collective-permute-done | bytes 4128 | tf_op jit(solution)/shard_map/ppermute | solution.py:337
  35.2 0.0 collective-permute-done.14.refs_2_
  35.2 0.8 %shard_map.92 = f32[8,512]{1,0:T(8,128)} custom-call(f32[8,128]{1,0:T(8,128)S(1)} %collective-permute-done.12.refs_0_, f32[8,128]{1,0:T(8,128)S(1)} %collective-permute-done.13.refs_1_, f32[8,128]{1,0:T(8,128)S(1)} %collective-permute-done.14.refs_2_, f32[8,128]{1,0:T(8,128)S(1)} %get-tuple-element.38.refs_3_, bf16[128,128]{1,0:T(8,128)(2,1)S(1)} %get-tuple-element.40.refs_4_), custom_call_target="tpu_custom_call" | custom-call | tf_op jit(solution)/shard_map/pallas_call | solution.py:359
  (5 shorter events, 0.0 us)
Async XLA Ops:
  0.6 7.1 %collective-permute-start = (f32[8,512]{1,0:T(8,128)}, f32[8,512]{1,0:T(8,128)S(1)}, u32[]{:S(2)}, u32[]{:S(2)}) collective-permute-start(f32[8,512]{1,0:T(8,128)} %flux_hbm.1), channel_id=1, source_target_pairs={{0,12},{4,8},{8,4},{12,0},{1,13},{5,9},{9,5},{13,1},{2,14},{6,10},... | collective-permute-start | bytes 49160 | tf_op jit(solution)/shard_map/ppermute | solution.py:337
  5.7 4.8 %collective-permute-start.2 = (f32[8,512]{1,0:T(8,128)}, f32[8,512]{1,0:T(8,128)S(1)}, u32[]{:S(2)}, u32[]{:S(2)}) collective-permute-start(f32[8,512]{1,0:T(8,128)} %flux_hbm.1), channel_id=1, source_target_pairs={{0,8},{4,12},{8,0},{12,4},{1,9},{5,13},{9,1},{13,5},{2,10},{6,14},... | collective-permute-start | bytes 49160 | tf_op jit(solution)/shard_map/ppermute | solution.py:337
  5.8 4.8 %collective-permute-start.1 = (f32[8,512]{1,0:T(8,128)}, f32[8,512]{1,0:T(8,128)S(1)}, u32[]{:S(2)}, u32[]{:S(2)}) collective-permute-start(f32[8,512]{1,0:T(8,128)} %flux_hbm.1), channel_id=1, source_target_pairs={{0,4},{4,0},{8,12},{12,8},{1,5},{5,1},{9,13},{13,9},{2,6},{6,2},{1... | collective-permute-start | bytes 49160 | tf_op jit(solution)/shard_map/ppermute | solution.py:337
  11.6 3.0 %collective-permute-start.5 = (f32[8,128]{1,0:T(8,128)S(1)}, f32[8,128]{1,0:T(8,128)S(1)}, u32[]{:S(2)}, u32[]{:S(2)}) collective-permute-start(f32[8,128]{1,0:T(8,128)S(1)} %get-tuple-element.27.refs_0_), channel_id=1, source_target_pairs={{0,3},{1,2},{2,1},{3,0},{4,7},{5,6},{6,5},{7,4},{8,11},{9,10},{10,... | collective-permute-start | bytes 12296 | tf_op jit(solution)/shard_map/ppermute | solution.py:337
  11.6 3.7 %collective-permute-start.4 = (f32[8,128]{1,0:T(8,128)S(1)}, f32[8,128]{1,0:T(8,128)S(1)}, u32[]{:S(2)}, u32[]{:S(2)}) collective-permute-start(f32[8,128]{1,0:T(8,128)S(1)} %get-tuple-element.27.refs_0_), channel_id=1, source_target_pairs={{0,2},{1,3},{2,0},{3,1},{4,6},{5,7},{6,4},{7,5},{8,10},{9,11},{10,... | collective-permute-start | bytes 12296 | tf_op jit(solution)/shard_map/ppermute | solution.py:337
  13.1 2.1 %collective-permute-start.3 = (f32[8,128]{1,0:T(8,128)S(1)}, f32[8,128]{1,0:T(8,128)S(1)}, u32[]{:S(2)}, u32[]{:S(2)}) collective-permute-start(f32[8,128]{1,0:T(8,128)S(1)} %get-tuple-element.27.refs_0_), channel_id=1, source_target_pairs={{0,1},{1,0},{2,3},{3,2},{4,5},{5,4},{6,7},{7,6},{8,9},{9,8},{10,11... | collective-permute-start | bytes 12296 | tf_op jit(solution)/shard_map/ppermute | solution.py:337
  16.3 5.7 %collective-permute-start.8 = (f32[40,128]{1,0:T(8,128)S(1)}, f32[40,128]{1,0:T(8,128)S(1)}, u32[]{:S(2)}, u32[]{:S(2)}) collective-permute-start(f32[40,128]{1,0:T(8,128)S(1)} %get-tuple-element.32.refs_0_), channel_id=1, source_target_pairs={{0,12},{4,8},{8,4},{12,0},{1,13},{5,9},{9,5},{13,1},{2,14},{6,10},... | collective-permute-start | bytes 61448 | tf_op jit(solution)/shard_map/ppermute | solution.py:337
  17.8 4.7 %collective-permute-start.7 = (f32[40,128]{1,0:T(8,128)S(1)}, f32[40,128]{1,0:T(8,128)S(1)}, u32[]{:S(2)}, u32[]{:S(2)}) collective-permute-start(f32[40,128]{1,0:T(8,128)S(1)} %get-tuple-element.32.refs_0_), channel_id=1, source_target_pairs={{0,8},{4,12},{8,0},{12,4},{1,9},{5,13},{9,1},{13,5},{2,10},{6,14},... | collective-permute-start | bytes 61448 | tf_op jit(solution)/shard_map/ppermute | solution.py:337
  18.4 4.3 %collective-permute-start.6 = (f32[40,128]{1,0:T(8,128)S(1)}, f32[40,128]{1,0:T(8,128)S(1)}, u32[]{:S(2)}, u32[]{:S(2)}) collective-permute-start(f32[40,128]{1,0:T(8,128)S(1)} %get-tuple-element.32.refs_0_), channel_id=1, source_target_pairs={{0,4},{4,0},{8,12},{12,8},{1,5},{5,1},{9,13},{13,9},{2,6},{6,2},{1... | collective-permute-start | bytes 61448 | tf_op jit(solution)/shard_map/ppermute | solution.py:337
  23.6 3.0 %collective-permute-start.11 = (f32[8,128]{1,0:T(8,128)S(1)}, f32[8,128]{1,0:T(8,128)S(1)}, u32[]{:S(2)}, u32[]{:S(2)}) collective-permute-start(f32[8,128]{1,0:T(8,128)S(1)} %shard_map.89.refs_0_), channel_id=1, source_target_pairs={{0,3},{1,2},{2,1},{3,0},{4,7},{5,6},{6,5},{7,4},{8,11},{9,10},{10,... | collective-permute-start | bytes 12296 | tf_op jit(solution)/shard_map/ppermute | solution.py:337
  23.6 3.7 %collective-permute-start.10 = (f32[8,128]{1,0:T(8,128)S(1)}, f32[8,128]{1,0:T(8,128)S(1)}, u32[]{:S(2)}, u32[]{:S(2)}) collective-permute-start(f32[8,128]{1,0:T(8,128)S(1)} %shard_map.89.refs_0_), channel_id=1, source_target_pairs={{0,2},{1,3},{2,0},{3,1},{4,6},{5,7},{6,4},{7,5},{8,10},{9,11},{10,... | collective-permute-start | bytes 12296 | tf_op jit(solution)/shard_map/ppermute | solution.py:337
  25.2 2.1 %collective-permute-start.9 = (f32[8,128]{1,0:T(8,128)S(1)}, f32[8,128]{1,0:T(8,128)S(1)}, u32[]{:S(2)}, u32[]{:S(2)}) collective-permute-start(f32[8,128]{1,0:T(8,128)S(1)} %shard_map.89.refs_0_), channel_id=1, source_target_pairs={{0,1},{1,0},{2,3},{3,2},{4,5},{5,4},{6,7},{7,6},{8,9},{9,8},{10,11... | collective-permute-start | bytes 12296 | tf_op jit(solution)/shard_map/ppermute | solution.py:337
  28.3 5.4 %collective-permute-start.12 = (f32[8,128]{1,0:T(8,128)S(1)}, f32[8,128]{1,0:T(8,128)S(1)}, u32[]{:S(2)}, u32[]{:S(2)}) collective-permute-start(f32[8,128]{1,0:T(8,128)S(1)} %get-tuple-element.35), channel_id=1, source_target_pairs={{0,12},{4,8},{8,4},{12,0},{1,13},{5,9},{9,5},{13,1},{2,14},{6,10},... | collective-permute-start | bytes 12296 | tf_op jit(solution)/shard_map/ppermute | solution.py:337
  30.7 4.5 %collective-permute-start.13 = (f32[8,128]{1,0:T(8,128)S(1)}, f32[8,128]{1,0:T(8,128)S(1)}, u32[]{:S(2)}, u32[]{:S(2)}) collective-permute-start(f32[8,128]{1,0:T(8,128)S(1)} %get-tuple-element.36), channel_id=1, source_target_pairs={{0,8},{4,12},{8,0},{12,4},{1,9},{5,13},{9,1},{13,5},{2,10},{6,14},... | collective-permute-start | bytes 12296 | tf_op jit(solution)/shard_map/ppermute | solution.py:337
  31.6 3.7 %collective-permute-start.14 = (f32[8,128]{1,0:T(8,128)S(1)}, f32[8,128]{1,0:T(8,128)S(1)}, u32[]{:S(2)}, u32[]{:S(2)}) collective-permute-start(f32[8,128]{1,0:T(8,128)S(1)} %get-tuple-element.37), channel_id=1, source_target_pairs={{0,4},{4,0},{8,12},{12,8},{1,5},{5,1},{9,13},{13,9},{2,6},{6,2},{1... | collective-permute-start | bytes 12296 | tf_op jit(solution)/shard_map/ppermute | solution.py:337

commit v6 on v5

--- a/solution.py
+++ b/solution.py
@@ -73,52 +73,60 @@
     return out
 
 
-def forward_tree(h_ref, owner, x, bits, base):
-    if bits == 0:
-        return h_ref[0, 0, owner, :, LANES * base : LANES * (base + 1)] * x
-    a = forward_tree(h_ref, owner, x, bits - 1, base)
-    b = forward_tree(h_ref, owner, x, bits - 1, base + 2 ** (bits - 1))
-    distance = 2**bits
-    clear = (iota(a.shape, 1) & distance) == 0
-    return jnp.where(clear, a, b) + swap(jnp.where(clear, b, a), distance)
-
-
-def for_owners(owners, body):
-    lax.fori_loop(0, owners, lambda o, c: (body(o), c)[1], 0, unroll=owners <= 4)
-
-
-def forward(h_ref, pick_obs, x_scr, value_scr):
-    owners, capacity = h_ref.shape[2], h_ref.shape[3]
-
-    def body(o):
-        rows = pl.ds(pl.multiple_of(o * capacity, capacity), capacity)
-        value_scr[rows, :] = forward_tree(h_ref, o, x_scr[rows, :], 5, 0)
-
-    for_owners(owners, body)
-    m = pick_rows(pick_obs, value_scr[...])[:OBLK_DEV]
+def merge_tree(tiles):
+    distance = 2
+    while len(tiles) > 1:
+        clear = (iota(tiles[0].shape, 1) & distance) == 0
+        tiles = [
+            jnp.where(clear, a, b) + swap(jnp.where(clear, b, a), distance)
+            for a, b in zip(tiles[::2], tiles[1::2])
+        ]
+        distance *= 2
+    return tiles[0]
+
+
+def h_columns(h_ref, first, last, start, size):
+    return jnp.concatenate([h_ref[0, 0, o, :, start : start + size] for o in range(first, last)], axis=0)
+
+
+def forward(h_ref, pick_obs, x):
+    x = jnp.concatenate([x, x], axis=1)
+    tiles = []
+    for t in range(TILES // 2):
+        sums = pick_rows(pick_obs, h_columns(h_ref, 0, h_ref.shape[2], 2 * LANES * t, 2 * LANES) * x)
+        tiles += [sums[:OBLK_DEV, :LANES], sums[:OBLK_DEV, LANES:]]
+    m = merge_tree(tiles)
     m = m + swap(m, 1)
     even = (iota(m.shape, 1) & 1) == 0
     return jnp.where(even == low(m.shape), m, half_swap(m))
 
 
-def adjoint(h_ref, slot_obs, d, picked_scr, store):
+def adjoint(h_ref, slot_obs, d, store):
     owners, capacity = h_ref.shape[2], h_ref.shape[3]
-    picked_scr[...] = pick_rows(slot_obs, d)
-
-    def body(o):
-        rows = pl.ds(pl.multiple_of(o * capacity, capacity), capacity)
-        picked = picked_scr[rows, :]
-        upper = jnp.where(low(picked.shape), 0, 1)
+    upper = jnp.where(low(d.shape), 0, 1)
+    spread = jnp.concatenate(
+        [
+            jnp.take_along_axis(d, upper + 2 * t, axis=1, mode="promise_in_bounds")
+            for t in range(TILES)
+        ],
+        axis=1,
+    )
+    spread = jnp.concatenate([term.astype(F32) for term in three(spread)], axis=0).astype(BF16)
+    group = min(owners, 4)
+    for first in range(0, owners, group):
+        rows = slice(first * capacity, (first + group) * capacity)
         total = None
-        for t in range(TILES):
-            spread = jnp.take_along_axis(picked, upper + 2 * t, axis=1, mode="promise_in_bounds")
-            term = h_ref[0, 0, o, :, LANES * t : LANES * (t + 1)] * spread
-            total = term if total is None else total + term
+        for t in range(TILES // 2):
+            columns = slice(2 * LANES * t, 2 * LANES * (t + 1))
+            given = jnp.dot(slot_obs[rows], spread[:, columns], preferred_element_type=F32)
+            terms = h_columns(h_ref, first, first + group, 2 * LANES * t, 2 * LANES) * given
+            total = terms if total is None else total + terms
+        total = total[:, :LANES] + total[:, LANES:]
         total = total + half_swap(total)
-        pair = total[: capacity // 2], total[capacity // 2 :]
-        store(o, jnp.where(low(pair[0].shape), *pair))
-
-    for_owners(owners, body)
+        for o in range(group):
+            upper_half = o * capacity + capacity // 2
+            pair = total[o * capacity : upper_half], total[upper_half : (o + 1) * capacity]
+            store(first + o, jnp.where(low(pair[0].shape), *pair))
 
 
 def prepare(
@@ -207,7 +215,7 @@
 
 def first_model(order, *refs):
     parts = len(order)
-    h_ref, pick_flux_ref, target_ref, pick_obs_ref, m_ref, x_ref, value_scr = refs[parts:]
+    h_ref, pick_flux_ref, target_ref, pick_obs_ref, m_ref, x_ref = refs[parts:]
     flux = jnp.concatenate(
         [
             ref[:, LANES * t : LANES * (t + 1)]
@@ -218,28 +226,29 @@
     )
     pair = pick_rows(pick_flux_ref[...], flux)
     odd = (target_ref[...].astype(jnp.int32) & 1) == 1
-    x_ref[...] = jnp.where(odd != low(pair.shape), pair, half_swap(pair))
-    m_ref[...] = forward(h_ref, pick_obs_ref[...], x_ref, value_scr)
+    x = jnp.where(odd != low(pair.shape), pair, half_swap(pair))
+    x_ref[...] = x
+    m_ref[...] = forward(h_ref, pick_obs_ref[...], x)
 
 
 def first_adjoint(parts, *refs):
-    observed_ref, weight_ref, slot_obs_ref, index_ref, h_ref, message_ref, d_ref, picked_scr = refs[parts:]
+    observed_ref, weight_ref, slot_obs_ref, index_ref, h_ref, message_ref, d_ref = refs[parts:]
     d = weight_ref[...] * (tree_sum([m[...] for m in refs[:parts]]) - observed_ref[...])
     d_ref[...] = d
     rows = h_ref.shape[3] // 2
     half = h_ref.shape[2] * rows
 
     def store(o, block):
-        message_ref[pl.ds(pl.multiple_of(o * rows, rows), rows), :] = block
-
-    adjoint(h_ref, slot_obs_ref[...], d, picked_scr, store)
+        message_ref[o * rows : (o + 1) * rows, :] = block
+
+    adjoint(h_ref, slot_obs_ref[...], d, store)
     message_ref[half:, :] = index_ref[...]
 
 
 def second_model(parts, *refs):
     messages = refs[:parts]
     cells = parts
-    target_ref, x_ref, h_ref, pick_obs_ref, m_ref, next_scr, value_scr = refs[parts:]
+    target_ref, x_ref, h_ref, pick_obs_ref, m_ref = refs[parts:]
     slots = target_ref.shape[0]
     half = slots // 2
     count = max(1, half // LANES)
@@ -262,13 +271,12 @@
         found = pick_rows(jnp.concatenate([pick] * 3, axis=1), values)
         total = found if total is None else total + found
     change = jnp.where(low((slots, LANES)), total[:slots], total[slots:])
-    next_scr[...] = x_ref[...] - 0.5 * (change + half_swap(change))
-    m_ref[...] = forward(h_ref, pick_obs_ref[...], next_scr, value_scr)
+    m_ref[...] = forward(h_ref, pick_obs_ref[...], x_ref[...] - 0.5 * (change + half_swap(change)))
 
 
 def second_adjoint(parts, *refs):
     observed_ref, weight_ref, first_ref, slot_obs_ref, h_ref = refs[parts : parts + 5]
-    *outs, d_ref, picked_scr, block_scr = refs[parts + 5 :]
+    *outs, d_ref, block_scr = refs[parts + 5 :]
     me = lax.axis_index("cell")
     owners = h_ref.shape[2]
     d = weight_ref[...] * (tree_sum([m[...] for m in refs[:parts]]) - observed_ref[...])
@@ -277,7 +285,7 @@
     def store(o, block):
         block_scr[o] = block
 
-    adjoint(h_ref, slot_obs_ref[...], -0.25 * first_ref[...] - 0.5 * d, picked_scr, store)
+    adjoint(h_ref, slot_obs_ref[...], -0.25 * first_ref[...] - 0.5 * d, store)
     for k in range(owners):
         outs[owners - 1 - k][...] = block_scr[me ^ k]
 
@@ -370,7 +378,6 @@
 
         obs_tile = ((OBLK_DEV, LANES), F32)
         slot_tile = ((slots, LANES), F32)
-        slot_scratch = pltpu.VMEM(*slot_tile)
         small = (flux_slot, obs_slot, slot_count, observed, obs_weight)
         pick_flux, target, slot_obs, pick_obs, index, observed_t, weight_t, flux, matrices = call(
             prepare,
@@ -393,32 +400,29 @@
             ],
             hbm,
         )
-        order = [0, cells - 1, *range(1, cells - 1)]
+        order = [0, cells // 2, *range(1, cells // 2), *range(cells // 2 + 1, cells)]
         fluxes = exchange(flux, prior_flux, "cell", cells)
         m0, x0 = call(
             functools.partial(first_model, order),
             [obs_tile, slot_tile],
             (*(fluxes[k] for k in order), matrices, pick_flux, target, pick_obs),
-            [slot_scratch],
         )
         message, d0 = call(
             functools.partial(first_adjoint, wins),
             [((half + index_rows, LANES), F32), obs_tile],
             (*exchange(m0, m0, "win", wins), observed_t, weight_t, slot_obs, index, matrices),
-            [slot_scratch],
         )
         messages = exchange(message, message, "cell", cells)
         (m1,) = call(
             functools.partial(second_model, cells),
             [obs_tile],
             (*messages, target, x0, matrices, pick_obs),
-            [slot_scratch, slot_scratch],
         )
         *blocks, d1 = call(
             functools.partial(second_adjoint, wins),
             [((capacity // 2, LANES), F32)] * owners + [obs_tile],
             (*exchange(m1, m1, "win", wins), observed_t, weight_t, d0, slot_obs, matrices),
-            [slot_scratch, pltpu.VMEM((owners, capacity // 2, LANES), F32)],
+            [pltpu.VMEM((owners, capacity // 2, LANES), F32)],
         )
         arrays = [send(block, "cell", cells, cells - 1 - i) for i, block in enumerate(blocks[:-1])]
         arrays = [blocks[-1]] + arrays[::-1]

time: 36.2 us -> 35.1 us (0.970)
  Pallas kernels: 6.79 us -> 5.74 us
    pallas_call x7, Pallas kernels: 6.79 us -> 5.74 us  [call(): pl.pallas_call(body, out_shape=outs_at, in_specs=[space] * len(ins), out_...]
  transfers between devices with their start and end apart: 15 -> 15, of which waited for: 10 -> 10; matrix products, arithmetic and copies ran while one was open for 0% -> 0% of each run, Pallas kernels for 5% -> 6%
where the time goes in v6:
time: 35.1 us; the launch traced here: 34.9 us
  starting transfers between devices  18.3 us (52%)
  waiting for transfers between devices  10.2 us (29%)
  Pallas kernels  5.74 us (16%)
  between operations  0.67 us (2%)
    ppermute x15, starting transfers between devices, send(): return lax.ppermute(value, axis, [(i, i ^ k) for i in range(size)])  18.3 us
    ppermute x15, waiting for transfers between devices, send(): return lax.ppermute(value, axis, [(i, i ^ k) for i in range(size)])  10.2 us
    pallas_call x7, Pallas kernels, call(): pl.pallas_call(body, out_shape=outs_at, in_specs=[space] * len(ins), out_...  5.74 us
  transfers between devices with their start and end apart: 15, of which 10 were waited for; matrix products, arithmetic and copies ran while one was open for 0% of the time, Pallas kernels for 6%

profile of v6, /device:TPU:0, one launch (start us, length us, event | category | flops | bytes accessed | tf_op | source)
XLA Modules:
  0.0 34.9 jit_solution(6118269893387154593)
XLA Ops:
  0.6 4.1 %collective-permute-start = (f32[8,512]{1,0:T(8,128)}, f32[8,512]{1,0:T(8,128)S(1)}, u32[]{:S(2)}, u32[]{:S(2)}) collective-permute-start(f32[8,512]{1,0:T(8,128)} %flux_hbm.1), channel_id=1, source_target_pairs={{0,8},{4,12},{8,0},{12,4},{1,9},{5,13},{9,1},{13,5},{2,10},{6,14},... | collective-permute-start | bytes 49160 | tf_op jit(solution)/shard_map/ppermute | solution.py:345
  4.7 1.3 %collective-permute-start.2 = (f32[8,512]{1,0:T(8,128)}, f32[8,512]{1,0:T(8,128)S(1)}, u32[]{:S(2)}, u32[]{:S(2)}) collective-permute-start(f32[8,512]{1,0:T(8,128)} %flux_hbm.1), channel_id=1, source_target_pairs={{0,12},{4,8},{8,4},{12,0},{1,13},{5,9},{9,5},{13,1},{2,14},{6,10},... | collective-permute-start | bytes 49160 | tf_op jit(solution)/shard_map/ppermute | solution.py:345
  6.1 0.2 collective-permute-start.1
  6.3 1.4 %shard_map.86 = (bf16[64,384]{1,0:T(8,128)(2,1)S(1)}, f32[64,128]{1,0:T(8,128)S(1)}, bf16[64,24]{1,0:T(8,128)(2,1)S(1)}, bf16[16,192]{1,0:T(8,128)(2,1)S(1)}, f3...) custom-call(s32[1,1,4,16]{3,2,1,0:T(4,128)} %fslot_hbm.1, ...), custom_call_target="tpu_custom_call" | custom-call | tf_op jit(solution)/shard_map/pallas_call | solution.py:367
  7.7 0.0 collective-permute-done.refs_1_
  7.7 2.8 %collective-permute-done.2.refs_3_ = f32[8,512]{1,0:T(8,128)S(1)} collective-permute-done((f32[8,512]{1,0:T(8,128)}, f32[8,512]{1,0:T(8,128)S(1)}, u32[]{:S(2)}, u32[]{:S(2)}) %collective-permute-start.2) | collective-permute-done | bytes 16416 | tf_op jit(solution)/shard_map/ppermute | solution.py:345
  10.5 1.0 %shard_map.87 = (f32[8,128]{1,0:T(8,128)S(1)}, f32[64,128]{1,0:T(8,128)S(1)}) custom-call(f32[8,512]{1,0:T(8,128)S(1)} %get-tuple-element.22.refs_0_, f32[8,512]{1,0:T(8,128)S(1)} %collective-permute-done.refs_1_, f32[8,512]{1,0:T(8,128)S(1)} %collective-permute-done.1.refs_2_, f32[8,512]{1,0:T(8,128)S(1)} %collective-permute-done.2.refs_3_, ...), custom_call_target="tpu_custom_call" | custom-call | tf_op jit(solution)/shard_map/pallas_call | solution.py:367
  11.5 0.0 collective-permute-start.5
  11.5 1.5 %collective-permute-start.4 = (f32[8,128]{1,0:T(8,128)S(1)}, f32[8,128]{1,0:T(8,128)S(1)}, u32[]{:S(2)}, u32[]{:S(2)}) collective-permute-start(f32[8,128]{1,0:T(8,128)S(1)} %get-tuple-element.27.refs_0_), channel_id=1, source_target_pairs={{0,2},{1,3},{2,0},{3,1},{4,6},{5,7},{6,4},{7,5},{8,10},{9,11},{10,... | collective-permute-start | bytes 12296 | tf_op jit(solution)/shard_map/ppermute | solution.py:345
  13.1 0.3 collective-permute-start.3
  13.4 1.2 %collective-permute-done.5.refs_3_ = f32[8,128]{1,0:T(8,128)S(1)} collective-permute-done((f32[8,128]{1,0:T(8,128)S(1)}, f32[8,128]{1,0:T(8,128)S(1)}, u32[]{:S(2)}, u32[]{:S(2)}) %collective-permute-start.5) | collective-permute-done | bytes 4128 | tf_op jit(solution)/shard_map/ppermute | solution.py:345
  14.6 0.6 %collective-permute-done.4.refs_2_ = f32[8,128]{1,0:T(8,128)S(1)} collective-permute-done((f32[8,128]{1,0:T(8,128)S(1)}, f32[8,128]{1,0:T(8,128)S(1)}, u32[]{:S(2)}, u32[]{:S(2)}) %collective-permute-start.4) | collective-permute-done | bytes 4128 | tf_op jit(solution)/shard_map/ppermute | solution.py:345
  15.2 0.4 %shard_map.88 = (f32[40,128]{1,0:T(8,128)S(1)}, f32[8,128]{1,0:T(8,128)S(1)}) custom-call(f32[8,128]{1,0:T(8,128)S(1)} %get-tuple-element.27.refs_0_, f32[8,128]{1,0:T(8,128)S(1)} %collective-permute-done.3.refs_1_, f32[8,128]{1,0:T(8,128)S(1)} %collective-permute-done.4.refs_2_, f32[8,128]{1,0:T(8,128)S(1)} %collective-permute-done.5.refs_3_, ...), custom_call_target="tpu_custom_call" | custom-call | tf_op jit(solution)/shard_map/pallas_call | solution.py:367
  15.6 2.1 %collective-permute-start.8 = (f32[40,128]{1,0:T(8,128)S(1)}, f32[40,128]{1,0:T(8,128)S(1)}, u32[]{:S(2)}, u32[]{:S(2)}) collective-permute-start(f32[40,128]{1,0:T(8,128)S(1)} %get-tuple-element.32.refs_0_), channel_id=1, source_target_pairs={{0,12},{4,8},{8,4},{12,0},{1,13},{5,9},{9,5},{13,1},{2,14},{6,10},... | collective-permute-start | bytes 61448 | tf_op jit(solution)/shard_map/ppermute | solution.py:345
  17.7 2.4 %collective-permute-start.6 = (f32[40,128]{1,0:T(8,128)S(1)}, f32[40,128]{1,0:T(8,128)S(1)}, u32[]{:S(2)}, u32[]{:S(2)}) collective-permute-start(f32[40,128]{1,0:T(8,128)S(1)} %get-tuple-element.32.refs_0_), channel_id=1, source_target_pairs={{0,4},{4,0},{8,12},{12,8},{1,5},{5,1},{9,13},{13,9},{2,6},{6,2},{1... | collective-permute-start | bytes 61448 | tf_op jit(solution)/shard_map/ppermute | solution.py:345
  20.1 1.2 %collective-permute-done.8.refs_3_ = f32[40,128]{1,0:T(8,128)S(1)} collective-permute-done((f32[40,128]{1,0:T(8,128)S(1)}, f32[40,128]{1,0:T(8,128)S(1)}, u32[]{:S(2)}, u32[]{:S(2)}) %collective-permute-start.8) | collective-permute-done | bytes 20512 | tf_op jit(solution)/shard_map/ppermute | solution.py:345
  21.3 1.1 %collective-permute-done.7.refs_2_ = f32[40,128]{1,0:T(8,128)S(1)} collective-permute-done((f32[40,128]{1,0:T(8,128)S(1)}, f32[40,128]{1,0:T(8,128)S(1)}, u32[]{:S(2)}, u32[]{:S(2)}) %collective-permute-start.7) | collective-permute-done | bytes 20512 | tf_op jit(solution)/shard_map/ppermute | solution.py:345
  22.4 0.0 collective-permute-done.6.refs_1_
  22.4 1.1 %shard_map.89.refs_0_ = f32[8,128]{1,0:T(8,128)S(1)} custom-call(f32[40,128]{1,0:T(8,128)S(1)} %get-tuple-element.32.refs_0_, f32[40,128]{1,0:T(8,128)S(1)} %collective-permute-done.6.refs_1_, f32[40,128]{1,0:T(8,128)S(1)} %collective-permute-done.7.refs_2_, f32[40,128]{1,0:T(8,128)S(1)} %collective-permute-done.8.refs_3_, ...), custom_call_target="tpu_custom_call" | custom-call | tf_op jit(solution)/shard_map/pallas_call | solution.py:367
  23.4 1.5 %collective-permute-start.10 = (f32[8,128]{1,0:T(8,128)S(1)}, f32[8,128]{1,0:T(8,128)S(1)}, u32[]{:S(2)}, u32[]{:S(2)}) collective-permute-start(f32[8,128]{1,0:T(8,128)S(1)} %shard_map.89.refs_0_), channel_id=1, source_target_pairs={{0,2},{1,3},{2,0},{3,1},{4,6},{5,7},{6,4},{7,5},{8,10},{9,11},{10,... | collective-permute-start | bytes 12296 | tf_op jit(solution)/shard_map/ppermute | solution.py:345
  25.0 0.3 collective-permute-start.9
  25.3 1.2 %collective-permute-done.11.refs_3_ = f32[8,128]{1,0:T(8,128)S(1)} collective-permute-done((f32[8,128]{1,0:T(8,128)S(1)}, f32[8,128]{1,0:T(8,128)S(1)}, u32[]{:S(2)}, u32[]{:S(2)}) %collective-permute-start.11) | collective-permute-done | bytes 4128 | tf_op jit(solution)/shard_map/ppermute | solution.py:345
  26.5 0.6 %collective-permute-done.10.refs_2_ = f32[8,128]{1,0:T(8,128)S(1)} collective-permute-done((f32[8,128]{1,0:T(8,128)S(1)}, f32[8,128]{1,0:T(8,128)S(1)}, u32[]{:S(2)}, u32[]{:S(2)}) %collective-permute-start.10) | collective-permute-done | bytes 4128 | tf_op jit(solution)/shard_map/ppermute | solution.py:345
  27.1 0.4 %shard_map.90 = (f32[8,128]{1,0:T(8,128)S(1)}, f32[8,128]{1,0:T(8,128)S(1)}, f32[8,128]{1,0:T(8,128)S(1)}, f32[8,128]{1,0:T(8,128)S(1)}, f32[8,128]{1,0:T(8,128)S(1)}) custom-call(f32[8,128]{1,0:T(8,128)S(1)} %shard_map.89.refs_0_, f32[8,128]{1,0:T(8,128)S(1)} %collective-permute-done.9.refs_1_, f32[8,128]{1,0:T(8,128)S(1)} %collective-permute-done.10.refs_2_, ...), custom_call_target="tpu_custom_call" | custom-call | tf_op jit(solution)/shard_map/pallas_call | solution.py:367
  27.5 1.9 %collective-permute-start.12 = (f32[8,128]{1,0:T(8,128)S(1)}, f32[8,128]{1,0:T(8,128)S(1)}, u32[]{:S(2)}, u32[]{:S(2)}) collective-permute-start(f32[8,128]{1,0:T(8,128)S(1)} %get-tuple-element.35), channel_id=1, source_target_pairs={{0,12},{4,8},{8,4},{12,0},{1,13},{5,9},{9,5},{13,1},{2,14},{6,10},... | collective-permute-start | bytes 12296 | tf_op jit(solution)/shard_map/ppermute | solution.py:345
  29.4 1.1 %collective-permute-start.13 = (f32[8,128]{1,0:T(8,128)S(1)}, f32[8,128]{1,0:T(8,128)S(1)}, u32[]{:S(2)}, u32[]{:S(2)}) collective-permute-start(f32[8,128]{1,0:T(8,128)S(1)} %get-tuple-element.36), channel_id=1, source_target_pairs={{0,8},{4,12},{8,0},{12,4},{1,9},{5,13},{9,1},{13,5},{2,10},{6,14},... | collective-permute-start | bytes 12296 | tf_op jit(solution)/shard_map/ppermute | solution.py:345
  30.5 1.5 %collective-permute-start.14 = (f32[8,128]{1,0:T(8,128)S(1)}, f32[8,128]{1,0:T(8,128)S(1)}, u32[]{:S(2)}, u32[]{:S(2)}) collective-permute-start(f32[8,128]{1,0:T(8,128)S(1)} %get-tuple-element.37), channel_id=1, source_target_pairs={{0,4},{4,0},{8,12},{12,8},{1,5},{5,1},{9,13},{13,9},{2,6},{6,2},{1... | collective-permute-start | bytes 12296 | tf_op jit(solution)/shard_map/ppermute | solution.py:345
  32.0 0.6 %shard_map.91 = (bf16[128,128]{1,0:T(8,128)(2,1)S(1)}, f32[1,512]{1,0:T(1,128)}) custom-call(f32[40,128]{1,0:T(8,128)S(1)} %get-tuple-element.32.refs_0_, f32[40,128]{1,0:T(8,128)S(1)} %collective-permute-done.6.refs_1_, f32[40,128]{1,0:T(8,128)S(1)} %collective-permute-done.7.refs_2_, f32[40,128]{1,0:T(8,128)S(1)} %collective-permute-done.8.refs_3_, ...), custom_call_target="tpu_custom_call" | custom-call | tf_op jit(solution)/shard_map/pallas_call | solution.py:367
  32.6 0.4 %collective-permute-done.12.refs_0_ = f32[8,128]{1,0:T(8,128)S(1)} collective-permute-done((f32[8,128]{1,0:T(8,128)S(1)}, f32[8,128]{1,0:T(8,128)S(1)}, u32[]{:S(2)}, u32[]{:S(2)}) %collective-permute-start.12) | collective-permute-done | bytes 4128 | tf_op jit(solution)/shard_map/ppermute | solution.py:345
  33.0 0.9 %collective-permute-done.13.refs_1_ = f32[8,128]{1,0:T(8,128)S(1)} collective-permute-done((f32[8,128]{1,0:T(8,128)S(1)}, f32[8,128]{1,0:T(8,128)S(1)}, u32[]{:S(2)}, u32[]{:S(2)}) %collective-permute-start.13) | collective-permute-done | bytes 4128 | tf_op jit(solution)/shard_map/ppermute | solution.py:345
  33.9 0.2 collective-permute-done.14.refs_2_
  34.1 0.8 %shard_map.92 = f32[8,512]{1,0:T(8,128)} custom-call(f32[8,128]{1,0:T(8,128)S(1)} %collective-permute-done.12.refs_0_, f32[8,128]{1,0:T(8,128)S(1)} %collective-permute-done.13.refs_1_, f32[8,128]{1,0:T(8,128)S(1)} %collective-permute-done.14.refs_2_, f32[8,128]{1,0:T(8,128)S(1)} %get-tuple-element.38.refs_3_, bf16[128,128]{1,0:T(8,128)(2,1)S(1)} %get-tuple-element.40.refs_4_), custom_call_target="tpu_custom_call" | custom-call | tf_op jit(solution)/shard_map/pallas_call | solution.py:367
  (5 shorter events, 0.0 us)
Async XLA Ops:
  0.6 7.1 %collective-permute-start = (f32[8,512]{1,0:T(8,128)}, f32[8,512]{1,0:T(8,128)S(1)}, u32[]{:S(2)}, u32[]{:S(2)}) collective-permute-start(f32[8,512]{1,0:T(8,128)} %flux_hbm.1), channel_id=1, source_target_pairs={{0,8},{4,12},{8,0},{12,4},{1,9},{5,13},{9,1},{13,5},{2,10},{6,14},... | collective-permute-start | bytes 49160 | tf_op jit(solution)/shard_map/ppermute | solution.py:345
  4.7 5.7 %collective-permute-start.2 = (f32[8,512]{1,0:T(8,128)}, f32[8,512]{1,0:T(8,128)S(1)}, u32[]{:S(2)}, u32[]{:S(2)}) collective-permute-start(f32[8,512]{1,0:T(8,128)} %flux_hbm.1), channel_id=1, source_target_pairs={{0,12},{4,8},{8,4},{12,0},{1,13},{5,9},{9,5},{13,1},{2,14},{6,10},... | collective-permute-start | bytes 49160 | tf_op jit(solution)/shard_map/ppermute | solution.py:345
  6.1 4.4 %collective-permute-start.1 = (f32[8,512]{1,0:T(8,128)}, f32[8,512]{1,0:T(8,128)S(1)}, u32[]{:S(2)}, u32[]{:S(2)}) collective-permute-start(f32[8,512]{1,0:T(8,128)} %flux_hbm.1), channel_id=1, source_target_pairs={{0,4},{4,0},{8,12},{12,8},{1,5},{5,1},{9,13},{13,9},{2,6},{6,2},{1... | collective-permute-start | bytes 49160 | tf_op jit(solution)/shard_map/ppermute | solution.py:345
  11.5 3.0 %collective-permute-start.5 = (f32[8,128]{1,0:T(8,128)S(1)}, f32[8,128]{1,0:T(8,128)S(1)}, u32[]{:S(2)}, u32[]{:S(2)}) collective-permute-start(f32[8,128]{1,0:T(8,128)S(1)} %get-tuple-element.27.refs_0_), channel_id=1, source_target_pairs={{0,3},{1,2},{2,1},{3,0},{4,7},{5,6},{6,5},{7,4},{8,11},{9,10},{10,... | collective-permute-start | bytes 12296 | tf_op jit(solution)/shard_map/ppermute | solution.py:345
  11.5 3.7 %collective-permute-start.4 = (f32[8,128]{1,0:T(8,128)S(1)}, f32[8,128]{1,0:T(8,128)S(1)}, u32[]{:S(2)}, u32[]{:S(2)}) collective-permute-start(f32[8,128]{1,0:T(8,128)S(1)} %get-tuple-element.27.refs_0_), channel_id=1, source_target_pairs={{0,2},{1,3},{2,0},{3,1},{4,6},{5,7},{6,4},{7,5},{8,10},{9,11},{10,... | collective-permute-start | bytes 12296 | tf_op jit(solution)/shard_map/ppermute | solution.py:345
  13.1 2.1 %collective-permute-start.3 = (f32[8,128]{1,0:T(8,128)S(1)}, f32[8,128]{1,0:T(8,128)S(1)}, u32[]{:S(2)}, u32[]{:S(2)}) collective-permute-start(f32[8,128]{1,0:T(8,128)S(1)} %get-tuple-element.27.refs_0_), channel_id=1, source_target_pairs={{0,1},{1,0},{2,3},{3,2},{4,5},{5,4},{6,7},{7,6},{8,9},{9,8},{10,11... | collective-permute-start | bytes 12296 | tf_op jit(solution)/shard_map/ppermute | solution.py:345
  15.6 5.6 %collective-permute-start.8 = (f32[40,128]{1,0:T(8,128)S(1)}, f32[40,128]{1,0:T(8,128)S(1)}, u32[]{:S(2)}, u32[]{:S(2)}) collective-permute-start(f32[40,128]{1,0:T(8,128)S(1)} %get-tuple-element.32.refs_0_), channel_id=1, source_target_pairs={{0,12},{4,8},{8,4},{12,0},{1,13},{5,9},{9,5},{13,1},{2,14},{6,10},... | collective-permute-start | bytes 61448 | tf_op jit(solution)/shard_map/ppermute | solution.py:345
  17.7 4.7 %collective-permute-start.7 = (f32[40,128]{1,0:T(8,128)S(1)}, f32[40,128]{1,0:T(8,128)S(1)}, u32[]{:S(2)}, u32[]{:S(2)}) collective-permute-start(f32[40,128]{1,0:T(8,128)S(1)} %get-tuple-element.32.refs_0_), channel_id=1, source_target_pairs={{0,8},{4,12},{8,0},{12,4},{1,9},{5,13},{9,1},{13,5},{2,10},{6,14},... | collective-permute-start | bytes 61448 | tf_op jit(solution)/shard_map/ppermute | solution.py:345
  17.7 4.7 %collective-permute-start.6 = (f32[40,128]{1,0:T(8,128)S(1)}, f32[40,128]{1,0:T(8,128)S(1)}, u32[]{:S(2)}, u32[]{:S(2)}) collective-permute-start(f32[40,128]{1,0:T(8,128)S(1)} %get-tuple-element.32.refs_0_), channel_id=1, source_target_pairs={{0,4},{4,0},{8,12},{12,8},{1,5},{5,1},{9,13},{13,9},{2,6},{6,2},{1... | collective-permute-start | bytes 61448 | tf_op jit(solution)/shard_map/ppermute | solution.py:345
  23.4 3.0 %collective-permute-start.11 = (f32[8,128]{1,0:T(8,128)S(1)}, f32[8,128]{1,0:T(8,128)S(1)}, u32[]{:S(2)}, u32[]{:S(2)}) collective-permute-start(f32[8,128]{1,0:T(8,128)S(1)} %shard_map.89.refs_0_), channel_id=1, source_target_pairs={{0,3},{1,2},{2,1},{3,0},{4,7},{5,6},{6,5},{7,4},{8,11},{9,10},{10,... | collective-permute-start | bytes 12296 | tf_op jit(solution)/shard_map/ppermute | solution.py:345
  23.4 3.7 %collective-permute-start.10 = (f32[8,128]{1,0:T(8,128)S(1)}, f32[8,128]{1,0:T(8,128)S(1)}, u32[]{:S(2)}, u32[]{:S(2)}) collective-permute-start(f32[8,128]{1,0:T(8,128)S(1)} %shard_map.89.refs_0_), channel_id=1, source_target_pairs={{0,2},{1,3},{2,0},{3,1},{4,6},{5,7},{6,4},{7,5},{8,10},{9,11},{10,... | collective-permute-start | bytes 12296 | tf_op jit(solution)/shard_map/ppermute | solution.py:345
  25.0 2.1 %collective-permute-start.9 = (f32[8,128]{1,0:T(8,128)S(1)}, f32[8,128]{1,0:T(8,128)S(1)}, u32[]{:S(2)}, u32[]{:S(2)}) collective-permute-start(f32[8,128]{1,0:T(8,128)S(1)} %shard_map.89.refs_0_), channel_id=1, source_target_pairs={{0,1},{1,0},{2,3},{3,2},{4,5},{5,4},{6,7},{7,6},{8,9},{9,8},{10,11... | collective-permute-start | bytes 12296 | tf_op jit(solution)/shard_map/ppermute | solution.py:345
  27.5 5.5 %collective-permute-start.12 = (f32[8,128]{1,0:T(8,128)S(1)}, f32[8,128]{1,0:T(8,128)S(1)}, u32[]{:S(2)}, u32[]{:S(2)}) collective-permute-start(f32[8,128]{1,0:T(8,128)S(1)} %get-tuple-element.35), channel_id=1, source_target_pairs={{0,12},{4,8},{8,4},{12,0},{1,13},{5,9},{9,5},{13,1},{2,14},{6,10},... | collective-permute-start | bytes 12296 | tf_op jit(solution)/shard_map/ppermute | solution.py:345
  29.4 4.5 %collective-permute-start.13 = (f32[8,128]{1,0:T(8,128)S(1)}, f32[8,128]{1,0:T(8,128)S(1)}, u32[]{:S(2)}, u32[]{:S(2)}) collective-permute-start(f32[8,128]{1,0:T(8,128)S(1)} %get-tuple-element.36), channel_id=1, source_target_pairs={{0,8},{4,12},{8,0},{12,4},{1,9},{5,13},{9,1},{13,5},{2,10},{6,14},... | collective-permute-start | bytes 12296 | tf_op jit(solution)/shard_map/ppermute | solution.py:345
  30.5 3.6 %collective-permute-start.14 = (f32[8,128]{1,0:T(8,128)S(1)}, f32[8,128]{1,0:T(8,128)S(1)}, u32[]{:S(2)}, u32[]{:S(2)}) collective-permute-start(f32[8,128]{1,0:T(8,128)S(1)} %get-tuple-element.37), channel_id=1, source_target_pairs={{0,4},{4,0},{8,12},{12,8},{1,5},{5,1},{9,13},{13,9},{2,6},{6,2},{1... | collective-permute-start | bytes 12296 | tf_op jit(solution)/shard_map/ppermute | solution.py:345

commit v7 on v6

--- a/solution.py
+++ b/solution.py
@@ -19,6 +19,11 @@
 BF16 = jnp.bfloat16
 VMEM = pl.BlockSpec(memory_space=pltpu.VMEM)
 
+GATHER_FLUX = [[(3, 2), (1, 0)], [(1, 2), (2, 0), (3, 1)], [(3, 0), (0, 2), (2, 3)], [(0, 3), (2, 1)], [(0, 1), (1, 3)]]
+GATHER_BLOCKS = [[(2, 0), (3, 2)], [(3, 1), (2, 3), (1, 0)], [(3, 0), (0, 1)], [(1, 2), (0, 3), (2, 1)], [(0, 2), (1, 3)]]
+SCATTER_BLOCKS = [[(3, 0), (2, 1)], [(2, 0), (0, 1)], [(1, 0), (3, 1), (0, 2), (2, 3)], [(0, 3), (1, 2)], [(3, 2), (1, 3)]]
+ORDERS = ([2, 1, 0, 4, 3], [4, 3, 2, 1, 0], [0, 1, 2, 3, 4])
+
 
 def iota(shape, dim):
     return lax.broadcasted_iota(jnp.int32, shape, dim)
@@ -52,6 +57,26 @@
 
 def low(shape):
     return iota(shape, 1) < LANES // 2
+
+
+def in_turn(refs, order):
+    return [refs[0]] + [refs[1 + order.index(j)] for j in range(len(order))]
+
+
+def readers(refs, ops, me):
+    if ops is None:
+        return [functools.partial(lambda ref, at: ref[at], ref) for ref in refs]
+
+    def read(source, at):
+        value = refs[0][at]
+        for ref, op in zip(refs[1:], ops):
+            for src, dst in op:
+                if src == source:
+                    value = jnp.where(me == dst, ref[at], value)
+        return value
+
+    cells = 1 + max(src for op in ops for src, _ in op)
+    return [functools.partial(read, c) for c in range(cells)]
 
 
 def tree_sum(parts):
@@ -130,6 +155,7 @@
 
 
 def prepare(
+    by_xor,
     fslot_hbm, oslot_hbm, count_hbm, observed_hbm, weight_hbm, flux_hbm, h_hbm,
     pick_flux_ref, target_ref, slot_obs_ref, pick_obs_ref, index_ref, observed_out, weight_out, flux_ref, h_ref,
     fslot_ref, oslot_ref, count_ref, observed_ref, weight_ref, sems, h_sems,
@@ -185,7 +211,7 @@
     target_ref[...] = jnp.broadcast_to(target.astype(F32), target_ref.shape)
 
     depth = owners * BLOCKS // 2
-    row = (owner ^ me) * (BLOCKS // 2) + ((fslot & 7) >> 1) * WIN_DEV + (fslot >> 3)
+    row = ((owner ^ me) if by_xor else owner) * (BLOCKS // 2) + ((fslot & 7) >> 1) * WIN_DEV + (fslot >> 3)
     pick_flux_ref[...] = one_hot(iota((slots, 3 * depth), 1) % depth == row)
     slot_obs_ref[...] = one_hot((iota((slots, 3 * OBLK_DEV), 1) % OBLK_DEV) == oslot)
 
@@ -213,13 +239,13 @@
         copy.wait()
 
 
-def first_model(order, *refs):
-    parts = len(order)
+def first_model(ops, order, *refs):
+    parts = 1 + len(order)
     h_ref, pick_flux_ref, target_ref, pick_obs_ref, m_ref, x_ref = refs[parts:]
     flux = jnp.concatenate(
         [
-            ref[:, LANES * t : LANES * (t + 1)]
-            for ref in [refs[order.index(k)] for k in range(parts)]
+            read((slice(None), slice(LANES * t, LANES * (t + 1))))
+            for read in readers(in_turn(refs, order), ops, lax.axis_index("cell"))
             for t in range(CBLK_DEV // 2)
         ],
         axis=0,
@@ -245,9 +271,10 @@
     message_ref[half:, :] = index_ref[...]
 
 
-def second_model(parts, *refs):
-    messages = refs[:parts]
-    cells = parts
+def second_model(ops, order, *refs):
+    parts = 1 + len(order)
+    messages = readers(in_turn(refs, order), ops, lax.axis_index("cell"))
+    cells = len(messages)
     target_ref, x_ref, h_ref, pick_obs_ref, m_ref = refs[parts:]
     slots = target_ref.shape[0]
     half = slots // 2
@@ -262,19 +289,19 @@
             for q in range(count):
                 at = half + part * count + q
                 row = jnp.zeros((1, LANES), F32)
-                for k, ref in enumerate(members):
-                    row = jnp.where(iota((1, LANES), 1) // half % group == k, ref[at : at + 1, :], row)
+                for k, read in enumerate(members):
+                    row = jnp.where(iota((1, LANES), 1) // half % group == k, read(slice(at, at + 1)), row)
                 rows.append(one_hot(target_ref[...] == row))
             picks.append(jnp.concatenate(rows, axis=1)[:, : group * half])
         pick = jnp.concatenate(picks, axis=0)
-        values = jnp.concatenate([ref[:half, :] for ref in members], axis=0)
+        values = jnp.concatenate([read(slice(0, half)) for read in members], axis=0)
         found = pick_rows(jnp.concatenate([pick] * 3, axis=1), values)
         total = found if total is None else total + found
     change = jnp.where(low((slots, LANES)), total[:slots], total[slots:])
     m_ref[...] = forward(h_ref, pick_obs_ref[...], x_ref[...] - 0.5 * (change + half_swap(change)))
 
 
-def second_adjoint(parts, *refs):
+def second_adjoint(ops, parts, *refs):
     observed_ref, weight_ref, first_ref, slot_obs_ref, h_ref = refs[parts : parts + 5]
     *outs, d_ref, block_scr = refs[parts + 5 :]
     me = lax.axis_index("cell")
@@ -286,15 +313,21 @@
         block_scr[o] = block
 
     adjoint(h_ref, slot_obs_ref[...], -0.25 * first_ref[...] - 0.5 * d, store)
-    for k in range(owners):
-        outs[owners - 1 - k][...] = block_scr[me ^ k]
-
-
-def prepare_increment(parts, rows, *refs):
-    d_ref, pick_ref, departure_ref = refs[parts:]
-    messages = refs[:parts]
-    cells = parts
+    for j, out in enumerate(outs):
+        if ops is None:
+            target = me ^ j
+        else:
+            target = me
+            for src, dst in ops[j - 1] if j else ():
+                target = jnp.where(me == src, dst, target)
+        out[...] = block_scr[target]
+
+
+def prepare_increment(ops, order, rows, *refs):
+    d_ref, pick_ref, departure_ref = refs[1 + len(order) :]
     me = lax.axis_index("cell")
+    messages = readers(in_turn(refs, order), ops, me)
+    cells = len(messages)
     half = cells * rows
     count = max(1, half // LANES)
     place = me * rows
@@ -307,7 +340,7 @@
             index = jnp.zeros((1, LANES), F32)
             for k in range(first // rows, min(cells, (first + LANES) // rows)):
                 turned = pltpu.roll(
-                    messages[k][half:, :], lax.rem(k * rows - place % LANES + 2 * LANES - first, LANES), 1
+                    messages[k](slice(half, None)), lax.rem(k * rows - place % LANES + 2 * LANES - first, LANES), 1
                 )
                 chosen = turned[part * count : part * count + 1]
                 for q in range(1, count):
@@ -322,9 +355,10 @@
         )
 
 
-def gather_increment(*refs):
+def gather_increment(ops, order, *refs):
     *arrays, pick_ref, out_ref = refs
-    values = jnp.concatenate([ref[...] for ref in arrays[::-1]], axis=0)
+    sources = readers(in_turn(arrays, order), ops, lax.axis_index("cell"))
+    values = jnp.concatenate([read(...) for read in sources], axis=0)
     half = values.shape[0]
     terms = three(values)
     pick = pick_ref[...]
@@ -341,12 +375,18 @@
         out_ref[:, LANES * t : LANES * (t + 1)] = jnp.where(low(even.shape), even, odd)
 
 
-def send(value, axis, size, k):
-    return lax.ppermute(value, axis, [(i, i ^ k) for i in range(size)])
-
-
 def exchange(own, sent, axis, size):
-    return [own] + [send(sent, axis, size, k) for k in range(size - 1, 0, -1)][::-1]
+    return [own] + [
+        lax.ppermute(sent, axis, [(i, i ^ k) for i in range(size)]) for k in range(1, size)
+    ]
+
+
+def exchange_by(ops, order, own, sent):
+    outs = [
+        lax.ppermute(sent[j] if isinstance(sent, list) else sent, "cell", op)
+        for j, op in enumerate(ops)
+    ]
+    return [own] + [outs[j] for j in order]
 
 
 def make_local(cells, wins):
@@ -354,6 +394,10 @@
         owners, capacity = footprint.shape[2:4]
         slots = owners * capacity
         half = slots // 2
+        xors = [[(i, i ^ k) for i in range(cells)] for k in range(1, cells)]
+        rounds = (GATHER_FLUX, GATHER_BLOCKS, SCATTER_BLOCKS) if cells == 4 else (xors,) * 3
+        orders = ORDERS if cells == 4 else (list(range(cells - 1)),) * 3
+        tables = rounds if cells == 4 else (None,) * 3
         index_rows = -(-2 * max(1, half // LANES) // 8) * 8
         params = pltpu.CompilerParams(vmem_limit_bytes=4 * footprint.size * 4 + 8 * 2**20)
         hbm = pl.BlockSpec(memory_space=pltpu.HBM)
@@ -380,7 +424,7 @@
         slot_tile = ((slots, LANES), F32)
         small = (flux_slot, obs_slot, slot_count, observed, obs_weight)
         pick_flux, target, slot_obs, pick_obs, index, observed_t, weight_t, flux, matrices = call(
-            prepare,
+            functools.partial(prepare, tables[0] is None),
             [
                 ((slots, 3 * owners * BLOCKS // 2), BF16),
                 slot_tile,
@@ -400,41 +444,41 @@
             ],
             hbm,
         )
-        order = [0, cells // 2, *range(1, cells // 2), *range(cells // 2 + 1, cells)]
-        fluxes = exchange(flux, prior_flux, "cell", cells)
         m0, x0 = call(
-            functools.partial(first_model, order),
+            functools.partial(first_model, tables[0], orders[0]),
             [obs_tile, slot_tile],
-            (*(fluxes[k] for k in order), matrices, pick_flux, target, pick_obs),
+            (
+                *exchange_by(rounds[0], orders[0], flux, prior_flux),
+                *(matrices, pick_flux, target, pick_obs),
+            ),
         )
         message, d0 = call(
             functools.partial(first_adjoint, wins),
             [((half + index_rows, LANES), F32), obs_tile],
             (*exchange(m0, m0, "win", wins), observed_t, weight_t, slot_obs, index, matrices),
         )
-        messages = exchange(message, message, "cell", cells)
+        messages = exchange_by(rounds[1], orders[1], message, message)
         (m1,) = call(
-            functools.partial(second_model, cells),
+            functools.partial(second_model, tables[1], orders[1]),
             [obs_tile],
             (*messages, target, x0, matrices, pick_obs),
         )
         *blocks, d1 = call(
-            functools.partial(second_adjoint, wins),
-            [((capacity // 2, LANES), F32)] * owners + [obs_tile],
+            functools.partial(second_adjoint, tables[2], wins),
+            [((capacity // 2, LANES), F32)] * (1 + len(rounds[2])) + [obs_tile],
             (*exchange(m1, m1, "win", wins), observed_t, weight_t, d0, slot_obs, matrices),
             [pltpu.VMEM((owners, capacity // 2, LANES), F32)],
         )
-        arrays = [send(block, "cell", cells, cells - 1 - i) for i, block in enumerate(blocks[:-1])]
-        arrays = [blocks[-1]] + arrays[::-1]
+        arrays = exchange_by(rounds[2], orders[2], blocks[0], blocks[1:])
         pick, departure = call(
-            functools.partial(prepare_increment, cells, capacity // 2),
+            functools.partial(prepare_increment, tables[1], orders[1], capacity // 2),
             [((2 * BLOCKS, max(LANES, half)), BF16), ((1, OBLK_DEV * OB), F32)],
             (*messages, d1),
         )
         (increment,) = call(
-            gather_increment,
+            functools.partial(gather_increment, tables[2], orders[2]),
             [((WIN_DEV, CBLK_DEV * CB), F32)],
-            (*arrays[::-1], pick),
+            (*arrays, pick),
         )
         return increment, departure
 

time: 35.1 us -> 51.7 us (1.47)
  starting transfers between devices: 18.3 us -> 39.1 us
  waiting for transfers between devices: 10.2 us -> 5.36 us
    ppermute x15 -> x21, starting transfers between devices: 18.3 us -> 39.1 us  [the longest x15 34.6 us: exchange_by(): lax.ppermute(sent[j] if isinstance(sent, list) else sent, 'cell', op)]
    ppermute x15 -> x21, waiting for transfers between devices: 10.2 us -> 5.36 us  [the longest x6 3.68 us: exchange(): lax.ppermute(sent, axis, [(i, i ^ k) for i in range(size)])]
  transfers between devices with their start and end apart: 15 -> 21, of which waited for: 10 -> 6; matrix products, arithmetic and copies ran while one was open for 0% -> 0% of each run, Pallas kernels for 6% -> 4%
where the time goes in v7:
time: 51.7 us; the launch traced here: 51.1 us
  starting transfers between devices  39.1 us (76%)
  Pallas kernels  5.79 us (11%)
  waiting for transfers between devices  5.36 us (10%)
  between operations  0.83 us (2%)
    ppermute x15, starting transfers between devices, exchange_by(): lax.ppermute(sent[j] if isinstance(sent, list) else sent, 'cell', op)  34.6 us
    pallas_call x7, Pallas kernels, call(): pl.pallas_call(body, out_shape=outs_at, in_specs=[space] * len(ins), out_...  5.79 us
    ppermute x6, starting transfers between devices, exchange(): lax.ppermute(sent, axis, [(i, i ^ k) for i in range(size)])  4.45 us
    ppermute x6, waiting for transfers between devices, exchange(): lax.ppermute(sent, axis, [(i, i ^ k) for i in range(size)])  3.68 us
    ppermute x15, waiting for transfers between devices, exchange_by(): lax.ppermute(sent[j] if isinstance(sent, list) else sent, 'cell', op)  1.68 us
  transfers between devices with their start and end apart: 21, of which 6 were waited for; matrix products, arithmetic and copies ran while one was open for 0% of the time, Pallas kernels for 4%

profile of v7, /device:TPU:0, one launch (start us, length us, event | category | flops | bytes accessed | tf_op | source)
XLA Modules:
  0.0 51.1 jit_solution(14317049871501263302)
XLA Ops:
  0.6 1.3 %collective-permute-start.2 = (f32[8,512]{1,0:T(8,128)}, f32[8,512]{1,0:T(8,128)S(1)}, u32[]{:S(2)}, u32[]{:S(2)}) collective-permute-start(f32[8,512]{1,0:T(8,128)} %flux_hbm.1), channel_id=1, source_target_pairs={{12,8},{4,0},{13,9},{5,1},{14,10},{6,2},{15,11},{7,3},{28,24},{20,... | collective-permute-start | bytes 49160 | tf_op jit(solution)/shard_map/ppermute | solution.py:386
  1.9 1.3 %collective-permute-start.1 = (f32[8,512]{1,0:T(8,128)}, f32[8,512]{1,0:T(8,128)S(1)}, u32[]{:S(2)}, u32[]{:S(2)}) collective-permute-start(f32[8,512]{1,0:T(8,128)} %flux_hbm.1), channel_id=1, source_target_pairs={{4,8},{8,0},{12,4},{5,9},{9,1},{13,5},{6,10},{10,2},{14,6},{7,11},... | collective-permute-start | bytes 49160 | tf_op jit(solution)/shard_map/ppermute | solution.py:386
  3.2 6.6 %collective-permute-start = (f32[8,512]{1,0:T(8,128)}, f32[8,512]{1,0:T(8,128)S(1)}, u32[]{:S(2)}, u32[]{:S(2)}) collective-permute-start(f32[8,512]{1,0:T(8,128)} %flux_hbm.1), channel_id=1, source_target_pairs={{12,0},{0,8},{8,12},{13,1},{1,9},{9,13},{14,2},{2,10},{10,14},{15,... | collective-permute-start | bytes 49160 | tf_op jit(solution)/shard_map/ppermute | solution.py:386
  9.8 3.4 %collective-permute-start.4 = (f32[8,512]{1,0:T(8,128)}, f32[8,512]{1,0:T(8,128)S(1)}, u32[]{:S(2)}, u32[]{:S(2)}) collective-permute-start(f32[8,512]{1,0:T(8,128)} %flux_hbm.1), channel_id=1, source_target_pairs={{0,12},{8,4},{1,13},{9,5},{2,14},{10,6},{3,15},{11,7},{16,28},{24,... | collective-permute-start | bytes 49160 | tf_op jit(solution)/shard_map/ppermute | solution.py:386
  13.2 1.3 %collective-permute-start.3 = (f32[8,512]{1,0:T(8,128)}, f32[8,512]{1,0:T(8,128)S(1)}, u32[]{:S(2)}, u32[]{:S(2)}) collective-permute-start(f32[8,512]{1,0:T(8,128)} %flux_hbm.1), channel_id=1, source_target_pairs={{0,4},{4,12},{1,5},{5,13},{2,6},{6,14},{3,7},{7,15},{16,20},{20,28... | collective-permute-start | bytes 49160 | tf_op jit(solution)/shard_map/ppermute | solution.py:386
  14.5 1.4 %shard_map.86 = (bf16[64,384]{1,0:T(8,128)(2,1)S(1)}, f32[64,128]{1,0:T(8,128)S(1)}, bf16[64,24]{1,0:T(8,128)(2,1)S(1)}, bf16[16,192]{1,0:T(8,128)(2,1)S(1)}, f3...) custom-call(s32[1,1,4,16]{3,2,1,0:T(4,128)} %fslot_hbm.1, ...), custom_call_target="tpu_custom_call" | custom-call | tf_op jit(solution)/shard_map/pallas_call | solution.py:411
  15.9 0.2 collective-permute-done.3.refs_4_
  16.1 1.0 %shard_map.87 = (f32[8,128]{1,0:T(8,128)S(1)}, f32[64,128]{1,0:T(8,128)S(1)}) custom-call(f32[8,512]{1,0:T(8,128)S(1)} %get-tuple-element.24.refs_0_, f32[8,512]{1,0:T(8,128)S(1)} %collective-permute-done.refs_1_, f32[8,512]{1,0:T(8,128)S(1)} %collective-permute-done.1.refs_2_, f32[8,512]{1,0:T(8,128)S(1)} %collective-permute-done.2.refs_3_, ...), custom_call_target="tpu_custom_call" | custom-call | tf_op jit(solution)/shard_map/pallas_call | solution.py:411
  17.1 0.9 %collective-permute-start.7 = (f32[8,128]{1,0:T(8,128)S(1)}, f32[8,128]{1,0:T(8,128)S(1)}, u32[]{:S(2)}, u32[]{:S(2)}) collective-permute-start(f32[8,128]{1,0:T(8,128)S(1)} %get-tuple-element.29.refs_0_), channel_id=1, source_target_pairs={{0,3},{1,2},{2,1},{3,0},{4,7},{5,6},{6,5},{7,4},{8,11},{9,10},{10,... | collective-permute-start | bytes 12296 | tf_op jit(solution)/shard_map/ppermute | solution.py:380
  18.0 1.6 %collective-permute-start.6 = (f32[8,128]{1,0:T(8,128)S(1)}, f32[8,128]{1,0:T(8,128)S(1)}, u32[]{:S(2)}, u32[]{:S(2)}) collective-permute-start(f32[8,128]{1,0:T(8,128)S(1)} %get-tuple-element.29.refs_0_), channel_id=1, source_target_pairs={{0,2},{1,3},{2,0},{3,1},{4,6},{5,7},{6,4},{7,5},{8,10},{9,11},{10,... | collective-permute-start | bytes 12296 | tf_op jit(solution)/shard_map/ppermute | solution.py:380
  19.7 0.5 collective-permute-done.7.refs_3_
  20.2 1.4 %collective-permute-done.6.refs_2_ = f32[8,128]{1,0:T(8,128)S(1)} collective-permute-done((f32[8,128]{1,0:T(8,128)S(1)}, f32[8,128]{1,0:T(8,128)S(1)}, u32[]{:S(2)}, u32[]{:S(2)}) %collective-permute-start.6) | collective-permute-done | bytes 4128 | tf_op jit(solution)/shard_map/ppermute | solution.py:380
  21.6 0.4 shard_map.88
  22.1 1.3 %collective-permute-start.12 = (f32[40,128]{1,0:T(8,128)S(1)}, f32[40,128]{1,0:T(8,128)S(1)}, u32[]{:S(2)}, u32[]{:S(2)}) collective-permute-start(f32[40,128]{1,0:T(8,128)S(1)} %get-tuple-element.34.refs_0_), channel_id=1, source_target_pairs={{8,0},{12,8},{9,1},{13,9},{10,2},{14,10},{11,3},{15,11},{24,16},{2... | collective-permute-start | bytes 61448 | tf_op jit(solution)/shard_map/ppermute | solution.py:386
  23.4 1.3 %collective-permute-start.11 = (f32[40,128]{1,0:T(8,128)S(1)}, f32[40,128]{1,0:T(8,128)S(1)}, u32[]{:S(2)}, u32[]{:S(2)}) collective-permute-start(f32[40,128]{1,0:T(8,128)S(1)} %get-tuple-element.34.refs_0_), channel_id=1, source_target_pairs={{12,4},{8,12},{4,0},{13,5},{9,13},{5,1},{14,6},{10,14},{6,2},{15,7... | collective-permute-start | bytes 61448 | tf_op jit(solution)/shard_map/ppermute | solution.py:386
  24.7 4.6 %collective-permute-start.10 = (f32[40,128]{1,0:T(8,128)S(1)}, f32[40,128]{1,0:T(8,128)S(1)}, u32[]{:S(2)}, u32[]{:S(2)}) collective-permute-start(f32[40,128]{1,0:T(8,128)S(1)} %get-tuple-element.34.refs_0_), channel_id=1, source_target_pairs={{12,0},{0,4},{13,1},{1,5},{14,2},{2,6},{15,3},{3,7},{28,16},{16,20... | collective-permute-start | bytes 61448 | tf_op jit(solution)/shard_map/ppermute | solution.py:386
  29.2 3.1 %collective-permute-start.9 = (f32[40,128]{1,0:T(8,128)S(1)}, f32[40,128]{1,0:T(8,128)S(1)}, u32[]{:S(2)}, u32[]{:S(2)}) collective-permute-start(f32[40,128]{1,0:T(8,128)S(1)} %get-tuple-element.34.refs_0_), channel_id=1, source_target_pairs={{4,8},{0,12},{8,4},{5,9},{1,13},{9,5},{6,10},{2,14},{10,6},{7,11},... | collective-permute-start | bytes 61448 | tf_op jit(solution)/shard_map/ppermute | solution.py:386
  32.3 1.6 %collective-permute-start.8 = (f32[40,128]{1,0:T(8,128)S(1)}, f32[40,128]{1,0:T(8,128)S(1)}, u32[]{:S(2)}, u32[]{:S(2)}) collective-permute-start(f32[40,128]{1,0:T(8,128)S(1)} %get-tuple-element.34.refs_0_), channel_id=1, source_target_pairs={{0,8},{4,12},{1,9},{5,13},{2,10},{6,14},{3,11},{7,15},{16,24},{20,... | collective-permute-start | bytes 61448 | tf_op jit(solution)/shard_map/ppermute | solution.py:386
  33.9 1.4 %collective-permute-done.8.refs_1_ = f32[40,128]{1,0:T(8,128)S(1)} collective-permute-done((f32[40,128]{1,0:T(8,128)S(1)}, f32[40,128]{1,0:T(8,128)S(1)}, u32[]{:S(2)}, u32[]{:S(2)}) %collective-permute-start.8) | collective-permute-done | bytes 20512 | tf_op jit(solution)/shard_map/ppermute | solution.py:386
  35.4 1.1 %shard_map.89.refs_0_ = f32[8,128]{1,0:T(8,128)S(1)} custom-call(f32[40,128]{1,0:T(8,128)S(1)} %get-tuple-element.34.refs_0_, f32[40,128]{1,0:T(8,128)S(1)} %collective-permute-done.8.refs_1_, f32[40,128]{1,0:T(8,128)S(1)} %collective-permute-done.9.refs_2_, f32[40,128]{1,0:T(8,128)S(1)} %collective-permute-done.10.refs_3_, ...), custom_call_target="tpu_custom_call" | custom-call | tf_op jit(solution)/shard_map/pallas_call | solution.py:411
  36.4 1.7 %collective-permute-start.14 = (f32[8,128]{1,0:T(8,128)S(1)}, f32[8,128]{1,0:T(8,128)S(1)}, u32[]{:S(2)}, u32[]{:S(2)}) collective-permute-start(f32[8,128]{1,0:T(8,128)S(1)} %shard_map.89.refs_0_), channel_id=1, source_target_pairs={{0,2},{1,3},{2,0},{3,1},{4,6},{5,7},{6,4},{7,5},{8,10},{9,11},{10,... | collective-permute-start | bytes 12296 | tf_op jit(solution)/shard_map/ppermute | solution.py:380
  38.1 0.2 collective-permute-start.13
  38.3 1.2 %collective-permute-done.15.refs_3_ = f32[8,128]{1,0:T(8,128)S(1)} collective-permute-done((f32[8,128]{1,0:T(8,128)S(1)}, f32[8,128]{1,0:T(8,128)S(1)}, u32[]{:S(2)}, u32[]{:S(2)}) %collective-permute-start.15) | collective-permute-done | bytes 4128 | tf_op jit(solution)/shard_map/ppermute | solution.py:380
  39.5 0.6 %collective-permute-done.14.refs_2_ = f32[8,128]{1,0:T(8,128)S(1)} collective-permute-done((f32[8,128]{1,0:T(8,128)S(1)}, f32[8,128]{1,0:T(8,128)S(1)}, u32[]{:S(2)}, u32[]{:S(2)}) %collective-permute-start.14) | collective-permute-done | bytes 4128 | tf_op jit(solution)/shard_map/ppermute | solution.py:380
  40.1 0.4 shard_map.90
  40.5 1.3 %collective-permute-start.16 = (f32[8,128]{1,0:T(8,128)S(1)}, f32[8,128]{1,0:T(8,128)S(1)}, u32[]{:S(2)}, u32[]{:S(2)}) collective-permute-start(f32[8,128]{1,0:T(8,128)S(1)} %get-tuple-element.38), channel_id=1, source_target_pairs={{12,0},{8,4},{13,1},{9,5},{14,2},{10,6},{15,3},{11,7},{28,16},{24,... | collective-permute-start | bytes 12296 | tf_op jit(solution)/shard_map/ppermute | solution.py:386
  41.8 2.2 %collective-permute-start.17 = (f32[8,128]{1,0:T(8,128)S(1)}, f32[8,128]{1,0:T(8,128)S(1)}, u32[]{:S(2)}, u32[]{:S(2)}) collective-permute-start(f32[8,128]{1,0:T(8,128)S(1)} %get-tuple-element.39), channel_id=1, source_target_pairs={{8,0},{0,4},{9,1},{1,5},{10,2},{2,6},{11,3},{3,7},{24,16},{16,20},... | collective-permute-start | bytes 12296 | tf_op jit(solution)/shard_map/ppermute | solution.py:386
  44.0 2.7 %collective-permute-start.18 = (f32[8,128]{1,0:T(8,128)S(1)}, f32[8,128]{1,0:T(8,128)S(1)}, u32[]{:S(2)}, u32[]{:S(2)}) collective-permute-start(f32[8,128]{1,0:T(8,128)S(1)} %get-tuple-element.40), channel_id=1, source_target_pairs={{4,0},{12,4},{0,8},{8,12},{5,1},{13,5},{1,9},{9,13},{6,2},{14,6},{... | collective-permute-start | bytes 12296 | tf_op jit(solution)/shard_map/ppermute | solution.py:386
  46.7 2.2 %collective-permute-start.19 = (f32[8,128]{1,0:T(8,128)S(1)}, f32[8,128]{1,0:T(8,128)S(1)}, u32[]{:S(2)}, u32[]{:S(2)}) collective-permute-start(f32[8,128]{1,0:T(8,128)S(1)} %get-tuple-element.41), channel_id=1, source_target_pairs={{0,12},{4,8},{1,13},{5,9},{2,14},{6,10},{3,15},{7,11},{16,28},{20,... | collective-permute-start | bytes 12296 | tf_op jit(solution)/shard_map/ppermute | solution.py:386
  48.9 0.7 %collective-permute-start.20 = (f32[8,128]{1,0:T(8,128)S(1)}, f32[8,128]{1,0:T(8,128)S(1)}, u32[]{:S(2)}, u32[]{:S(2)}) collective-permute-start(f32[8,128]{1,0:T(8,128)S(1)} %get-tuple-element.42), channel_id=1, source_target_pairs={{12,8},{4,12},{13,9},{5,13},{14,10},{6,14},{15,11},{7,15},{28,24},... | collective-permute-start | bytes 12296 | tf_op jit(solution)/shard_map/ppermute | solution.py:386
  49.6 0.6 %shard_map.91 = (bf16[128,128]{1,0:T(8,128)(2,1)S(1)}, f32[1,512]{1,0:T(1,128)}) custom-call(f32[40,128]{1,0:T(8,128)S(1)} %get-tuple-element.34.refs_0_, f32[40,128]{1,0:T(8,128)S(1)} %collective-permute-done.8.refs_1_, f32[40,128]{1,0:T(8,128)S(1)} %collective-permute-done.9.refs_2_, f32[40,128]{1,0:T(8,128)S(1)} %collective-permute-done.10.refs_3_, ...), custom_call_target="tpu_custom_call" | custom-call | tf_op jit(solution)/shard_map/pallas_call | solution.py:411
  50.2 0.8 %shard_map.92 = f32[8,512]{1,0:T(8,128)} custom-call(f32[8,128]{1,0:T(8,128)S(1)} %get-tuple-element.37.refs_0_, f32[8,128]{1,0:T(8,128)S(1)} %collective-permute-done.16.refs_1_, f32[8,128]{1,0:T(8,128)S(1)} %collective-permute-done.17.refs_2_, f32[8,128]{1,0:T(8,128)S(1)} %collective-permute-done.18.refs_3_, f32[8,128]{1,0:T(8,128)S(1)} %collective-permute-done.19.refs_4_, ...), custom_call_target="tpu_custom_call" | custom-call | tf_op jit(solution)/shard_map/pallas_call | solution.py:411
  (17 shorter events, 0.1 us)
Async XLA Ops:
  0.6 15.2 %collective-permute-start.2 = (f32[8,512]{1,0:T(8,128)}, f32[8,512]{1,0:T(8,128)S(1)}, u32[]{:S(2)}, u32[]{:S(2)}) collective-permute-start(f32[8,512]{1,0:T(8,128)} %flux_hbm.1), channel_id=1, source_target_pairs={{12,8},{4,0},{13,9},{5,1},{14,10},{6,2},{15,11},{7,3},{28,24},{20,... | collective-permute-start | bytes 49160 | tf_op jit(solution)/shard_map/ppermute | solution.py:386
  1.9 13.9 %collective-permute-start.1 = (f32[8,512]{1,0:T(8,128)}, f32[8,512]{1,0:T(8,128)S(1)}, u32[]{:S(2)}, u32[]{:S(2)}) collective-permute-start(f32[8,512]{1,0:T(8,128)} %flux_hbm.1), channel_id=1, source_target_pairs={{4,8},{8,0},{12,4},{5,9},{9,1},{13,5},{6,10},{10,2},{14,6},{7,11},... | collective-permute-start | bytes 49160 | tf_op jit(solution)/shard_map/ppermute | solution.py:386
  3.2 12.7 %collective-permute-start = (f32[8,512]{1,0:T(8,128)}, f32[8,512]{1,0:T(8,128)S(1)}, u32[]{:S(2)}, u32[]{:S(2)}) collective-permute-start(f32[8,512]{1,0:T(8,128)} %flux_hbm.1), channel_id=1, source_target_pairs={{12,0},{0,8},{8,12},{13,1},{1,9},{9,13},{14,2},{2,10},{10,14},{15,... | collective-permute-start | bytes 49160 | tf_op jit(solution)/shard_map/ppermute | solution.py:386
  9.8 6.1 %collective-permute-start.4 = (f32[8,512]{1,0:T(8,128)}, f32[8,512]{1,0:T(8,128)S(1)}, u32[]{:S(2)}, u32[]{:S(2)}) collective-permute-start(f32[8,512]{1,0:T(8,128)} %flux_hbm.1), channel_id=1, source_target_pairs={{0,12},{8,4},{1,13},{9,5},{2,14},{10,6},{3,15},{11,7},{16,28},{24,... | collective-permute-start | bytes 49160 | tf_op jit(solution)/shard_map/ppermute | solution.py:386
  13.2 2.9 %collective-permute-start.3 = (f32[8,512]{1,0:T(8,128)}, f32[8,512]{1,0:T(8,128)S(1)}, u32[]{:S(2)}, u32[]{:S(2)}) collective-permute-start(f32[8,512]{1,0:T(8,128)} %flux_hbm.1), channel_id=1, source_target_pairs={{0,4},{4,12},{1,5},{5,13},{2,6},{6,14},{3,7},{7,15},{16,20},{20,28... | collective-permute-start | bytes 49160 | tf_op jit(solution)/shard_map/ppermute | solution.py:386
  17.1 3.0 %collective-permute-start.7 = (f32[8,128]{1,0:T(8,128)S(1)}, f32[8,128]{1,0:T(8,128)S(1)}, u32[]{:S(2)}, u32[]{:S(2)}) collective-permute-start(f32[8,128]{1,0:T(8,128)S(1)} %get-tuple-element.29.refs_0_), channel_id=1, source_target_pairs={{0,3},{1,2},{2,1},{3,0},{4,7},{5,6},{6,5},{7,4},{8,11},{9,10},{10,... | collective-permute-start | bytes 12296 | tf_op jit(solution)/shard_map/ppermute | solution.py:380
  18.0 3.6 %collective-permute-start.6 = (f32[8,128]{1,0:T(8,128)S(1)}, f32[8,128]{1,0:T(8,128)S(1)}, u32[]{:S(2)}, u32[]{:S(2)}) collective-permute-start(f32[8,128]{1,0:T(8,128)S(1)} %get-tuple-element.29.refs_0_), channel_id=1, source_target_pairs={{0,2},{1,3},{2,0},{3,1},{4,6},{5,7},{6,4},{7,5},{8,10},{9,11},{10,... | collective-permute-start | bytes 12296 | tf_op jit(solution)/shard_map/ppermute | solution.py:380
  19.6 2.0 %collective-permute-start.5 = (f32[8,128]{1,0:T(8,128)S(1)}, f32[8,128]{1,0:T(8,128)S(1)}, u32[]{:S(2)}, u32[]{:S(2)}) collective-permute-start(f32[8,128]{1,0:T(8,128)S(1)} %get-tuple-element.29.refs_0_), channel_id=1, source_target_pairs={{0,1},{1,0},{2,3},{3,2},{4,5},{5,4},{6,7},{7,6},{8,9},{9,8},{10,11... | collective-permute-start | bytes 12296 | tf_op jit(solution)/shard_map/ppermute | solution.py:380
  22.1 11.8 %collective-permute-start.12 = (f32[40,128]{1,0:T(8,128)S(1)}, f32[40,128]{1,0:T(8,128)S(1)}, u32[]{:S(2)}, u32[]{:S(2)}) collective-permute-start(f32[40,128]{1,0:T(8,128)S(1)} %get-tuple-element.34.refs_0_), channel_id=1, source_target_pairs={{8,0},{12,8},{9,1},{13,9},{10,2},{14,10},{11,3},{15,11},{24,16},{2... | collective-permute-start | bytes 61448 | tf_op jit(solution)/shard_map/ppermute | solution.py:386
  23.4 10.5 %collective-permute-start.11 = (f32[40,128]{1,0:T(8,128)S(1)}, f32[40,128]{1,0:T(8,128)S(1)}, u32[]{:S(2)}, u32[]{:S(2)}) collective-permute-start(f32[40,128]{1,0:T(8,128)S(1)} %get-tuple-element.34.refs_0_), channel_id=1, source_target_pairs={{12,4},{8,12},{4,0},{13,5},{9,13},{5,1},{14,6},{10,14},{6,2},{15,7... | collective-permute-start | bytes 61448 | tf_op jit(solution)/shard_map/ppermute | solution.py:386
  24.7 9.3 %collective-permute-start.10 = (f32[40,128]{1,0:T(8,128)S(1)}, f32[40,128]{1,0:T(8,128)S(1)}, u32[]{:S(2)}, u32[]{:S(2)}) collective-permute-start(f32[40,128]{1,0:T(8,128)S(1)} %get-tuple-element.34.refs_0_), channel_id=1, source_target_pairs={{12,0},{0,4},{13,1},{1,5},{14,2},{2,6},{15,3},{3,7},{28,16},{16,20... | collective-permute-start | bytes 61448 | tf_op jit(solution)/shard_map/ppermute | solution.py:386
  29.2 4.7 %collective-permute-start.9 = (f32[40,128]{1,0:T(8,128)S(1)}, f32[40,128]{1,0:T(8,128)S(1)}, u32[]{:S(2)}, u32[]{:S(2)}) collective-permute-start(f32[40,128]{1,0:T(8,128)S(1)} %get-tuple-element.34.refs_0_), channel_id=1, source_target_pairs={{4,8},{0,12},{8,4},{5,9},{1,13},{9,5},{6,10},{2,14},{10,6},{7,11},... | collective-permute-start | bytes 61448 | tf_op jit(solution)/shard_map/ppermute | solution.py:386
  32.3 3.0 %collective-permute-start.8 = (f32[40,128]{1,0:T(8,128)S(1)}, f32[40,128]{1,0:T(8,128)S(1)}, u32[]{:S(2)}, u32[]{:S(2)}) collective-permute-start(f32[40,128]{1,0:T(8,128)S(1)} %get-tuple-element.34.refs_0_), channel_id=1, source_target_pairs={{0,8},{4,12},{1,9},{5,13},{2,10},{6,14},{3,11},{7,15},{16,24},{20,... | collective-permute-start | bytes 61448 | tf_op jit(solution)/shard_map/ppermute | solution.py:386
  36.4 3.0 %collective-permute-start.15 = (f32[8,128]{1,0:T(8,128)S(1)}, f32[8,128]{1,0:T(8,128)S(1)}, u32[]{:S(2)}, u32[]{:S(2)}) collective-permute-start(f32[8,128]{1,0:T(8,128)S(1)} %shard_map.89.refs_0_), channel_id=1, source_target_pairs={{0,3},{1,2},{2,1},{3,0},{4,7},{5,6},{6,5},{7,4},{8,11},{9,10},{10,... | collective-permute-start | bytes 12296 | tf_op jit(solution)/shard_map/ppermute | solution.py:380
  36.4 3.7 %collective-permute-start.14 = (f32[8,128]{1,0:T(8,128)S(1)}, f32[8,128]{1,0:T(8,128)S(1)}, u32[]{:S(2)}, u32[]{:S(2)}) collective-permute-start(f32[8,128]{1,0:T(8,128)S(1)} %shard_map.89.refs_0_), channel_id=1, source_target_pairs={{0,2},{1,3},{2,0},{3,1},{4,6},{5,7},{6,4},{7,5},{8,10},{9,11},{10,... | collective-permute-start | bytes 12296 | tf_op jit(solution)/shard_map/ppermute | solution.py:380
  38.1 2.0 %collective-permute-start.13 = (f32[8,128]{1,0:T(8,128)S(1)}, f32[8,128]{1,0:T(8,128)S(1)}, u32[]{:S(2)}, u32[]{:S(2)}) collective-permute-start(f32[8,128]{1,0:T(8,128)S(1)} %shard_map.89.refs_0_), channel_id=1, source_target_pairs={{0,1},{1,0},{2,3},{3,2},{4,5},{5,4},{6,7},{7,6},{8,9},{9,8},{10,11... | collective-permute-start | bytes 12296 | tf_op jit(solution)/shard_map/ppermute | solution.py:380
  40.5 9.7 %collective-permute-start.16 = (f32[8,128]{1,0:T(8,128)S(1)}, f32[8,128]{1,0:T(8,128)S(1)}, u32[]{:S(2)}, u32[]{:S(2)}) collective-permute-start(f32[8,128]{1,0:T(8,128)S(1)} %get-tuple-element.38), channel_id=1, source_target_pairs={{12,0},{8,4},{13,1},{9,5},{14,2},{10,6},{15,3},{11,7},{28,16},{24,... | collective-permute-start | bytes 12296 | tf_op jit(solution)/shard_map/ppermute | solution.py:386
  41.8 8.4 %collective-permute-start.17 = (f32[8,128]{1,0:T(8,128)S(1)}, f32[8,128]{1,0:T(8,128)S(1)}, u32[]{:S(2)}, u32[]{:S(2)}) collective-permute-start(f32[8,128]{1,0:T(8,128)S(1)} %get-tuple-element.39), channel_id=1, source_target_pairs={{8,0},{0,4},{9,1},{1,5},{10,2},{2,6},{11,3},{3,7},{24,16},{16,20},... | collective-permute-start | bytes 12296 | tf_op jit(solution)/shard_map/ppermute | solution.py:386
  44.0 6.2 %collective-permute-start.18 = (f32[8,128]{1,0:T(8,128)S(1)}, f32[8,128]{1,0:T(8,128)S(1)}, u32[]{:S(2)}, u32[]{:S(2)}) collective-permute-start(f32[8,128]{1,0:T(8,128)S(1)} %get-tuple-element.40), channel_id=1, source_target_pairs={{4,0},{12,4},{0,8},{8,12},{5,1},{13,5},{1,9},{9,13},{6,2},{14,6},{... | collective-permute-start | bytes 12296 | tf_op jit(solution)/shard_map/ppermute | solution.py:386
  46.7 3.5 %collective-permute-start.19 = (f32[8,128]{1,0:T(8,128)S(1)}, f32[8,128]{1,0:T(8,128)S(1)}, u32[]{:S(2)}, u32[]{:S(2)}) collective-permute-start(f32[8,128]{1,0:T(8,128)S(1)} %get-tuple-element.41), channel_id=1, source_target_pairs={{0,12},{4,8},{1,13},{5,9},{2,14},{6,10},{3,15},{7,11},{16,28},{20,... | collective-permute-start | bytes 12296 | tf_op jit(solution)/shard_map/ppermute | solution.py:386
  48.9 1.3 %collective-permute-start.20 = (f32[8,128]{1,0:T(8,128)S(1)}, f32[8,128]{1,0:T(8,128)S(1)}, u32[]{:S(2)}, u32[]{:S(2)}) collective-permute-start(f32[8,128]{1,0:T(8,128)S(1)} %get-tuple-element.42), channel_id=1, source_target_pairs={{12,8},{4,12},{13,9},{5,13},{14,10},{6,14},{15,11},{7,15},{28,24},... | collective-permute-start | bytes 12296 | tf_op jit(solution)/shard_map/ppermute | solution.py:386

commit v8 on v7

--- a/solution.py
+++ b/solution.py
@@ -19,10 +19,10 @@
 BF16 = jnp.bfloat16
 VMEM = pl.BlockSpec(memory_space=pltpu.VMEM)
 
-GATHER_FLUX = [[(3, 2), (1, 0)], [(1, 2), (2, 0), (3, 1)], [(3, 0), (0, 2), (2, 3)], [(0, 3), (2, 1)], [(0, 1), (1, 3)]]
-GATHER_BLOCKS = [[(2, 0), (3, 2)], [(3, 1), (2, 3), (1, 0)], [(3, 0), (0, 1)], [(1, 2), (0, 3), (2, 1)], [(0, 2), (1, 3)]]
-SCATTER_BLOCKS = [[(3, 0), (2, 1)], [(2, 0), (0, 1)], [(1, 0), (3, 1), (0, 2), (2, 3)], [(0, 3), (1, 2)], [(3, 2), (1, 3)]]
-ORDERS = ([2, 1, 0, 4, 3], [4, 3, 2, 1, 0], [0, 1, 2, 3, 4])
+GATHER_FLUX = [[(2, 3), (3, 2), (0, 0), (1, 1)], [(0, 1), (1, 3), (3, 0), (2, 2)], [(0, 3), (1, 2), (2, 0), (3, 1)], [(0, 2), (1, 0), (2, 1), (3, 3)]]
+GATHER_BLOCKS = [[(0, 1), (1, 3), (3, 0), (2, 2)], [(0, 3), (1, 2), (2, 0), (3, 1)], [(0, 2), (1, 0), (2, 1), (3, 3)], [(2, 3), (3, 2), (0, 0), (1, 1)]]
+SCATTER_BLOCKS = [[(0, 1), (1, 2), (2, 0), (3, 3)], [(0, 3), (3, 0), (1, 1), (2, 2)], [(0, 2), (1, 0), (2, 3), (3, 1)], [(1, 3), (2, 1), (3, 2), (0, 0)]]
+ORDERS = ([1, 0, 3, 2], [3, 2, 1, 0], [0, 1, 2, 3])
 
 
 def iota(shape, dim):
@@ -71,7 +71,7 @@
         value = refs[0][at]
         for ref, op in zip(refs[1:], ops):
             for src, dst in op:
-                if src == source:
+                if src == source and src != dst:
                     value = jnp.where(me == dst, ref[at], value)
         return value
 

time: 51.7 us -> 48.6 us (0.940)
  starting transfers between devices: 39.1 us -> 29.6 us
  waiting for transfers between devices: 5.36 us -> 11.5 us
    ppermute x15 -> x12, starting transfers between devices: 34.6 us -> 25.8 us  [exchange_by(): lax.ppermute(sent[j] if isinstance(sent, list) else sent, 'cell', op)]
    ppermute x15 -> x12, waiting for transfers between devices: 1.68 us -> 7.97 us  [exchange_by(): lax.ppermute(sent[j] if isinstance(sent, list) else sent, 'cell', op)]
    ppermute x6, starting transfers between devices: 4.45 us -> 3.76 us  [exchange(): lax.ppermute(sent, axis, [(i, i ^ k) for i in range(size)])]
  transfers between devices with their start and end apart: 21 -> 18, of which waited for: 6 -> 7; matrix products, arithmetic and copies ran while one was open for 0% -> 0% of each run, Pallas kernels for 4% -> 4%
where the time goes in v8:
time: 48.6 us; the launch traced here: 47.7 us
  starting transfers between devices  29.6 us (61%)
  waiting for transfers between devices  11.5 us (24%)
  Pallas kernels  5.78 us (12%)
  between operations  0.76 us (2%)
    ppermute x12, starting transfers between devices, exchange_by(): lax.ppermute(sent[j] if isinstance(sent, list) else sent, 'cell', op)  25.8 us
    ppermute x12, waiting for transfers between devices, exchange_by(): lax.ppermute(sent[j] if isinstance(sent, list) else sent, 'cell', op)  7.97 us
    pallas_call x7, Pallas kernels, call(): pl.pallas_call(body, out_shape=outs_at, in_specs=[space] * len(ins), out_...  5.78 us
    ppermute x6, starting transfers between devices, exchange(): lax.ppermute(sent, axis, [(i, i ^ k) for i in range(size)])  3.76 us
    ppermute x6, waiting for transfers between devices, exchange(): lax.ppermute(sent, axis, [(i, i ^ k) for i in range(size)])  3.56 us
  transfers between devices with their start and end apart: 18, of which 7 were waited for; matrix products, arithmetic and copies ran while one was open for 0% of the time, Pallas kernels for 4%

profile of v8, /device:TPU:0, one launch (start us, length us, event | category | flops | bytes accessed | tf_op | source)
XLA Modules:
  0.0 47.7 jit_solution(4615937432112670093)
XLA Ops:
  0.6 1.4 %collective-permute-start.1 = (f32[8,512]{1,0:T(8,128)}, f32[8,512]{1,0:T(8,128)S(1)}, u32[]{:S(2)}, u32[]{:S(2)}) collective-permute-start(f32[8,512]{1,0:T(8,128)} %flux_hbm.1), channel_id=1, source_target_pairs={{8,12},{12,8},{0,0},{4,4},{9,13},{13,9},{1,1},{5,5},{10,14},{14,10... | collective-permute-start | bytes 49160 | tf_op jit(solution)/shard_map/ppermute | solution.py:386
  2.0 4.9 %collective-permute-start = (f32[8,512]{1,0:T(8,128)}, f32[8,512]{1,0:T(8,128)S(1)}, u32[]{:S(2)}, u32[]{:S(2)}) collective-permute-start(f32[8,512]{1,0:T(8,128)} %flux_hbm.1), channel_id=1, source_target_pairs={{0,4},{4,12},{12,0},{8,8},{1,5},{5,13},{13,1},{9,9},{2,6},{6,14},{... | collective-permute-start | bytes 49160 | tf_op jit(solution)/shard_map/ppermute | solution.py:386
  6.9 3.1 %collective-permute-start.3 = (f32[8,512]{1,0:T(8,128)}, f32[8,512]{1,0:T(8,128)S(1)}, u32[]{:S(2)}, u32[]{:S(2)}) collective-permute-start(f32[8,512]{1,0:T(8,128)} %flux_hbm.1), channel_id=1, source_target_pairs={{0,12},{4,8},{8,0},{12,4},{1,13},{5,9},{9,1},{13,5},{2,14},{6,10},... | collective-permute-start | bytes 49160 | tf_op jit(solution)/shard_map/ppermute | solution.py:386
  10.0 1.9 %collective-permute-start.2 = (f32[8,512]{1,0:T(8,128)}, f32[8,512]{1,0:T(8,128)S(1)}, u32[]{:S(2)}, u32[]{:S(2)}) collective-permute-start(f32[8,512]{1,0:T(8,128)} %flux_hbm.1), channel_id=1, source_target_pairs={{0,8},{4,0},{8,4},{12,12},{1,9},{5,1},{9,5},{13,13},{2,10},{6,2},{... | collective-permute-start | bytes 49160 | tf_op jit(solution)/shard_map/ppermute | solution.py:386
  11.9 1.4 %shard_map.86 = (bf16[64,384]{1,0:T(8,128)(2,1)S(1)}, f32[64,128]{1,0:T(8,128)S(1)}, bf16[64,24]{1,0:T(8,128)(2,1)S(1)}, bf16[16,192]{1,0:T(8,128)(2,1)S(1)}, f3...) custom-call(s32[1,1,4,16]{3,2,1,0:T(4,128)} %fslot_hbm.1, ...), custom_call_target="tpu_custom_call" | custom-call | tf_op jit(solution)/shard_map/pallas_call | solution.py:411
  13.4 0.0 collective-permute-done.3.refs_4_
  13.4 2.5 %collective-permute-done.2.refs_3_ = f32[8,512]{1,0:T(8,128)S(1)} collective-permute-done((f32[8,512]{1,0:T(8,128)}, f32[8,512]{1,0:T(8,128)S(1)}, u32[]{:S(2)}, u32[]{:S(2)}) %collective-permute-start.2) | collective-permute-done | bytes 16416 | tf_op jit(solution)/shard_map/ppermute | solution.py:386
  15.9 1.0 %shard_map.87 = (f32[8,128]{1,0:T(8,128)S(1)}, f32[64,128]{1,0:T(8,128)S(1)}) custom-call(f32[8,512]{1,0:T(8,128)S(1)} %get-tuple-element.23.refs_0_, f32[8,512]{1,0:T(8,128)S(1)} %collective-permute-done.refs_1_, f32[8,512]{1,0:T(8,128)S(1)} %collective-permute-done.1.refs_2_, f32[8,512]{1,0:T(8,128)S(1)} %collective-permute-done.2.refs_3_, ...), custom_call_target="tpu_custom_call" | custom-call | tf_op jit(solution)/shard_map/pallas_call | solution.py:411
  16.9 0.0 collective-permute-start.6
  16.9 1.5 %collective-permute-start.5 = (f32[8,128]{1,0:T(8,128)S(1)}, f32[8,128]{1,0:T(8,128)S(1)}, u32[]{:S(2)}, u32[]{:S(2)}) collective-permute-start(f32[8,128]{1,0:T(8,128)S(1)} %get-tuple-element.28.refs_0_), channel_id=1, source_target_pairs={{0,2},{1,3},{2,0},{3,1},{4,6},{5,7},{6,4},{7,5},{8,10},{9,11},{10,... | collective-permute-start | bytes 12296 | tf_op jit(solution)/shard_map/ppermute | solution.py:380
  18.4 0.3 collective-permute-start.4
  18.8 1.2 %collective-permute-done.6.refs_3_ = f32[8,128]{1,0:T(8,128)S(1)} collective-permute-done((f32[8,128]{1,0:T(8,128)S(1)}, f32[8,128]{1,0:T(8,128)S(1)}, u32[]{:S(2)}, u32[]{:S(2)}) %collective-permute-start.6) | collective-permute-done | bytes 4128 | tf_op jit(solution)/shard_map/ppermute | solution.py:380
  19.9 0.6 %collective-permute-done.5.refs_2_ = f32[8,128]{1,0:T(8,128)S(1)} collective-permute-done((f32[8,128]{1,0:T(8,128)S(1)}, f32[8,128]{1,0:T(8,128)S(1)}, u32[]{:S(2)}, u32[]{:S(2)}) %collective-permute-start.5) | collective-permute-done | bytes 4128 | tf_op jit(solution)/shard_map/ppermute | solution.py:380
  20.6 0.4 shard_map.88
  21.0 2.5 %collective-permute-start.10 = (f32[40,128]{1,0:T(8,128)S(1)}, f32[40,128]{1,0:T(8,128)S(1)}, u32[]{:S(2)}, u32[]{:S(2)}) collective-permute-start(f32[40,128]{1,0:T(8,128)S(1)} %get-tuple-element.33.refs_0_), channel_id=1, source_target_pairs={{0,4},{4,12},{12,0},{8,8},{1,5},{5,13},{13,1},{9,9},{2,6},{6,14},{... | collective-permute-start | bytes 61448 | tf_op jit(solution)/shard_map/ppermute | solution.py:386
  23.5 3.3 %collective-permute-start.9 = (f32[40,128]{1,0:T(8,128)S(1)}, f32[40,128]{1,0:T(8,128)S(1)}, u32[]{:S(2)}, u32[]{:S(2)}) collective-permute-start(f32[40,128]{1,0:T(8,128)S(1)} %get-tuple-element.33.refs_0_), channel_id=1, source_target_pairs={{0,12},{4,8},{8,0},{12,4},{1,13},{5,9},{9,1},{13,5},{2,14},{6,10},... | collective-permute-start | bytes 61448 | tf_op jit(solution)/shard_map/ppermute | solution.py:386
  26.8 1.9 %collective-permute-start.8 = (f32[40,128]{1,0:T(8,128)S(1)}, f32[40,128]{1,0:T(8,128)S(1)}, u32[]{:S(2)}, u32[]{:S(2)}) collective-permute-start(f32[40,128]{1,0:T(8,128)S(1)} %get-tuple-element.33.refs_0_), channel_id=1, source_target_pairs={{0,8},{4,0},{8,4},{12,12},{1,9},{5,1},{9,5},{13,13},{2,10},{6,2},{... | collective-permute-start | bytes 61448 | tf_op jit(solution)/shard_map/ppermute | solution.py:386
  28.7 0.7 %collective-permute-start.7 = (f32[40,128]{1,0:T(8,128)S(1)}, f32[40,128]{1,0:T(8,128)S(1)}, u32[]{:S(2)}, u32[]{:S(2)}) collective-permute-start(f32[40,128]{1,0:T(8,128)S(1)} %get-tuple-element.33.refs_0_), channel_id=1, source_target_pairs={{8,12},{12,8},{0,0},{4,4},{9,13},{13,9},{1,1},{5,5},{10,14},{14,10... | collective-permute-start | bytes 61448 | tf_op jit(solution)/shard_map/ppermute | solution.py:386
  29.4 3.1 %collective-permute-done.8.refs_2_ = f32[40,128]{1,0:T(8,128)S(1)} collective-permute-done((f32[40,128]{1,0:T(8,128)S(1)}, f32[40,128]{1,0:T(8,128)S(1)}, u32[]{:S(2)}, u32[]{:S(2)}) %collective-permute-start.8) | collective-permute-done | bytes 20512 | tf_op jit(solution)/shard_map/ppermute | solution.py:386
  32.4 1.1 %shard_map.89.refs_0_ = f32[8,128]{1,0:T(8,128)S(1)} custom-call(f32[40,128]{1,0:T(8,128)S(1)} %get-tuple-element.33.refs_0_, f32[40,128]{1,0:T(8,128)S(1)} %collective-permute-done.7.refs_1_, f32[40,128]{1,0:T(8,128)S(1)} %collective-permute-done.8.refs_2_, f32[40,128]{1,0:T(8,128)S(1)} %collective-permute-done.9.refs_3_, ...), custom_call_target="tpu_custom_call" | custom-call | tf_op jit(solution)/shard_map/pallas_call | solution.py:411
  33.5 1.5 %collective-permute-start.12 = (f32[8,128]{1,0:T(8,128)S(1)}, f32[8,128]{1,0:T(8,128)S(1)}, u32[]{:S(2)}, u32[]{:S(2)}) collective-permute-start(f32[8,128]{1,0:T(8,128)S(1)} %shard_map.89.refs_0_), channel_id=1, source_target_pairs={{0,2},{1,3},{2,0},{3,1},{4,6},{5,7},{6,4},{7,5},{8,10},{9,11},{10,... | collective-permute-start | bytes 12296 | tf_op jit(solution)/shard_map/ppermute | solution.py:380
  35.1 0.3 collective-permute-start.11
  35.4 1.2 %collective-permute-done.13.refs_3_ = f32[8,128]{1,0:T(8,128)S(1)} collective-permute-done((f32[8,128]{1,0:T(8,128)S(1)}, f32[8,128]{1,0:T(8,128)S(1)}, u32[]{:S(2)}, u32[]{:S(2)}) %collective-permute-start.13) | collective-permute-done | bytes 4128 | tf_op jit(solution)/shard_map/ppermute | solution.py:380
  36.6 0.6 %collective-permute-done.12.refs_2_ = f32[8,128]{1,0:T(8,128)S(1)} collective-permute-done((f32[8,128]{1,0:T(8,128)S(1)}, f32[8,128]{1,0:T(8,128)S(1)}, u32[]{:S(2)}, u32[]{:S(2)}) %collective-permute-start.12) | collective-permute-done | bytes 4128 | tf_op jit(solution)/shard_map/ppermute | solution.py:380
  37.2 0.4 shard_map.90
  37.6 1.9 %collective-permute-start.14 = (f32[8,128]{1,0:T(8,128)S(1)}, f32[8,128]{1,0:T(8,128)S(1)}, u32[]{:S(2)}, u32[]{:S(2)}) collective-permute-start(f32[8,128]{1,0:T(8,128)S(1)} %get-tuple-element.37), channel_id=1, source_target_pairs={{0,4},{4,8},{8,0},{12,12},{1,5},{5,9},{9,1},{13,13},{2,6},{6,10},{... | collective-permute-start | bytes 12296 | tf_op jit(solution)/shard_map/ppermute | solution.py:386
  39.5 1.9 %collective-permute-start.15 = (f32[8,128]{1,0:T(8,128)S(1)}, f32[8,128]{1,0:T(8,128)S(1)}, u32[]{:S(2)}, u32[]{:S(2)}) collective-permute-start(f32[8,128]{1,0:T(8,128)S(1)} %get-tuple-element.38), channel_id=1, source_target_pairs={{0,12},{12,0},{4,4},{8,8},{1,13},{13,1},{5,5},{9,9},{2,14},{14,2},... | collective-permute-start | bytes 12296 | tf_op jit(solution)/shard_map/ppermute | solution.py:386
  41.5 1.7 %collective-permute-start.16 = (f32[8,128]{1,0:T(8,128)S(1)}, f32[8,128]{1,0:T(8,128)S(1)}, u32[]{:S(2)}, u32[]{:S(2)}) collective-permute-start(f32[8,128]{1,0:T(8,128)S(1)} %get-tuple-element.39), channel_id=1, source_target_pairs={{0,8},{4,0},{8,12},{12,4},{1,9},{5,1},{9,13},{13,5},{2,10},{6,2},{... | collective-permute-start | bytes 12296 | tf_op jit(solution)/shard_map/ppermute | solution.py:386
  43.2 0.6 %collective-permute-start.17 = (f32[8,128]{1,0:T(8,128)S(1)}, f32[8,128]{1,0:T(8,128)S(1)}, u32[]{:S(2)}, u32[]{:S(2)}) collective-permute-start(f32[8,128]{1,0:T(8,128)S(1)} %get-tuple-element.40), channel_id=1, source_target_pairs={{4,12},{8,4},{12,8},{0,0},{5,13},{9,5},{13,9},{1,1},{6,14},{10,6},... | collective-permute-start | bytes 12296 | tf_op jit(solution)/shard_map/ppermute | solution.py:386
  43.8 0.6 %shard_map.91 = (bf16[128,128]{1,0:T(8,128)(2,1)S(1)}, f32[1,512]{1,0:T(1,128)}) custom-call(f32[40,128]{1,0:T(8,128)S(1)} %get-tuple-element.33.refs_0_, f32[40,128]{1,0:T(8,128)S(1)} %collective-permute-done.7.refs_1_, f32[40,128]{1,0:T(8,128)S(1)} %collective-permute-done.8.refs_2_, f32[40,128]{1,0:T(8,128)S(1)} %collective-permute-done.9.refs_3_, ...), custom_call_target="tpu_custom_call" | custom-call | tf_op jit(solution)/shard_map/pallas_call | solution.py:411
  44.5 2.4 %collective-permute-done.15.refs_2_ = f32[8,128]{1,0:T(8,128)S(1)} collective-permute-done((f32[8,128]{1,0:T(8,128)S(1)}, f32[8,128]{1,0:T(8,128)S(1)}, u32[]{:S(2)}, u32[]{:S(2)}) %collective-permute-start.15) | collective-permute-done | bytes 4128 | tf_op jit(solution)/shard_map/ppermute | solution.py:386
  46.9 0.8 %shard_map.92 = f32[8,512]{1,0:T(8,128)} custom-call(f32[8,128]{1,0:T(8,128)S(1)} %get-tuple-element.36.refs_0_, f32[8,128]{1,0:T(8,128)S(1)} %collective-permute-done.14.refs_1_, f32[8,128]{1,0:T(8,128)S(1)} %collective-permute-done.15.refs_2_, f32[8,128]{1,0:T(8,128)S(1)} %collective-permute-done.16.refs_3_, f32[8,128]{1,0:T(8,128)S(1)} %collective-permute-done.17.refs_4_, ...), custom_call_target="tpu_custom_call" | custom-call | tf_op jit(solution)/shard_map/pallas_call | solution.py:411
  (11 shorter events, 0.0 us)
Async XLA Ops:
  0.6 12.7 %collective-permute-start.1 = (f32[8,512]{1,0:T(8,128)}, f32[8,512]{1,0:T(8,128)S(1)}, u32[]{:S(2)}, u32[]{:S(2)}) collective-permute-start(f32[8,512]{1,0:T(8,128)} %flux_hbm.1), channel_id=1, source_target_pairs={{8,12},{12,8},{0,0},{4,4},{9,13},{13,9},{1,1},{5,5},{10,14},{14,10... | collective-permute-start | bytes 49160 | tf_op jit(solution)/shard_map/ppermute | solution.py:386
  2.0 11.3 %collective-permute-start = (f32[8,512]{1,0:T(8,128)}, f32[8,512]{1,0:T(8,128)S(1)}, u32[]{:S(2)}, u32[]{:S(2)}) collective-permute-start(f32[8,512]{1,0:T(8,128)} %flux_hbm.1), channel_id=1, source_target_pairs={{0,4},{4,12},{12,0},{8,8},{1,5},{5,13},{13,1},{9,9},{2,6},{6,14},{... | collective-permute-start | bytes 49160 | tf_op jit(solution)/shard_map/ppermute | solution.py:386
  6.9 6.4 %collective-permute-start.3 = (f32[8,512]{1,0:T(8,128)}, f32[8,512]{1,0:T(8,128)S(1)}, u32[]{:S(2)}, u32[]{:S(2)}) collective-permute-start(f32[8,512]{1,0:T(8,128)} %flux_hbm.1), channel_id=1, source_target_pairs={{0,12},{4,8},{8,0},{12,4},{1,13},{5,9},{9,1},{13,5},{2,14},{6,10},... | collective-permute-start | bytes 49160 | tf_op jit(solution)/shard_map/ppermute | solution.py:386
  10.0 5.8 %collective-permute-start.2 = (f32[8,512]{1,0:T(8,128)}, f32[8,512]{1,0:T(8,128)S(1)}, u32[]{:S(2)}, u32[]{:S(2)}) collective-permute-start(f32[8,512]{1,0:T(8,128)} %flux_hbm.1), channel_id=1, source_target_pairs={{0,8},{4,0},{8,4},{12,12},{1,9},{5,1},{9,5},{13,13},{2,10},{6,2},{... | collective-permute-start | bytes 49160 | tf_op jit(solution)/shard_map/ppermute | solution.py:386
  16.9 3.0 %collective-permute-start.6 = (f32[8,128]{1,0:T(8,128)S(1)}, f32[8,128]{1,0:T(8,128)S(1)}, u32[]{:S(2)}, u32[]{:S(2)}) collective-permute-start(f32[8,128]{1,0:T(8,128)S(1)} %get-tuple-element.28.refs_0_), channel_id=1, source_target_pairs={{0,3},{1,2},{2,1},{3,0},{4,7},{5,6},{6,5},{7,4},{8,11},{9,10},{10,... | collective-permute-start | bytes 12296 | tf_op jit(solution)/shard_map/ppermute | solution.py:380
  16.9 3.7 %collective-permute-start.5 = (f32[8,128]{1,0:T(8,128)S(1)}, f32[8,128]{1,0:T(8,128)S(1)}, u32[]{:S(2)}, u32[]{:S(2)}) collective-permute-start(f32[8,128]{1,0:T(8,128)S(1)} %get-tuple-element.28.refs_0_), channel_id=1, source_target_pairs={{0,2},{1,3},{2,0},{3,1},{4,6},{5,7},{6,4},{7,5},{8,10},{9,11},{10,... | collective-permute-start | bytes 12296 | tf_op jit(solution)/shard_map/ppermute | solution.py:380
  18.4 2.1 %collective-permute-start.4 = (f32[8,128]{1,0:T(8,128)S(1)}, f32[8,128]{1,0:T(8,128)S(1)}, u32[]{:S(2)}, u32[]{:S(2)}) collective-permute-start(f32[8,128]{1,0:T(8,128)S(1)} %get-tuple-element.28.refs_0_), channel_id=1, source_target_pairs={{0,1},{1,0},{2,3},{3,2},{4,5},{5,4},{6,7},{7,6},{8,9},{9,8},{10,11... | collective-permute-start | bytes 12296 | tf_op jit(solution)/shard_map/ppermute | solution.py:380
  21.0 8.4 %collective-permute-start.10 = (f32[40,128]{1,0:T(8,128)S(1)}, f32[40,128]{1,0:T(8,128)S(1)}, u32[]{:S(2)}, u32[]{:S(2)}) collective-permute-start(f32[40,128]{1,0:T(8,128)S(1)} %get-tuple-element.33.refs_0_), channel_id=1, source_target_pairs={{0,4},{4,12},{12,0},{8,8},{1,5},{5,13},{13,1},{9,9},{2,6},{6,14},{... | collective-permute-start | bytes 61448 | tf_op jit(solution)/shard_map/ppermute | solution.py:386
  23.5 5.9 %collective-permute-start.9 = (f32[40,128]{1,0:T(8,128)S(1)}, f32[40,128]{1,0:T(8,128)S(1)}, u32[]{:S(2)}, u32[]{:S(2)}) collective-permute-start(f32[40,128]{1,0:T(8,128)S(1)} %get-tuple-element.33.refs_0_), channel_id=1, source_target_pairs={{0,12},{4,8},{8,0},{12,4},{1,13},{5,9},{9,1},{13,5},{2,14},{6,10},... | collective-permute-start | bytes 61448 | tf_op jit(solution)/shard_map/ppermute | solution.py:386
  26.8 5.7 %collective-permute-start.8 = (f32[40,128]{1,0:T(8,128)S(1)}, f32[40,128]{1,0:T(8,128)S(1)}, u32[]{:S(2)}, u32[]{:S(2)}) collective-permute-start(f32[40,128]{1,0:T(8,128)S(1)} %get-tuple-element.33.refs_0_), channel_id=1, source_target_pairs={{0,8},{4,0},{8,4},{12,12},{1,9},{5,1},{9,5},{13,13},{2,10},{6,2},{... | collective-permute-start | bytes 61448 | tf_op jit(solution)/shard_map/ppermute | solution.py:386
  28.7 3.8 %collective-permute-start.7 = (f32[40,128]{1,0:T(8,128)S(1)}, f32[40,128]{1,0:T(8,128)S(1)}, u32[]{:S(2)}, u32[]{:S(2)}) collective-permute-start(f32[40,128]{1,0:T(8,128)S(1)} %get-tuple-element.33.refs_0_), channel_id=1, source_target_pairs={{8,12},{12,8},{0,0},{4,4},{9,13},{13,9},{1,1},{5,5},{10,14},{14,10... | collective-permute-start | bytes 61448 | tf_op jit(solution)/shard_map/ppermute | solution.py:386
  33.5 3.0 %collective-permute-start.13 = (f32[8,128]{1,0:T(8,128)S(1)}, f32[8,128]{1,0:T(8,128)S(1)}, u32[]{:S(2)}, u32[]{:S(2)}) collective-permute-start(f32[8,128]{1,0:T(8,128)S(1)} %shard_map.89.refs_0_), channel_id=1, source_target_pairs={{0,3},{1,2},{2,1},{3,0},{4,7},{5,6},{6,5},{7,4},{8,11},{9,10},{10,... | collective-permute-start | bytes 12296 | tf_op jit(solution)/shard_map/ppermute | solution.py:380
  33.5 3.7 %collective-permute-start.12 = (f32[8,128]{1,0:T(8,128)S(1)}, f32[8,128]{1,0:T(8,128)S(1)}, u32[]{:S(2)}, u32[]{:S(2)}) collective-permute-start(f32[8,128]{1,0:T(8,128)S(1)} %shard_map.89.refs_0_), channel_id=1, source_target_pairs={{0,2},{1,3},{2,0},{3,1},{4,6},{5,7},{6,4},{7,5},{8,10},{9,11},{10,... | collective-permute-start | bytes 12296 | tf_op jit(solution)/shard_map/ppermute | solution.py:380
  35.1 2.1 %collective-permute-start.11 = (f32[8,128]{1,0:T(8,128)S(1)}, f32[8,128]{1,0:T(8,128)S(1)}, u32[]{:S(2)}, u32[]{:S(2)}) collective-permute-start(f32[8,128]{1,0:T(8,128)S(1)} %shard_map.89.refs_0_), channel_id=1, source_target_pairs={{0,1},{1,0},{2,3},{3,2},{4,5},{5,4},{6,7},{7,6},{8,9},{9,8},{10,11... | collective-permute-start | bytes 12296 | tf_op jit(solution)/shard_map/ppermute | solution.py:380
  37.6 6.8 %collective-permute-start.14 = (f32[8,128]{1,0:T(8,128)S(1)}, f32[8,128]{1,0:T(8,128)S(1)}, u32[]{:S(2)}, u32[]{:S(2)}) collective-permute-start(f32[8,128]{1,0:T(8,128)S(1)} %get-tuple-element.37), channel_id=1, source_target_pairs={{0,4},{4,8},{8,0},{12,12},{1,5},{5,9},{9,1},{13,13},{2,6},{6,10},{... | collective-permute-start | bytes 12296 | tf_op jit(solution)/shard_map/ppermute | solution.py:386
  39.5 7.3 %collective-permute-start.15 = (f32[8,128]{1,0:T(8,128)S(1)}, f32[8,128]{1,0:T(8,128)S(1)}, u32[]{:S(2)}, u32[]{:S(2)}) collective-permute-start(f32[8,128]{1,0:T(8,128)S(1)} %get-tuple-element.38), channel_id=1, source_target_pairs={{0,12},{12,0},{4,4},{8,8},{1,13},{13,1},{5,5},{9,9},{2,14},{14,2},... | collective-permute-start | bytes 12296 | tf_op jit(solution)/shard_map/ppermute | solution.py:386
  41.5 5.4 %collective-permute-start.16 = (f32[8,128]{1,0:T(8,128)S(1)}, f32[8,128]{1,0:T(8,128)S(1)}, u32[]{:S(2)}, u32[]{:S(2)}) collective-permute-start(f32[8,128]{1,0:T(8,128)S(1)} %get-tuple-element.39), channel_id=1, source_target_pairs={{0,8},{4,0},{8,12},{12,4},{1,9},{5,1},{9,13},{13,5},{2,10},{6,2},{... | collective-permute-start | bytes 12296 | tf_op jit(solution)/shard_map/ppermute | solution.py:386
  43.2 3.7 %collective-permute-start.17 = (f32[8,128]{1,0:T(8,128)S(1)}, f32[8,128]{1,0:T(8,128)S(1)}, u32[]{:S(2)}, u32[]{:S(2)}) collective-permute-start(f32[8,128]{1,0:T(8,128)S(1)} %get-tuple-element.40), channel_id=1, source_target_pairs={{4,12},{8,4},{12,8},{0,0},{5,13},{9,5},{13,9},{1,1},{6,14},{10,6},... | collective-permute-start | bytes 12296 | tf_op jit(solution)/shard_map/ppermute | solution.py:386

commit v9 on v6

--- a/solution.py
+++ b/solution.py
@@ -89,16 +89,38 @@
     return jnp.concatenate([h_ref[0, 0, o, :, start : start + size] for o in range(first, last)], axis=0)
 
 
-def forward(h_ref, pick_obs, x):
-    x = jnp.concatenate([x, x], axis=1)
+def forward(g_ref, obs_ref, x, x_scr, sums):
+    slots = x.shape[0]
+    sets = len(sums)
+    x_scr[...] = x
+    for ref in sums:
+        ref[...] = jnp.zeros(ref.shape, F32)
+
+    def add(s, ref):
+        block = obs_ref[s]
+        ref[block] = ref[block] + g_ref[s] * x_scr[pl.ds(s, 1), :]
+
+    def step(j, carry):
+        for n, ref in enumerate(sums):
+            add(n * (slots // sets) + j, ref)
+        return carry
+
+    lax.fori_loop(0, slots // sets, step, 0, unroll=min(slots // sets, 16))
+    rows = OBLK_DEV * TILES // 8
     tiles = []
-    for t in range(TILES // 2):
-        sums = pick_rows(pick_obs, h_columns(h_ref, 0, h_ref.shape[2], 2 * LANES * t, 2 * LANES) * x)
-        tiles += [sums[:OBLK_DEV, :LANES], sums[:OBLK_DEV, LANES:]]
+    for q in range(rows):
+        at = (q // 4, slice(8 * (q % 4), 8 * (q % 4) + 8))
+        tiles.append(tree_sum([ref[at] for ref in sums]))
     m = merge_tree(tiles)
     m = m + swap(m, 1)
-    even = (iota(m.shape, 1) & 1) == 0
-    return jnp.where(even == low(m.shape), m, half_swap(m))
+    lane = iota((OBLK_DEV, LANES), 1) & (OB - 1)
+    place = (lane & 1) * OB + 2 * (4 * iota(lane.shape, 0) + (lane >> 4))
+    out = jnp.zeros(m.shape, F32)
+    for u in range(8):
+        row = jnp.broadcast_to(m[u : u + 1], m.shape)
+        found = jnp.take_along_axis(row, place, axis=1, mode="promise_in_bounds")
+        out = jnp.where((lane & 15) >> 1 == u, found, out)
+    return out
 
 
 def adjoint(h_ref, slot_obs, d, store):
@@ -130,9 +152,9 @@
 
 
 def prepare(
-    fslot_hbm, oslot_hbm, count_hbm, observed_hbm, weight_hbm, flux_hbm, h_hbm,
-    pick_flux_ref, target_ref, slot_obs_ref, pick_obs_ref, index_ref, observed_out, weight_out, flux_ref, h_ref,
-    fslot_ref, oslot_ref, count_ref, observed_ref, weight_ref, sems, h_sems,
+    fslot_hbm, oslot_hbm, count_hbm, observed_hbm, weight_hbm, flux_hbm, h_hbm, g_hbm,
+    pick_flux_ref, target_ref, slot_obs_ref, index_ref, observed_out, weight_out, flux_ref, h_ref, g_ref, obs_ref,
+    fslot_ref, oslot_ref, count_ref, observed_ref, weight_ref, oslot_scalars, count_scalars, sems, h_sems, g_sems,
 ):
     me = lax.axis_index("cell")
     owners, capacity = fslot_ref.shape[2:]
@@ -143,6 +165,8 @@
         (observed_hbm, observed_ref),
         (weight_hbm, weight_ref),
         (flux_hbm, flux_ref),
+        (oslot_hbm, oslot_scalars),
+        (count_hbm, count_scalars),
     )
     small = [pltpu.make_async_copy(src, dst, sems.at[i]) for i, (src, dst) in enumerate(pairs)]
     large = [
@@ -151,8 +175,30 @@
     ]
     for copy in small + large:
         copy.start()
+
+    def turned(n, r):
+        return pltpu.make_async_copy(g_hbm.at[n, :, r], g_ref.at[8 * n + r], g_sems.at[8 * n + r])
+
+    def each_turned(action):
+        def step(n, carry):
+            for r in range(8):
+                action(turned(n, r))
+            return carry
+
+        lax.fori_loop(0, owners * capacity // 8, step, 0, unroll=owners <= 4)
+
+    each_turned(lambda copy: copy.start())
     for copy in small:
         copy.wait()
+
+    def scalar_step(o, carry):
+        for j in range(capacity):
+            obs_ref[o * capacity + j] = jnp.where(
+                j < count_scalars[0, 0, o], oslot_scalars[0, 0, o, j], OBLK_DEV
+            )
+        return carry
+
+    lax.fori_loop(0, owners, scalar_step, 0, unroll=owners <= 4)
     slots = owners * capacity
     eye = iota((capacity, capacity), 0) == iota((capacity, capacity), 1)
 
@@ -188,12 +234,6 @@
     row = (owner ^ me) * (BLOCKS // 2) + ((fslot & 7) >> 1) * WIN_DEV + (fslot >> 3)
     pick_flux_ref[...] = one_hot(iota((slots, 3 * depth), 1) % depth == row)
     slot_obs_ref[...] = one_hot((iota((slots, 3 * OBLK_DEV), 1) % OBLK_DEV) == oslot)
-
-    eye3 = iota((slots, 3 * slots), 1) % slots == iota((slots, 3 * slots), 0)
-    obs_row = jnp.sum(jnp.where(eye3, oslot, 0), axis=0, keepdims=True)
-    pick_obs_ref[...] = one_hot(iota((16, 3 * slots), 0) == obs_row) * one_hot(
-        iota((16, 3 * slots), 0) < OBLK_DEV
-    )
 
     half = slots // 2
     count = max(1, half // LANES)
@@ -211,11 +251,12 @@
     weight_out[...] = spread_obs(weight_ref[...])
     for copy in large:
         copy.wait()
+    each_turned(lambda copy: copy.wait())
 
 
 def first_model(order, *refs):
     parts = len(order)
-    h_ref, pick_flux_ref, target_ref, pick_obs_ref, m_ref, x_ref = refs[parts:]
+    g_ref, pick_flux_ref, target_ref, obs_ref, m_ref, x_ref, x_scr, *sums = refs[parts:]
     flux = jnp.concatenate(
         [
             ref[:, LANES * t : LANES * (t + 1)]
@@ -228,7 +269,7 @@
     odd = (target_ref[...].astype(jnp.int32) & 1) == 1
     x = jnp.where(odd != low(pair.shape), pair, half_swap(pair))
     x_ref[...] = x
-    m_ref[...] = forward(h_ref, pick_obs_ref[...], x)
+    m_ref[...] = forward(g_ref, obs_ref, x, x_scr, sums)
 
 
 def first_adjoint(parts, *refs):
@@ -248,7 +289,7 @@
 def second_model(parts, *refs):
     messages = refs[:parts]
     cells = parts
-    target_ref, x_ref, h_ref, pick_obs_ref, m_ref = refs[parts:]
+    target_ref, x_ref, g_ref, obs_ref, m_ref, x_scr, *sums = refs[parts:]
     slots = target_ref.shape[0]
     half = slots // 2
     count = max(1, half // LANES)
@@ -271,7 +312,8 @@
         found = pick_rows(jnp.concatenate([pick] * 3, axis=1), values)
         total = found if total is None else total + found
     change = jnp.where(low((slots, LANES)), total[:slots], total[slots:])
-    m_ref[...] = forward(h_ref, pick_obs_ref[...], x_ref[...] - 0.5 * (change + half_swap(change)))
+    x = x_ref[...] - 0.5 * (change + half_swap(change))
+    m_ref[...] = forward(g_ref, obs_ref, x, x_scr, sums)
 
 
 def second_adjoint(parts, *refs):
@@ -355,20 +397,22 @@
         slots = owners * capacity
         half = slots // 2
         index_rows = -(-2 * max(1, half // LANES) // 8) * 8
-        params = pltpu.CompilerParams(vmem_limit_bytes=4 * footprint.size * 4 + 8 * 2**20)
+        params = pltpu.CompilerParams(vmem_limit_bytes=footprint.size * 4 + 16 * 2**20)
         hbm = pl.BlockSpec(memory_space=pltpu.HBM)
+        smem = pl.BlockSpec(memory_space=pltpu.SMEM)
+        obs, obs_out = None, pltpu.SMEM((slots,), jnp.int32)
 
         def call(body, outs, ins, scratch=(), space=VMEM):
             if space is hbm:
                 ins = [pltpu.with_memory_space_constraint(value, pltpu.HBM) for value in ins]
-                outs_at = [pltpu.VMEM(s, t) for s, t in outs]
+                outs_at = [pltpu.VMEM(s, t) for s, t in outs[:-1]] + [obs_out]
             else:
                 outs_at = [jax.ShapeDtypeStruct(s, t) for s, t in outs]
             return pl.pallas_call(
                 body,
                 out_shape=outs_at,
-                in_specs=[space] * len(ins),
-                out_specs=[VMEM] * len(outs),
+                in_specs=[smem if value is obs else space for value in ins],
+                out_specs=[smem if outs_at[n] is obs_out else VMEM for n in range(len(outs))],
                 scratch_shapes=list(scratch),
                 compiler_params=params,
             )(*ins)
@@ -378,25 +422,31 @@
 
         obs_tile = ((OBLK_DEV, LANES), F32)
         slot_tile = ((slots, LANES), F32)
+        sum_scratch = [pltpu.VMEM(*slot_tile)] + [pltpu.VMEM((OBLK_DEV + 1, TILES, LANES), F32)] * 4
         small = (flux_slot, obs_slot, slot_count, observed, obs_weight)
-        pick_flux, target, slot_obs, pick_obs, index, observed_t, weight_t, flux, matrices = call(
+        turned = footprint.reshape(slots // 8, 8, TILES, LANES).transpose(0, 2, 1, 3)
+        pick_flux, target, slot_obs, index, observed_t, weight_t, flux, matrices, by_slot, obs = call(
             prepare,
             [
                 ((slots, 3 * owners * BLOCKS // 2), BF16),
                 slot_tile,
                 ((slots, 3 * OBLK_DEV), BF16),
-                ((16, 3 * slots), BF16),
                 ((index_rows, LANES), F32),
                 obs_tile,
                 obs_tile,
                 like(prior_flux),
                 like(footprint),
+                ((slots, TILES, LANES), F32),
+                ((slots,), jnp.int32),
             ],
-            (*small, prior_flux, footprint),
+            (*small, prior_flux, footprint, turned),
             [
                 *(pltpu.VMEM(*like(value)) for value in small),
-                pltpu.SemaphoreType.DMA((len(small) + 1,)),
+                pltpu.SMEM(*like(obs_slot)),
+                pltpu.SMEM(*like(slot_count)),
+                pltpu.SemaphoreType.DMA((len(small) + 3,)),
                 pltpu.SemaphoreType.DMA((owners,)),
+                pltpu.SemaphoreType.DMA((slots,)),
             ],
             hbm,
         )
@@ -405,7 +455,8 @@
         m0, x0 = call(
             functools.partial(first_model, order),
             [obs_tile, slot_tile],
-            (*(fluxes[k] for k in order), matrices, pick_flux, target, pick_obs),
+            (*(fluxes[k] for k in order), by_slot, pick_flux, target, obs),
+            sum_scratch,
         )
         message, d0 = call(
             functools.partial(first_adjoint, wins),
@@ -416,7 +467,8 @@
         (m1,) = call(
             functools.partial(second_model, cells),
             [obs_tile],
-            (*messages, target, x0, matrices, pick_obs),
+            (*messages, target, x0, by_slot, obs),
+            sum_scratch,
         )
         *blocks, d1 = call(
             functools.partial(second_adjoint, wins),

time: 35.1 us -> 34.9 us (level)
  waiting for transfers between devices: 10.2 us -> 9.26 us
  Pallas kernels: 5.74 us -> 6.48 us
    ppermute x15, waiting for transfers between devices: 10.2 us -> 9.26 us  [send(): return lax.ppermute(value, axis, [(i, i ^ k) for i in range(size)])]
    pallas_call x7, Pallas kernels: 5.74 us -> 6.48 us  [call(): pl.pallas_call(body, out_shape=outs_at, in_specs=[smem if value is obs el...]
  transfers between devices with their start and end apart: 15 -> 15, of which waited for: 10 -> 10; matrix products, arithmetic and copies ran while one was open for 0% -> 0% of each run, Pallas kernels for 6% -> 9%
where the time goes in v9:
time: 34.9 us; the launch traced here: 34.8 us
  starting transfers between devices  18.4 us (53%)
  waiting for transfers between devices  9.26 us (27%)
  Pallas kernels  6.48 us (19%)
  between operations  0.69 us (2%)
    ppermute x15, starting transfers between devices, send(): return lax.ppermute(value, axis, [(i, i ^ k) for i in range(size)])  18.4 us
    ppermute x15, waiting for transfers between devices, send(): return lax.ppermute(value, axis, [(i, i ^ k) for i in range(size)])  9.26 us
    pallas_call x7, Pallas kernels, call(): pl.pallas_call(body, out_shape=outs_at, in_specs=[smem if value is obs el...  6.48 us
  transfers between devices with their start and end apart: 15, of which 10 were waited for; matrix products, arithmetic and copies ran while one was open for 0% of the time, Pallas kernels for 9%

profile of v9, /device:TPU:0, one launch (start us, length us, event | category | flops | bytes accessed | tf_op | source)
XLA Modules:
  0.0 34.8 jit_solution(7490591014844692133)
XLA Ops:
  0.6 4.1 %collective-permute-start = (f32[8,512]{1,0:T(8,128)}, f32[8,512]{1,0:T(8,128)S(1)}, u32[]{:S(2)}, u32[]{:S(2)}) collective-permute-start(f32[8,512]{1,0:T(8,128)} %flux_hbm.1), channel_id=1, source_target_pairs={{0,8},{4,12},{8,0},{12,4},{1,9},{5,13},{9,1},{13,5},{2,10},{6,14},... | collective-permute-start | bytes 49160 | tf_op jit(solution)/shard_map/ppermute | solution.py:387
  4.7 1.3 %collective-permute-start.2 = (f32[8,512]{1,0:T(8,128)}, f32[8,512]{1,0:T(8,128)S(1)}, u32[]{:S(2)}, u32[]{:S(2)}) collective-permute-start(f32[8,512]{1,0:T(8,128)} %flux_hbm.1), channel_id=1, source_target_pairs={{0,12},{4,8},{8,4},{12,0},{1,13},{5,9},{9,5},{13,1},{2,14},{6,10},... | collective-permute-start | bytes 49160 | tf_op jit(solution)/shard_map/ppermute | solution.py:387
  6.1 0.2 collective-permute-start.1
  6.3 2.4 %shard_map.86 = (bf16[64,384]{1,0:T(8,128)(2,1)S(1)}, f32[64,128]{1,0:T(8,128)S(1)}, bf16[64,24]{1,0:T(8,128)(2,1)S(1)}, f32[8,128]{1,0:T(8,128)S(1)}, f32[8,128...) custom-call(s32[1,1,4,16]{3,2,1,0:T(4,128)} %fslot_hbm.1, ...), custom_call_target="tpu_custom_call" | custom-call | tf_op jit(solution)/shard_map/pallas_call | solution.py:411
  8.7 1.7 %collective-permute-done.2.refs_3_ = f32[8,512]{1,0:T(8,128)S(1)} collective-permute-done((f32[8,512]{1,0:T(8,128)}, f32[8,512]{1,0:T(8,128)S(1)}, u32[]{:S(2)}, u32[]{:S(2)}) %collective-permute-start.2) | collective-permute-done | bytes 16416 | tf_op jit(solution)/shard_map/ppermute | solution.py:387
  10.5 0.9 %shard_map.87 = (f32[8,128]{1,0:T(8,128)S(1)}, f32[64,128]{1,0:T(8,128)S(1)}) custom-call(f32[8,512]{1,0:T(8,128)S(1)} %get-tuple-element.23.refs_0_, f32[8,512]{1,0:T(8,128)S(1)} %collective-permute-done.refs_1_, f32[8,512]{1,0:T(8,128)S(1)} %collective-permute-done.1.refs_2_, f32[8,512]{1,0:T(8,128)S(1)} %collective-permute-done.2.refs_3_, ...), custom_call_target="tpu_custom_call" | custom-call | tf_op jit(solution)/shard_map/pallas_call | solution.py:411
  11.4 0.0 collective-permute-start.5
  11.4 1.6 %collective-permute-start.4 = (f32[8,128]{1,0:T(8,128)S(1)}, f32[8,128]{1,0:T(8,128)S(1)}, u32[]{:S(2)}, u32[]{:S(2)}) collective-permute-start(f32[8,128]{1,0:T(8,128)S(1)} %get-tuple-element.28.refs_0_), channel_id=1, source_target_pairs={{0,2},{1,3},{2,0},{3,1},{4,6},{5,7},{6,4},{7,5},{8,10},{9,11},{10,... | collective-permute-start | bytes 12296 | tf_op jit(solution)/shard_map/ppermute | solution.py:387
  13.0 0.3 collective-permute-start.3
  13.2 1.2 %collective-permute-done.5.refs_3_ = f32[8,128]{1,0:T(8,128)S(1)} collective-permute-done((f32[8,128]{1,0:T(8,128)S(1)}, f32[8,128]{1,0:T(8,128)S(1)}, u32[]{:S(2)}, u32[]{:S(2)}) %collective-permute-start.5) | collective-permute-done | bytes 4128 | tf_op jit(solution)/shard_map/ppermute | solution.py:387
  14.4 0.7 %collective-permute-done.4.refs_2_ = f32[8,128]{1,0:T(8,128)S(1)} collective-permute-done((f32[8,128]{1,0:T(8,128)S(1)}, f32[8,128]{1,0:T(8,128)S(1)}, u32[]{:S(2)}, u32[]{:S(2)}) %collective-permute-start.4) | collective-permute-done | bytes 4128 | tf_op jit(solution)/shard_map/ppermute | solution.py:387
  15.1 0.0 collective-permute-done.3.refs_1_
  15.1 0.4 %shard_map.88 = (f32[40,128]{1,0:T(8,128)S(1)}, f32[8,128]{1,0:T(8,128)S(1)}) custom-call(f32[8,128]{1,0:T(8,128)S(1)} %get-tuple-element.28.refs_0_, f32[8,128]{1,0:T(8,128)S(1)} %collective-permute-done.3.refs_1_, f32[8,128]{1,0:T(8,128)S(1)} %collective-permute-done.4.refs_2_, f32[8,128]{1,0:T(8,128)S(1)} %collective-permute-done.5.refs_3_, ...), custom_call_target="tpu_custom_call" | custom-call | tf_op jit(solution)/shard_map/pallas_call | solution.py:411
  15.5 2.1 %collective-permute-start.8 = (f32[40,128]{1,0:T(8,128)S(1)}, f32[40,128]{1,0:T(8,128)S(1)}, u32[]{:S(2)}, u32[]{:S(2)}) collective-permute-start(f32[40,128]{1,0:T(8,128)S(1)} %get-tuple-element.34.refs_0_), channel_id=1, source_target_pairs={{0,12},{4,8},{8,4},{12,0},{1,13},{5,9},{9,5},{13,1},{2,14},{6,10},... | collective-permute-start | bytes 61448 | tf_op jit(solution)/shard_map/ppermute | solution.py:387
  17.6 2.4 %collective-permute-start.6 = (f32[40,128]{1,0:T(8,128)S(1)}, f32[40,128]{1,0:T(8,128)S(1)}, u32[]{:S(2)}, u32[]{:S(2)}) collective-permute-start(f32[40,128]{1,0:T(8,128)S(1)} %get-tuple-element.34.refs_0_), channel_id=1, source_target_pairs={{0,4},{4,0},{8,12},{12,8},{1,5},{5,1},{9,13},{13,9},{2,6},{6,2},{1... | collective-permute-start | bytes 61448 | tf_op jit(solution)/shard_map/ppermute | solution.py:387
  20.0 1.2 %collective-permute-done.8.refs_3_ = f32[40,128]{1,0:T(8,128)S(1)} collective-permute-done((f32[40,128]{1,0:T(8,128)S(1)}, f32[40,128]{1,0:T(8,128)S(1)}, u32[]{:S(2)}, u32[]{:S(2)}) %collective-permute-start.8) | collective-permute-done | bytes 20512 | tf_op jit(solution)/shard_map/ppermute | solution.py:387
  21.2 1.1 %collective-permute-done.7.refs_2_ = f32[40,128]{1,0:T(8,128)S(1)} collective-permute-done((f32[40,128]{1,0:T(8,128)S(1)}, f32[40,128]{1,0:T(8,128)S(1)}, u32[]{:S(2)}, u32[]{:S(2)}) %collective-permute-start.7) | collective-permute-done | bytes 20512 | tf_op jit(solution)/shard_map/ppermute | solution.py:387
  22.3 0.9 %shard_map.89.refs_0_ = f32[8,128]{1,0:T(8,128)S(1)} custom-call(f32[40,128]{1,0:T(8,128)S(1)} %get-tuple-element.34.refs_0_, f32[40,128]{1,0:T(8,128)S(1)} %collective-permute-done.6.refs_1_, f32[40,128]{1,0:T(8,128)S(1)} %collective-permute-done.7.refs_2_, f32[40,128]{1,0:T(8,128)S(1)} %collective-permute-done.8.refs_3_, ...), custom_call_target="tpu_custom_call" | custom-call | tf_op jit(solution)/shard_map/pallas_call | solution.py:411
  23.2 0.0 collective-permute-start.11
  23.2 1.5 %collective-permute-start.10 = (f32[8,128]{1,0:T(8,128)S(1)}, f32[8,128]{1,0:T(8,128)S(1)}, u32[]{:S(2)}, u32[]{:S(2)}) collective-permute-start(f32[8,128]{1,0:T(8,128)S(1)} %shard_map.89.refs_0_), channel_id=1, source_target_pairs={{0,2},{1,3},{2,0},{3,1},{4,6},{5,7},{6,4},{7,5},{8,10},{9,11},{10,... | collective-permute-start | bytes 12296 | tf_op jit(solution)/shard_map/ppermute | solution.py:387
  24.8 0.3 collective-permute-start.9
  25.1 1.2 %collective-permute-done.11.refs_3_ = f32[8,128]{1,0:T(8,128)S(1)} collective-permute-done((f32[8,128]{1,0:T(8,128)S(1)}, f32[8,128]{1,0:T(8,128)S(1)}, u32[]{:S(2)}, u32[]{:S(2)}) %collective-permute-start.11) | collective-permute-done | bytes 4128 | tf_op jit(solution)/shard_map/ppermute | solution.py:387
  26.3 0.6 %collective-permute-done.10.refs_2_ = f32[8,128]{1,0:T(8,128)S(1)} collective-permute-done((f32[8,128]{1,0:T(8,128)S(1)}, f32[8,128]{1,0:T(8,128)S(1)}, u32[]{:S(2)}, u32[]{:S(2)}) %collective-permute-start.10) | collective-permute-done | bytes 4128 | tf_op jit(solution)/shard_map/ppermute | solution.py:387
  26.9 0.4 %shard_map.90 = (f32[8,128]{1,0:T(8,128)S(1)}, f32[8,128]{1,0:T(8,128)S(1)}, f32[8,128]{1,0:T(8,128)S(1)}, f32[8,128]{1,0:T(8,128)S(1)}, f32[8,128]{1,0:T(8,128)S(1)}) custom-call(f32[8,128]{1,0:T(8,128)S(1)} %shard_map.89.refs_0_, f32[8,128]{1,0:T(8,128)S(1)} %collective-permute-done.9.refs_1_, f32[8,128]{1,0:T(8,128)S(1)} %collective-permute-done.10.refs_2_, ...), custom_call_target="tpu_custom_call" | custom-call | tf_op jit(solution)/shard_map/pallas_call | solution.py:411
  27.4 1.9 %collective-permute-start.12 = (f32[8,128]{1,0:T(8,128)S(1)}, f32[8,128]{1,0:T(8,128)S(1)}, u32[]{:S(2)}, u32[]{:S(2)}) collective-permute-start(f32[8,128]{1,0:T(8,128)S(1)} %get-tuple-element.37), channel_id=1, source_target_pairs={{0,12},{4,8},{8,4},{12,0},{1,13},{5,9},{9,5},{13,1},{2,14},{6,10},... | collective-permute-start | bytes 12296 | tf_op jit(solution)/shard_map/ppermute | solution.py:387
  29.2 1.1 %collective-permute-start.13 = (f32[8,128]{1,0:T(8,128)S(1)}, f32[8,128]{1,0:T(8,128)S(1)}, u32[]{:S(2)}, u32[]{:S(2)}) collective-permute-start(f32[8,128]{1,0:T(8,128)S(1)} %get-tuple-element.38), channel_id=1, source_target_pairs={{0,8},{4,12},{8,0},{12,4},{1,9},{5,13},{9,1},{13,5},{2,10},{6,14},... | collective-permute-start | bytes 12296 | tf_op jit(solution)/shard_map/ppermute | solution.py:387
  30.4 1.5 %collective-permute-start.14 = (f32[8,128]{1,0:T(8,128)S(1)}, f32[8,128]{1,0:T(8,128)S(1)}, u32[]{:S(2)}, u32[]{:S(2)}) collective-permute-start(f32[8,128]{1,0:T(8,128)S(1)} %get-tuple-element.39), channel_id=1, source_target_pairs={{0,4},{4,0},{8,12},{12,8},{1,5},{5,1},{9,13},{13,9},{2,6},{6,2},{1... | collective-permute-start | bytes 12296 | tf_op jit(solution)/shard_map/ppermute | solution.py:387
  31.8 0.6 %shard_map.91 = (bf16[128,128]{1,0:T(8,128)(2,1)S(1)}, f32[1,512]{1,0:T(1,128)}) custom-call(f32[40,128]{1,0:T(8,128)S(1)} %get-tuple-element.34.refs_0_, f32[40,128]{1,0:T(8,128)S(1)} %collective-permute-done.6.refs_1_, f32[40,128]{1,0:T(8,128)S(1)} %collective-permute-done.7.refs_2_, f32[40,128]{1,0:T(8,128)S(1)} %collective-permute-done.8.refs_3_, ...), custom_call_target="tpu_custom_call" | custom-call | tf_op jit(solution)/shard_map/pallas_call | solution.py:411
  32.4 0.4 %collective-permute-done.12.refs_0_ = f32[8,128]{1,0:T(8,128)S(1)} collective-permute-done((f32[8,128]{1,0:T(8,128)S(1)}, f32[8,128]{1,0:T(8,128)S(1)}, u32[]{:S(2)}, u32[]{:S(2)}) %collective-permute-start.12) | collective-permute-done | bytes 4128 | tf_op jit(solution)/shard_map/ppermute | solution.py:387
  32.8 0.9 %collective-permute-done.13.refs_1_ = f32[8,128]{1,0:T(8,128)S(1)} collective-permute-done((f32[8,128]{1,0:T(8,128)S(1)}, f32[8,128]{1,0:T(8,128)S(1)}, u32[]{:S(2)}, u32[]{:S(2)}) %collective-permute-start.13) | collective-permute-done | bytes 4128 | tf_op jit(solution)/shard_map/ppermute | solution.py:387
  33.7 0.2 collective-permute-done.14.refs_2_
  34.0 0.8 %shard_map.92 = f32[8,512]{1,0:T(8,128)} custom-call(f32[8,128]{1,0:T(8,128)S(1)} %collective-permute-done.12.refs_0_, f32[8,128]{1,0:T(8,128)S(1)} %collective-permute-done.13.refs_1_, f32[8,128]{1,0:T(8,128)S(1)} %collective-permute-done.14.refs_2_, f32[8,128]{1,0:T(8,128)S(1)} %get-tuple-element.40.refs_3_, bf16[128,128]{1,0:T(8,128)(2,1)S(1)} %get-tuple-element.42.refs_4_), custom_call_target="tpu_custom_call" | custom-call | tf_op jit(solution)/shard_map/pallas_call | solution.py:411
  (5 shorter events, 0.0 us)
Async XLA Ops:
  0.6 8.1 %collective-permute-start = (f32[8,512]{1,0:T(8,128)}, f32[8,512]{1,0:T(8,128)S(1)}, u32[]{:S(2)}, u32[]{:S(2)}) collective-permute-start(f32[8,512]{1,0:T(8,128)} %flux_hbm.1), channel_id=1, source_target_pairs={{0,8},{4,12},{8,0},{12,4},{1,9},{5,13},{9,1},{13,5},{2,10},{6,14},... | collective-permute-start | bytes 49160 | tf_op jit(solution)/shard_map/ppermute | solution.py:387
  4.7 5.7 %collective-permute-start.2 = (f32[8,512]{1,0:T(8,128)}, f32[8,512]{1,0:T(8,128)S(1)}, u32[]{:S(2)}, u32[]{:S(2)}) collective-permute-start(f32[8,512]{1,0:T(8,128)} %flux_hbm.1), channel_id=1, source_target_pairs={{0,12},{4,8},{8,4},{12,0},{1,13},{5,9},{9,5},{13,1},{2,14},{6,10},... | collective-permute-start | bytes 49160 | tf_op jit(solution)/shard_map/ppermute | solution.py:387
  6.1 4.4 %collective-permute-start.1 = (f32[8,512]{1,0:T(8,128)}, f32[8,512]{1,0:T(8,128)S(1)}, u32[]{:S(2)}, u32[]{:S(2)}) collective-permute-start(f32[8,512]{1,0:T(8,128)} %flux_hbm.1), channel_id=1, source_target_pairs={{0,4},{4,0},{8,12},{12,8},{1,5},{5,1},{9,13},{13,9},{2,6},{6,2},{1... | collective-permute-start | bytes 49160 | tf_op jit(solution)/shard_map/ppermute | solution.py:387
  11.4 3.1 %collective-permute-start.5 = (f32[8,128]{1,0:T(8,128)S(1)}, f32[8,128]{1,0:T(8,128)S(1)}, u32[]{:S(2)}, u32[]{:S(2)}) collective-permute-start(f32[8,128]{1,0:T(8,128)S(1)} %get-tuple-element.28.refs_0_), channel_id=1, source_target_pairs={{0,3},{1,2},{2,1},{3,0},{4,7},{5,6},{6,5},{7,4},{8,11},{9,10},{10,... | collective-permute-start | bytes 12296 | tf_op jit(solution)/shard_map/ppermute | solution.py:387
  11.4 3.7 %collective-permute-start.4 = (f32[8,128]{1,0:T(8,128)S(1)}, f32[8,128]{1,0:T(8,128)S(1)}, u32[]{:S(2)}, u32[]{:S(2)}) collective-permute-start(f32[8,128]{1,0:T(8,128)S(1)} %get-tuple-element.28.refs_0_), channel_id=1, source_target_pairs={{0,2},{1,3},{2,0},{3,1},{4,6},{5,7},{6,4},{7,5},{8,10},{9,11},{10,... | collective-permute-start | bytes 12296 | tf_op jit(solution)/shard_map/ppermute | solution.py:387
  13.0 2.1 %collective-permute-start.3 = (f32[8,128]{1,0:T(8,128)S(1)}, f32[8,128]{1,0:T(8,128)S(1)}, u32[]{:S(2)}, u32[]{:S(2)}) collective-permute-start(f32[8,128]{1,0:T(8,128)S(1)} %get-tuple-element.28.refs_0_), channel_id=1, source_target_pairs={{0,1},{1,0},{2,3},{3,2},{4,5},{5,4},{6,7},{7,6},{8,9},{9,8},{10,11... | collective-permute-start | bytes 12296 | tf_op jit(solution)/shard_map/ppermute | solution.py:387
  15.5 5.7 %collective-permute-start.8 = (f32[40,128]{1,0:T(8,128)S(1)}, f32[40,128]{1,0:T(8,128)S(1)}, u32[]{:S(2)}, u32[]{:S(2)}) collective-permute-start(f32[40,128]{1,0:T(8,128)S(1)} %get-tuple-element.34.refs_0_), channel_id=1, source_target_pairs={{0,12},{4,8},{8,4},{12,0},{1,13},{5,9},{9,5},{13,1},{2,14},{6,10},... | collective-permute-start | bytes 61448 | tf_op jit(solution)/shard_map/ppermute | solution.py:387
  17.6 4.7 %collective-permute-start.7 = (f32[40,128]{1,0:T(8,128)S(1)}, f32[40,128]{1,0:T(8,128)S(1)}, u32[]{:S(2)}, u32[]{:S(2)}) collective-permute-start(f32[40,128]{1,0:T(8,128)S(1)} %get-tuple-element.34.refs_0_), channel_id=1, source_target_pairs={{0,8},{4,12},{8,0},{12,4},{1,9},{5,13},{9,1},{13,5},{2,10},{6,14},... | collective-permute-start | bytes 61448 | tf_op jit(solution)/shard_map/ppermute | solution.py:387
  17.6 4.7 %collective-permute-start.6 = (f32[40,128]{1,0:T(8,128)S(1)}, f32[40,128]{1,0:T(8,128)S(1)}, u32[]{:S(2)}, u32[]{:S(2)}) collective-permute-start(f32[40,128]{1,0:T(8,128)S(1)} %get-tuple-element.34.refs_0_), channel_id=1, source_target_pairs={{0,4},{4,0},{8,12},{12,8},{1,5},{5,1},{9,13},{13,9},{2,6},{6,2},{1... | collective-permute-start | bytes 61448 | tf_op jit(solution)/shard_map/ppermute | solution.py:387
  23.2 3.1 %collective-permute-start.11 = (f32[8,128]{1,0:T(8,128)S(1)}, f32[8,128]{1,0:T(8,128)S(1)}, u32[]{:S(2)}, u32[]{:S(2)}) collective-permute-start(f32[8,128]{1,0:T(8,128)S(1)} %shard_map.89.refs_0_), channel_id=1, source_target_pairs={{0,3},{1,2},{2,1},{3,0},{4,7},{5,6},{6,5},{7,4},{8,11},{9,10},{10,... | collective-permute-start | bytes 12296 | tf_op jit(solution)/shard_map/ppermute | solution.py:387
  23.2 3.7 %collective-permute-start.10 = (f32[8,128]{1,0:T(8,128)S(1)}, f32[8,128]{1,0:T(8,128)S(1)}, u32[]{:S(2)}, u32[]{:S(2)}) collective-permute-start(f32[8,128]{1,0:T(8,128)S(1)} %shard_map.89.refs_0_), channel_id=1, source_target_pairs={{0,2},{1,3},{2,0},{3,1},{4,6},{5,7},{6,4},{7,5},{8,10},{9,11},{10,... | collective-permute-start | bytes 12296 | tf_op jit(solution)/shard_map/ppermute | solution.py:387
  24.8 2.1 %collective-permute-start.9 = (f32[8,128]{1,0:T(8,128)S(1)}, f32[8,128]{1,0:T(8,128)S(1)}, u32[]{:S(2)}, u32[]{:S(2)}) collective-permute-start(f32[8,128]{1,0:T(8,128)S(1)} %shard_map.89.refs_0_), channel_id=1, source_target_pairs={{0,1},{1,0},{2,3},{3,2},{4,5},{5,4},{6,7},{7,6},{8,9},{9,8},{10,11... | collective-permute-start | bytes 12296 | tf_op jit(solution)/shard_map/ppermute | solution.py:387
  27.4 5.5 %collective-permute-start.12 = (f32[8,128]{1,0:T(8,128)S(1)}, f32[8,128]{1,0:T(8,128)S(1)}, u32[]{:S(2)}, u32[]{:S(2)}) collective-permute-start(f32[8,128]{1,0:T(8,128)S(1)} %get-tuple-element.37), channel_id=1, source_target_pairs={{0,12},{4,8},{8,4},{12,0},{1,13},{5,9},{9,5},{13,1},{2,14},{6,10},... | collective-permute-start | bytes 12296 | tf_op jit(solution)/shard_map/ppermute | solution.py:387
  29.2 4.5 %collective-permute-start.13 = (f32[8,128]{1,0:T(8,128)S(1)}, f32[8,128]{1,0:T(8,128)S(1)}, u32[]{:S(2)}, u32[]{:S(2)}) collective-permute-start(f32[8,128]{1,0:T(8,128)S(1)} %get-tuple-element.38), channel_id=1, source_target_pairs={{0,8},{4,12},{8,0},{12,4},{1,9},{5,13},{9,1},{13,5},{2,10},{6,14},... | collective-permute-start | bytes 12296 | tf_op jit(solution)/shard_map/ppermute | solution.py:387
  30.4 3.6 %collective-permute-start.14 = (f32[8,128]{1,0:T(8,128)S(1)}, f32[8,128]{1,0:T(8,128)S(1)}, u32[]{:S(2)}, u32[]{:S(2)}) collective-permute-start(f32[8,128]{1,0:T(8,128)S(1)} %get-tuple-element.39), channel_id=1, source_target_pairs={{0,4},{4,0},{8,12},{12,8},{1,5},{5,1},{9,13},{13,9},{2,6},{6,2},{1... | collective-permute-start | bytes 12296 | tf_op jit(solution)/shard_map/ppermute | solution.py:387

commit v10 on v9

--- a/solution.py
+++ b/solution.py
@@ -61,16 +61,24 @@
     return parts[0]
 
 
-def spread_obs(row):
-    out = jnp.zeros((OBLK_DEV, LANES), F32)
-    block = iota((OBLK_DEV, LANES), 0)
-    lower = low((OBLK_DEV, LANES))
+def pack_obs(row):
+    lane = iota((8, LANES), 1)
+    block = (lane >> 1) & 31
+    place = 16 * (block & 7) + 2 * iota(lane.shape, 0) + (lane >> 6)
+    out = jnp.zeros(lane.shape, F32)
     for t in range(OBLK_DEV // 2):
-        tile = jnp.broadcast_to(row[:, LANES * t : LANES * (t + 1)], (OBLK_DEV, LANES))
-        turned = half_swap(tile)
-        out = jnp.where(block == 2 * t, jnp.where(lower, tile, turned), out)
-        out = jnp.where(block == 2 * t + 1, jnp.where(lower, turned, tile), out)
+        tile = jnp.broadcast_to(row[:, LANES * t : LANES * (t + 1)], lane.shape)
+        found = jnp.take_along_axis(tile, place, axis=1, mode="promise_in_bounds")
+        out = jnp.where(block >> 3 == t, found, out)
     return out
+
+
+def unpack_obs(packed, t):
+    lane = iota(packed.shape, 1)
+    place = (lane & 1) * OB + 2 * (8 * t + (lane >> 4))
+    found = jnp.take_along_axis(packed, place, axis=1, mode="promise_in_bounds")
+    here = (lane & 15) >> 1 == iota(packed.shape, 0)
+    return jnp.sum(jnp.where(here, found, 0.0), axis=0, keepdims=True)
 
 
 def merge_tree(tiles):
@@ -112,23 +120,20 @@
         at = (q // 4, slice(8 * (q % 4), 8 * (q % 4) + 8))
         tiles.append(tree_sum([ref[at] for ref in sums]))
     m = merge_tree(tiles)
-    m = m + swap(m, 1)
-    lane = iota((OBLK_DEV, LANES), 1) & (OB - 1)
-    place = (lane & 1) * OB + 2 * (4 * iota(lane.shape, 0) + (lane >> 4))
-    out = jnp.zeros(m.shape, F32)
-    for u in range(8):
-        row = jnp.broadcast_to(m[u : u + 1], m.shape)
-        found = jnp.take_along_axis(row, place, axis=1, mode="promise_in_bounds")
-        out = jnp.where((lane & 15) >> 1 == u, found, out)
-    return out
+    return m + swap(m, 1)
 
 
 def adjoint(h_ref, slot_obs, d, store):
     owners, capacity = h_ref.shape[2], h_ref.shape[3]
-    upper = jnp.where(low(d.shape), 0, 1)
+    place = (iota(d.shape, 1) & OB) + 8 * iota(d.shape, 0)
     spread = jnp.concatenate(
         [
-            jnp.take_along_axis(d, upper + 2 * t, axis=1, mode="promise_in_bounds")
+            jnp.take_along_axis(
+                jnp.broadcast_to(d[t % 8 : t % 8 + 1], d.shape),
+                place + 2 * (t // 8),
+                axis=1,
+                mode="promise_in_bounds",
+            )
             for t in range(TILES)
         ],
         axis=1,
@@ -247,8 +252,8 @@
                 axis=0,
                 keepdims=True,
             )
-    observed_out[...] = spread_obs(observed_ref[...])
-    weight_out[...] = spread_obs(weight_ref[...])
+    observed_out[...] = pack_obs(observed_ref[...])
+    weight_out[...] = pack_obs(weight_ref[...])
     for copy in large:
         copy.wait()
     each_turned(lambda copy: copy.wait())
@@ -359,9 +364,7 @@
                 index = jnp.where((lane // rows) % cells == k - first // rows, chosen, index)
             pick_ref[BLOCKS * part : BLOCKS * (part + 1), first : first + LANES] = one_hot(block == index)
     for t in range(OBLK_DEV // 2):
-        departure_ref[:, LANES * t : LANES * (t + 1)] = jnp.where(
-            low((1, LANES)), d_ref[2 * t : 2 * t + 1, :], d_ref[2 * t + 1 : 2 * t + 2, :]
-        )
+        departure_ref[:, LANES * t : LANES * (t + 1)] = unpack_obs(d_ref[...], t)
 
 
 def gather_increment(*refs):

time: 34.9 us -> 34.6 us (level)
  no operation moved by 1% of the time
where the time goes in v10:
time: 34.6 us; the launch traced here: 34.5 us
  starting transfers between devices  18.3 us (53%)
  waiting for transfers between devices  9.1 us (26%)
  Pallas kernels  6.39 us (18%)
  between operations  0.67 us (2%)
    ppermute x15, starting transfers between devices, send(): return lax.ppermute(value, axis, [(i, i ^ k) for i in range(size)])  18.3 us
    ppermute x15, waiting for transfers between devices, send(): return lax.ppermute(value, axis, [(i, i ^ k) for i in range(size)])  9.1 us
    pallas_call x7, Pallas kernels, call(): pl.pallas_call(body, out_shape=outs_at, in_specs=[smem if value is obs el...  6.39 us
  transfers between devices with their start and end apart: 15, of which 10 were waited for; matrix products, arithmetic and copies ran while one was open for 0% of the time, Pallas kernels for 9%

profile of v10, /device:TPU:0, one launch (start us, length us, event | category | flops | bytes accessed | tf_op | source)
XLA Modules:
  0.0 34.5 jit_solution(10970464514725016566)
XLA Ops:
  0.6 4.1 %collective-permute-start = (f32[8,512]{1,0:T(8,128)}, f32[8,512]{1,0:T(8,128)S(1)}, u32[]{:S(2)}, u32[]{:S(2)}) collective-permute-start(f32[8,512]{1,0:T(8,128)} %flux_hbm.1), channel_id=1, source_target_pairs={{0,8},{4,12},{8,0},{12,4},{1,9},{5,13},{9,1},{13,5},{2,10},{6,14},... | collective-permute-start | bytes 49160 | tf_op jit(solution)/shard_map/ppermute | solution.py:390
  4.7 1.3 %collective-permute-start.2 = (f32[8,512]{1,0:T(8,128)}, f32[8,512]{1,0:T(8,128)S(1)}, u32[]{:S(2)}, u32[]{:S(2)}) collective-permute-start(f32[8,512]{1,0:T(8,128)} %flux_hbm.1), channel_id=1, source_target_pairs={{0,12},{4,8},{8,4},{12,0},{1,13},{5,9},{9,5},{13,1},{2,14},{6,10},... | collective-permute-start | bytes 49160 | tf_op jit(solution)/shard_map/ppermute | solution.py:390
  6.1 0.2 collective-permute-start.1
  6.3 2.4 %shard_map.86 = (bf16[64,384]{1,0:T(8,128)(2,1)S(1)}, f32[64,128]{1,0:T(8,128)S(1)}, bf16[64,24]{1,0:T(8,128)(2,1)S(1)}, f32[8,128]{1,0:T(8,128)S(1)}, f32[8,128...) custom-call(s32[1,1,4,16]{3,2,1,0:T(4,128)} %fslot_hbm.1, ...), custom_call_target="tpu_custom_call" | custom-call | tf_op jit(solution)/shard_map/pallas_call | solution.py:414
  8.7 1.7 %collective-permute-done.2.refs_3_ = f32[8,512]{1,0:T(8,128)S(1)} collective-permute-done((f32[8,512]{1,0:T(8,128)}, f32[8,512]{1,0:T(8,128)S(1)}, u32[]{:S(2)}, u32[]{:S(2)}) %collective-permute-start.2) | collective-permute-done | bytes 16416 | tf_op jit(solution)/shard_map/ppermute | solution.py:390
  10.5 0.8 %shard_map.87 = (f32[8,128]{1,0:T(8,128)S(1)}, f32[64,128]{1,0:T(8,128)S(1)}) custom-call(f32[8,512]{1,0:T(8,128)S(1)} %get-tuple-element.23.refs_0_, f32[8,512]{1,0:T(8,128)S(1)} %collective-permute-done.refs_1_, f32[8,512]{1,0:T(8,128)S(1)} %collective-permute-done.1.refs_2_, f32[8,512]{1,0:T(8,128)S(1)} %collective-permute-done.2.refs_3_, ...), custom_call_target="tpu_custom_call" | custom-call | tf_op jit(solution)/shard_map/pallas_call | solution.py:414
  11.3 1.5 %collective-permute-start.4 = (f32[8,128]{1,0:T(8,128)S(1)}, f32[8,128]{1,0:T(8,128)S(1)}, u32[]{:S(2)}, u32[]{:S(2)}) collective-permute-start(f32[8,128]{1,0:T(8,128)S(1)} %get-tuple-element.28.refs_0_), channel_id=1, source_target_pairs={{0,2},{1,3},{2,0},{3,1},{4,6},{5,7},{6,4},{7,5},{8,10},{9,11},{10,... | collective-permute-start | bytes 12296 | tf_op jit(solution)/shard_map/ppermute | solution.py:390
  12.8 0.3 collective-permute-start.3
  13.2 1.2 %collective-permute-done.5.refs_3_ = f32[8,128]{1,0:T(8,128)S(1)} collective-permute-done((f32[8,128]{1,0:T(8,128)S(1)}, f32[8,128]{1,0:T(8,128)S(1)}, u32[]{:S(2)}, u32[]{:S(2)}) %collective-permute-start.5) | collective-permute-done | bytes 4128 | tf_op jit(solution)/shard_map/ppermute | solution.py:390
  14.3 0.6 %collective-permute-done.4.refs_2_ = f32[8,128]{1,0:T(8,128)S(1)} collective-permute-done((f32[8,128]{1,0:T(8,128)S(1)}, f32[8,128]{1,0:T(8,128)S(1)}, u32[]{:S(2)}, u32[]{:S(2)}) %collective-permute-start.4) | collective-permute-done | bytes 4128 | tf_op jit(solution)/shard_map/ppermute | solution.py:390
  14.9 0.4 %shard_map.88 = (f32[40,128]{1,0:T(8,128)S(1)}, f32[8,128]{1,0:T(8,128)S(1)}) custom-call(f32[8,128]{1,0:T(8,128)S(1)} %get-tuple-element.28.refs_0_, f32[8,128]{1,0:T(8,128)S(1)} %collective-permute-done.3.refs_1_, f32[8,128]{1,0:T(8,128)S(1)} %collective-permute-done.4.refs_2_, f32[8,128]{1,0:T(8,128)S(1)} %collective-permute-done.5.refs_3_, ...), custom_call_target="tpu_custom_call" | custom-call | tf_op jit(solution)/shard_map/pallas_call | solution.py:414
  15.4 2.1 %collective-permute-start.8 = (f32[40,128]{1,0:T(8,128)S(1)}, f32[40,128]{1,0:T(8,128)S(1)}, u32[]{:S(2)}, u32[]{:S(2)}) collective-permute-start(f32[40,128]{1,0:T(8,128)S(1)} %get-tuple-element.34.refs_0_), channel_id=1, source_target_pairs={{0,12},{4,8},{8,4},{12,0},{1,13},{5,9},{9,5},{13,1},{2,14},{6,10},... | collective-permute-start | bytes 61448 | tf_op jit(solution)/shard_map/ppermute | solution.py:390
  17.5 2.4 %collective-permute-start.6 = (f32[40,128]{1,0:T(8,128)S(1)}, f32[40,128]{1,0:T(8,128)S(1)}, u32[]{:S(2)}, u32[]{:S(2)}) collective-permute-start(f32[40,128]{1,0:T(8,128)S(1)} %get-tuple-element.34.refs_0_), channel_id=1, source_target_pairs={{0,4},{4,0},{8,12},{12,8},{1,5},{5,1},{9,13},{13,9},{2,6},{6,2},{1... | collective-permute-start | bytes 61448 | tf_op jit(solution)/shard_map/ppermute | solution.py:390
  19.8 1.2 %collective-permute-done.8.refs_3_ = f32[40,128]{1,0:T(8,128)S(1)} collective-permute-done((f32[40,128]{1,0:T(8,128)S(1)}, f32[40,128]{1,0:T(8,128)S(1)}, u32[]{:S(2)}, u32[]{:S(2)}) %collective-permute-start.8) | collective-permute-done | bytes 20512 | tf_op jit(solution)/shard_map/ppermute | solution.py:390
  21.0 1.1 %collective-permute-done.7.refs_2_ = f32[40,128]{1,0:T(8,128)S(1)} collective-permute-done((f32[40,128]{1,0:T(8,128)S(1)}, f32[40,128]{1,0:T(8,128)S(1)}, u32[]{:S(2)}, u32[]{:S(2)}) %collective-permute-start.7) | collective-permute-done | bytes 20512 | tf_op jit(solution)/shard_map/ppermute | solution.py:390
  22.1 0.0 collective-permute-done.6.refs_1_
  22.2 0.8 %shard_map.89.refs_0_ = f32[8,128]{1,0:T(8,128)S(1)} custom-call(f32[40,128]{1,0:T(8,128)S(1)} %get-tuple-element.34.refs_0_, f32[40,128]{1,0:T(8,128)S(1)} %collective-permute-done.6.refs_1_, f32[40,128]{1,0:T(8,128)S(1)} %collective-permute-done.7.refs_2_, f32[40,128]{1,0:T(8,128)S(1)} %collective-permute-done.8.refs_3_, ...), custom_call_target="tpu_custom_call" | custom-call | tf_op jit(solution)/shard_map/pallas_call | solution.py:414
  23.0 0.0 collective-permute-start.11
  23.0 1.5 %collective-permute-start.10 = (f32[8,128]{1,0:T(8,128)S(1)}, f32[8,128]{1,0:T(8,128)S(1)}, u32[]{:S(2)}, u32[]{:S(2)}) collective-permute-start(f32[8,128]{1,0:T(8,128)S(1)} %shard_map.89.refs_0_), channel_id=1, source_target_pairs={{0,2},{1,3},{2,0},{3,1},{4,6},{5,7},{6,4},{7,5},{8,10},{9,11},{10,... | collective-permute-start | bytes 12296 | tf_op jit(solution)/shard_map/ppermute | solution.py:390
  24.5 0.3 collective-permute-start.9
  24.9 1.2 %collective-permute-done.11.refs_3_ = f32[8,128]{1,0:T(8,128)S(1)} collective-permute-done((f32[8,128]{1,0:T(8,128)S(1)}, f32[8,128]{1,0:T(8,128)S(1)}, u32[]{:S(2)}, u32[]{:S(2)}) %collective-permute-start.11) | collective-permute-done | bytes 4128 | tf_op jit(solution)/shard_map/ppermute | solution.py:390
  26.0 0.6 %collective-permute-done.10.refs_2_ = f32[8,128]{1,0:T(8,128)S(1)} collective-permute-done((f32[8,128]{1,0:T(8,128)S(1)}, f32[8,128]{1,0:T(8,128)S(1)}, u32[]{:S(2)}, u32[]{:S(2)}) %collective-permute-start.10) | collective-permute-done | bytes 4128 | tf_op jit(solution)/shard_map/ppermute | solution.py:390
  26.6 0.0 collective-permute-done.9.refs_1_
  26.6 0.4 %shard_map.90 = (f32[8,128]{1,0:T(8,128)S(1)}, f32[8,128]{1,0:T(8,128)S(1)}, f32[8,128]{1,0:T(8,128)S(1)}, f32[8,128]{1,0:T(8,128)S(1)}, f32[8,128]{1,0:T(8,128)S(1)}) custom-call(f32[8,128]{1,0:T(8,128)S(1)} %shard_map.89.refs_0_, f32[8,128]{1,0:T(8,128)S(1)} %collective-permute-done.9.refs_1_, f32[8,128]{1,0:T(8,128)S(1)} %collective-permute-done.10.refs_2_, ...), custom_call_target="tpu_custom_call" | custom-call | tf_op jit(solution)/shard_map/pallas_call | solution.py:414
  27.1 1.9 %collective-permute-start.12 = (f32[8,128]{1,0:T(8,128)S(1)}, f32[8,128]{1,0:T(8,128)S(1)}, u32[]{:S(2)}, u32[]{:S(2)}) collective-permute-start(f32[8,128]{1,0:T(8,128)S(1)} %get-tuple-element.37), channel_id=1, source_target_pairs={{0,12},{4,8},{8,4},{12,0},{1,13},{5,9},{9,5},{13,1},{2,14},{6,10},... | collective-permute-start | bytes 12296 | tf_op jit(solution)/shard_map/ppermute | solution.py:390
  28.9 1.1 %collective-permute-start.13 = (f32[8,128]{1,0:T(8,128)S(1)}, f32[8,128]{1,0:T(8,128)S(1)}, u32[]{:S(2)}, u32[]{:S(2)}) collective-permute-start(f32[8,128]{1,0:T(8,128)S(1)} %get-tuple-element.38), channel_id=1, source_target_pairs={{0,8},{4,12},{8,0},{12,4},{1,9},{5,13},{9,1},{13,5},{2,10},{6,14},... | collective-permute-start | bytes 12296 | tf_op jit(solution)/shard_map/ppermute | solution.py:390
  30.1 1.5 %collective-permute-start.14 = (f32[8,128]{1,0:T(8,128)S(1)}, f32[8,128]{1,0:T(8,128)S(1)}, u32[]{:S(2)}, u32[]{:S(2)}) collective-permute-start(f32[8,128]{1,0:T(8,128)S(1)} %get-tuple-element.39), channel_id=1, source_target_pairs={{0,4},{4,0},{8,12},{12,8},{1,5},{5,1},{9,13},{13,9},{2,6},{6,2},{1... | collective-permute-start | bytes 12296 | tf_op jit(solution)/shard_map/ppermute | solution.py:390
  31.5 0.7 %shard_map.91 = (bf16[128,128]{1,0:T(8,128)(2,1)S(1)}, f32[1,512]{1,0:T(1,128)}) custom-call(f32[40,128]{1,0:T(8,128)S(1)} %get-tuple-element.34.refs_0_, f32[40,128]{1,0:T(8,128)S(1)} %collective-permute-done.6.refs_1_, f32[40,128]{1,0:T(8,128)S(1)} %collective-permute-done.7.refs_2_, f32[40,128]{1,0:T(8,128)S(1)} %collective-permute-done.8.refs_3_, ...), custom_call_target="tpu_custom_call" | custom-call | tf_op jit(solution)/shard_map/pallas_call | solution.py:414
  32.2 0.3 %collective-permute-done.12.refs_0_ = f32[8,128]{1,0:T(8,128)S(1)} collective-permute-done((f32[8,128]{1,0:T(8,128)S(1)}, f32[8,128]{1,0:T(8,128)S(1)}, u32[]{:S(2)}, u32[]{:S(2)}) %collective-permute-start.12) | collective-permute-done | bytes 4128 | tf_op jit(solution)/shard_map/ppermute | solution.py:390
  32.6 0.9 %collective-permute-done.13.refs_1_ = f32[8,128]{1,0:T(8,128)S(1)} collective-permute-done((f32[8,128]{1,0:T(8,128)S(1)}, f32[8,128]{1,0:T(8,128)S(1)}, u32[]{:S(2)}, u32[]{:S(2)}) %collective-permute-start.13) | collective-permute-done | bytes 4128 | tf_op jit(solution)/shard_map/ppermute | solution.py:390
  33.5 0.2 collective-permute-done.14.refs_2_
  33.7 0.8 %shard_map.92 = f32[8,512]{1,0:T(8,128)} custom-call(f32[8,128]{1,0:T(8,128)S(1)} %collective-permute-done.12.refs_0_, f32[8,128]{1,0:T(8,128)S(1)} %collective-permute-done.13.refs_1_, f32[8,128]{1,0:T(8,128)S(1)} %collective-permute-done.14.refs_2_, f32[8,128]{1,0:T(8,128)S(1)} %get-tuple-element.40.refs_3_, bf16[128,128]{1,0:T(8,128)(2,1)S(1)} %get-tuple-element.42.refs_4_), custom_call_target="tpu_custom_call" | custom-call | tf_op jit(solution)/shard_map/pallas_call | solution.py:414
  (5 shorter events, 0.0 us)
Async XLA Ops:
  0.6 8.1 %collective-permute-start = (f32[8,512]{1,0:T(8,128)}, f32[8,512]{1,0:T(8,128)S(1)}, u32[]{:S(2)}, u32[]{:S(2)}) collective-permute-start(f32[8,512]{1,0:T(8,128)} %flux_hbm.1), channel_id=1, source_target_pairs={{0,8},{4,12},{8,0},{12,4},{1,9},{5,13},{9,1},{13,5},{2,10},{6,14},... | collective-permute-start | bytes 49160 | tf_op jit(solution)/shard_map/ppermute | solution.py:390
  4.7 5.7 %collective-permute-start.2 = (f32[8,512]{1,0:T(8,128)}, f32[8,512]{1,0:T(8,128)S(1)}, u32[]{:S(2)}, u32[]{:S(2)}) collective-permute-start(f32[8,512]{1,0:T(8,128)} %flux_hbm.1), channel_id=1, source_target_pairs={{0,12},{4,8},{8,4},{12,0},{1,13},{5,9},{9,5},{13,1},{2,14},{6,10},... | collective-permute-start | bytes 49160 | tf_op jit(solution)/shard_map/ppermute | solution.py:390
  6.1 4.4 %collective-permute-start.1 = (f32[8,512]{1,0:T(8,128)}, f32[8,512]{1,0:T(8,128)S(1)}, u32[]{:S(2)}, u32[]{:S(2)}) collective-permute-start(f32[8,512]{1,0:T(8,128)} %flux_hbm.1), channel_id=1, source_target_pairs={{0,4},{4,0},{8,12},{12,8},{1,5},{5,1},{9,13},{13,9},{2,6},{6,2},{1... | collective-permute-start | bytes 49160 | tf_op jit(solution)/shard_map/ppermute | solution.py:390
  11.3 3.0 %collective-permute-start.5 = (f32[8,128]{1,0:T(8,128)S(1)}, f32[8,128]{1,0:T(8,128)S(1)}, u32[]{:S(2)}, u32[]{:S(2)}) collective-permute-start(f32[8,128]{1,0:T(8,128)S(1)} %get-tuple-element.28.refs_0_), channel_id=1, source_target_pairs={{0,3},{1,2},{2,1},{3,0},{4,7},{5,6},{6,5},{7,4},{8,11},{9,10},{10,... | collective-permute-start | bytes 12296 | tf_op jit(solution)/shard_map/ppermute | solution.py:390
  11.3 3.7 %collective-permute-start.4 = (f32[8,128]{1,0:T(8,128)S(1)}, f32[8,128]{1,0:T(8,128)S(1)}, u32[]{:S(2)}, u32[]{:S(2)}) collective-permute-start(f32[8,128]{1,0:T(8,128)S(1)} %get-tuple-element.28.refs_0_), channel_id=1, source_target_pairs={{0,2},{1,3},{2,0},{3,1},{4,6},{5,7},{6,4},{7,5},{8,10},{9,11},{10,... | collective-permute-start | bytes 12296 | tf_op jit(solution)/shard_map/ppermute | solution.py:390
  12.8 2.1 %collective-permute-start.3 = (f32[8,128]{1,0:T(8,128)S(1)}, f32[8,128]{1,0:T(8,128)S(1)}, u32[]{:S(2)}, u32[]{:S(2)}) collective-permute-start(f32[8,128]{1,0:T(8,128)S(1)} %get-tuple-element.28.refs_0_), channel_id=1, source_target_pairs={{0,1},{1,0},{2,3},{3,2},{4,5},{5,4},{6,7},{7,6},{8,9},{9,8},{10,11... | collective-permute-start | bytes 12296 | tf_op jit(solution)/shard_map/ppermute | solution.py:390
  15.4 5.6 %collective-permute-start.8 = (f32[40,128]{1,0:T(8,128)S(1)}, f32[40,128]{1,0:T(8,128)S(1)}, u32[]{:S(2)}, u32[]{:S(2)}) collective-permute-start(f32[40,128]{1,0:T(8,128)S(1)} %get-tuple-element.34.refs_0_), channel_id=1, source_target_pairs={{0,12},{4,8},{8,4},{12,0},{1,13},{5,9},{9,5},{13,1},{2,14},{6,10},... | collective-permute-start | bytes 61448 | tf_op jit(solution)/shard_map/ppermute | solution.py:390
  17.5 4.7 %collective-permute-start.7 = (f32[40,128]{1,0:T(8,128)S(1)}, f32[40,128]{1,0:T(8,128)S(1)}, u32[]{:S(2)}, u32[]{:S(2)}) collective-permute-start(f32[40,128]{1,0:T(8,128)S(1)} %get-tuple-element.34.refs_0_), channel_id=1, source_target_pairs={{0,8},{4,12},{8,0},{12,4},{1,9},{5,13},{9,1},{13,5},{2,10},{6,14},... | collective-permute-start | bytes 61448 | tf_op jit(solution)/shard_map/ppermute | solution.py:390
  17.5 4.7 %collective-permute-start.6 = (f32[40,128]{1,0:T(8,128)S(1)}, f32[40,128]{1,0:T(8,128)S(1)}, u32[]{:S(2)}, u32[]{:S(2)}) collective-permute-start(f32[40,128]{1,0:T(8,128)S(1)} %get-tuple-element.34.refs_0_), channel_id=1, source_target_pairs={{0,4},{4,0},{8,12},{12,8},{1,5},{5,1},{9,13},{13,9},{2,6},{6,2},{1... | collective-permute-start | bytes 61448 | tf_op jit(solution)/shard_map/ppermute | solution.py:390
  23.0 3.0 %collective-permute-start.11 = (f32[8,128]{1,0:T(8,128)S(1)}, f32[8,128]{1,0:T(8,128)S(1)}, u32[]{:S(2)}, u32[]{:S(2)}) collective-permute-start(f32[8,128]{1,0:T(8,128)S(1)} %shard_map.89.refs_0_), channel_id=1, source_target_pairs={{0,3},{1,2},{2,1},{3,0},{4,7},{5,6},{6,5},{7,4},{8,11},{9,10},{10,... | collective-permute-start | bytes 12296 | tf_op jit(solution)/shard_map/ppermute | solution.py:390
  23.0 3.7 %collective-permute-start.10 = (f32[8,128]{1,0:T(8,128)S(1)}, f32[8,128]{1,0:T(8,128)S(1)}, u32[]{:S(2)}, u32[]{:S(2)}) collective-permute-start(f32[8,128]{1,0:T(8,128)S(1)} %shard_map.89.refs_0_), channel_id=1, source_target_pairs={{0,2},{1,3},{2,0},{3,1},{4,6},{5,7},{6,4},{7,5},{8,10},{9,11},{10,... | collective-permute-start | bytes 12296 | tf_op jit(solution)/shard_map/ppermute | solution.py:390
  24.5 2.1 %collective-permute-start.9 = (f32[8,128]{1,0:T(8,128)S(1)}, f32[8,128]{1,0:T(8,128)S(1)}, u32[]{:S(2)}, u32[]{:S(2)}) collective-permute-start(f32[8,128]{1,0:T(8,128)S(1)} %shard_map.89.refs_0_), channel_id=1, source_target_pairs={{0,1},{1,0},{2,3},{3,2},{4,5},{5,4},{6,7},{7,6},{8,9},{9,8},{10,11... | collective-permute-start | bytes 12296 | tf_op jit(solution)/shard_map/ppermute | solution.py:390
  27.1 5.5 %collective-permute-start.12 = (f32[8,128]{1,0:T(8,128)S(1)}, f32[8,128]{1,0:T(8,128)S(1)}, u32[]{:S(2)}, u32[]{:S(2)}) collective-permute-start(f32[8,128]{1,0:T(8,128)S(1)} %get-tuple-element.37), channel_id=1, source_target_pairs={{0,12},{4,8},{8,4},{12,0},{1,13},{5,9},{9,5},{13,1},{2,14},{6,10},... | collective-permute-start | bytes 12296 | tf_op jit(solution)/shard_map/ppermute | solution.py:390
  28.9 4.5 %collective-permute-start.13 = (f32[8,128]{1,0:T(8,128)S(1)}, f32[8,128]{1,0:T(8,128)S(1)}, u32[]{:S(2)}, u32[]{:S(2)}) collective-permute-start(f32[8,128]{1,0:T(8,128)S(1)} %get-tuple-element.38), channel_id=1, source_target_pairs={{0,8},{4,12},{8,0},{12,4},{1,9},{5,13},{9,1},{13,5},{2,10},{6,14},... | collective-permute-start | bytes 12296 | tf_op jit(solution)/shard_map/ppermute | solution.py:390
  30.1 3.6 %collective-permute-start.14 = (f32[8,128]{1,0:T(8,128)S(1)}, f32[8,128]{1,0:T(8,128)S(1)}, u32[]{:S(2)}, u32[]{:S(2)}) collective-permute-start(f32[8,128]{1,0:T(8,128)S(1)} %get-tuple-element.39), channel_id=1, source_target_pairs={{0,4},{4,0},{8,12},{12,8},{1,5},{5,1},{9,13},{13,9},{2,6},{6,2},{1... | collective-permute-start | bytes 12296 | tf_op jit(solution)/shard_map/ppermute | solution.py:390

commit v11 on v10

--- a/solution.py
+++ b/solution.py
@@ -104,16 +104,25 @@
     for ref in sums:
         ref[...] = jnp.zeros(ref.shape, F32)
 
-    def add(s, ref):
-        block = obs_ref[s]
-        ref[block] = ref[block] + g_ref[s] * x_scr[pl.ds(s, 1), :]
-
-    def step(j, carry):
-        for n, ref in enumerate(sums):
-            add(n * (slots // sets) + j, ref)
+    steps = slots // sets
+    run = min(steps, 16)
+
+    def products(j):
+        at = [n * steps + j for n in range(sets)]
+        return [(obs_ref[s], g_ref[s] * x_scr[pl.ds(s, 1), :]) for s in at]
+
+    def step(first, carry):
+        coming = products(first * run)
+        for j in range(run):
+            now = coming
+            totals = [ref[block] + value for ref, (block, value) in zip(sums, now)]
+            if j + 1 < run:
+                coming = products(first * run + j + 1)
+            for ref, (block, _), total in zip(sums, now, totals):
+                ref[block] = total
         return carry
 
-    lax.fori_loop(0, slots // sets, step, 0, unroll=min(slots // sets, 16))
+    lax.fori_loop(0, steps // run, step, 0)
     rows = OBLK_DEV * TILES // 8
     tiles = []
     for q in range(rows):

time: 34.6 us -> 34.6 us (level)
  no operation moved by 1% of the time
where the time goes in v11:
time: 34.6 us; the launch traced here: 34.5 us
  starting transfers between devices  18.3 us (53%)
  waiting for transfers between devices  9.1 us (26%)
  Pallas kernels  6.39 us (18%)
  between operations  0.67 us (2%)
    ppermute x15, starting transfers between devices, send(): return lax.ppermute(value, axis, [(i, i ^ k) for i in range(size)])  18.3 us
    ppermute x15, waiting for transfers between devices, send(): return lax.ppermute(value, axis, [(i, i ^ k) for i in range(size)])  9.1 us
    pallas_call x7, Pallas kernels, call(): pl.pallas_call(body, out_shape=outs_at, in_specs=[smem if value is obs el...  6.39 us
  transfers between devices with their start and end apart: 15, of which 10 were waited for; matrix products, arithmetic and copies ran while one was open for 0% of the time, Pallas kernels for 9%

profile of v11, /device:TPU:0, one launch (start us, length us, event | category | flops | bytes accessed | tf_op | source)
XLA Modules:
  0.0 34.5 jit_solution(10487555113205342171)
XLA Ops:
  0.6 4.1 %collective-permute-start = (f32[8,512]{1,0:T(8,128)}, f32[8,512]{1,0:T(8,128)S(1)}, u32[]{:S(2)}, u32[]{:S(2)}) collective-permute-start(f32[8,512]{1,0:T(8,128)} %flux_hbm.1), channel_id=1, source_target_pairs={{0,8},{4,12},{8,0},{12,4},{1,9},{5,13},{9,1},{13,5},{2,10},{6,14},... | collective-permute-start | bytes 49160 | tf_op jit(solution)/shard_map/ppermute | solution.py:399
  4.7 1.3 %collective-permute-start.2 = (f32[8,512]{1,0:T(8,128)}, f32[8,512]{1,0:T(8,128)S(1)}, u32[]{:S(2)}, u32[]{:S(2)}) collective-permute-start(f32[8,512]{1,0:T(8,128)} %flux_hbm.1), channel_id=1, source_target_pairs={{0,12},{4,8},{8,4},{12,0},{1,13},{5,9},{9,5},{13,1},{2,14},{6,10},... | collective-permute-start | bytes 49160 | tf_op jit(solution)/shard_map/ppermute | solution.py:399
  6.1 0.2 collective-permute-start.1
  6.3 2.4 %shard_map.86 = (bf16[64,384]{1,0:T(8,128)(2,1)S(1)}, f32[64,128]{1,0:T(8,128)S(1)}, bf16[64,24]{1,0:T(8,128)(2,1)S(1)}, f32[8,128]{1,0:T(8,128)S(1)}, f32[8,128...) custom-call(s32[1,1,4,16]{3,2,1,0:T(4,128)} %fslot_hbm.1, ...), custom_call_target="tpu_custom_call" | custom-call | tf_op jit(solution)/shard_map/pallas_call | solution.py:423
  8.7 1.7 %collective-permute-done.2.refs_3_ = f32[8,512]{1,0:T(8,128)S(1)} collective-permute-done((f32[8,512]{1,0:T(8,128)}, f32[8,512]{1,0:T(8,128)S(1)}, u32[]{:S(2)}, u32[]{:S(2)}) %collective-permute-start.2) | collective-permute-done | bytes 16416 | tf_op jit(solution)/shard_map/ppermute | solution.py:399
  10.5 0.8 %shard_map.87 = (f32[8,128]{1,0:T(8,128)S(1)}, f32[64,128]{1,0:T(8,128)S(1)}) custom-call(f32[8,512]{1,0:T(8,128)S(1)} %get-tuple-element.23.refs_0_, f32[8,512]{1,0:T(8,128)S(1)} %collective-permute-done.refs_1_, f32[8,512]{1,0:T(8,128)S(1)} %collective-permute-done.1.refs_2_, f32[8,512]{1,0:T(8,128)S(1)} %collective-permute-done.2.refs_3_, ...), custom_call_target="tpu_custom_call" | custom-call | tf_op jit(solution)/shard_map/pallas_call | solution.py:423
  11.3 1.5 %collective-permute-start.4 = (f32[8,128]{1,0:T(8,128)S(1)}, f32[8,128]{1,0:T(8,128)S(1)}, u32[]{:S(2)}, u32[]{:S(2)}) collective-permute-start(f32[8,128]{1,0:T(8,128)S(1)} %get-tuple-element.28.refs_0_), channel_id=1, source_target_pairs={{0,2},{1,3},{2,0},{3,1},{4,6},{5,7},{6,4},{7,5},{8,10},{9,11},{10,... | collective-permute-start | bytes 12296 | tf_op jit(solution)/shard_map/ppermute | solution.py:399
  12.8 0.3 collective-permute-start.3
  13.2 1.2 %collective-permute-done.5.refs_3_ = f32[8,128]{1,0:T(8,128)S(1)} collective-permute-done((f32[8,128]{1,0:T(8,128)S(1)}, f32[8,128]{1,0:T(8,128)S(1)}, u32[]{:S(2)}, u32[]{:S(2)}) %collective-permute-start.5) | collective-permute-done | bytes 4128 | tf_op jit(solution)/shard_map/ppermute | solution.py:399
  14.3 0.6 %collective-permute-done.4.refs_2_ = f32[8,128]{1,0:T(8,128)S(1)} collective-permute-done((f32[8,128]{1,0:T(8,128)S(1)}, f32[8,128]{1,0:T(8,128)S(1)}, u32[]{:S(2)}, u32[]{:S(2)}) %collective-permute-start.4) | collective-permute-done | bytes 4128 | tf_op jit(solution)/shard_map/ppermute | solution.py:399
  15.0 0.4 %shard_map.88 = (f32[40,128]{1,0:T(8,128)S(1)}, f32[8,128]{1,0:T(8,128)S(1)}) custom-call(f32[8,128]{1,0:T(8,128)S(1)} %get-tuple-element.28.refs_0_, f32[8,128]{1,0:T(8,128)S(1)} %collective-permute-done.3.refs_1_, f32[8,128]{1,0:T(8,128)S(1)} %collective-permute-done.4.refs_2_, f32[8,128]{1,0:T(8,128)S(1)} %collective-permute-done.5.refs_3_, ...), custom_call_target="tpu_custom_call" | custom-call | tf_op jit(solution)/shard_map/pallas_call | solution.py:423
  15.4 2.1 %collective-permute-start.8 = (f32[40,128]{1,0:T(8,128)S(1)}, f32[40,128]{1,0:T(8,128)S(1)}, u32[]{:S(2)}, u32[]{:S(2)}) collective-permute-start(f32[40,128]{1,0:T(8,128)S(1)} %get-tuple-element.34.refs_0_), channel_id=1, source_target_pairs={{0,12},{4,8},{8,4},{12,0},{1,13},{5,9},{9,5},{13,1},{2,14},{6,10},... | collective-permute-start | bytes 61448 | tf_op jit(solution)/shard_map/ppermute | solution.py:399
  17.5 0.0 collective-permute-start.7
  17.5 2.4 %collective-permute-start.6 = (f32[40,128]{1,0:T(8,128)S(1)}, f32[40,128]{1,0:T(8,128)S(1)}, u32[]{:S(2)}, u32[]{:S(2)}) collective-permute-start(f32[40,128]{1,0:T(8,128)S(1)} %get-tuple-element.34.refs_0_), channel_id=1, source_target_pairs={{0,4},{4,0},{8,12},{12,8},{1,5},{5,1},{9,13},{13,9},{2,6},{6,2},{1... | collective-permute-start | bytes 61448 | tf_op jit(solution)/shard_map/ppermute | solution.py:399
  19.8 1.2 %collective-permute-done.8.refs_3_ = f32[40,128]{1,0:T(8,128)S(1)} collective-permute-done((f32[40,128]{1,0:T(8,128)S(1)}, f32[40,128]{1,0:T(8,128)S(1)}, u32[]{:S(2)}, u32[]{:S(2)}) %collective-permute-start.8) | collective-permute-done | bytes 20512 | tf_op jit(solution)/shard_map/ppermute | solution.py:399
  21.0 1.1 %collective-permute-done.7.refs_2_ = f32[40,128]{1,0:T(8,128)S(1)} collective-permute-done((f32[40,128]{1,0:T(8,128)S(1)}, f32[40,128]{1,0:T(8,128)S(1)}, u32[]{:S(2)}, u32[]{:S(2)}) %collective-permute-start.7) | collective-permute-done | bytes 20512 | tf_op jit(solution)/shard_map/ppermute | solution.py:399
  22.2 0.8 %shard_map.89.refs_0_ = f32[8,128]{1,0:T(8,128)S(1)} custom-call(f32[40,128]{1,0:T(8,128)S(1)} %get-tuple-element.34.refs_0_, f32[40,128]{1,0:T(8,128)S(1)} %collective-permute-done.6.refs_1_, f32[40,128]{1,0:T(8,128)S(1)} %collective-permute-done.7.refs_2_, f32[40,128]{1,0:T(8,128)S(1)} %collective-permute-done.8.refs_3_, ...), custom_call_target="tpu_custom_call" | custom-call | tf_op jit(solution)/shard_map/pallas_call | solution.py:423
  23.0 0.0 collective-permute-start.11
  23.0 1.5 %collective-permute-start.10 = (f32[8,128]{1,0:T(8,128)S(1)}, f32[8,128]{1,0:T(8,128)S(1)}, u32[]{:S(2)}, u32[]{:S(2)}) collective-permute-start(f32[8,128]{1,0:T(8,128)S(1)} %shard_map.89.refs_0_), channel_id=1, source_target_pairs={{0,2},{1,3},{2,0},{3,1},{4,6},{5,7},{6,4},{7,5},{8,10},{9,11},{10,... | collective-permute-start | bytes 12296 | tf_op jit(solution)/shard_map/ppermute | solution.py:399
  24.5 0.3 collective-permute-start.9
  24.9 1.2 %collective-permute-done.11.refs_3_ = f32[8,128]{1,0:T(8,128)S(1)} collective-permute-done((f32[8,128]{1,0:T(8,128)S(1)}, f32[8,128]{1,0:T(8,128)S(1)}, u32[]{:S(2)}, u32[]{:S(2)}) %collective-permute-start.11) | collective-permute-done | bytes 4128 | tf_op jit(solution)/shard_map/ppermute | solution.py:399
  26.0 0.6 %collective-permute-done.10.refs_2_ = f32[8,128]{1,0:T(8,128)S(1)} collective-permute-done((f32[8,128]{1,0:T(8,128)S(1)}, f32[8,128]{1,0:T(8,128)S(1)}, u32[]{:S(2)}, u32[]{:S(2)}) %collective-permute-start.10) | collective-permute-done | bytes 4128 | tf_op jit(solution)/shard_map/ppermute | solution.py:399
  26.7 0.0 collective-permute-done.9.refs_1_
  26.7 0.4 %shard_map.90 = (f32[8,128]{1,0:T(8,128)S(1)}, f32[8,128]{1,0:T(8,128)S(1)}, f32[8,128]{1,0:T(8,128)S(1)}, f32[8,128]{1,0:T(8,128)S(1)}, f32[8,128]{1,0:T(8,128)S(1)}) custom-call(f32[8,128]{1,0:T(8,128)S(1)} %shard_map.89.refs_0_, f32[8,128]{1,0:T(8,128)S(1)} %collective-permute-done.9.refs_1_, f32[8,128]{1,0:T(8,128)S(1)} %collective-permute-done.10.refs_2_, ...), custom_call_target="tpu_custom_call" | custom-call | tf_op jit(solution)/shard_map/pallas_call | solution.py:423
  27.1 1.9 %collective-permute-start.12 = (f32[8,128]{1,0:T(8,128)S(1)}, f32[8,128]{1,0:T(8,128)S(1)}, u32[]{:S(2)}, u32[]{:S(2)}) collective-permute-start(f32[8,128]{1,0:T(8,128)S(1)} %get-tuple-element.37), channel_id=1, source_target_pairs={{0,12},{4,8},{8,4},{12,0},{1,13},{5,9},{9,5},{13,1},{2,14},{6,10},... | collective-permute-start | bytes 12296 | tf_op jit(solution)/shard_map/ppermute | solution.py:399
  29.0 1.1 %collective-permute-start.13 = (f32[8,128]{1,0:T(8,128)S(1)}, f32[8,128]{1,0:T(8,128)S(1)}, u32[]{:S(2)}, u32[]{:S(2)}) collective-permute-start(f32[8,128]{1,0:T(8,128)S(1)} %get-tuple-element.38), channel_id=1, source_target_pairs={{0,8},{4,12},{8,0},{12,4},{1,9},{5,13},{9,1},{13,5},{2,10},{6,14},... | collective-permute-start | bytes 12296 | tf_op jit(solution)/shard_map/ppermute | solution.py:399
  30.1 1.5 %collective-permute-start.14 = (f32[8,128]{1,0:T(8,128)S(1)}, f32[8,128]{1,0:T(8,128)S(1)}, u32[]{:S(2)}, u32[]{:S(2)}) collective-permute-start(f32[8,128]{1,0:T(8,128)S(1)} %get-tuple-element.39), channel_id=1, source_target_pairs={{0,4},{4,0},{8,12},{12,8},{1,5},{5,1},{9,13},{13,9},{2,6},{6,2},{1... | collective-permute-start | bytes 12296 | tf_op jit(solution)/shard_map/ppermute | solution.py:399
  31.5 0.7 %shard_map.91 = (bf16[128,128]{1,0:T(8,128)(2,1)S(1)}, f32[1,512]{1,0:T(1,128)}) custom-call(f32[40,128]{1,0:T(8,128)S(1)} %get-tuple-element.34.refs_0_, f32[40,128]{1,0:T(8,128)S(1)} %collective-permute-done.6.refs_1_, f32[40,128]{1,0:T(8,128)S(1)} %collective-permute-done.7.refs_2_, f32[40,128]{1,0:T(8,128)S(1)} %collective-permute-done.8.refs_3_, ...), custom_call_target="tpu_custom_call" | custom-call | tf_op jit(solution)/shard_map/pallas_call | solution.py:423
  32.2 0.3 %collective-permute-done.12.refs_0_ = f32[8,128]{1,0:T(8,128)S(1)} collective-permute-done((f32[8,128]{1,0:T(8,128)S(1)}, f32[8,128]{1,0:T(8,128)S(1)}, u32[]{:S(2)}, u32[]{:S(2)}) %collective-permute-start.12) | collective-permute-done | bytes 4128 | tf_op jit(solution)/shard_map/ppermute | solution.py:399
  32.6 0.9 %collective-permute-done.13.refs_1_ = f32[8,128]{1,0:T(8,128)S(1)} collective-permute-done((f32[8,128]{1,0:T(8,128)S(1)}, f32[8,128]{1,0:T(8,128)S(1)}, u32[]{:S(2)}, u32[]{:S(2)}) %collective-permute-start.13) | collective-permute-done | bytes 4128 | tf_op jit(solution)/shard_map/ppermute | solution.py:399
  33.5 0.2 collective-permute-done.14.refs_2_
  33.7 0.8 %shard_map.92 = f32[8,512]{1,0:T(8,128)} custom-call(f32[8,128]{1,0:T(8,128)S(1)} %collective-permute-done.12.refs_0_, f32[8,128]{1,0:T(8,128)S(1)} %collective-permute-done.13.refs_1_, f32[8,128]{1,0:T(8,128)S(1)} %collective-permute-done.14.refs_2_, f32[8,128]{1,0:T(8,128)S(1)} %get-tuple-element.40.refs_3_, bf16[128,128]{1,0:T(8,128)(2,1)S(1)} %get-tuple-element.42.refs_4_), custom_call_target="tpu_custom_call" | custom-call | tf_op jit(solution)/shard_map/pallas_call | solution.py:423
  (5 shorter events, 0.0 us)
Async XLA Ops:
  0.6 8.1 %collective-permute-start = (f32[8,512]{1,0:T(8,128)}, f32[8,512]{1,0:T(8,128)S(1)}, u32[]{:S(2)}, u32[]{:S(2)}) collective-permute-start(f32[8,512]{1,0:T(8,128)} %flux_hbm.1), channel_id=1, source_target_pairs={{0,8},{4,12},{8,0},{12,4},{1,9},{5,13},{9,1},{13,5},{2,10},{6,14},... | collective-permute-start | bytes 49160 | tf_op jit(solution)/shard_map/ppermute | solution.py:399
  4.7 5.7 %collective-permute-start.2 = (f32[8,512]{1,0:T(8,128)}, f32[8,512]{1,0:T(8,128)S(1)}, u32[]{:S(2)}, u32[]{:S(2)}) collective-permute-start(f32[8,512]{1,0:T(8,128)} %flux_hbm.1), channel_id=1, source_target_pairs={{0,12},{4,8},{8,4},{12,0},{1,13},{5,9},{9,5},{13,1},{2,14},{6,10},... | collective-permute-start | bytes 49160 | tf_op jit(solution)/shard_map/ppermute | solution.py:399
  6.1 4.4 %collective-permute-start.1 = (f32[8,512]{1,0:T(8,128)}, f32[8,512]{1,0:T(8,128)S(1)}, u32[]{:S(2)}, u32[]{:S(2)}) collective-permute-start(f32[8,512]{1,0:T(8,128)} %flux_hbm.1), channel_id=1, source_target_pairs={{0,4},{4,0},{8,12},{12,8},{1,5},{5,1},{9,13},{13,9},{2,6},{6,2},{1... | collective-permute-start | bytes 49160 | tf_op jit(solution)/shard_map/ppermute | solution.py:399
  11.3 3.0 %collective-permute-start.5 = (f32[8,128]{1,0:T(8,128)S(1)}, f32[8,128]{1,0:T(8,128)S(1)}, u32[]{:S(2)}, u32[]{:S(2)}) collective-permute-start(f32[8,128]{1,0:T(8,128)S(1)} %get-tuple-element.28.refs_0_), channel_id=1, source_target_pairs={{0,3},{1,2},{2,1},{3,0},{4,7},{5,6},{6,5},{7,4},{8,11},{9,10},{10,... | collective-permute-start | bytes 12296 | tf_op jit(solution)/shard_map/ppermute | solution.py:399
  11.3 3.7 %collective-permute-start.4 = (f32[8,128]{1,0:T(8,128)S(1)}, f32[8,128]{1,0:T(8,128)S(1)}, u32[]{:S(2)}, u32[]{:S(2)}) collective-permute-start(f32[8,128]{1,0:T(8,128)S(1)} %get-tuple-element.28.refs_0_), channel_id=1, source_target_pairs={{0,2},{1,3},{2,0},{3,1},{4,6},{5,7},{6,4},{7,5},{8,10},{9,11},{10,... | collective-permute-start | bytes 12296 | tf_op jit(solution)/shard_map/ppermute | solution.py:399
  12.8 2.1 %collective-permute-start.3 = (f32[8,128]{1,0:T(8,128)S(1)}, f32[8,128]{1,0:T(8,128)S(1)}, u32[]{:S(2)}, u32[]{:S(2)}) collective-permute-start(f32[8,128]{1,0:T(8,128)S(1)} %get-tuple-element.28.refs_0_), channel_id=1, source_target_pairs={{0,1},{1,0},{2,3},{3,2},{4,5},{5,4},{6,7},{7,6},{8,9},{9,8},{10,11... | collective-permute-start | bytes 12296 | tf_op jit(solution)/shard_map/ppermute | solution.py:399
  15.4 5.6 %collective-permute-start.8 = (f32[40,128]{1,0:T(8,128)S(1)}, f32[40,128]{1,0:T(8,128)S(1)}, u32[]{:S(2)}, u32[]{:S(2)}) collective-permute-start(f32[40,128]{1,0:T(8,128)S(1)} %get-tuple-element.34.refs_0_), channel_id=1, source_target_pairs={{0,12},{4,8},{8,4},{12,0},{1,13},{5,9},{9,5},{13,1},{2,14},{6,10},... | collective-permute-start | bytes 61448 | tf_op jit(solution)/shard_map/ppermute | solution.py:399
  17.5 4.7 %collective-permute-start.7 = (f32[40,128]{1,0:T(8,128)S(1)}, f32[40,128]{1,0:T(8,128)S(1)}, u32[]{:S(2)}, u32[]{:S(2)}) collective-permute-start(f32[40,128]{1,0:T(8,128)S(1)} %get-tuple-element.34.refs_0_), channel_id=1, source_target_pairs={{0,8},{4,12},{8,0},{12,4},{1,9},{5,13},{9,1},{13,5},{2,10},{6,14},... | collective-permute-start | bytes 61448 | tf_op jit(solution)/shard_map/ppermute | solution.py:399
  17.5 4.7 %collective-permute-start.6 = (f32[40,128]{1,0:T(8,128)S(1)}, f32[40,128]{1,0:T(8,128)S(1)}, u32[]{:S(2)}, u32[]{:S(2)}) collective-permute-start(f32[40,128]{1,0:T(8,128)S(1)} %get-tuple-element.34.refs_0_), channel_id=1, source_target_pairs={{0,4},{4,0},{8,12},{12,8},{1,5},{5,1},{9,13},{13,9},{2,6},{6,2},{1... | collective-permute-start | bytes 61448 | tf_op jit(solution)/shard_map/ppermute | solution.py:399
  23.0 3.0 %collective-permute-start.11 = (f32[8,128]{1,0:T(8,128)S(1)}, f32[8,128]{1,0:T(8,128)S(1)}, u32[]{:S(2)}, u32[]{:S(2)}) collective-permute-start(f32[8,128]{1,0:T(8,128)S(1)} %shard_map.89.refs_0_), channel_id=1, source_target_pairs={{0,3},{1,2},{2,1},{3,0},{4,7},{5,6},{6,5},{7,4},{8,11},{9,10},{10,... | collective-permute-start | bytes 12296 | tf_op jit(solution)/shard_map/ppermute | solution.py:399
  23.0 3.7 %collective-permute-start.10 = (f32[8,128]{1,0:T(8,128)S(1)}, f32[8,128]{1,0:T(8,128)S(1)}, u32[]{:S(2)}, u32[]{:S(2)}) collective-permute-start(f32[8,128]{1,0:T(8,128)S(1)} %shard_map.89.refs_0_), channel_id=1, source_target_pairs={{0,2},{1,3},{2,0},{3,1},{4,6},{5,7},{6,4},{7,5},{8,10},{9,11},{10,... | collective-permute-start | bytes 12296 | tf_op jit(solution)/shard_map/ppermute | solution.py:399
  24.5 2.1 %collective-permute-start.9 = (f32[8,128]{1,0:T(8,128)S(1)}, f32[8,128]{1,0:T(8,128)S(1)}, u32[]{:S(2)}, u32[]{:S(2)}) collective-permute-start(f32[8,128]{1,0:T(8,128)S(1)} %shard_map.89.refs_0_), channel_id=1, source_target_pairs={{0,1},{1,0},{2,3},{3,2},{4,5},{5,4},{6,7},{7,6},{8,9},{9,8},{10,11... | collective-permute-start | bytes 12296 | tf_op jit(solution)/shard_map/ppermute | solution.py:399
  27.1 5.5 %collective-permute-start.12 = (f32[8,128]{1,0:T(8,128)S(1)}, f32[8,128]{1,0:T(8,128)S(1)}, u32[]{:S(2)}, u32[]{:S(2)}) collective-permute-start(f32[8,128]{1,0:T(8,128)S(1)} %get-tuple-element.37), channel_id=1, source_target_pairs={{0,12},{4,8},{8,4},{12,0},{1,13},{5,9},{9,5},{13,1},{2,14},{6,10},... | collective-permute-start | bytes 12296 | tf_op jit(solution)/shard_map/ppermute | solution.py:399
  29.0 4.5 %collective-permute-start.13 = (f32[8,128]{1,0:T(8,128)S(1)}, f32[8,128]{1,0:T(8,128)S(1)}, u32[]{:S(2)}, u32[]{:S(2)}) collective-permute-start(f32[8,128]{1,0:T(8,128)S(1)} %get-tuple-element.38), channel_id=1, source_target_pairs={{0,8},{4,12},{8,0},{12,4},{1,9},{5,13},{9,1},{13,5},{2,10},{6,14},... | collective-permute-start | bytes 12296 | tf_op jit(solution)/shard_map/ppermute | solution.py:399
  30.1 3.6 %collective-permute-start.14 = (f32[8,128]{1,0:T(8,128)S(1)}, f32[8,128]{1,0:T(8,128)S(1)}, u32[]{:S(2)}, u32[]{:S(2)}) collective-permute-start(f32[8,128]{1,0:T(8,128)S(1)} %get-tuple-element.39), channel_id=1, source_target_pairs={{0,4},{4,0},{8,12},{12,8},{1,5},{5,1},{9,13},{13,9},{2,6},{6,2},{1... | collective-permute-start | bytes 12296 | tf_op jit(solution)/shard_map/ppermute | solution.py:399

commit v12 on v11

--- a/solution.py
+++ b/solution.py
@@ -38,12 +38,6 @@
 
 def pick_rows(pick3, value):
     return jnp.dot(pick3, jnp.concatenate(three(value), axis=0), preferred_element_type=F32)
-
-
-def swap(value, distance):
-    return jnp.take_along_axis(
-        value, iota(value.shape, 1) ^ distance, axis=1, mode="promise_in_bounds"
-    )
 
 
 def half_swap(value):
@@ -81,16 +75,16 @@
     return jnp.sum(jnp.where(here, found, 0.0), axis=0, keepdims=True)
 
 
-def merge_tree(tiles):
-    distance = 2
-    while len(tiles) > 1:
-        clear = (iota(tiles[0].shape, 1) & distance) == 0
-        tiles = [
-            jnp.where(clear, a, b) + swap(jnp.where(clear, b, a), distance)
-            for a, b in zip(tiles[::2], tiles[1::2])
-        ]
-        distance *= 2
-    return tiles[0]
+def lane_sums(tiles):
+    terms = jnp.concatenate(three(jnp.concatenate(tiles, axis=0)), axis=1)
+    shape = (3 * LANES, LANES)
+    ones = one_hot((iota(shape, 0) // OB) % 2 == iota(shape, 1) // OB)
+    sums = jnp.dot(terms, ones, preferred_element_type=F32)
+    out = sums[:8]
+    tile = (iota(out.shape, 1) >> 1) & 31
+    for q in range(1, len(tiles)):
+        out = jnp.where(tile == q, sums[8 * q : 8 * q + 8], out)
+    return out
 
 
 def h_columns(h_ref, first, last, start, size):
@@ -128,8 +122,7 @@
     for q in range(rows):
         at = (q // 4, slice(8 * (q % 4), 8 * (q % 4) + 8))
         tiles.append(tree_sum([ref[at] for ref in sums]))
-    m = merge_tree(tiles)
-    return m + swap(m, 1)
+    return lane_sums(tiles)
 
 
 def adjoint(h_ref, slot_obs, d, store):

time: 34.6 us -> 34.5 us (level)
  Pallas kernels: 6.39 us -> 6.02 us
    pallas_call x7, Pallas kernels: 6.39 us -> 6.02 us  [call(): pl.pallas_call(body, out_shape=outs_at, in_specs=[smem if value is obs el...]
where the time goes in v12:
time: 34.5 us; the launch traced here: 34.4 us
  starting transfers between devices  18.5 us (54%)
  waiting for transfers between devices  9.2 us (27%)
  Pallas kernels  6.02 us (17%)
  between operations  0.7 us (2%)
    ppermute x15, starting transfers between devices, send(): return lax.ppermute(value, axis, [(i, i ^ k) for i in range(size)])  18.5 us
    ppermute x15, waiting for transfers between devices, send(): return lax.ppermute(value, axis, [(i, i ^ k) for i in range(size)])  9.2 us
    pallas_call x7, Pallas kernels, call(): pl.pallas_call(body, out_shape=outs_at, in_specs=[smem if value is obs el...  6.02 us
  transfers between devices with their start and end apart: 15, of which 10 were waited for; matrix products, arithmetic and copies ran while one was open for 0% of the time, Pallas kernels for 9%

profile of v12, /device:TPU:0, one launch (start us, length us, event | category | flops | bytes accessed | tf_op | source)
XLA Modules:
  0.0 34.4 jit_solution(11751798009586877430)
XLA Ops:
  0.6 4.1 %collective-permute-start = (f32[8,512]{1,0:T(8,128)}, f32[8,512]{1,0:T(8,128)S(1)}, u32[]{:S(2)}, u32[]{:S(2)}) collective-permute-start(f32[8,512]{1,0:T(8,128)} %flux_hbm.1), channel_id=1, source_target_pairs={{0,8},{4,12},{8,0},{12,4},{1,9},{5,13},{9,1},{13,5},{2,10},{6,14},... | collective-permute-start | bytes 49160 | tf_op jit(solution)/shard_map/ppermute | solution.py:392
  4.7 1.3 %collective-permute-start.2 = (f32[8,512]{1,0:T(8,128)}, f32[8,512]{1,0:T(8,128)S(1)}, u32[]{:S(2)}, u32[]{:S(2)}) collective-permute-start(f32[8,512]{1,0:T(8,128)} %flux_hbm.1), channel_id=1, source_target_pairs={{0,12},{4,8},{8,4},{12,0},{1,13},{5,9},{9,5},{13,1},{2,14},{6,10},... | collective-permute-start | bytes 49160 | tf_op jit(solution)/shard_map/ppermute | solution.py:392
  6.1 0.2 collective-permute-start.1
  6.3 2.4 %shard_map.86 = (bf16[64,384]{1,0:T(8,128)(2,1)S(1)}, f32[64,128]{1,0:T(8,128)S(1)}, bf16[64,24]{1,0:T(8,128)(2,1)S(1)}, f32[8,128]{1,0:T(8,128)S(1)}, f32[8,128...) custom-call(s32[1,1,4,16]{3,2,1,0:T(4,128)} %fslot_hbm.1, ...), custom_call_target="tpu_custom_call" | custom-call | tf_op jit(solution)/shard_map/pallas_call | solution.py:416
  8.7 0.0 collective-permute-done.refs_1_
  8.7 1.7 %collective-permute-done.2.refs_3_ = f32[8,512]{1,0:T(8,128)S(1)} collective-permute-done((f32[8,512]{1,0:T(8,128)}, f32[8,512]{1,0:T(8,128)S(1)}, u32[]{:S(2)}, u32[]{:S(2)}) %collective-permute-start.2) | collective-permute-done | bytes 16416 | tf_op jit(solution)/shard_map/ppermute | solution.py:392
  10.5 0.6 %shard_map.87 = (f32[8,128]{1,0:T(8,128)S(1)}, f32[64,128]{1,0:T(8,128)S(1)}) custom-call(f32[8,512]{1,0:T(8,128)S(1)} %get-tuple-element.23.refs_0_, f32[8,512]{1,0:T(8,128)S(1)} %collective-permute-done.refs_1_, f32[8,512]{1,0:T(8,128)S(1)} %collective-permute-done.1.refs_2_, f32[8,512]{1,0:T(8,128)S(1)} %collective-permute-done.2.refs_3_, ...), custom_call_target="tpu_custom_call" | custom-call | tf_op jit(solution)/shard_map/pallas_call | solution.py:416
  11.1 0.1 collective-permute-start.5
  11.2 1.6 %collective-permute-start.4 = (f32[8,128]{1,0:T(8,128)S(1)}, f32[8,128]{1,0:T(8,128)S(1)}, u32[]{:S(2)}, u32[]{:S(2)}) collective-permute-start(f32[8,128]{1,0:T(8,128)S(1)} %get-tuple-element.28.refs_0_), channel_id=1, source_target_pairs={{0,2},{1,3},{2,0},{3,1},{4,6},{5,7},{6,4},{7,5},{8,10},{9,11},{10,... | collective-permute-start | bytes 12296 | tf_op jit(solution)/shard_map/ppermute | solution.py:392
  12.8 0.3 collective-permute-start.3
  13.0 1.2 %collective-permute-done.5.refs_3_ = f32[8,128]{1,0:T(8,128)S(1)} collective-permute-done((f32[8,128]{1,0:T(8,128)S(1)}, f32[8,128]{1,0:T(8,128)S(1)}, u32[]{:S(2)}, u32[]{:S(2)}) %collective-permute-start.5) | collective-permute-done | bytes 4128 | tf_op jit(solution)/shard_map/ppermute | solution.py:392
  14.2 0.7 %collective-permute-done.4.refs_2_ = f32[8,128]{1,0:T(8,128)S(1)} collective-permute-done((f32[8,128]{1,0:T(8,128)S(1)}, f32[8,128]{1,0:T(8,128)S(1)}, u32[]{:S(2)}, u32[]{:S(2)}) %collective-permute-start.4) | collective-permute-done | bytes 4128 | tf_op jit(solution)/shard_map/ppermute | solution.py:392
  14.9 0.4 %shard_map.88 = (f32[40,128]{1,0:T(8,128)S(1)}, f32[8,128]{1,0:T(8,128)S(1)}) custom-call(f32[8,128]{1,0:T(8,128)S(1)} %get-tuple-element.28.refs_0_, f32[8,128]{1,0:T(8,128)S(1)} %collective-permute-done.3.refs_1_, f32[8,128]{1,0:T(8,128)S(1)} %collective-permute-done.4.refs_2_, f32[8,128]{1,0:T(8,128)S(1)} %collective-permute-done.5.refs_3_, ...), custom_call_target="tpu_custom_call" | custom-call | tf_op jit(solution)/shard_map/pallas_call | solution.py:416
  15.3 2.1 %collective-permute-start.8 = (f32[40,128]{1,0:T(8,128)S(1)}, f32[40,128]{1,0:T(8,128)S(1)}, u32[]{:S(2)}, u32[]{:S(2)}) collective-permute-start(f32[40,128]{1,0:T(8,128)S(1)} %get-tuple-element.34.refs_0_), channel_id=1, source_target_pairs={{0,12},{4,8},{8,4},{12,0},{1,13},{5,9},{9,5},{13,1},{2,14},{6,10},... | collective-permute-start | bytes 61448 | tf_op jit(solution)/shard_map/ppermute | solution.py:392
  17.4 2.4 %collective-permute-start.6 = (f32[40,128]{1,0:T(8,128)S(1)}, f32[40,128]{1,0:T(8,128)S(1)}, u32[]{:S(2)}, u32[]{:S(2)}) collective-permute-start(f32[40,128]{1,0:T(8,128)S(1)} %get-tuple-element.34.refs_0_), channel_id=1, source_target_pairs={{0,4},{4,0},{8,12},{12,8},{1,5},{5,1},{9,13},{13,9},{2,6},{6,2},{1... | collective-permute-start | bytes 61448 | tf_op jit(solution)/shard_map/ppermute | solution.py:392
  19.8 1.2 %collective-permute-done.8.refs_3_ = f32[40,128]{1,0:T(8,128)S(1)} collective-permute-done((f32[40,128]{1,0:T(8,128)S(1)}, f32[40,128]{1,0:T(8,128)S(1)}, u32[]{:S(2)}, u32[]{:S(2)}) %collective-permute-start.8) | collective-permute-done | bytes 20512 | tf_op jit(solution)/shard_map/ppermute | solution.py:392
  21.0 1.1 %collective-permute-done.7.refs_2_ = f32[40,128]{1,0:T(8,128)S(1)} collective-permute-done((f32[40,128]{1,0:T(8,128)S(1)}, f32[40,128]{1,0:T(8,128)S(1)}, u32[]{:S(2)}, u32[]{:S(2)}) %collective-permute-start.7) | collective-permute-done | bytes 20512 | tf_op jit(solution)/shard_map/ppermute | solution.py:392
  22.1 0.6 %shard_map.89.refs_0_ = f32[8,128]{1,0:T(8,128)S(1)} custom-call(f32[40,128]{1,0:T(8,128)S(1)} %get-tuple-element.34.refs_0_, f32[40,128]{1,0:T(8,128)S(1)} %collective-permute-done.6.refs_1_, f32[40,128]{1,0:T(8,128)S(1)} %collective-permute-done.7.refs_2_, f32[40,128]{1,0:T(8,128)S(1)} %collective-permute-done.8.refs_3_, ...), custom_call_target="tpu_custom_call" | custom-call | tf_op jit(solution)/shard_map/pallas_call | solution.py:416
  22.7 0.1 collective-permute-start.11
  22.8 1.5 %collective-permute-start.10 = (f32[8,128]{1,0:T(8,128)S(1)}, f32[8,128]{1,0:T(8,128)S(1)}, u32[]{:S(2)}, u32[]{:S(2)}) collective-permute-start(f32[8,128]{1,0:T(8,128)S(1)} %shard_map.89.refs_0_), channel_id=1, source_target_pairs={{0,2},{1,3},{2,0},{3,1},{4,6},{5,7},{6,4},{7,5},{8,10},{9,11},{10,... | collective-permute-start | bytes 12296 | tf_op jit(solution)/shard_map/ppermute | solution.py:392
  24.4 0.3 collective-permute-start.9
  24.7 1.2 %collective-permute-done.11.refs_3_ = f32[8,128]{1,0:T(8,128)S(1)} collective-permute-done((f32[8,128]{1,0:T(8,128)S(1)}, f32[8,128]{1,0:T(8,128)S(1)}, u32[]{:S(2)}, u32[]{:S(2)}) %collective-permute-start.11) | collective-permute-done | bytes 4128 | tf_op jit(solution)/shard_map/ppermute | solution.py:392
  25.9 0.6 %collective-permute-done.10.refs_2_ = f32[8,128]{1,0:T(8,128)S(1)} collective-permute-done((f32[8,128]{1,0:T(8,128)S(1)}, f32[8,128]{1,0:T(8,128)S(1)}, u32[]{:S(2)}, u32[]{:S(2)}) %collective-permute-start.10) | collective-permute-done | bytes 4128 | tf_op jit(solution)/shard_map/ppermute | solution.py:392
  26.5 0.4 %shard_map.90 = (f32[8,128]{1,0:T(8,128)S(1)}, f32[8,128]{1,0:T(8,128)S(1)}, f32[8,128]{1,0:T(8,128)S(1)}, f32[8,128]{1,0:T(8,128)S(1)}, f32[8,128]{1,0:T(8,128)S(1)}) custom-call(f32[8,128]{1,0:T(8,128)S(1)} %shard_map.89.refs_0_, f32[8,128]{1,0:T(8,128)S(1)} %collective-permute-done.9.refs_1_, f32[8,128]{1,0:T(8,128)S(1)} %collective-permute-done.10.refs_2_, ...), custom_call_target="tpu_custom_call" | custom-call | tf_op jit(solution)/shard_map/pallas_call | solution.py:416
  26.9 1.9 %collective-permute-start.12 = (f32[8,128]{1,0:T(8,128)S(1)}, f32[8,128]{1,0:T(8,128)S(1)}, u32[]{:S(2)}, u32[]{:S(2)}) collective-permute-start(f32[8,128]{1,0:T(8,128)S(1)} %get-tuple-element.37), channel_id=1, source_target_pairs={{0,12},{4,8},{8,4},{12,0},{1,13},{5,9},{9,5},{13,1},{2,14},{6,10},... | collective-permute-start | bytes 12296 | tf_op jit(solution)/shard_map/ppermute | solution.py:392
  28.8 1.1 %collective-permute-start.13 = (f32[8,128]{1,0:T(8,128)S(1)}, f32[8,128]{1,0:T(8,128)S(1)}, u32[]{:S(2)}, u32[]{:S(2)}) collective-permute-start(f32[8,128]{1,0:T(8,128)S(1)} %get-tuple-element.38), channel_id=1, source_target_pairs={{0,8},{4,12},{8,0},{12,4},{1,9},{5,13},{9,1},{13,5},{2,10},{6,14},... | collective-permute-start | bytes 12296 | tf_op jit(solution)/shard_map/ppermute | solution.py:392
  30.0 1.5 %collective-permute-start.14 = (f32[8,128]{1,0:T(8,128)S(1)}, f32[8,128]{1,0:T(8,128)S(1)}, u32[]{:S(2)}, u32[]{:S(2)}) collective-permute-start(f32[8,128]{1,0:T(8,128)S(1)} %get-tuple-element.39), channel_id=1, source_target_pairs={{0,4},{4,0},{8,12},{12,8},{1,5},{5,1},{9,13},{13,9},{2,6},{6,2},{1... | collective-permute-start | bytes 12296 | tf_op jit(solution)/shard_map/ppermute | solution.py:392
  31.4 0.7 %shard_map.91 = (bf16[128,128]{1,0:T(8,128)(2,1)S(1)}, f32[1,512]{1,0:T(1,128)}) custom-call(f32[40,128]{1,0:T(8,128)S(1)} %get-tuple-element.34.refs_0_, f32[40,128]{1,0:T(8,128)S(1)} %collective-permute-done.6.refs_1_, f32[40,128]{1,0:T(8,128)S(1)} %collective-permute-done.7.refs_2_, f32[40,128]{1,0:T(8,128)S(1)} %collective-permute-done.8.refs_3_, ...), custom_call_target="tpu_custom_call" | custom-call | tf_op jit(solution)/shard_map/pallas_call | solution.py:416
  32.1 0.4 %collective-permute-done.12.refs_0_ = f32[8,128]{1,0:T(8,128)S(1)} collective-permute-done((f32[8,128]{1,0:T(8,128)S(1)}, f32[8,128]{1,0:T(8,128)S(1)}, u32[]{:S(2)}, u32[]{:S(2)}) %collective-permute-start.12) | collective-permute-done | bytes 4128 | tf_op jit(solution)/shard_map/ppermute | solution.py:392
  32.5 0.9 %collective-permute-done.13.refs_1_ = f32[8,128]{1,0:T(8,128)S(1)} collective-permute-done((f32[8,128]{1,0:T(8,128)S(1)}, f32[8,128]{1,0:T(8,128)S(1)}, u32[]{:S(2)}, u32[]{:S(2)}) %collective-permute-start.13) | collective-permute-done | bytes 4128 | tf_op jit(solution)/shard_map/ppermute | solution.py:392
  33.3 0.2 collective-permute-done.14.refs_2_
  33.6 0.8 %shard_map.92 = f32[8,512]{1,0:T(8,128)} custom-call(f32[8,128]{1,0:T(8,128)S(1)} %collective-permute-done.12.refs_0_, f32[8,128]{1,0:T(8,128)S(1)} %collective-permute-done.13.refs_1_, f32[8,128]{1,0:T(8,128)S(1)} %collective-permute-done.14.refs_2_, f32[8,128]{1,0:T(8,128)S(1)} %get-tuple-element.40.refs_3_, bf16[128,128]{1,0:T(8,128)(2,1)S(1)} %get-tuple-element.42.refs_4_), custom_call_target="tpu_custom_call" | custom-call | tf_op jit(solution)/shard_map/pallas_call | solution.py:416
  (5 shorter events, 0.0 us)
Async XLA Ops:
  0.6 8.1 %collective-permute-start = (f32[8,512]{1,0:T(8,128)}, f32[8,512]{1,0:T(8,128)S(1)}, u32[]{:S(2)}, u32[]{:S(2)}) collective-permute-start(f32[8,512]{1,0:T(8,128)} %flux_hbm.1), channel_id=1, source_target_pairs={{0,8},{4,12},{8,0},{12,4},{1,9},{5,13},{9,1},{13,5},{2,10},{6,14},... | collective-permute-start | bytes 49160 | tf_op jit(solution)/shard_map/ppermute | solution.py:392
  4.7 5.7 %collective-permute-start.2 = (f32[8,512]{1,0:T(8,128)}, f32[8,512]{1,0:T(8,128)S(1)}, u32[]{:S(2)}, u32[]{:S(2)}) collective-permute-start(f32[8,512]{1,0:T(8,128)} %flux_hbm.1), channel_id=1, source_target_pairs={{0,12},{4,8},{8,4},{12,0},{1,13},{5,9},{9,5},{13,1},{2,14},{6,10},... | collective-permute-start | bytes 49160 | tf_op jit(solution)/shard_map/ppermute | solution.py:392
  6.1 4.4 %collective-permute-start.1 = (f32[8,512]{1,0:T(8,128)}, f32[8,512]{1,0:T(8,128)S(1)}, u32[]{:S(2)}, u32[]{:S(2)}) collective-permute-start(f32[8,512]{1,0:T(8,128)} %flux_hbm.1), channel_id=1, source_target_pairs={{0,4},{4,0},{8,12},{12,8},{1,5},{5,1},{9,13},{13,9},{2,6},{6,2},{1... | collective-permute-start | bytes 49160 | tf_op jit(solution)/shard_map/ppermute | solution.py:392
  11.1 3.1 %collective-permute-start.5 = (f32[8,128]{1,0:T(8,128)S(1)}, f32[8,128]{1,0:T(8,128)S(1)}, u32[]{:S(2)}, u32[]{:S(2)}) collective-permute-start(f32[8,128]{1,0:T(8,128)S(1)} %get-tuple-element.28.refs_0_), channel_id=1, source_target_pairs={{0,3},{1,2},{2,1},{3,0},{4,7},{5,6},{6,5},{7,4},{8,11},{9,10},{10,... | collective-permute-start | bytes 12296 | tf_op jit(solution)/shard_map/ppermute | solution.py:392
  11.2 3.7 %collective-permute-start.4 = (f32[8,128]{1,0:T(8,128)S(1)}, f32[8,128]{1,0:T(8,128)S(1)}, u32[]{:S(2)}, u32[]{:S(2)}) collective-permute-start(f32[8,128]{1,0:T(8,128)S(1)} %get-tuple-element.28.refs_0_), channel_id=1, source_target_pairs={{0,2},{1,3},{2,0},{3,1},{4,6},{5,7},{6,4},{7,5},{8,10},{9,11},{10,... | collective-permute-start | bytes 12296 | tf_op jit(solution)/shard_map/ppermute | solution.py:392
  12.8 2.1 %collective-permute-start.3 = (f32[8,128]{1,0:T(8,128)S(1)}, f32[8,128]{1,0:T(8,128)S(1)}, u32[]{:S(2)}, u32[]{:S(2)}) collective-permute-start(f32[8,128]{1,0:T(8,128)S(1)} %get-tuple-element.28.refs_0_), channel_id=1, source_target_pairs={{0,1},{1,0},{2,3},{3,2},{4,5},{5,4},{6,7},{7,6},{8,9},{9,8},{10,11... | collective-permute-start | bytes 12296 | tf_op jit(solution)/shard_map/ppermute | solution.py:392
  15.3 5.7 %collective-permute-start.8 = (f32[40,128]{1,0:T(8,128)S(1)}, f32[40,128]{1,0:T(8,128)S(1)}, u32[]{:S(2)}, u32[]{:S(2)}) collective-permute-start(f32[40,128]{1,0:T(8,128)S(1)} %get-tuple-element.34.refs_0_), channel_id=1, source_target_pairs={{0,12},{4,8},{8,4},{12,0},{1,13},{5,9},{9,5},{13,1},{2,14},{6,10},... | collective-permute-start | bytes 61448 | tf_op jit(solution)/shard_map/ppermute | solution.py:392
  17.4 4.7 %collective-permute-start.7 = (f32[40,128]{1,0:T(8,128)S(1)}, f32[40,128]{1,0:T(8,128)S(1)}, u32[]{:S(2)}, u32[]{:S(2)}) collective-permute-start(f32[40,128]{1,0:T(8,128)S(1)} %get-tuple-element.34.refs_0_), channel_id=1, source_target_pairs={{0,8},{4,12},{8,0},{12,4},{1,9},{5,13},{9,1},{13,5},{2,10},{6,14},... | collective-permute-start | bytes 61448 | tf_op jit(solution)/shard_map/ppermute | solution.py:392
  17.4 4.7 %collective-permute-start.6 = (f32[40,128]{1,0:T(8,128)S(1)}, f32[40,128]{1,0:T(8,128)S(1)}, u32[]{:S(2)}, u32[]{:S(2)}) collective-permute-start(f32[40,128]{1,0:T(8,128)S(1)} %get-tuple-element.34.refs_0_), channel_id=1, source_target_pairs={{0,4},{4,0},{8,12},{12,8},{1,5},{5,1},{9,13},{13,9},{2,6},{6,2},{1... | collective-permute-start | bytes 61448 | tf_op jit(solution)/shard_map/ppermute | solution.py:392
  22.7 3.1 %collective-permute-start.11 = (f32[8,128]{1,0:T(8,128)S(1)}, f32[8,128]{1,0:T(8,128)S(1)}, u32[]{:S(2)}, u32[]{:S(2)}) collective-permute-start(f32[8,128]{1,0:T(8,128)S(1)} %shard_map.89.refs_0_), channel_id=1, source_target_pairs={{0,3},{1,2},{2,1},{3,0},{4,7},{5,6},{6,5},{7,4},{8,11},{9,10},{10,... | collective-permute-start | bytes 12296 | tf_op jit(solution)/shard_map/ppermute | solution.py:392
  22.8 3.7 %collective-permute-start.10 = (f32[8,128]{1,0:T(8,128)S(1)}, f32[8,128]{1,0:T(8,128)S(1)}, u32[]{:S(2)}, u32[]{:S(2)}) collective-permute-start(f32[8,128]{1,0:T(8,128)S(1)} %shard_map.89.refs_0_), channel_id=1, source_target_pairs={{0,2},{1,3},{2,0},{3,1},{4,6},{5,7},{6,4},{7,5},{8,10},{9,11},{10,... | collective-permute-start | bytes 12296 | tf_op jit(solution)/shard_map/ppermute | solution.py:392
  24.4 2.1 %collective-permute-start.9 = (f32[8,128]{1,0:T(8,128)S(1)}, f32[8,128]{1,0:T(8,128)S(1)}, u32[]{:S(2)}, u32[]{:S(2)}) collective-permute-start(f32[8,128]{1,0:T(8,128)S(1)} %shard_map.89.refs_0_), channel_id=1, source_target_pairs={{0,1},{1,0},{2,3},{3,2},{4,5},{5,4},{6,7},{7,6},{8,9},{9,8},{10,11... | collective-permute-start | bytes 12296 | tf_op jit(solution)/shard_map/ppermute | solution.py:392
  26.9 5.5 %collective-permute-start.12 = (f32[8,128]{1,0:T(8,128)S(1)}, f32[8,128]{1,0:T(8,128)S(1)}, u32[]{:S(2)}, u32[]{:S(2)}) collective-permute-start(f32[8,128]{1,0:T(8,128)S(1)} %get-tuple-element.37), channel_id=1, source_target_pairs={{0,12},{4,8},{8,4},{12,0},{1,13},{5,9},{9,5},{13,1},{2,14},{6,10},... | collective-permute-start | bytes 12296 | tf_op jit(solution)/shard_map/ppermute | solution.py:392
  28.8 4.5 %collective-permute-start.13 = (f32[8,128]{1,0:T(8,128)S(1)}, f32[8,128]{1,0:T(8,128)S(1)}, u32[]{:S(2)}, u32[]{:S(2)}) collective-permute-start(f32[8,128]{1,0:T(8,128)S(1)} %get-tuple-element.38), channel_id=1, source_target_pairs={{0,8},{4,12},{8,0},{12,4},{1,9},{5,13},{9,1},{13,5},{2,10},{6,14},... | collective-permute-start | bytes 12296 | tf_op jit(solution)/shard_map/ppermute | solution.py:392
  30.0 3.6 %collective-permute-start.14 = (f32[8,128]{1,0:T(8,128)S(1)}, f32[8,128]{1,0:T(8,128)S(1)}, u32[]{:S(2)}, u32[]{:S(2)}) collective-permute-start(f32[8,128]{1,0:T(8,128)S(1)} %get-tuple-element.39), channel_id=1, source_target_pairs={{0,4},{4,0},{8,12},{12,8},{1,5},{5,1},{9,13},{13,9},{2,6},{6,2},{1... | collective-permute-start | bytes 12296 | tf_op jit(solution)/shard_map/ppermute | solution.py:392

commit v13 on v12

--- a/solution.py
+++ b/solution.py
@@ -103,7 +103,7 @@
 
     def products(j):
         at = [n * steps + j for n in range(sets)]
-        return [(obs_ref[s], g_ref[s] * x_scr[pl.ds(s, 1), :]) for s in at]
+        return [(obs_ref[s], g_ref[s // 8, s % 8] * x_scr[pl.ds(s, 1), :]) for s in at]
 
     def step(first, carry):
         coming = products(first * run)
@@ -183,18 +183,11 @@
     for copy in small + large:
         copy.start()
 
-    def turned(n, r):
-        return pltpu.make_async_copy(g_hbm.at[n, :, r], g_ref.at[8 * n + r], g_sems.at[8 * n + r])
-
-    def each_turned(action):
-        def step(n, carry):
-            for r in range(8):
-                action(turned(n, r))
-            return carry
-
-        lax.fori_loop(0, owners * capacity // 8, step, 0, unroll=owners <= 4)
-
-    each_turned(lambda copy: copy.start())
+    turned = [
+        pltpu.make_async_copy(g_hbm.at[:, :, r], g_ref.at[:, r], g_sems.at[r]) for r in range(8)
+    ]
+    for copy in turned:
+        copy.start()
     for copy in small:
         copy.wait()
 
@@ -256,9 +249,8 @@
             )
     observed_out[...] = pack_obs(observed_ref[...])
     weight_out[...] = pack_obs(weight_ref[...])
-    for copy in large:
+    for copy in large + turned:
         copy.wait()
-    each_turned(lambda copy: copy.wait())
 
 
 def first_model(order, *refs):
@@ -441,7 +433,7 @@
                 obs_tile,
                 like(prior_flux),
                 like(footprint),
-                ((slots, TILES, LANES), F32),
+                ((slots // 8, 8, TILES, LANES), F32),
                 ((slots,), jnp.int32),
             ],
             (*small, prior_flux, footprint, turned),
@@ -451,11 +443,11 @@
                 pltpu.SMEM(*like(slot_count)),
                 pltpu.SemaphoreType.DMA((len(small) + 3,)),
                 pltpu.SemaphoreType.DMA((owners,)),
-                pltpu.SemaphoreType.DMA((slots,)),
+                pltpu.SemaphoreType.DMA((8,)),
             ],
             hbm,
         )
-        order = [0, cells // 2, *range(1, cells // 2), *range(cells // 2 + 1, cells)]
+        order = [0, cells - 1, *range(1, cells - 1)]
         fluxes = exchange(flux, prior_flux, "cell", cells)
         m0, x0 = call(
             functools.partial(first_model, order),

time: 34.5 us -> 34.7 us (level)
  waiting for transfers between devices: 9.2 us -> 9.9 us
  Pallas kernels: 6.02 us -> 5.37 us
    ppermute x15, waiting for transfers between devices: 9.2 us -> 9.9 us  [send(): return lax.ppermute(value, axis, [(i, i ^ k) for i in range(size)])]
    pallas_call x7, Pallas kernels: 6.02 us -> 5.37 us  [call(): pl.pallas_call(body, out_shape=outs_at, in_specs=[smem if value is obs el...]
  transfers between devices with their start and end apart: 15 -> 15, of which waited for: 10 -> 10; matrix products, arithmetic and copies ran while one was open for 0% -> 0% of each run, Pallas kernels for 9% -> 7%
where the time goes in v13:
time: 34.7 us; the launch traced here: 34.5 us
  starting transfers between devices  18.5 us (53%)
  waiting for transfers between devices  9.9 us (29%)
  Pallas kernels  5.37 us (15%)
  between operations  0.7 us (2%)
    ppermute x15, starting transfers between devices, send(): return lax.ppermute(value, axis, [(i, i ^ k) for i in range(size)])  18.5 us
    ppermute x15, waiting for transfers between devices, send(): return lax.ppermute(value, axis, [(i, i ^ k) for i in range(size)])  9.9 us
    pallas_call x7, Pallas kernels, call(): pl.pallas_call(body, out_shape=outs_at, in_specs=[smem if value is obs el...  5.37 us
  transfers between devices with their start and end apart: 15, of which 10 were waited for; matrix products, arithmetic and copies ran while one was open for 0% of the time, Pallas kernels for 7%

profile of v13, /device:TPU:0, one launch (start us, length us, event | category | flops | bytes accessed | tf_op | source)
XLA Modules:
  0.0 34.5 jit_solution(728873712267627766)
XLA Ops:
  0.6 5.1 %collective-permute-start = (f32[8,512]{1,0:T(8,128)}, f32[8,512]{1,0:T(8,128)S(1)}, u32[]{:S(2)}, u32[]{:S(2)}) collective-permute-start(f32[8,512]{1,0:T(8,128)} %flux_hbm.1), channel_id=1, source_target_pairs={{0,12},{4,8},{8,4},{12,0},{1,13},{5,9},{9,5},{13,1},{2,14},{6,10},... | collective-permute-start | bytes 49160 | tf_op jit(solution)/shard_map/ppermute | solution.py:384
  5.8 0.6 %collective-permute-start.1 = (f32[8,512]{1,0:T(8,128)}, f32[8,512]{1,0:T(8,128)S(1)}, u32[]{:S(2)}, u32[]{:S(2)}) collective-permute-start(f32[8,512]{1,0:T(8,128)} %flux_hbm.1), channel_id=1, source_target_pairs={{0,4},{4,0},{8,12},{12,8},{1,5},{5,1},{9,13},{13,9},{2,6},{6,2},{1... | collective-permute-start | bytes 49160 | tf_op jit(solution)/shard_map/ppermute | solution.py:384
  6.4 1.8 %shard_map.86 = (bf16[64,384]{1,0:T(8,128)(2,1)S(1)}, f32[64,128]{1,0:T(8,128)S(1)}, bf16[64,24]{1,0:T(8,128)(2,1)S(1)}, f32[8,128]{1,0:T(8,128)S(1)}, f32[8,128...) custom-call(s32[1,1,4,16]{3,2,1,0:T(4,128)} %fslot_hbm.1, ...), custom_call_target="tpu_custom_call" | custom-call | tf_op jit(solution)/shard_map/pallas_call | solution.py:408
  8.2 2.4 %collective-permute-done.2.refs_3_ = f32[8,512]{1,0:T(8,128)S(1)} collective-permute-done((f32[8,512]{1,0:T(8,128)}, f32[8,512]{1,0:T(8,128)S(1)}, u32[]{:S(2)}, u32[]{:S(2)}) %collective-permute-start.2) | collective-permute-done | bytes 16416 | tf_op jit(solution)/shard_map/ppermute | solution.py:384
  10.6 0.6 %shard_map.87 = (f32[8,128]{1,0:T(8,128)S(1)}, f32[64,128]{1,0:T(8,128)S(1)}) custom-call(f32[8,512]{1,0:T(8,128)S(1)} %get-tuple-element.23.refs_0_, f32[8,512]{1,0:T(8,128)S(1)} %collective-permute-done.refs_1_, f32[8,512]{1,0:T(8,128)S(1)} %collective-permute-done.1.refs_2_, f32[8,512]{1,0:T(8,128)S(1)} %collective-permute-done.2.refs_3_, ...), custom_call_target="tpu_custom_call" | custom-call | tf_op jit(solution)/shard_map/pallas_call | solution.py:408
  11.2 0.1 collective-permute-start.5
  11.3 1.6 %collective-permute-start.4 = (f32[8,128]{1,0:T(8,128)S(1)}, f32[8,128]{1,0:T(8,128)S(1)}, u32[]{:S(2)}, u32[]{:S(2)}) collective-permute-start(f32[8,128]{1,0:T(8,128)S(1)} %get-tuple-element.28.refs_0_), channel_id=1, source_target_pairs={{0,2},{1,3},{2,0},{3,1},{4,6},{5,7},{6,4},{7,5},{8,10},{9,11},{10,... | collective-permute-start | bytes 12296 | tf_op jit(solution)/shard_map/ppermute | solution.py:384
  12.9 0.3 collective-permute-start.3
  13.2 1.2 %collective-permute-done.5.refs_3_ = f32[8,128]{1,0:T(8,128)S(1)} collective-permute-done((f32[8,128]{1,0:T(8,128)S(1)}, f32[8,128]{1,0:T(8,128)S(1)}, u32[]{:S(2)}, u32[]{:S(2)}) %collective-permute-start.5) | collective-permute-done | bytes 4128 | tf_op jit(solution)/shard_map/ppermute | solution.py:384
  14.3 0.7 %collective-permute-done.4.refs_2_ = f32[8,128]{1,0:T(8,128)S(1)} collective-permute-done((f32[8,128]{1,0:T(8,128)S(1)}, f32[8,128]{1,0:T(8,128)S(1)}, u32[]{:S(2)}, u32[]{:S(2)}) %collective-permute-start.4) | collective-permute-done | bytes 4128 | tf_op jit(solution)/shard_map/ppermute | solution.py:384
  15.0 0.4 %shard_map.88 = (f32[40,128]{1,0:T(8,128)S(1)}, f32[8,128]{1,0:T(8,128)S(1)}) custom-call(f32[8,128]{1,0:T(8,128)S(1)} %get-tuple-element.28.refs_0_, f32[8,128]{1,0:T(8,128)S(1)} %collective-permute-done.3.refs_1_, f32[8,128]{1,0:T(8,128)S(1)} %collective-permute-done.4.refs_2_, f32[8,128]{1,0:T(8,128)S(1)} %collective-permute-done.5.refs_3_, ...), custom_call_target="tpu_custom_call" | custom-call | tf_op jit(solution)/shard_map/pallas_call | solution.py:408
  15.4 1.6 %collective-permute-start.8 = (f32[40,128]{1,0:T(8,128)S(1)}, f32[40,128]{1,0:T(8,128)S(1)}, u32[]{:S(2)}, u32[]{:S(2)}) collective-permute-start(f32[40,128]{1,0:T(8,128)S(1)} %get-tuple-element.34.refs_0_), channel_id=1, source_target_pairs={{0,12},{4,8},{8,4},{12,0},{1,13},{5,9},{9,5},{13,1},{2,14},{6,10},... | collective-permute-start | bytes 61448 | tf_op jit(solution)/shard_map/ppermute | solution.py:384
  17.0 0.6 %collective-permute-start.7 = (f32[40,128]{1,0:T(8,128)S(1)}, f32[40,128]{1,0:T(8,128)S(1)}, u32[]{:S(2)}, u32[]{:S(2)}) collective-permute-start(f32[40,128]{1,0:T(8,128)S(1)} %get-tuple-element.34.refs_0_), channel_id=1, source_target_pairs={{0,8},{4,12},{8,0},{12,4},{1,9},{5,13},{9,1},{13,5},{2,10},{6,14},... | collective-permute-start | bytes 61448 | tf_op jit(solution)/shard_map/ppermute | solution.py:384
  17.6 2.3 %collective-permute-start.6 = (f32[40,128]{1,0:T(8,128)S(1)}, f32[40,128]{1,0:T(8,128)S(1)}, u32[]{:S(2)}, u32[]{:S(2)}) collective-permute-start(f32[40,128]{1,0:T(8,128)S(1)} %get-tuple-element.34.refs_0_), channel_id=1, source_target_pairs={{0,4},{4,0},{8,12},{12,8},{1,5},{5,1},{9,13},{13,9},{2,6},{6,2},{1... | collective-permute-start | bytes 61448 | tf_op jit(solution)/shard_map/ppermute | solution.py:384
  19.9 1.2 %collective-permute-done.8.refs_3_ = f32[40,128]{1,0:T(8,128)S(1)} collective-permute-done((f32[40,128]{1,0:T(8,128)S(1)}, f32[40,128]{1,0:T(8,128)S(1)}, u32[]{:S(2)}, u32[]{:S(2)}) %collective-permute-start.8) | collective-permute-done | bytes 20512 | tf_op jit(solution)/shard_map/ppermute | solution.py:384
  21.1 0.6 %collective-permute-done.7.refs_2_ = f32[40,128]{1,0:T(8,128)S(1)} collective-permute-done((f32[40,128]{1,0:T(8,128)S(1)}, f32[40,128]{1,0:T(8,128)S(1)}, u32[]{:S(2)}, u32[]{:S(2)}) %collective-permute-start.7) | collective-permute-done | bytes 20512 | tf_op jit(solution)/shard_map/ppermute | solution.py:384
  21.7 0.2 collective-permute-done.6.refs_1_
  21.9 0.6 %shard_map.89.refs_0_ = f32[8,128]{1,0:T(8,128)S(1)} custom-call(f32[40,128]{1,0:T(8,128)S(1)} %get-tuple-element.34.refs_0_, f32[40,128]{1,0:T(8,128)S(1)} %collective-permute-done.6.refs_1_, f32[40,128]{1,0:T(8,128)S(1)} %collective-permute-done.7.refs_2_, f32[40,128]{1,0:T(8,128)S(1)} %collective-permute-done.8.refs_3_, ...), custom_call_target="tpu_custom_call" | custom-call | tf_op jit(solution)/shard_map/pallas_call | solution.py:408
  22.5 0.1 collective-permute-start.11
  22.6 1.5 %collective-permute-start.10 = (f32[8,128]{1,0:T(8,128)S(1)}, f32[8,128]{1,0:T(8,128)S(1)}, u32[]{:S(2)}, u32[]{:S(2)}) collective-permute-start(f32[8,128]{1,0:T(8,128)S(1)} %shard_map.89.refs_0_), channel_id=1, source_target_pairs={{0,2},{1,3},{2,0},{3,1},{4,6},{5,7},{6,4},{7,5},{8,10},{9,11},{10,... | collective-permute-start | bytes 12296 | tf_op jit(solution)/shard_map/ppermute | solution.py:384
  24.1 0.3 collective-permute-start.9
  24.4 1.2 %collective-permute-done.11.refs_3_ = f32[8,128]{1,0:T(8,128)S(1)} collective-permute-done((f32[8,128]{1,0:T(8,128)S(1)}, f32[8,128]{1,0:T(8,128)S(1)}, u32[]{:S(2)}, u32[]{:S(2)}) %collective-permute-start.11) | collective-permute-done | bytes 4128 | tf_op jit(solution)/shard_map/ppermute | solution.py:384
  25.6 0.6 %collective-permute-done.10.refs_2_ = f32[8,128]{1,0:T(8,128)S(1)} collective-permute-done((f32[8,128]{1,0:T(8,128)S(1)}, f32[8,128]{1,0:T(8,128)S(1)}, u32[]{:S(2)}, u32[]{:S(2)}) %collective-permute-start.10) | collective-permute-done | bytes 4128 | tf_op jit(solution)/shard_map/ppermute | solution.py:384
  26.3 0.4 %shard_map.90 = (f32[8,128]{1,0:T(8,128)S(1)}, f32[8,128]{1,0:T(8,128)S(1)}, f32[8,128]{1,0:T(8,128)S(1)}, f32[8,128]{1,0:T(8,128)S(1)}, f32[8,128]{1,0:T(8,128)S(1)}) custom-call(f32[8,128]{1,0:T(8,128)S(1)} %shard_map.89.refs_0_, f32[8,128]{1,0:T(8,128)S(1)} %collective-permute-done.9.refs_1_, f32[8,128]{1,0:T(8,128)S(1)} %collective-permute-done.10.refs_2_, ...), custom_call_target="tpu_custom_call" | custom-call | tf_op jit(solution)/shard_map/pallas_call | solution.py:408
  26.7 2.4 %collective-permute-start.12 = (f32[8,128]{1,0:T(8,128)S(1)}, f32[8,128]{1,0:T(8,128)S(1)}, u32[]{:S(2)}, u32[]{:S(2)}) collective-permute-start(f32[8,128]{1,0:T(8,128)S(1)} %get-tuple-element.37), channel_id=1, source_target_pairs={{0,12},{4,8},{8,4},{12,0},{1,13},{5,9},{9,5},{13,1},{2,14},{6,10},... | collective-permute-start | bytes 12296 | tf_op jit(solution)/shard_map/ppermute | solution.py:384
  29.1 0.9 %collective-permute-start.13 = (f32[8,128]{1,0:T(8,128)S(1)}, f32[8,128]{1,0:T(8,128)S(1)}, u32[]{:S(2)}, u32[]{:S(2)}) collective-permute-start(f32[8,128]{1,0:T(8,128)S(1)} %get-tuple-element.38), channel_id=1, source_target_pairs={{0,8},{4,12},{8,0},{12,4},{1,9},{5,13},{9,1},{13,5},{2,10},{6,14},... | collective-permute-start | bytes 12296 | tf_op jit(solution)/shard_map/ppermute | solution.py:384
  30.1 1.1 %collective-permute-start.14 = (f32[8,128]{1,0:T(8,128)S(1)}, f32[8,128]{1,0:T(8,128)S(1)}, u32[]{:S(2)}, u32[]{:S(2)}) collective-permute-start(f32[8,128]{1,0:T(8,128)S(1)} %get-tuple-element.39), channel_id=1, source_target_pairs={{0,4},{4,0},{8,12},{12,8},{1,5},{5,1},{9,13},{13,9},{2,6},{6,2},{1... | collective-permute-start | bytes 12296 | tf_op jit(solution)/shard_map/ppermute | solution.py:384
  31.2 0.7 %shard_map.91 = (bf16[128,128]{1,0:T(8,128)(2,1)S(1)}, f32[1,512]{1,0:T(1,128)}) custom-call(f32[40,128]{1,0:T(8,128)S(1)} %get-tuple-element.34.refs_0_, f32[40,128]{1,0:T(8,128)S(1)} %collective-permute-done.6.refs_1_, f32[40,128]{1,0:T(8,128)S(1)} %collective-permute-done.7.refs_2_, f32[40,128]{1,0:T(8,128)S(1)} %collective-permute-done.8.refs_3_, ...), custom_call_target="tpu_custom_call" | custom-call | tf_op jit(solution)/shard_map/pallas_call | solution.py:408
  31.8 0.4 %collective-permute-done.12.refs_0_ = f32[8,128]{1,0:T(8,128)S(1)} collective-permute-done((f32[8,128]{1,0:T(8,128)S(1)}, f32[8,128]{1,0:T(8,128)S(1)}, u32[]{:S(2)}, u32[]{:S(2)}) %collective-permute-start.12) | collective-permute-done | bytes 4128 | tf_op jit(solution)/shard_map/ppermute | solution.py:384
  32.2 1.4 %collective-permute-done.13.refs_1_ = f32[8,128]{1,0:T(8,128)S(1)} collective-permute-done((f32[8,128]{1,0:T(8,128)S(1)}, f32[8,128]{1,0:T(8,128)S(1)}, u32[]{:S(2)}, u32[]{:S(2)}) %collective-permute-start.13) | collective-permute-done | bytes 4128 | tf_op jit(solution)/shard_map/ppermute | solution.py:384
  33.7 0.0 collective-permute-done.14.refs_2_
  33.7 0.8 %shard_map.92 = f32[8,512]{1,0:T(8,128)} custom-call(f32[8,128]{1,0:T(8,128)S(1)} %collective-permute-done.12.refs_0_, f32[8,128]{1,0:T(8,128)S(1)} %collective-permute-done.13.refs_1_, f32[8,128]{1,0:T(8,128)S(1)} %collective-permute-done.14.refs_2_, f32[8,128]{1,0:T(8,128)S(1)} %get-tuple-element.40.refs_3_, bf16[128,128]{1,0:T(8,128)(2,1)S(1)} %get-tuple-element.42.refs_4_), custom_call_target="tpu_custom_call" | custom-call | tf_op jit(solution)/shard_map/pallas_call | solution.py:408
  (5 shorter events, 0.0 us)
Async XLA Ops:
  0.6 7.5 %collective-permute-start = (f32[8,512]{1,0:T(8,128)}, f32[8,512]{1,0:T(8,128)S(1)}, u32[]{:S(2)}, u32[]{:S(2)}) collective-permute-start(f32[8,512]{1,0:T(8,128)} %flux_hbm.1), channel_id=1, source_target_pairs={{0,12},{4,8},{8,4},{12,0},{1,13},{5,9},{9,5},{13,1},{2,14},{6,10},... | collective-permute-start | bytes 49160 | tf_op jit(solution)/shard_map/ppermute | solution.py:384
  5.7 4.8 %collective-permute-start.2 = (f32[8,512]{1,0:T(8,128)}, f32[8,512]{1,0:T(8,128)S(1)}, u32[]{:S(2)}, u32[]{:S(2)}) collective-permute-start(f32[8,512]{1,0:T(8,128)} %flux_hbm.1), channel_id=1, source_target_pairs={{0,8},{4,12},{8,0},{12,4},{1,9},{5,13},{9,1},{13,5},{2,10},{6,14},... | collective-permute-start | bytes 49160 | tf_op jit(solution)/shard_map/ppermute | solution.py:384
  5.8 4.8 %collective-permute-start.1 = (f32[8,512]{1,0:T(8,128)}, f32[8,512]{1,0:T(8,128)S(1)}, u32[]{:S(2)}, u32[]{:S(2)}) collective-permute-start(f32[8,512]{1,0:T(8,128)} %flux_hbm.1), channel_id=1, source_target_pairs={{0,4},{4,0},{8,12},{12,8},{1,5},{5,1},{9,13},{13,9},{2,6},{6,2},{1... | collective-permute-start | bytes 49160 | tf_op jit(solution)/shard_map/ppermute | solution.py:384
  11.2 3.1 %collective-permute-start.5 = (f32[8,128]{1,0:T(8,128)S(1)}, f32[8,128]{1,0:T(8,128)S(1)}, u32[]{:S(2)}, u32[]{:S(2)}) collective-permute-start(f32[8,128]{1,0:T(8,128)S(1)} %get-tuple-element.28.refs_0_), channel_id=1, source_target_pairs={{0,3},{1,2},{2,1},{3,0},{4,7},{5,6},{6,5},{7,4},{8,11},{9,10},{10,... | collective-permute-start | bytes 12296 | tf_op jit(solution)/shard_map/ppermute | solution.py:384
  11.3 3.7 %collective-permute-start.4 = (f32[8,128]{1,0:T(8,128)S(1)}, f32[8,128]{1,0:T(8,128)S(1)}, u32[]{:S(2)}, u32[]{:S(2)}) collective-permute-start(f32[8,128]{1,0:T(8,128)S(1)} %get-tuple-element.28.refs_0_), channel_id=1, source_target_pairs={{0,2},{1,3},{2,0},{3,1},{4,6},{5,7},{6,4},{7,5},{8,10},{9,11},{10,... | collective-permute-start | bytes 12296 | tf_op jit(solution)/shard_map/ppermute | solution.py:384
  12.9 2.1 %collective-permute-start.3 = (f32[8,128]{1,0:T(8,128)S(1)}, f32[8,128]{1,0:T(8,128)S(1)}, u32[]{:S(2)}, u32[]{:S(2)}) collective-permute-start(f32[8,128]{1,0:T(8,128)S(1)} %get-tuple-element.28.refs_0_), channel_id=1, source_target_pairs={{0,1},{1,0},{2,3},{3,2},{4,5},{5,4},{6,7},{7,6},{8,9},{9,8},{10,11... | collective-permute-start | bytes 12296 | tf_op jit(solution)/shard_map/ppermute | solution.py:384
  15.4 5.7 %collective-permute-start.8 = (f32[40,128]{1,0:T(8,128)S(1)}, f32[40,128]{1,0:T(8,128)S(1)}, u32[]{:S(2)}, u32[]{:S(2)}) collective-permute-start(f32[40,128]{1,0:T(8,128)S(1)} %get-tuple-element.34.refs_0_), channel_id=1, source_target_pairs={{0,12},{4,8},{8,4},{12,0},{1,13},{5,9},{9,5},{13,1},{2,14},{6,10},... | collective-permute-start | bytes 61448 | tf_op jit(solution)/shard_map/ppermute | solution.py:384
  17.0 4.7 %collective-permute-start.7 = (f32[40,128]{1,0:T(8,128)S(1)}, f32[40,128]{1,0:T(8,128)S(1)}, u32[]{:S(2)}, u32[]{:S(2)}) collective-permute-start(f32[40,128]{1,0:T(8,128)S(1)} %get-tuple-element.34.refs_0_), channel_id=1, source_target_pairs={{0,8},{4,12},{8,0},{12,4},{1,9},{5,13},{9,1},{13,5},{2,10},{6,14},... | collective-permute-start | bytes 61448 | tf_op jit(solution)/shard_map/ppermute | solution.py:384
  17.6 4.3 %collective-permute-start.6 = (f32[40,128]{1,0:T(8,128)S(1)}, f32[40,128]{1,0:T(8,128)S(1)}, u32[]{:S(2)}, u32[]{:S(2)}) collective-permute-start(f32[40,128]{1,0:T(8,128)S(1)} %get-tuple-element.34.refs_0_), channel_id=1, source_target_pairs={{0,4},{4,0},{8,12},{12,8},{1,5},{5,1},{9,13},{13,9},{2,6},{6,2},{1... | collective-permute-start | bytes 61448 | tf_op jit(solution)/shard_map/ppermute | solution.py:384
  22.5 3.1 %collective-permute-start.11 = (f32[8,128]{1,0:T(8,128)S(1)}, f32[8,128]{1,0:T(8,128)S(1)}, u32[]{:S(2)}, u32[]{:S(2)}) collective-permute-start(f32[8,128]{1,0:T(8,128)S(1)} %shard_map.89.refs_0_), channel_id=1, source_target_pairs={{0,3},{1,2},{2,1},{3,0},{4,7},{5,6},{6,5},{7,4},{8,11},{9,10},{10,... | collective-permute-start | bytes 12296 | tf_op jit(solution)/shard_map/ppermute | solution.py:384
  22.6 3.7 %collective-permute-start.10 = (f32[8,128]{1,0:T(8,128)S(1)}, f32[8,128]{1,0:T(8,128)S(1)}, u32[]{:S(2)}, u32[]{:S(2)}) collective-permute-start(f32[8,128]{1,0:T(8,128)S(1)} %shard_map.89.refs_0_), channel_id=1, source_target_pairs={{0,2},{1,3},{2,0},{3,1},{4,6},{5,7},{6,4},{7,5},{8,10},{9,11},{10,... | collective-permute-start | bytes 12296 | tf_op jit(solution)/shard_map/ppermute | solution.py:384
  24.1 2.1 %collective-permute-start.9 = (f32[8,128]{1,0:T(8,128)S(1)}, f32[8,128]{1,0:T(8,128)S(1)}, u32[]{:S(2)}, u32[]{:S(2)}) collective-permute-start(f32[8,128]{1,0:T(8,128)S(1)} %shard_map.89.refs_0_), channel_id=1, source_target_pairs={{0,1},{1,0},{2,3},{3,2},{4,5},{5,4},{6,7},{7,6},{8,9},{9,8},{10,11... | collective-permute-start | bytes 12296 | tf_op jit(solution)/shard_map/ppermute | solution.py:384
  26.7 5.5 %collective-permute-start.12 = (f32[8,128]{1,0:T(8,128)S(1)}, f32[8,128]{1,0:T(8,128)S(1)}, u32[]{:S(2)}, u32[]{:S(2)}) collective-permute-start(f32[8,128]{1,0:T(8,128)S(1)} %get-tuple-element.37), channel_id=1, source_target_pairs={{0,12},{4,8},{8,4},{12,0},{1,13},{5,9},{9,5},{13,1},{2,14},{6,10},... | collective-permute-start | bytes 12296 | tf_op jit(solution)/shard_map/ppermute | solution.py:384
  29.1 4.5 %collective-permute-start.13 = (f32[8,128]{1,0:T(8,128)S(1)}, f32[8,128]{1,0:T(8,128)S(1)}, u32[]{:S(2)}, u32[]{:S(2)}) collective-permute-start(f32[8,128]{1,0:T(8,128)S(1)} %get-tuple-element.38), channel_id=1, source_target_pairs={{0,8},{4,12},{8,0},{12,4},{1,9},{5,13},{9,1},{13,5},{2,10},{6,14},... | collective-permute-start | bytes 12296 | tf_op jit(solution)/shard_map/ppermute | solution.py:384
  30.1 3.6 %collective-permute-start.14 = (f32[8,128]{1,0:T(8,128)S(1)}, f32[8,128]{1,0:T(8,128)S(1)}, u32[]{:S(2)}, u32[]{:S(2)}) collective-permute-start(f32[8,128]{1,0:T(8,128)S(1)} %get-tuple-element.39), channel_id=1, source_target_pairs={{0,4},{4,0},{8,12},{12,8},{1,5},{5,1},{9,13},{13,9},{2,6},{6,2},{1... | collective-permute-start | bytes 12296 | tf_op jit(solution)/shard_map/ppermute | solution.py:384

commit v14 on v13

--- a/solution.py
+++ b/solution.py
@@ -46,6 +46,10 @@
 
 def low(shape):
     return iota(shape, 1) < LANES // 2
+
+
+def in_turn(refs, order):
+    return [refs[0]] + [refs[1 + order.index(k)] for k in range(1, 1 + len(order))]
 
 
 def tree_sum(parts):
@@ -91,7 +95,7 @@
     return jnp.concatenate([h_ref[0, 0, o, :, start : start + size] for o in range(first, last)], axis=0)
 
 
-def forward(g_ref, obs_ref, x, x_scr, sums):
+def forward(g_ref, obs_ref, x, x_scr, sums, slot_of):
     slots = x.shape[0]
     sets = len(sums)
     x_scr[...] = x
@@ -103,7 +107,11 @@
 
     def products(j):
         at = [n * steps + j for n in range(sets)]
-        return [(obs_ref[s], g_ref[s // 8, s % 8] * x_scr[pl.ds(s, 1), :]) for s in at]
+        found = []
+        for i in at:
+            s = slot_of(i)
+            found.append((obs_ref[s], g_ref[s // 8, s % 8] * x_scr[pl.ds(i, 1), :]))
+        return found
 
     def step(first, carry):
         coming = products(first * run)
@@ -253,27 +261,48 @@
         copy.wait()
 
 
-def first_model(order, *refs):
-    parts = len(order)
-    g_ref, pick_flux_ref, target_ref, obs_ref, m_ref, x_ref, x_scr, *sums = refs[parts:]
-    flux = jnp.concatenate(
-        [
-            ref[:, LANES * t : LANES * (t + 1)]
-            for ref in [refs[order.index(k)] for k in range(parts)]
-            for t in range(CBLK_DEV // 2)
-        ],
-        axis=0,
-    )
-    pair = pick_rows(pick_flux_ref[...], flux)
-    odd = (target_ref[...].astype(jnp.int32) & 1) == 1
+def first_model(half, owners, *refs):
+    count = owners // 2
+    fluxes, refs = refs[:count], refs[count:]
+    if half:
+        fluxes = fluxes[::-1]
+        before_ref, *refs = refs
+    g_ref, pick_flux_ref, target_ref, obs_ref, m_ref, x_ref, x_scr, *sums = refs
+    me = lax.axis_index("cell")
+    capacity = target_ref.shape[0] // owners
+    absent = [jnp.zeros((BLOCKS // 2, LANES), F32)]
+    flux = []
+    for ref in fluxes:
+        rows = [ref[:, LANES * t : LANES * (t + 1)] for t in range(CBLK_DEV // 2)]
+        flux += absent + rows if half else rows + absent
+
+    def owner_rows(ref):
+        return jnp.concatenate(
+            [
+                ref[pl.ds(pl.multiple_of((me ^ (2 * n + half)) * capacity, capacity), capacity), :]
+                for n in range(count)
+            ],
+            axis=0,
+        )
+
+    pair = pick_rows(owner_rows(pick_flux_ref), jnp.concatenate(flux, axis=0))
+    odd = (owner_rows(target_ref).astype(jnp.int32) & 1) == 1
     x = jnp.where(odd != low(pair.shape), pair, half_swap(pair))
-    x_ref[...] = x
-    m_ref[...] = forward(g_ref, obs_ref, x, x_scr, sums)
-
-
-def first_adjoint(parts, *refs):
+    for n in range(count):
+        x_ref[n] = x[n * capacity : (n + 1) * capacity]
+
+    def slot_of(i):
+        return (me ^ (2 * (i // capacity) + half)) * capacity + i % capacity
+
+    m = forward(g_ref, obs_ref, x, x_scr, sums, slot_of)
+    m_ref[...] = m + before_ref[...] if half else m
+
+
+def first_adjoint(order, *refs):
+    parts = 1 + len(order)
+    m_parts = in_turn(refs, order)
     observed_ref, weight_ref, slot_obs_ref, index_ref, h_ref, message_ref, d_ref = refs[parts:]
-    d = weight_ref[...] * (tree_sum([m[...] for m in refs[:parts]]) - observed_ref[...])
+    d = weight_ref[...] * (tree_sum([m[...] for m in m_parts]) - observed_ref[...])
     d_ref[...] = d
     rows = h_ref.shape[3] // 2
     half = h_ref.shape[2] * rows
@@ -285,10 +314,11 @@
     message_ref[half:, :] = index_ref[...]
 
 
-def second_model(parts, *refs):
-    messages = refs[:parts]
-    cells = parts
-    target_ref, x_ref, g_ref, obs_ref, m_ref, x_scr, *sums = refs[parts:]
+def second_model(order, *refs):
+    parts = cells = 1 + len(order)
+    messages = in_turn(refs, order)
+    target_ref, even_ref, odd_ref, g_ref, obs_ref, m_ref, x_scr, *sums = refs[parts:]
+    me = lax.axis_index("cell")
     slots = target_ref.shape[0]
     half = slots // 2
     count = max(1, half // LANES)
@@ -311,16 +341,22 @@
         found = pick_rows(jnp.concatenate([pick] * 3, axis=1), values)
         total = found if total is None else total + found
     change = jnp.where(low((slots, LANES)), total[:slots], total[slots:])
-    x = x_ref[...] - 0.5 * (change + half_swap(change))
-    m_ref[...] = forward(g_ref, obs_ref, x, x_scr, sums)
-
-
-def second_adjoint(parts, *refs):
+    before = []
+    for o in range(cells):
+        far = me ^ o
+        before.append(jnp.where(far % 2 == 1, odd_ref[far // 2], even_ref[far // 2]))
+    x = jnp.concatenate(before, axis=0) - 0.5 * (change + half_swap(change))
+    m_ref[...] = forward(g_ref, obs_ref, x, x_scr, sums, lambda i: i)
+
+
+def second_adjoint(order, *refs):
+    parts = 1 + len(order)
+    m_parts = in_turn(refs, order)
     observed_ref, weight_ref, first_ref, slot_obs_ref, h_ref = refs[parts : parts + 5]
     *outs, d_ref, block_scr = refs[parts + 5 :]
     me = lax.axis_index("cell")
     owners = h_ref.shape[2]
-    d = weight_ref[...] * (tree_sum([m[...] for m in refs[:parts]]) - observed_ref[...])
+    d = weight_ref[...] * (tree_sum([m[...] for m in m_parts]) - observed_ref[...])
     d_ref[...] = d
 
     def store(o, block):
@@ -331,10 +367,10 @@
         outs[owners - 1 - k][...] = block_scr[me ^ k]
 
 
-def prepare_increment(parts, rows, *refs):
+def prepare_increment(order, rows, *refs):
+    parts = cells = 1 + len(order)
     d_ref, pick_ref, departure_ref = refs[parts:]
-    messages = refs[:parts]
-    cells = parts
+    messages = in_turn(refs, order)
     me = lax.axis_index("cell")
     half = cells * rows
     count = max(1, half // LANES)
@@ -384,8 +420,8 @@
     return lax.ppermute(value, axis, [(i, i ^ k) for i in range(size)])
 
 
-def exchange(own, sent, axis, size):
-    return [own] + [send(sent, axis, size, k) for k in range(size - 1, 0, -1)][::-1]
+def exchange(own, sent, axis, size, order):
+    return [own] + [send(sent, axis, size, k) for k in order]
 
 
 def make_local(cells, wins):
@@ -447,36 +483,46 @@
             ],
             hbm,
         )
-        order = [0, cells - 1, *range(1, cells - 1)]
-        fluxes = exchange(flux, prior_flux, "cell", cells)
-        m0, x0 = call(
-            functools.partial(first_model, order),
-            [obs_tile, slot_tile],
-            (*(fluxes[k] for k in order), by_slot, pick_flux, target, obs),
+        near_cells = list(range(1, cells))
+        far_cells, far_wins = near_cells[::-1], list(range(1, wins))[::-1]
+        last_wins = far_wins[-1:] + far_wins[:-1]
+        fluxes = exchange(flux, prior_flux, "cell", cells, near_cells)
+        half_tile = ((cells // 2, capacity, LANES), F32)
+        half_scratch = [pltpu.VMEM((slots // 2, LANES), F32)] + sum_scratch[1:]
+        m_even, x_even = call(
+            functools.partial(first_model, 0, owners),
+            [obs_tile, half_tile],
+            (*fluxes[::2], by_slot, pick_flux, target, obs),
+            half_scratch,
+        )
+        m0, x_odd = call(
+            functools.partial(first_model, 1, owners),
+            [obs_tile, half_tile],
+            (*fluxes[1::2][::-1], m_even, by_slot, pick_flux, target, obs),
+            half_scratch,
+        )
+        message, d0 = call(
+            functools.partial(first_adjoint, far_wins),
+            [((half + index_rows, LANES), F32), obs_tile],
+            (*exchange(m0, m0, "win", wins, far_wins), observed_t, weight_t, slot_obs, index, matrices),
+        )
+        messages = exchange(message, message, "cell", cells, far_cells)
+        (m1,) = call(
+            functools.partial(second_model, far_cells),
+            [obs_tile],
+            (*messages, target, x_even, x_odd, by_slot, obs),
             sum_scratch,
         )
-        message, d0 = call(
-            functools.partial(first_adjoint, wins),
-            [((half + index_rows, LANES), F32), obs_tile],
-            (*exchange(m0, m0, "win", wins), observed_t, weight_t, slot_obs, index, matrices),
-        )
-        messages = exchange(message, message, "cell", cells)
-        (m1,) = call(
-            functools.partial(second_model, cells),
-            [obs_tile],
-            (*messages, target, x0, by_slot, obs),
-            sum_scratch,
-        )
         *blocks, d1 = call(
-            functools.partial(second_adjoint, wins),
+            functools.partial(second_adjoint, last_wins),
             [((capacity // 2, LANES), F32)] * owners + [obs_tile],
-            (*exchange(m1, m1, "win", wins), observed_t, weight_t, d0, slot_obs, matrices),
+            (*exchange(m1, m1, "win", wins, last_wins), observed_t, weight_t, d0, slot_obs, matrices),
             [pltpu.VMEM((owners, capacity // 2, LANES), F32)],
         )
         arrays = [send(block, "cell", cells, cells - 1 - i) for i, block in enumerate(blocks[:-1])]
         arrays = [blocks[-1]] + arrays[::-1]
         pick, departure = call(
-            functools.partial(prepare_increment, cells, capacity // 2),
+            functools.partial(prepare_increment, far_cells, capacity // 2),
             [((2 * BLOCKS, max(LANES, half)), BF16), ((1, OBLK_DEV * OB), F32)],
             (*messages, d1),
         )

time: 34.7 us -> 34.5 us (level)
  waiting for transfers between devices: 9.9 us -> 9.26 us
  Pallas kernels: 5.37 us -> 5.9 us
    ppermute x15, waiting for transfers between devices: 9.9 us -> 9.26 us  [send(): return lax.ppermute(value, axis, [(i, i ^ k) for i in range(size)])]
    pallas_call x7 -> x8, Pallas kernels: 5.37 us -> 5.9 us  [call(): pl.pallas_call(body, out_shape=outs_at, in_specs=[smem if value is obs el...]
  transfers between devices with their start and end apart: 15 -> 15, of which waited for: 10 -> 10; matrix products, arithmetic and copies ran while one was open for 0% -> 0% of each run, Pallas kernels for 7% -> 9%
where the time goes in v14:
time: 34.5 us; the launch traced here: 34.3 us
  starting transfers between devices  18.4 us (53%)
  waiting for transfers between devices  9.26 us (27%)
  Pallas kernels  5.9 us (17%)
  between operations  0.71 us (2%)
    ppermute x15, starting transfers between devices, send(): return lax.ppermute(value, axis, [(i, i ^ k) for i in range(size)])  18.4 us
    ppermute x15, waiting for transfers between devices, send(): return lax.ppermute(value, axis, [(i, i ^ k) for i in range(size)])  9.26 us
    pallas_call x8, Pallas kernels, call(): pl.pallas_call(body, out_shape=outs_at, in_specs=[smem if value is obs el...  5.9 us
  transfers between devices with their start and end apart: 15, of which 10 were waited for; matrix products, arithmetic and copies ran while one was open for 0% of the time, Pallas kernels for 9%

profile of v14, /device:TPU:0, one launch (start us, length us, event | category | flops | bytes accessed | tf_op | source)
XLA Modules:
  0.0 34.3 jit_solution(17347124018794084406)
XLA Ops:
  0.6 4.1 %collective-permute-start.2 = (f32[8,512]{1,0:T(8,128)}, f32[8,512]{1,0:T(8,128)S(1)}, u32[]{:S(2)}, u32[]{:S(2)}) collective-permute-start(f32[8,512]{1,0:T(8,128)} %flux_hbm.1), channel_id=1, source_target_pairs={{0,8},{4,12},{8,0},{12,4},{1,9},{5,13},{9,1},{13,5},{2,10},{6,14},... | collective-permute-start | bytes 49160 | tf_op jit(solution)/shard_map/ppermute | solution.py:420
  4.7 1.3 %collective-permute-start = (f32[8,512]{1,0:T(8,128)}, f32[8,512]{1,0:T(8,128)S(1)}, u32[]{:S(2)}, u32[]{:S(2)}) collective-permute-start(f32[8,512]{1,0:T(8,128)} %flux_hbm.1), channel_id=1, source_target_pairs={{0,12},{4,8},{8,4},{12,0},{1,13},{5,9},{9,5},{13,1},{2,14},{6,10},... | collective-permute-start | bytes 49160 | tf_op jit(solution)/shard_map/ppermute | solution.py:420
  6.1 0.2 collective-permute-start.1
  6.3 1.8 %shard_map.86 = (bf16[64,384]{1,0:T(8,128)(2,1)S(1)}, f32[64,128]{1,0:T(8,128)S(1)}, bf16[64,24]{1,0:T(8,128)(2,1)S(1)}, f32[8,128]{1,0:T(8,128)S(1)}, f32[8,128...) custom-call(s32[1,1,4,16]{3,2,1,0:T(4,128)} %fslot_hbm.1, ...), custom_call_target="tpu_custom_call" | custom-call | tf_op jit(solution)/shard_map/pallas_call | solution.py:444
  8.1 0.6 %shard_map.87 = (f32[8,128]{1,0:T(8,128)S(1)}, f32[2,16,128]{2,1,0:T(8,128)S(1)}) custom-call(f32[8,512]{1,0:T(8,128)S(1)} %get-tuple-element.25.refs_0_, f32[8,512]{1,0:T(8,128)S(1)} %collective-permute-done.2.refs_1_, f32[8,8,32,128]{3,2,1,0:T(8,128)S(1)} %get-tuple-element.26.refs_2_.refs_3_.refs_7_, ...), custom_call_target="tpu_custom_call" | custom-call | tf_op jit(solution)/shard_map/pallas_call | solution.py:444
  8.7 1.8 %collective-permute-done.refs_0_ = f32[8,512]{1,0:T(8,128)S(1)} collective-permute-done((f32[8,512]{1,0:T(8,128)}, f32[8,512]{1,0:T(8,128)S(1)}, u32[]{:S(2)}, u32[]{:S(2)}) %collective-permute-start) | collective-permute-done | bytes 16416 | tf_op jit(solution)/shard_map/ppermute | solution.py:420
  10.5 0.6 %shard_map.88 = (f32[8,128]{1,0:T(8,128)S(1)}, f32[2,16,128]{2,1,0:T(8,128)S(1)}) custom-call(f32[8,512]{1,0:T(8,128)S(1)} %collective-permute-done.refs_0_, f32[8,512]{1,0:T(8,128)S(1)} %collective-permute-done.1.refs_1_, f32[8,128]{1,0:T(8,128)S(1)} %get-tuple-element.30.refs_2_, f32[8,8,32,128]{3,2,1,0:T(8,128)S(1)} %get-tuple-element.26.refs_2_.refs_3_.refs_7_, ...), custom_call_target="tpu_custom_call" | custom-call | tf_op jit(solution)/shard_map/pallas_call | solution.py:444
  11.1 0.1 collective-permute-start.3
  11.1 1.6 %collective-permute-start.4 = (f32[8,128]{1,0:T(8,128)S(1)}, f32[8,128]{1,0:T(8,128)S(1)}, u32[]{:S(2)}, u32[]{:S(2)}) collective-permute-start(f32[8,128]{1,0:T(8,128)S(1)} %get-tuple-element.31.refs_0_), channel_id=1, source_target_pairs={{0,2},{1,3},{2,0},{3,1},{4,6},{5,7},{6,4},{7,5},{8,10},{9,11},{10,... | collective-permute-start | bytes 12296 | tf_op jit(solution)/shard_map/ppermute | solution.py:420
  12.7 0.3 collective-permute-start.5
  13.0 1.2 %collective-permute-done.3.refs_1_ = f32[8,128]{1,0:T(8,128)S(1)} collective-permute-done((f32[8,128]{1,0:T(8,128)S(1)}, f32[8,128]{1,0:T(8,128)S(1)}, u32[]{:S(2)}, u32[]{:S(2)}) %collective-permute-start.3) | collective-permute-done | bytes 4128 | tf_op jit(solution)/shard_map/ppermute | solution.py:420
  14.2 0.7 %collective-permute-done.4.refs_2_ = f32[8,128]{1,0:T(8,128)S(1)} collective-permute-done((f32[8,128]{1,0:T(8,128)S(1)}, f32[8,128]{1,0:T(8,128)S(1)}, u32[]{:S(2)}, u32[]{:S(2)}) %collective-permute-start.4) | collective-permute-done | bytes 4128 | tf_op jit(solution)/shard_map/ppermute | solution.py:420
  14.8 0.4 %shard_map.89 = (f32[40,128]{1,0:T(8,128)S(1)}, f32[8,128]{1,0:T(8,128)S(1)}) custom-call(f32[8,128]{1,0:T(8,128)S(1)} %get-tuple-element.31.refs_0_, f32[8,128]{1,0:T(8,128)S(1)} %collective-permute-done.3.refs_1_, f32[8,128]{1,0:T(8,128)S(1)} %collective-permute-done.4.refs_2_, f32[8,128]{1,0:T(8,128)S(1)} %collective-permute-done.5.refs_3_, ...), custom_call_target="tpu_custom_call" | custom-call | tf_op jit(solution)/shard_map/pallas_call | solution.py:444
  15.3 2.1 %collective-permute-start.6 = (f32[40,128]{1,0:T(8,128)S(1)}, f32[40,128]{1,0:T(8,128)S(1)}, u32[]{:S(2)}, u32[]{:S(2)}) collective-permute-start(f32[40,128]{1,0:T(8,128)S(1)} %get-tuple-element.37.refs_0_), channel_id=1, source_target_pairs={{0,12},{4,8},{8,4},{12,0},{1,13},{5,9},{9,5},{13,1},{2,14},{6,10},... | collective-permute-start | bytes 61448 | tf_op jit(solution)/shard_map/ppermute | solution.py:420
  17.4 2.4 %collective-permute-start.8 = (f32[40,128]{1,0:T(8,128)S(1)}, f32[40,128]{1,0:T(8,128)S(1)}, u32[]{:S(2)}, u32[]{:S(2)}) collective-permute-start(f32[40,128]{1,0:T(8,128)S(1)} %get-tuple-element.37.refs_0_), channel_id=1, source_target_pairs={{0,4},{4,0},{8,12},{12,8},{1,5},{5,1},{9,13},{13,9},{2,6},{6,2},{1... | collective-permute-start | bytes 61448 | tf_op jit(solution)/shard_map/ppermute | solution.py:420
  19.7 1.2 %collective-permute-done.6.refs_1_ = f32[40,128]{1,0:T(8,128)S(1)} collective-permute-done((f32[40,128]{1,0:T(8,128)S(1)}, f32[40,128]{1,0:T(8,128)S(1)}, u32[]{:S(2)}, u32[]{:S(2)}) %collective-permute-start.6) | collective-permute-done | bytes 20512 | tf_op jit(solution)/shard_map/ppermute | solution.py:420
  20.9 1.1 %collective-permute-done.7.refs_2_ = f32[40,128]{1,0:T(8,128)S(1)} collective-permute-done((f32[40,128]{1,0:T(8,128)S(1)}, f32[40,128]{1,0:T(8,128)S(1)}, u32[]{:S(2)}, u32[]{:S(2)}) %collective-permute-start.7) | collective-permute-done | bytes 20512 | tf_op jit(solution)/shard_map/ppermute | solution.py:420
  22.0 0.6 %shard_map.90.refs_0_ = f32[8,128]{1,0:T(8,128)S(1)} custom-call(f32[40,128]{1,0:T(8,128)S(1)} %get-tuple-element.37.refs_0_, f32[40,128]{1,0:T(8,128)S(1)} %collective-permute-done.6.refs_1_, f32[40,128]{1,0:T(8,128)S(1)} %collective-permute-done.7.refs_2_, f32[40,128]{1,0:T(8,128)S(1)} %collective-permute-done.8.refs_3_, ...), custom_call_target="tpu_custom_call" | custom-call | tf_op jit(solution)/shard_map/pallas_call | solution.py:444
  22.7 0.1 collective-permute-start.10
  22.8 1.5 %collective-permute-start.11 = (f32[8,128]{1,0:T(8,128)S(1)}, f32[8,128]{1,0:T(8,128)S(1)}, u32[]{:S(2)}, u32[]{:S(2)}) collective-permute-start(f32[8,128]{1,0:T(8,128)S(1)} %shard_map.90.refs_0_), channel_id=1, source_target_pairs={{0,2},{1,3},{2,0},{3,1},{4,6},{5,7},{6,4},{7,5},{8,10},{9,11},{10,... | collective-permute-start | bytes 12296 | tf_op jit(solution)/shard_map/ppermute | solution.py:420
  24.3 0.3 collective-permute-start.9
  24.6 1.2 %collective-permute-done.10.refs_2_ = f32[8,128]{1,0:T(8,128)S(1)} collective-permute-done((f32[8,128]{1,0:T(8,128)S(1)}, f32[8,128]{1,0:T(8,128)S(1)}, u32[]{:S(2)}, u32[]{:S(2)}) %collective-permute-start.10) | collective-permute-done | bytes 4128 | tf_op jit(solution)/shard_map/ppermute | solution.py:420
  25.8 0.6 %collective-permute-done.11.refs_3_ = f32[8,128]{1,0:T(8,128)S(1)} collective-permute-done((f32[8,128]{1,0:T(8,128)S(1)}, f32[8,128]{1,0:T(8,128)S(1)}, u32[]{:S(2)}, u32[]{:S(2)}) %collective-permute-start.11) | collective-permute-done | bytes 4128 | tf_op jit(solution)/shard_map/ppermute | solution.py:420
  26.4 0.4 %shard_map.91 = (f32[8,128]{1,0:T(8,128)S(1)}, f32[8,128]{1,0:T(8,128)S(1)}, f32[8,128]{1,0:T(8,128)S(1)}, f32[8,128]{1,0:T(8,128)S(1)}, f32[8,128]{1,0:T(8,128)S(1)}) custom-call(f32[8,128]{1,0:T(8,128)S(1)} %shard_map.90.refs_0_, f32[8,128]{1,0:T(8,128)S(1)} %collective-permute-done.9.refs_1_, f32[8,128]{1,0:T(8,128)S(1)} %collective-permute-done.10.refs_2_, ...), custom_call_target="tpu_custom_call" | custom-call | tf_op jit(solution)/shard_map/pallas_call | solution.py:444
  26.9 1.9 %collective-permute-start.12 = (f32[8,128]{1,0:T(8,128)S(1)}, f32[8,128]{1,0:T(8,128)S(1)}, u32[]{:S(2)}, u32[]{:S(2)}) collective-permute-start(f32[8,128]{1,0:T(8,128)S(1)} %get-tuple-element.41), channel_id=1, source_target_pairs={{0,12},{4,8},{8,4},{12,0},{1,13},{5,9},{9,5},{13,1},{2,14},{6,10},... | collective-permute-start | bytes 12296 | tf_op jit(solution)/shard_map/ppermute | solution.py:420
  28.8 1.1 %collective-permute-start.13 = (f32[8,128]{1,0:T(8,128)S(1)}, f32[8,128]{1,0:T(8,128)S(1)}, u32[]{:S(2)}, u32[]{:S(2)}) collective-permute-start(f32[8,128]{1,0:T(8,128)S(1)} %get-tuple-element.42), channel_id=1, source_target_pairs={{0,8},{4,12},{8,0},{12,4},{1,9},{5,13},{9,1},{13,5},{2,10},{6,14},... | collective-permute-start | bytes 12296 | tf_op jit(solution)/shard_map/ppermute | solution.py:420
  29.9 1.4 %collective-permute-start.14 = (f32[8,128]{1,0:T(8,128)S(1)}, f32[8,128]{1,0:T(8,128)S(1)}, u32[]{:S(2)}, u32[]{:S(2)}) collective-permute-start(f32[8,128]{1,0:T(8,128)S(1)} %get-tuple-element.43), channel_id=1, source_target_pairs={{0,4},{4,0},{8,12},{12,8},{1,5},{5,1},{9,13},{13,9},{2,6},{6,2},{1... | collective-permute-start | bytes 12296 | tf_op jit(solution)/shard_map/ppermute | solution.py:420
  31.3 0.7 %shard_map.92 = (bf16[128,128]{1,0:T(8,128)(2,1)S(1)}, f32[1,512]{1,0:T(1,128)}) custom-call(f32[40,128]{1,0:T(8,128)S(1)} %get-tuple-element.37.refs_0_, f32[40,128]{1,0:T(8,128)S(1)} %collective-permute-done.6.refs_1_, f32[40,128]{1,0:T(8,128)S(1)} %collective-permute-done.7.refs_2_, f32[40,128]{1,0:T(8,128)S(1)} %collective-permute-done.8.refs_3_, ...), custom_call_target="tpu_custom_call" | custom-call | tf_op jit(solution)/shard_map/pallas_call | solution.py:444
  32.0 0.4 %collective-permute-done.12.refs_0_ = f32[8,128]{1,0:T(8,128)S(1)} collective-permute-done((f32[8,128]{1,0:T(8,128)S(1)}, f32[8,128]{1,0:T(8,128)S(1)}, u32[]{:S(2)}, u32[]{:S(2)}) %collective-permute-start.12) | collective-permute-done | bytes 4128 | tf_op jit(solution)/shard_map/ppermute | solution.py:420
  32.4 0.9 %collective-permute-done.13.refs_1_ = f32[8,128]{1,0:T(8,128)S(1)} collective-permute-done((f32[8,128]{1,0:T(8,128)S(1)}, f32[8,128]{1,0:T(8,128)S(1)}, u32[]{:S(2)}, u32[]{:S(2)}) %collective-permute-start.13) | collective-permute-done | bytes 4128 | tf_op jit(solution)/shard_map/ppermute | solution.py:420
  33.3 0.2 collective-permute-done.14.refs_2_
  33.5 0.8 %shard_map.93 = f32[8,512]{1,0:T(8,128)} custom-call(f32[8,128]{1,0:T(8,128)S(1)} %collective-permute-done.12.refs_0_, f32[8,128]{1,0:T(8,128)S(1)} %collective-permute-done.13.refs_1_, f32[8,128]{1,0:T(8,128)S(1)} %collective-permute-done.14.refs_2_, f32[8,128]{1,0:T(8,128)S(1)} %get-tuple-element.44.refs_3_, bf16[128,128]{1,0:T(8,128)(2,1)S(1)} %get-tuple-element.46.refs_4_), custom_call_target="tpu_custom_call" | custom-call | tf_op jit(solution)/shard_map/pallas_call | solution.py:444
  (6 shorter events, 0.0 us)
Async XLA Ops:
  0.6 7.5 %collective-permute-start.2 = (f32[8,512]{1,0:T(8,128)}, f32[8,512]{1,0:T(8,128)S(1)}, u32[]{:S(2)}, u32[]{:S(2)}) collective-permute-start(f32[8,512]{1,0:T(8,128)} %flux_hbm.1), channel_id=1, source_target_pairs={{0,8},{4,12},{8,0},{12,4},{1,9},{5,13},{9,1},{13,5},{2,10},{6,14},... | collective-permute-start | bytes 49160 | tf_op jit(solution)/shard_map/ppermute | solution.py:420
  4.7 5.7 %collective-permute-start = (f32[8,512]{1,0:T(8,128)}, f32[8,512]{1,0:T(8,128)S(1)}, u32[]{:S(2)}, u32[]{:S(2)}) collective-permute-start(f32[8,512]{1,0:T(8,128)} %flux_hbm.1), channel_id=1, source_target_pairs={{0,12},{4,8},{8,4},{12,0},{1,13},{5,9},{9,5},{13,1},{2,14},{6,10},... | collective-permute-start | bytes 49160 | tf_op jit(solution)/shard_map/ppermute | solution.py:420
  6.1 4.4 %collective-permute-start.1 = (f32[8,512]{1,0:T(8,128)}, f32[8,512]{1,0:T(8,128)S(1)}, u32[]{:S(2)}, u32[]{:S(2)}) collective-permute-start(f32[8,512]{1,0:T(8,128)} %flux_hbm.1), channel_id=1, source_target_pairs={{0,4},{4,0},{8,12},{12,8},{1,5},{5,1},{9,13},{13,9},{2,6},{6,2},{1... | collective-permute-start | bytes 49160 | tf_op jit(solution)/shard_map/ppermute | solution.py:420
  11.1 3.1 %collective-permute-start.3 = (f32[8,128]{1,0:T(8,128)S(1)}, f32[8,128]{1,0:T(8,128)S(1)}, u32[]{:S(2)}, u32[]{:S(2)}) collective-permute-start(f32[8,128]{1,0:T(8,128)S(1)} %get-tuple-element.31.refs_0_), channel_id=1, source_target_pairs={{0,3},{1,2},{2,1},{3,0},{4,7},{5,6},{6,5},{7,4},{8,11},{9,10},{10,... | collective-permute-start | bytes 12296 | tf_op jit(solution)/shard_map/ppermute | solution.py:420
  11.1 3.7 %collective-permute-start.4 = (f32[8,128]{1,0:T(8,128)S(1)}, f32[8,128]{1,0:T(8,128)S(1)}, u32[]{:S(2)}, u32[]{:S(2)}) collective-permute-start(f32[8,128]{1,0:T(8,128)S(1)} %get-tuple-element.31.refs_0_), channel_id=1, source_target_pairs={{0,2},{1,3},{2,0},{3,1},{4,6},{5,7},{6,4},{7,5},{8,10},{9,11},{10,... | collective-permute-start | bytes 12296 | tf_op jit(solution)/shard_map/ppermute | solution.py:420
  12.7 2.1 %collective-permute-start.5 = (f32[8,128]{1,0:T(8,128)S(1)}, f32[8,128]{1,0:T(8,128)S(1)}, u32[]{:S(2)}, u32[]{:S(2)}) collective-permute-start(f32[8,128]{1,0:T(8,128)S(1)} %get-tuple-element.31.refs_0_), channel_id=1, source_target_pairs={{0,1},{1,0},{2,3},{3,2},{4,5},{5,4},{6,7},{7,6},{8,9},{9,8},{10,11... | collective-permute-start | bytes 12296 | tf_op jit(solution)/shard_map/ppermute | solution.py:420
  15.3 5.7 %collective-permute-start.6 = (f32[40,128]{1,0:T(8,128)S(1)}, f32[40,128]{1,0:T(8,128)S(1)}, u32[]{:S(2)}, u32[]{:S(2)}) collective-permute-start(f32[40,128]{1,0:T(8,128)S(1)} %get-tuple-element.37.refs_0_), channel_id=1, source_target_pairs={{0,12},{4,8},{8,4},{12,0},{1,13},{5,9},{9,5},{13,1},{2,14},{6,10},... | collective-permute-start | bytes 61448 | tf_op jit(solution)/shard_map/ppermute | solution.py:420
  17.3 4.7 %collective-permute-start.7 = (f32[40,128]{1,0:T(8,128)S(1)}, f32[40,128]{1,0:T(8,128)S(1)}, u32[]{:S(2)}, u32[]{:S(2)}) collective-permute-start(f32[40,128]{1,0:T(8,128)S(1)} %get-tuple-element.37.refs_0_), channel_id=1, source_target_pairs={{0,8},{4,12},{8,0},{12,4},{1,9},{5,13},{9,1},{13,5},{2,10},{6,14},... | collective-permute-start | bytes 61448 | tf_op jit(solution)/shard_map/ppermute | solution.py:420
  17.4 4.7 %collective-permute-start.8 = (f32[40,128]{1,0:T(8,128)S(1)}, f32[40,128]{1,0:T(8,128)S(1)}, u32[]{:S(2)}, u32[]{:S(2)}) collective-permute-start(f32[40,128]{1,0:T(8,128)S(1)} %get-tuple-element.37.refs_0_), channel_id=1, source_target_pairs={{0,4},{4,0},{8,12},{12,8},{1,5},{5,1},{9,13},{13,9},{2,6},{6,2},{1... | collective-permute-start | bytes 61448 | tf_op jit(solution)/shard_map/ppermute | solution.py:420
  22.7 3.1 %collective-permute-start.10 = (f32[8,128]{1,0:T(8,128)S(1)}, f32[8,128]{1,0:T(8,128)S(1)}, u32[]{:S(2)}, u32[]{:S(2)}) collective-permute-start(f32[8,128]{1,0:T(8,128)S(1)} %shard_map.90.refs_0_), channel_id=1, source_target_pairs={{0,3},{1,2},{2,1},{3,0},{4,7},{5,6},{6,5},{7,4},{8,11},{9,10},{10,... | collective-permute-start | bytes 12296 | tf_op jit(solution)/shard_map/ppermute | solution.py:420
  22.8 3.7 %collective-permute-start.11 = (f32[8,128]{1,0:T(8,128)S(1)}, f32[8,128]{1,0:T(8,128)S(1)}, u32[]{:S(2)}, u32[]{:S(2)}) collective-permute-start(f32[8,128]{1,0:T(8,128)S(1)} %shard_map.90.refs_0_), channel_id=1, source_target_pairs={{0,2},{1,3},{2,0},{3,1},{4,6},{5,7},{6,4},{7,5},{8,10},{9,11},{10,... | collective-permute-start | bytes 12296 | tf_op jit(solution)/shard_map/ppermute | solution.py:420
  24.3 2.1 %collective-permute-start.9 = (f32[8,128]{1,0:T(8,128)S(1)}, f32[8,128]{1,0:T(8,128)S(1)}, u32[]{:S(2)}, u32[]{:S(2)}) collective-permute-start(f32[8,128]{1,0:T(8,128)S(1)} %shard_map.90.refs_0_), channel_id=1, source_target_pairs={{0,1},{1,0},{2,3},{3,2},{4,5},{5,4},{6,7},{7,6},{8,9},{9,8},{10,11... | collective-permute-start | bytes 12296 | tf_op jit(solution)/shard_map/ppermute | solution.py:420
  26.9 5.5 %collective-permute-start.12 = (f32[8,128]{1,0:T(8,128)S(1)}, f32[8,128]{1,0:T(8,128)S(1)}, u32[]{:S(2)}, u32[]{:S(2)}) collective-permute-start(f32[8,128]{1,0:T(8,128)S(1)} %get-tuple-element.41), channel_id=1, source_target_pairs={{0,12},{4,8},{8,4},{12,0},{1,13},{5,9},{9,5},{13,1},{2,14},{6,10},... | collective-permute-start | bytes 12296 | tf_op jit(solution)/shard_map/ppermute | solution.py:420
  28.8 4.5 %collective-permute-start.13 = (f32[8,128]{1,0:T(8,128)S(1)}, f32[8,128]{1,0:T(8,128)S(1)}, u32[]{:S(2)}, u32[]{:S(2)}) collective-permute-start(f32[8,128]{1,0:T(8,128)S(1)} %get-tuple-element.42), channel_id=1, source_target_pairs={{0,8},{4,12},{8,0},{12,4},{1,9},{5,13},{9,1},{13,5},{2,10},{6,14},... | collective-permute-start | bytes 12296 | tf_op jit(solution)/shard_map/ppermute | solution.py:420
  29.9 3.6 %collective-permute-start.14 = (f32[8,128]{1,0:T(8,128)S(1)}, f32[8,128]{1,0:T(8,128)S(1)}, u32[]{:S(2)}, u32[]{:S(2)}) collective-permute-start(f32[8,128]{1,0:T(8,128)S(1)} %get-tuple-element.43), channel_id=1, source_target_pairs={{0,4},{4,0},{8,12},{12,8},{1,5},{5,1},{9,13},{13,9},{2,6},{6,2},{1... | collective-permute-start | bytes 12296 | tf_op jit(solution)/shard_map/ppermute | solution.py:420

commit v15 on v13

--- a/solution.py
+++ b/solution.py
@@ -99,7 +99,7 @@
         ref[...] = jnp.zeros(ref.shape, F32)
 
     steps = slots // sets
-    run = min(steps, 16)
+    run = min(steps, 32)
 
     def products(j):
         at = [n * steps + j for n in range(sets)]
@@ -419,7 +419,7 @@
 
         obs_tile = ((OBLK_DEV, LANES), F32)
         slot_tile = ((slots, LANES), F32)
-        sum_scratch = [pltpu.VMEM(*slot_tile)] + [pltpu.VMEM((OBLK_DEV + 1, TILES, LANES), F32)] * 4
+        sum_scratch = [pltpu.VMEM(*slot_tile)] + [pltpu.VMEM((OBLK_DEV + 1, TILES, LANES), F32)] * 2
         small = (flux_slot, obs_slot, slot_count, observed, obs_weight)
         turned = footprint.reshape(slots // 8, 8, TILES, LANES).transpose(0, 2, 1, 3)
         pick_flux, target, slot_obs, index, observed_t, weight_t, flux, matrices, by_slot, obs = call(
@@ -447,7 +447,7 @@
             ],
             hbm,
         )
-        order = [0, cells - 1, *range(1, cells - 1)]
+        order = [0, cells // 2, *range(1, cells // 2), *range(cells // 2 + 1, cells)]
         fluxes = exchange(flux, prior_flux, "cell", cells)
         m0, x0 = call(
             functools.partial(first_model, order),

time: 34.7 us -> 34.6 us (level)
  no operation moved by 1% of the time
where the time goes in v15:
time: 34.6 us; the launch traced here: 34.4 us
  starting transfers between devices  18.5 us (53%)
  waiting for transfers between devices  9.82 us (28%)
  Pallas kernels  5.45 us (16%)
  between operations  0.7 us (2%)
    ppermute x15, starting transfers between devices, send(): return lax.ppermute(value, axis, [(i, i ^ k) for i in range(size)])  18.5 us
    ppermute x15, waiting for transfers between devices, send(): return lax.ppermute(value, axis, [(i, i ^ k) for i in range(size)])  9.82 us
    pallas_call x7, Pallas kernels, call(): pl.pallas_call(body, out_shape=outs_at, in_specs=[smem if value is obs el...  5.45 us
  transfers between devices with their start and end apart: 15, of which 10 were waited for; matrix products, arithmetic and copies ran while one was open for 0% of the time, Pallas kernels for 7%

profile of v15, /device:TPU:0, one launch (start us, length us, event | category | flops | bytes accessed | tf_op | source)
XLA Modules:
  0.0 34.4 jit_solution(8065098733601762769)
XLA Ops:
  0.6 4.1 %collective-permute-start = (f32[8,512]{1,0:T(8,128)}, f32[8,512]{1,0:T(8,128)S(1)}, u32[]{:S(2)}, u32[]{:S(2)}) collective-permute-start(f32[8,512]{1,0:T(8,128)} %flux_hbm.1), channel_id=1, source_target_pairs={{0,8},{4,12},{8,0},{12,4},{1,9},{5,13},{9,1},{13,5},{2,10},{6,14},... | collective-permute-start | bytes 49160 | tf_op jit(solution)/shard_map/ppermute | solution.py:384
  4.7 1.3 %collective-permute-start.2 = (f32[8,512]{1,0:T(8,128)}, f32[8,512]{1,0:T(8,128)S(1)}, u32[]{:S(2)}, u32[]{:S(2)}) collective-permute-start(f32[8,512]{1,0:T(8,128)} %flux_hbm.1), channel_id=1, source_target_pairs={{0,12},{4,8},{8,4},{12,0},{1,13},{5,9},{9,5},{13,1},{2,14},{6,10},... | collective-permute-start | bytes 49160 | tf_op jit(solution)/shard_map/ppermute | solution.py:384
  6.1 0.2 collective-permute-start.1
  6.3 1.8 %shard_map.86 = (bf16[64,384]{1,0:T(8,128)(2,1)S(1)}, f32[64,128]{1,0:T(8,128)S(1)}, bf16[64,24]{1,0:T(8,128)(2,1)S(1)}, f32[8,128]{1,0:T(8,128)S(1)}, f32[8,128...) custom-call(s32[1,1,4,16]{3,2,1,0:T(4,128)} %fslot_hbm.1, ...), custom_call_target="tpu_custom_call" | custom-call | tf_op jit(solution)/shard_map/pallas_call | solution.py:408
  8.1 0.0 collective-permute-done.refs_1_
  8.1 2.4 %collective-permute-done.2.refs_3_ = f32[8,512]{1,0:T(8,128)S(1)} collective-permute-done((f32[8,512]{1,0:T(8,128)}, f32[8,512]{1,0:T(8,128)S(1)}, u32[]{:S(2)}, u32[]{:S(2)}) %collective-permute-start.2) | collective-permute-done | bytes 16416 | tf_op jit(solution)/shard_map/ppermute | solution.py:384
  10.5 0.7 %shard_map.87 = (f32[8,128]{1,0:T(8,128)S(1)}, f32[64,128]{1,0:T(8,128)S(1)}) custom-call(f32[8,512]{1,0:T(8,128)S(1)} %get-tuple-element.23.refs_0_, f32[8,512]{1,0:T(8,128)S(1)} %collective-permute-done.refs_1_, f32[8,512]{1,0:T(8,128)S(1)} %collective-permute-done.1.refs_2_, f32[8,512]{1,0:T(8,128)S(1)} %collective-permute-done.2.refs_3_, ...), custom_call_target="tpu_custom_call" | custom-call | tf_op jit(solution)/shard_map/pallas_call | solution.py:408
  11.1 0.1 collective-permute-start.5
  11.2 1.6 %collective-permute-start.4 = (f32[8,128]{1,0:T(8,128)S(1)}, f32[8,128]{1,0:T(8,128)S(1)}, u32[]{:S(2)}, u32[]{:S(2)}) collective-permute-start(f32[8,128]{1,0:T(8,128)S(1)} %get-tuple-element.28.refs_0_), channel_id=1, source_target_pairs={{0,2},{1,3},{2,0},{3,1},{4,6},{5,7},{6,4},{7,5},{8,10},{9,11},{10,... | collective-permute-start | bytes 12296 | tf_op jit(solution)/shard_map/ppermute | solution.py:384
  12.8 0.3 collective-permute-start.3
  13.1 1.2 %collective-permute-done.5.refs_3_ = f32[8,128]{1,0:T(8,128)S(1)} collective-permute-done((f32[8,128]{1,0:T(8,128)S(1)}, f32[8,128]{1,0:T(8,128)S(1)}, u32[]{:S(2)}, u32[]{:S(2)}) %collective-permute-start.5) | collective-permute-done | bytes 4128 | tf_op jit(solution)/shard_map/ppermute | solution.py:384
  14.2 0.7 %collective-permute-done.4.refs_2_ = f32[8,128]{1,0:T(8,128)S(1)} collective-permute-done((f32[8,128]{1,0:T(8,128)S(1)}, f32[8,128]{1,0:T(8,128)S(1)}, u32[]{:S(2)}, u32[]{:S(2)}) %collective-permute-start.4) | collective-permute-done | bytes 4128 | tf_op jit(solution)/shard_map/ppermute | solution.py:384
  14.9 0.4 %shard_map.88 = (f32[40,128]{1,0:T(8,128)S(1)}, f32[8,128]{1,0:T(8,128)S(1)}) custom-call(f32[8,128]{1,0:T(8,128)S(1)} %get-tuple-element.28.refs_0_, f32[8,128]{1,0:T(8,128)S(1)} %collective-permute-done.3.refs_1_, f32[8,128]{1,0:T(8,128)S(1)} %collective-permute-done.4.refs_2_, f32[8,128]{1,0:T(8,128)S(1)} %collective-permute-done.5.refs_3_, ...), custom_call_target="tpu_custom_call" | custom-call | tf_op jit(solution)/shard_map/pallas_call | solution.py:408
  15.3 2.1 %collective-permute-start.8 = (f32[40,128]{1,0:T(8,128)S(1)}, f32[40,128]{1,0:T(8,128)S(1)}, u32[]{:S(2)}, u32[]{:S(2)}) collective-permute-start(f32[40,128]{1,0:T(8,128)S(1)} %get-tuple-element.34.refs_0_), channel_id=1, source_target_pairs={{0,12},{4,8},{8,4},{12,0},{1,13},{5,9},{9,5},{13,1},{2,14},{6,10},... | collective-permute-start | bytes 61448 | tf_op jit(solution)/shard_map/ppermute | solution.py:384
  17.4 2.4 %collective-permute-start.6 = (f32[40,128]{1,0:T(8,128)S(1)}, f32[40,128]{1,0:T(8,128)S(1)}, u32[]{:S(2)}, u32[]{:S(2)}) collective-permute-start(f32[40,128]{1,0:T(8,128)S(1)} %get-tuple-element.34.refs_0_), channel_id=1, source_target_pairs={{0,4},{4,0},{8,12},{12,8},{1,5},{5,1},{9,13},{13,9},{2,6},{6,2},{1... | collective-permute-start | bytes 61448 | tf_op jit(solution)/shard_map/ppermute | solution.py:384
  19.8 1.2 %collective-permute-done.8.refs_3_ = f32[40,128]{1,0:T(8,128)S(1)} collective-permute-done((f32[40,128]{1,0:T(8,128)S(1)}, f32[40,128]{1,0:T(8,128)S(1)}, u32[]{:S(2)}, u32[]{:S(2)}) %collective-permute-start.8) | collective-permute-done | bytes 20512 | tf_op jit(solution)/shard_map/ppermute | solution.py:384
  21.0 1.1 %collective-permute-done.7.refs_2_ = f32[40,128]{1,0:T(8,128)S(1)} collective-permute-done((f32[40,128]{1,0:T(8,128)S(1)}, f32[40,128]{1,0:T(8,128)S(1)}, u32[]{:S(2)}, u32[]{:S(2)}) %collective-permute-start.7) | collective-permute-done | bytes 20512 | tf_op jit(solution)/shard_map/ppermute | solution.py:384
  22.1 0.7 %shard_map.89.refs_0_ = f32[8,128]{1,0:T(8,128)S(1)} custom-call(f32[40,128]{1,0:T(8,128)S(1)} %get-tuple-element.34.refs_0_, f32[40,128]{1,0:T(8,128)S(1)} %collective-permute-done.6.refs_1_, f32[40,128]{1,0:T(8,128)S(1)} %collective-permute-done.7.refs_2_, f32[40,128]{1,0:T(8,128)S(1)} %collective-permute-done.8.refs_3_, ...), custom_call_target="tpu_custom_call" | custom-call | tf_op jit(solution)/shard_map/pallas_call | solution.py:408
  22.8 0.1 collective-permute-start.11
  22.9 1.6 %collective-permute-start.10 = (f32[8,128]{1,0:T(8,128)S(1)}, f32[8,128]{1,0:T(8,128)S(1)}, u32[]{:S(2)}, u32[]{:S(2)}) collective-permute-start(f32[8,128]{1,0:T(8,128)S(1)} %shard_map.89.refs_0_), channel_id=1, source_target_pairs={{0,2},{1,3},{2,0},{3,1},{4,6},{5,7},{6,4},{7,5},{8,10},{9,11},{10,... | collective-permute-start | bytes 12296 | tf_op jit(solution)/shard_map/ppermute | solution.py:384
  24.4 0.3 collective-permute-start.9
  24.7 1.2 %collective-permute-done.11.refs_3_ = f32[8,128]{1,0:T(8,128)S(1)} collective-permute-done((f32[8,128]{1,0:T(8,128)S(1)}, f32[8,128]{1,0:T(8,128)S(1)}, u32[]{:S(2)}, u32[]{:S(2)}) %collective-permute-start.11) | collective-permute-done | bytes 4128 | tf_op jit(solution)/shard_map/ppermute | solution.py:384
  25.9 0.7 %collective-permute-done.10.refs_2_ = f32[8,128]{1,0:T(8,128)S(1)} collective-permute-done((f32[8,128]{1,0:T(8,128)S(1)}, f32[8,128]{1,0:T(8,128)S(1)}, u32[]{:S(2)}, u32[]{:S(2)}) %collective-permute-start.10) | collective-permute-done | bytes 4128 | tf_op jit(solution)/shard_map/ppermute | solution.py:384
  26.6 0.4 %shard_map.90 = (f32[8,128]{1,0:T(8,128)S(1)}, f32[8,128]{1,0:T(8,128)S(1)}, f32[8,128]{1,0:T(8,128)S(1)}, f32[8,128]{1,0:T(8,128)S(1)}, f32[8,128]{1,0:T(8,128)S(1)}) custom-call(f32[8,128]{1,0:T(8,128)S(1)} %shard_map.89.refs_0_, f32[8,128]{1,0:T(8,128)S(1)} %collective-permute-done.9.refs_1_, f32[8,128]{1,0:T(8,128)S(1)} %collective-permute-done.10.refs_2_, ...), custom_call_target="tpu_custom_call" | custom-call | tf_op jit(solution)/shard_map/pallas_call | solution.py:408
  27.0 1.9 %collective-permute-start.12 = (f32[8,128]{1,0:T(8,128)S(1)}, f32[8,128]{1,0:T(8,128)S(1)}, u32[]{:S(2)}, u32[]{:S(2)}) collective-permute-start(f32[8,128]{1,0:T(8,128)S(1)} %get-tuple-element.37), channel_id=1, source_target_pairs={{0,12},{4,8},{8,4},{12,0},{1,13},{5,9},{9,5},{13,1},{2,14},{6,10},... | collective-permute-start | bytes 12296 | tf_op jit(solution)/shard_map/ppermute | solution.py:384
  28.9 1.1 %collective-permute-start.13 = (f32[8,128]{1,0:T(8,128)S(1)}, f32[8,128]{1,0:T(8,128)S(1)}, u32[]{:S(2)}, u32[]{:S(2)}) collective-permute-start(f32[8,128]{1,0:T(8,128)S(1)} %get-tuple-element.38), channel_id=1, source_target_pairs={{0,8},{4,12},{8,0},{12,4},{1,9},{5,13},{9,1},{13,5},{2,10},{6,14},... | collective-permute-start | bytes 12296 | tf_op jit(solution)/shard_map/ppermute | solution.py:384
  30.0 1.5 %collective-permute-start.14 = (f32[8,128]{1,0:T(8,128)S(1)}, f32[8,128]{1,0:T(8,128)S(1)}, u32[]{:S(2)}, u32[]{:S(2)}) collective-permute-start(f32[8,128]{1,0:T(8,128)S(1)} %get-tuple-element.39), channel_id=1, source_target_pairs={{0,4},{4,0},{8,12},{12,8},{1,5},{5,1},{9,13},{13,9},{2,6},{6,2},{1... | collective-permute-start | bytes 12296 | tf_op jit(solution)/shard_map/ppermute | solution.py:384
  31.5 0.7 %shard_map.91 = (bf16[128,128]{1,0:T(8,128)(2,1)S(1)}, f32[1,512]{1,0:T(1,128)}) custom-call(f32[40,128]{1,0:T(8,128)S(1)} %get-tuple-element.34.refs_0_, f32[40,128]{1,0:T(8,128)S(1)} %collective-permute-done.6.refs_1_, f32[40,128]{1,0:T(8,128)S(1)} %collective-permute-done.7.refs_2_, f32[40,128]{1,0:T(8,128)S(1)} %collective-permute-done.8.refs_3_, ...), custom_call_target="tpu_custom_call" | custom-call | tf_op jit(solution)/shard_map/pallas_call | solution.py:408
  32.1 0.3 %collective-permute-done.12.refs_0_ = f32[8,128]{1,0:T(8,128)S(1)} collective-permute-done((f32[8,128]{1,0:T(8,128)S(1)}, f32[8,128]{1,0:T(8,128)S(1)}, u32[]{:S(2)}, u32[]{:S(2)}) %collective-permute-start.12) | collective-permute-done | bytes 4128 | tf_op jit(solution)/shard_map/ppermute | solution.py:384
  32.5 0.9 %collective-permute-done.13.refs_1_ = f32[8,128]{1,0:T(8,128)S(1)} collective-permute-done((f32[8,128]{1,0:T(8,128)S(1)}, f32[8,128]{1,0:T(8,128)S(1)}, u32[]{:S(2)}, u32[]{:S(2)}) %collective-permute-start.13) | collective-permute-done | bytes 4128 | tf_op jit(solution)/shard_map/ppermute | solution.py:384
  33.4 0.2 collective-permute-done.14.refs_2_
  33.6 0.8 %shard_map.92 = f32[8,512]{1,0:T(8,128)} custom-call(f32[8,128]{1,0:T(8,128)S(1)} %collective-permute-done.12.refs_0_, f32[8,128]{1,0:T(8,128)S(1)} %collective-permute-done.13.refs_1_, f32[8,128]{1,0:T(8,128)S(1)} %collective-permute-done.14.refs_2_, f32[8,128]{1,0:T(8,128)S(1)} %get-tuple-element.40.refs_3_, bf16[128,128]{1,0:T(8,128)(2,1)S(1)} %get-tuple-element.42.refs_4_), custom_call_target="tpu_custom_call" | custom-call | tf_op jit(solution)/shard_map/pallas_call | solution.py:408
  (5 shorter events, 0.0 us)
Async XLA Ops:
  0.6 7.5 %collective-permute-start = (f32[8,512]{1,0:T(8,128)}, f32[8,512]{1,0:T(8,128)S(1)}, u32[]{:S(2)}, u32[]{:S(2)}) collective-permute-start(f32[8,512]{1,0:T(8,128)} %flux_hbm.1), channel_id=1, source_target_pairs={{0,8},{4,12},{8,0},{12,4},{1,9},{5,13},{9,1},{13,5},{2,10},{6,14},... | collective-permute-start | bytes 49160 | tf_op jit(solution)/shard_map/ppermute | solution.py:384
  4.7 5.7 %collective-permute-start.2 = (f32[8,512]{1,0:T(8,128)}, f32[8,512]{1,0:T(8,128)S(1)}, u32[]{:S(2)}, u32[]{:S(2)}) collective-permute-start(f32[8,512]{1,0:T(8,128)} %flux_hbm.1), channel_id=1, source_target_pairs={{0,12},{4,8},{8,4},{12,0},{1,13},{5,9},{9,5},{13,1},{2,14},{6,10},... | collective-permute-start | bytes 49160 | tf_op jit(solution)/shard_map/ppermute | solution.py:384
  6.1 4.4 %collective-permute-start.1 = (f32[8,512]{1,0:T(8,128)}, f32[8,512]{1,0:T(8,128)S(1)}, u32[]{:S(2)}, u32[]{:S(2)}) collective-permute-start(f32[8,512]{1,0:T(8,128)} %flux_hbm.1), channel_id=1, source_target_pairs={{0,4},{4,0},{8,12},{12,8},{1,5},{5,1},{9,13},{13,9},{2,6},{6,2},{1... | collective-permute-start | bytes 49160 | tf_op jit(solution)/shard_map/ppermute | solution.py:384
  11.1 3.1 %collective-permute-start.5 = (f32[8,128]{1,0:T(8,128)S(1)}, f32[8,128]{1,0:T(8,128)S(1)}, u32[]{:S(2)}, u32[]{:S(2)}) collective-permute-start(f32[8,128]{1,0:T(8,128)S(1)} %get-tuple-element.28.refs_0_), channel_id=1, source_target_pairs={{0,3},{1,2},{2,1},{3,0},{4,7},{5,6},{6,5},{7,4},{8,11},{9,10},{10,... | collective-permute-start | bytes 12296 | tf_op jit(solution)/shard_map/ppermute | solution.py:384
  11.2 3.7 %collective-permute-start.4 = (f32[8,128]{1,0:T(8,128)S(1)}, f32[8,128]{1,0:T(8,128)S(1)}, u32[]{:S(2)}, u32[]{:S(2)}) collective-permute-start(f32[8,128]{1,0:T(8,128)S(1)} %get-tuple-element.28.refs_0_), channel_id=1, source_target_pairs={{0,2},{1,3},{2,0},{3,1},{4,6},{5,7},{6,4},{7,5},{8,10},{9,11},{10,... | collective-permute-start | bytes 12296 | tf_op jit(solution)/shard_map/ppermute | solution.py:384
  12.8 2.1 %collective-permute-start.3 = (f32[8,128]{1,0:T(8,128)S(1)}, f32[8,128]{1,0:T(8,128)S(1)}, u32[]{:S(2)}, u32[]{:S(2)}) collective-permute-start(f32[8,128]{1,0:T(8,128)S(1)} %get-tuple-element.28.refs_0_), channel_id=1, source_target_pairs={{0,1},{1,0},{2,3},{3,2},{4,5},{5,4},{6,7},{7,6},{8,9},{9,8},{10,11... | collective-permute-start | bytes 12296 | tf_op jit(solution)/shard_map/ppermute | solution.py:384
  15.3 5.7 %collective-permute-start.8 = (f32[40,128]{1,0:T(8,128)S(1)}, f32[40,128]{1,0:T(8,128)S(1)}, u32[]{:S(2)}, u32[]{:S(2)}) collective-permute-start(f32[40,128]{1,0:T(8,128)S(1)} %get-tuple-element.34.refs_0_), channel_id=1, source_target_pairs={{0,12},{4,8},{8,4},{12,0},{1,13},{5,9},{9,5},{13,1},{2,14},{6,10},... | collective-permute-start | bytes 61448 | tf_op jit(solution)/shard_map/ppermute | solution.py:384
  17.4 4.7 %collective-permute-start.7 = (f32[40,128]{1,0:T(8,128)S(1)}, f32[40,128]{1,0:T(8,128)S(1)}, u32[]{:S(2)}, u32[]{:S(2)}) collective-permute-start(f32[40,128]{1,0:T(8,128)S(1)} %get-tuple-element.34.refs_0_), channel_id=1, source_target_pairs={{0,8},{4,12},{8,0},{12,4},{1,9},{5,13},{9,1},{13,5},{2,10},{6,14},... | collective-permute-start | bytes 61448 | tf_op jit(solution)/shard_map/ppermute | solution.py:384
  17.4 4.7 %collective-permute-start.6 = (f32[40,128]{1,0:T(8,128)S(1)}, f32[40,128]{1,0:T(8,128)S(1)}, u32[]{:S(2)}, u32[]{:S(2)}) collective-permute-start(f32[40,128]{1,0:T(8,128)S(1)} %get-tuple-element.34.refs_0_), channel_id=1, source_target_pairs={{0,4},{4,0},{8,12},{12,8},{1,5},{5,1},{9,13},{13,9},{2,6},{6,2},{1... | collective-permute-start | bytes 61448 | tf_op jit(solution)/shard_map/ppermute | solution.py:384
  22.8 3.1 %collective-permute-start.11 = (f32[8,128]{1,0:T(8,128)S(1)}, f32[8,128]{1,0:T(8,128)S(1)}, u32[]{:S(2)}, u32[]{:S(2)}) collective-permute-start(f32[8,128]{1,0:T(8,128)S(1)} %shard_map.89.refs_0_), channel_id=1, source_target_pairs={{0,3},{1,2},{2,1},{3,0},{4,7},{5,6},{6,5},{7,4},{8,11},{9,10},{10,... | collective-permute-start | bytes 12296 | tf_op jit(solution)/shard_map/ppermute | solution.py:384
  22.9 3.7 %collective-permute-start.10 = (f32[8,128]{1,0:T(8,128)S(1)}, f32[8,128]{1,0:T(8,128)S(1)}, u32[]{:S(2)}, u32[]{:S(2)}) collective-permute-start(f32[8,128]{1,0:T(8,128)S(1)} %shard_map.89.refs_0_), channel_id=1, source_target_pairs={{0,2},{1,3},{2,0},{3,1},{4,6},{5,7},{6,4},{7,5},{8,10},{9,11},{10,... | collective-permute-start | bytes 12296 | tf_op jit(solution)/shard_map/ppermute | solution.py:384
  24.4 2.1 %collective-permute-start.9 = (f32[8,128]{1,0:T(8,128)S(1)}, f32[8,128]{1,0:T(8,128)S(1)}, u32[]{:S(2)}, u32[]{:S(2)}) collective-permute-start(f32[8,128]{1,0:T(8,128)S(1)} %shard_map.89.refs_0_), channel_id=1, source_target_pairs={{0,1},{1,0},{2,3},{3,2},{4,5},{5,4},{6,7},{7,6},{8,9},{9,8},{10,11... | collective-permute-start | bytes 12296 | tf_op jit(solution)/shard_map/ppermute | solution.py:384
  27.0 5.5 %collective-permute-start.12 = (f32[8,128]{1,0:T(8,128)S(1)}, f32[8,128]{1,0:T(8,128)S(1)}, u32[]{:S(2)}, u32[]{:S(2)}) collective-permute-start(f32[8,128]{1,0:T(8,128)S(1)} %get-tuple-element.37), channel_id=1, source_target_pairs={{0,12},{4,8},{8,4},{12,0},{1,13},{5,9},{9,5},{13,1},{2,14},{6,10},... | collective-permute-start | bytes 12296 | tf_op jit(solution)/shard_map/ppermute | solution.py:384
  28.9 4.5 %collective-permute-start.13 = (f32[8,128]{1,0:T(8,128)S(1)}, f32[8,128]{1,0:T(8,128)S(1)}, u32[]{:S(2)}, u32[]{:S(2)}) collective-permute-start(f32[8,128]{1,0:T(8,128)S(1)} %get-tuple-element.38), channel_id=1, source_target_pairs={{0,8},{4,12},{8,0},{12,4},{1,9},{5,13},{9,1},{13,5},{2,10},{6,14},... | collective-permute-start | bytes 12296 | tf_op jit(solution)/shard_map/ppermute | solution.py:384
  30.0 3.6 %collective-permute-start.14 = (f32[8,128]{1,0:T(8,128)S(1)}, f32[8,128]{1,0:T(8,128)S(1)}, u32[]{:S(2)}, u32[]{:S(2)}) collective-permute-start(f32[8,128]{1,0:T(8,128)S(1)} %get-tuple-element.39), channel_id=1, source_target_pairs={{0,4},{4,0},{8,12},{12,8},{1,5},{5,1},{9,13},{13,9},{2,6},{6,2},{1... | collective-permute-start | bytes 12296 | tf_op jit(solution)/shard_map/ppermute | solution.py:384

commit v16 on v15

--- a/solution.py
+++ b/solution.py
@@ -419,7 +419,7 @@
 
         obs_tile = ((OBLK_DEV, LANES), F32)
         slot_tile = ((slots, LANES), F32)
-        sum_scratch = [pltpu.VMEM(*slot_tile)] + [pltpu.VMEM((OBLK_DEV + 1, TILES, LANES), F32)] * 2
+        sum_scratch = [pltpu.VMEM(*slot_tile)] + [pltpu.VMEM((OBLK_DEV + 1, TILES, LANES), F32)] * 8
         small = (flux_slot, obs_slot, slot_count, observed, obs_weight)
         turned = footprint.reshape(slots // 8, 8, TILES, LANES).transpose(0, 2, 1, 3)
         pick_flux, target, slot_obs, index, observed_t, weight_t, flux, matrices, by_slot, obs = call(

time: 34.6 us -> 34.5 us (level)
  no operation moved by 1% of the time
where the time goes in v16:
time: 34.5 us; the launch traced here: 34.3 us
  starting transfers between devices  18.5 us (54%)
  waiting for transfers between devices  9.83 us (28%)
  Pallas kernels  5.36 us (16%)
  between operations  0.7 us (2%)
    ppermute x15, starting transfers between devices, send(): return lax.ppermute(value, axis, [(i, i ^ k) for i in range(size)])  18.5 us
    ppermute x15, waiting for transfers between devices, send(): return lax.ppermute(value, axis, [(i, i ^ k) for i in range(size)])  9.83 us
    pallas_call x7, Pallas kernels, call(): pl.pallas_call(body, out_shape=outs_at, in_specs=[smem if value is obs el...  5.36 us
  transfers between devices with their start and end apart: 15, of which 10 were waited for; matrix products, arithmetic and copies ran while one was open for 0% of the time, Pallas kernels for 7%

profile of v16, /device:TPU:0, one launch (start us, length us, event | category | flops | bytes accessed | tf_op | source)
XLA Modules:
  0.0 34.3 jit_solution(8107392365990627877)
XLA Ops:
  0.6 4.1 %collective-permute-start = (f32[8,512]{1,0:T(8,128)}, f32[8,512]{1,0:T(8,128)S(1)}, u32[]{:S(2)}, u32[]{:S(2)}) collective-permute-start(f32[8,512]{1,0:T(8,128)} %flux_hbm.1), channel_id=1, source_target_pairs={{0,8},{4,12},{8,0},{12,4},{1,9},{5,13},{9,1},{13,5},{2,10},{6,14},... | collective-permute-start | bytes 49160 | tf_op jit(solution)/shard_map/ppermute | solution.py:384
  4.7 1.3 %collective-permute-start.2 = (f32[8,512]{1,0:T(8,128)}, f32[8,512]{1,0:T(8,128)S(1)}, u32[]{:S(2)}, u32[]{:S(2)}) collective-permute-start(f32[8,512]{1,0:T(8,128)} %flux_hbm.1), channel_id=1, source_target_pairs={{0,12},{4,8},{8,4},{12,0},{1,13},{5,9},{9,5},{13,1},{2,14},{6,10},... | collective-permute-start | bytes 49160 | tf_op jit(solution)/shard_map/ppermute | solution.py:384
  6.1 0.2 collective-permute-start.1
  6.3 1.8 %shard_map.86 = (bf16[64,384]{1,0:T(8,128)(2,1)S(1)}, f32[64,128]{1,0:T(8,128)S(1)}, bf16[64,24]{1,0:T(8,128)(2,1)S(1)}, f32[8,128]{1,0:T(8,128)S(1)}, f32[8,128...) custom-call(s32[1,1,4,16]{3,2,1,0:T(4,128)} %fslot_hbm.1, ...), custom_call_target="tpu_custom_call" | custom-call | tf_op jit(solution)/shard_map/pallas_call | solution.py:408
  8.1 0.0 collective-permute-done.refs_1_
  8.1 2.4 %collective-permute-done.2.refs_3_ = f32[8,512]{1,0:T(8,128)S(1)} collective-permute-done((f32[8,512]{1,0:T(8,128)}, f32[8,512]{1,0:T(8,128)S(1)}, u32[]{:S(2)}, u32[]{:S(2)}) %collective-permute-start.2) | collective-permute-done | bytes 16416 | tf_op jit(solution)/shard_map/ppermute | solution.py:384
  10.5 0.6 %shard_map.87 = (f32[8,128]{1,0:T(8,128)S(1)}, f32[64,128]{1,0:T(8,128)S(1)}) custom-call(f32[8,512]{1,0:T(8,128)S(1)} %get-tuple-element.23.refs_0_, f32[8,512]{1,0:T(8,128)S(1)} %collective-permute-done.refs_1_, f32[8,512]{1,0:T(8,128)S(1)} %collective-permute-done.1.refs_2_, f32[8,512]{1,0:T(8,128)S(1)} %collective-permute-done.2.refs_3_, ...), custom_call_target="tpu_custom_call" | custom-call | tf_op jit(solution)/shard_map/pallas_call | solution.py:408
  11.1 0.1 collective-permute-start.5
  11.2 1.6 %collective-permute-start.4 = (f32[8,128]{1,0:T(8,128)S(1)}, f32[8,128]{1,0:T(8,128)S(1)}, u32[]{:S(2)}, u32[]{:S(2)}) collective-permute-start(f32[8,128]{1,0:T(8,128)S(1)} %get-tuple-element.28.refs_0_), channel_id=1, source_target_pairs={{0,2},{1,3},{2,0},{3,1},{4,6},{5,7},{6,4},{7,5},{8,10},{9,11},{10,... | collective-permute-start | bytes 12296 | tf_op jit(solution)/shard_map/ppermute | solution.py:384
  12.8 0.3 collective-permute-start.3
  13.0 1.2 %collective-permute-done.5.refs_3_ = f32[8,128]{1,0:T(8,128)S(1)} collective-permute-done((f32[8,128]{1,0:T(8,128)S(1)}, f32[8,128]{1,0:T(8,128)S(1)}, u32[]{:S(2)}, u32[]{:S(2)}) %collective-permute-start.5) | collective-permute-done | bytes 4128 | tf_op jit(solution)/shard_map/ppermute | solution.py:384
  14.2 0.7 %collective-permute-done.4.refs_2_ = f32[8,128]{1,0:T(8,128)S(1)} collective-permute-done((f32[8,128]{1,0:T(8,128)S(1)}, f32[8,128]{1,0:T(8,128)S(1)}, u32[]{:S(2)}, u32[]{:S(2)}) %collective-permute-start.4) | collective-permute-done | bytes 4128 | tf_op jit(solution)/shard_map/ppermute | solution.py:384
  14.9 0.4 %shard_map.88 = (f32[40,128]{1,0:T(8,128)S(1)}, f32[8,128]{1,0:T(8,128)S(1)}) custom-call(f32[8,128]{1,0:T(8,128)S(1)} %get-tuple-element.28.refs_0_, f32[8,128]{1,0:T(8,128)S(1)} %collective-permute-done.3.refs_1_, f32[8,128]{1,0:T(8,128)S(1)} %collective-permute-done.4.refs_2_, f32[8,128]{1,0:T(8,128)S(1)} %collective-permute-done.5.refs_3_, ...), custom_call_target="tpu_custom_call" | custom-call | tf_op jit(solution)/shard_map/pallas_call | solution.py:408
  15.3 2.1 %collective-permute-start.8 = (f32[40,128]{1,0:T(8,128)S(1)}, f32[40,128]{1,0:T(8,128)S(1)}, u32[]{:S(2)}, u32[]{:S(2)}) collective-permute-start(f32[40,128]{1,0:T(8,128)S(1)} %get-tuple-element.34.refs_0_), channel_id=1, source_target_pairs={{0,12},{4,8},{8,4},{12,0},{1,13},{5,9},{9,5},{13,1},{2,14},{6,10},... | collective-permute-start | bytes 61448 | tf_op jit(solution)/shard_map/ppermute | solution.py:384
  17.4 2.4 %collective-permute-start.6 = (f32[40,128]{1,0:T(8,128)S(1)}, f32[40,128]{1,0:T(8,128)S(1)}, u32[]{:S(2)}, u32[]{:S(2)}) collective-permute-start(f32[40,128]{1,0:T(8,128)S(1)} %get-tuple-element.34.refs_0_), channel_id=1, source_target_pairs={{0,4},{4,0},{8,12},{12,8},{1,5},{5,1},{9,13},{13,9},{2,6},{6,2},{1... | collective-permute-start | bytes 61448 | tf_op jit(solution)/shard_map/ppermute | solution.py:384
  19.8 1.2 %collective-permute-done.8.refs_3_ = f32[40,128]{1,0:T(8,128)S(1)} collective-permute-done((f32[40,128]{1,0:T(8,128)S(1)}, f32[40,128]{1,0:T(8,128)S(1)}, u32[]{:S(2)}, u32[]{:S(2)}) %collective-permute-start.8) | collective-permute-done | bytes 20512 | tf_op jit(solution)/shard_map/ppermute | solution.py:384
  21.0 1.1 %collective-permute-done.7.refs_2_ = f32[40,128]{1,0:T(8,128)S(1)} collective-permute-done((f32[40,128]{1,0:T(8,128)S(1)}, f32[40,128]{1,0:T(8,128)S(1)}, u32[]{:S(2)}, u32[]{:S(2)}) %collective-permute-start.7) | collective-permute-done | bytes 20512 | tf_op jit(solution)/shard_map/ppermute | solution.py:384
  22.1 0.6 %shard_map.89.refs_0_ = f32[8,128]{1,0:T(8,128)S(1)} custom-call(f32[40,128]{1,0:T(8,128)S(1)} %get-tuple-element.34.refs_0_, f32[40,128]{1,0:T(8,128)S(1)} %collective-permute-done.6.refs_1_, f32[40,128]{1,0:T(8,128)S(1)} %collective-permute-done.7.refs_2_, f32[40,128]{1,0:T(8,128)S(1)} %collective-permute-done.8.refs_3_, ...), custom_call_target="tpu_custom_call" | custom-call | tf_op jit(solution)/shard_map/pallas_call | solution.py:408
  22.7 0.1 collective-permute-start.11
  22.8 1.5 %collective-permute-start.10 = (f32[8,128]{1,0:T(8,128)S(1)}, f32[8,128]{1,0:T(8,128)S(1)}, u32[]{:S(2)}, u32[]{:S(2)}) collective-permute-start(f32[8,128]{1,0:T(8,128)S(1)} %shard_map.89.refs_0_), channel_id=1, source_target_pairs={{0,2},{1,3},{2,0},{3,1},{4,6},{5,7},{6,4},{7,5},{8,10},{9,11},{10,... | collective-permute-start | bytes 12296 | tf_op jit(solution)/shard_map/ppermute | solution.py:384
  24.4 0.3 collective-permute-start.9
  24.7 1.2 %collective-permute-done.11.refs_3_ = f32[8,128]{1,0:T(8,128)S(1)} collective-permute-done((f32[8,128]{1,0:T(8,128)S(1)}, f32[8,128]{1,0:T(8,128)S(1)}, u32[]{:S(2)}, u32[]{:S(2)}) %collective-permute-start.11) | collective-permute-done | bytes 4128 | tf_op jit(solution)/shard_map/ppermute | solution.py:384
  25.8 0.6 %collective-permute-done.10.refs_2_ = f32[8,128]{1,0:T(8,128)S(1)} collective-permute-done((f32[8,128]{1,0:T(8,128)S(1)}, f32[8,128]{1,0:T(8,128)S(1)}, u32[]{:S(2)}, u32[]{:S(2)}) %collective-permute-start.10) | collective-permute-done | bytes 4128 | tf_op jit(solution)/shard_map/ppermute | solution.py:384
  26.5 0.4 %shard_map.90 = (f32[8,128]{1,0:T(8,128)S(1)}, f32[8,128]{1,0:T(8,128)S(1)}, f32[8,128]{1,0:T(8,128)S(1)}, f32[8,128]{1,0:T(8,128)S(1)}, f32[8,128]{1,0:T(8,128)S(1)}) custom-call(f32[8,128]{1,0:T(8,128)S(1)} %shard_map.89.refs_0_, f32[8,128]{1,0:T(8,128)S(1)} %collective-permute-done.9.refs_1_, f32[8,128]{1,0:T(8,128)S(1)} %collective-permute-done.10.refs_2_, ...), custom_call_target="tpu_custom_call" | custom-call | tf_op jit(solution)/shard_map/pallas_call | solution.py:408
  26.9 1.9 %collective-permute-start.12 = (f32[8,128]{1,0:T(8,128)S(1)}, f32[8,128]{1,0:T(8,128)S(1)}, u32[]{:S(2)}, u32[]{:S(2)}) collective-permute-start(f32[8,128]{1,0:T(8,128)S(1)} %get-tuple-element.37), channel_id=1, source_target_pairs={{0,12},{4,8},{8,4},{12,0},{1,13},{5,9},{9,5},{13,1},{2,14},{6,10},... | collective-permute-start | bytes 12296 | tf_op jit(solution)/shard_map/ppermute | solution.py:384
  28.8 1.1 %collective-permute-start.13 = (f32[8,128]{1,0:T(8,128)S(1)}, f32[8,128]{1,0:T(8,128)S(1)}, u32[]{:S(2)}, u32[]{:S(2)}) collective-permute-start(f32[8,128]{1,0:T(8,128)S(1)} %get-tuple-element.38), channel_id=1, source_target_pairs={{0,8},{4,12},{8,0},{12,4},{1,9},{5,13},{9,1},{13,5},{2,10},{6,14},... | collective-permute-start | bytes 12296 | tf_op jit(solution)/shard_map/ppermute | solution.py:384
  29.9 1.5 %collective-permute-start.14 = (f32[8,128]{1,0:T(8,128)S(1)}, f32[8,128]{1,0:T(8,128)S(1)}, u32[]{:S(2)}, u32[]{:S(2)}) collective-permute-start(f32[8,128]{1,0:T(8,128)S(1)} %get-tuple-element.39), channel_id=1, source_target_pairs={{0,4},{4,0},{8,12},{12,8},{1,5},{5,1},{9,13},{13,9},{2,6},{6,2},{1... | collective-permute-start | bytes 12296 | tf_op jit(solution)/shard_map/ppermute | solution.py:384
  31.4 0.7 %shard_map.91 = (bf16[128,128]{1,0:T(8,128)(2,1)S(1)}, f32[1,512]{1,0:T(1,128)}) custom-call(f32[40,128]{1,0:T(8,128)S(1)} %get-tuple-element.34.refs_0_, f32[40,128]{1,0:T(8,128)S(1)} %collective-permute-done.6.refs_1_, f32[40,128]{1,0:T(8,128)S(1)} %collective-permute-done.7.refs_2_, f32[40,128]{1,0:T(8,128)S(1)} %collective-permute-done.8.refs_3_, ...), custom_call_target="tpu_custom_call" | custom-call | tf_op jit(solution)/shard_map/pallas_call | solution.py:408
  32.1 0.3 %collective-permute-done.12.refs_0_ = f32[8,128]{1,0:T(8,128)S(1)} collective-permute-done((f32[8,128]{1,0:T(8,128)S(1)}, f32[8,128]{1,0:T(8,128)S(1)}, u32[]{:S(2)}, u32[]{:S(2)}) %collective-permute-start.12) | collective-permute-done | bytes 4128 | tf_op jit(solution)/shard_map/ppermute | solution.py:384
  32.4 0.9 %collective-permute-done.13.refs_1_ = f32[8,128]{1,0:T(8,128)S(1)} collective-permute-done((f32[8,128]{1,0:T(8,128)S(1)}, f32[8,128]{1,0:T(8,128)S(1)}, u32[]{:S(2)}, u32[]{:S(2)}) %collective-permute-start.13) | collective-permute-done | bytes 4128 | tf_op jit(solution)/shard_map/ppermute | solution.py:384
  33.3 0.2 collective-permute-done.14.refs_2_
  33.5 0.8 %shard_map.92 = f32[8,512]{1,0:T(8,128)} custom-call(f32[8,128]{1,0:T(8,128)S(1)} %collective-permute-done.12.refs_0_, f32[8,128]{1,0:T(8,128)S(1)} %collective-permute-done.13.refs_1_, f32[8,128]{1,0:T(8,128)S(1)} %collective-permute-done.14.refs_2_, f32[8,128]{1,0:T(8,128)S(1)} %get-tuple-element.40.refs_3_, bf16[128,128]{1,0:T(8,128)(2,1)S(1)} %get-tuple-element.42.refs_4_), custom_call_target="tpu_custom_call" | custom-call | tf_op jit(solution)/shard_map/pallas_call | solution.py:408
  (5 shorter events, 0.0 us)
Async XLA Ops:
  0.6 7.5 %collective-permute-start = (f32[8,512]{1,0:T(8,128)}, f32[8,512]{1,0:T(8,128)S(1)}, u32[]{:S(2)}, u32[]{:S(2)}) collective-permute-start(f32[8,512]{1,0:T(8,128)} %flux_hbm.1), channel_id=1, source_target_pairs={{0,8},{4,12},{8,0},{12,4},{1,9},{5,13},{9,1},{13,5},{2,10},{6,14},... | collective-permute-start | bytes 49160 | tf_op jit(solution)/shard_map/ppermute | solution.py:384
  4.7 5.7 %collective-permute-start.2 = (f32[8,512]{1,0:T(8,128)}, f32[8,512]{1,0:T(8,128)S(1)}, u32[]{:S(2)}, u32[]{:S(2)}) collective-permute-start(f32[8,512]{1,0:T(8,128)} %flux_hbm.1), channel_id=1, source_target_pairs={{0,12},{4,8},{8,4},{12,0},{1,13},{5,9},{9,5},{13,1},{2,14},{6,10},... | collective-permute-start | bytes 49160 | tf_op jit(solution)/shard_map/ppermute | solution.py:384
  6.1 4.4 %collective-permute-start.1 = (f32[8,512]{1,0:T(8,128)}, f32[8,512]{1,0:T(8,128)S(1)}, u32[]{:S(2)}, u32[]{:S(2)}) collective-permute-start(f32[8,512]{1,0:T(8,128)} %flux_hbm.1), channel_id=1, source_target_pairs={{0,4},{4,0},{8,12},{12,8},{1,5},{5,1},{9,13},{13,9},{2,6},{6,2},{1... | collective-permute-start | bytes 49160 | tf_op jit(solution)/shard_map/ppermute | solution.py:384
  11.1 3.1 %collective-permute-start.5 = (f32[8,128]{1,0:T(8,128)S(1)}, f32[8,128]{1,0:T(8,128)S(1)}, u32[]{:S(2)}, u32[]{:S(2)}) collective-permute-start(f32[8,128]{1,0:T(8,128)S(1)} %get-tuple-element.28.refs_0_), channel_id=1, source_target_pairs={{0,3},{1,2},{2,1},{3,0},{4,7},{5,6},{6,5},{7,4},{8,11},{9,10},{10,... | collective-permute-start | bytes 12296 | tf_op jit(solution)/shard_map/ppermute | solution.py:384
  11.2 3.7 %collective-permute-start.4 = (f32[8,128]{1,0:T(8,128)S(1)}, f32[8,128]{1,0:T(8,128)S(1)}, u32[]{:S(2)}, u32[]{:S(2)}) collective-permute-start(f32[8,128]{1,0:T(8,128)S(1)} %get-tuple-element.28.refs_0_), channel_id=1, source_target_pairs={{0,2},{1,3},{2,0},{3,1},{4,6},{5,7},{6,4},{7,5},{8,10},{9,11},{10,... | collective-permute-start | bytes 12296 | tf_op jit(solution)/shard_map/ppermute | solution.py:384
  12.8 2.1 %collective-permute-start.3 = (f32[8,128]{1,0:T(8,128)S(1)}, f32[8,128]{1,0:T(8,128)S(1)}, u32[]{:S(2)}, u32[]{:S(2)}) collective-permute-start(f32[8,128]{1,0:T(8,128)S(1)} %get-tuple-element.28.refs_0_), channel_id=1, source_target_pairs={{0,1},{1,0},{2,3},{3,2},{4,5},{5,4},{6,7},{7,6},{8,9},{9,8},{10,11... | collective-permute-start | bytes 12296 | tf_op jit(solution)/shard_map/ppermute | solution.py:384
  15.3 5.7 %collective-permute-start.8 = (f32[40,128]{1,0:T(8,128)S(1)}, f32[40,128]{1,0:T(8,128)S(1)}, u32[]{:S(2)}, u32[]{:S(2)}) collective-permute-start(f32[40,128]{1,0:T(8,128)S(1)} %get-tuple-element.34.refs_0_), channel_id=1, source_target_pairs={{0,12},{4,8},{8,4},{12,0},{1,13},{5,9},{9,5},{13,1},{2,14},{6,10},... | collective-permute-start | bytes 61448 | tf_op jit(solution)/shard_map/ppermute | solution.py:384
  17.4 4.7 %collective-permute-start.7 = (f32[40,128]{1,0:T(8,128)S(1)}, f32[40,128]{1,0:T(8,128)S(1)}, u32[]{:S(2)}, u32[]{:S(2)}) collective-permute-start(f32[40,128]{1,0:T(8,128)S(1)} %get-tuple-element.34.refs_0_), channel_id=1, source_target_pairs={{0,8},{4,12},{8,0},{12,4},{1,9},{5,13},{9,1},{13,5},{2,10},{6,14},... | collective-permute-start | bytes 61448 | tf_op jit(solution)/shard_map/ppermute | solution.py:384
  17.4 4.7 %collective-permute-start.6 = (f32[40,128]{1,0:T(8,128)S(1)}, f32[40,128]{1,0:T(8,128)S(1)}, u32[]{:S(2)}, u32[]{:S(2)}) collective-permute-start(f32[40,128]{1,0:T(8,128)S(1)} %get-tuple-element.34.refs_0_), channel_id=1, source_target_pairs={{0,4},{4,0},{8,12},{12,8},{1,5},{5,1},{9,13},{13,9},{2,6},{6,2},{1... | collective-permute-start | bytes 61448 | tf_op jit(solution)/shard_map/ppermute | solution.py:384
  22.7 3.1 %collective-permute-start.11 = (f32[8,128]{1,0:T(8,128)S(1)}, f32[8,128]{1,0:T(8,128)S(1)}, u32[]{:S(2)}, u32[]{:S(2)}) collective-permute-start(f32[8,128]{1,0:T(8,128)S(1)} %shard_map.89.refs_0_), channel_id=1, source_target_pairs={{0,3},{1,2},{2,1},{3,0},{4,7},{5,6},{6,5},{7,4},{8,11},{9,10},{10,... | collective-permute-start | bytes 12296 | tf_op jit(solution)/shard_map/ppermute | solution.py:384
  22.8 3.7 %collective-permute-start.10 = (f32[8,128]{1,0:T(8,128)S(1)}, f32[8,128]{1,0:T(8,128)S(1)}, u32[]{:S(2)}, u32[]{:S(2)}) collective-permute-start(f32[8,128]{1,0:T(8,128)S(1)} %shard_map.89.refs_0_), channel_id=1, source_target_pairs={{0,2},{1,3},{2,0},{3,1},{4,6},{5,7},{6,4},{7,5},{8,10},{9,11},{10,... | collective-permute-start | bytes 12296 | tf_op jit(solution)/shard_map/ppermute | solution.py:384
  24.4 2.1 %collective-permute-start.9 = (f32[8,128]{1,0:T(8,128)S(1)}, f32[8,128]{1,0:T(8,128)S(1)}, u32[]{:S(2)}, u32[]{:S(2)}) collective-permute-start(f32[8,128]{1,0:T(8,128)S(1)} %shard_map.89.refs_0_), channel_id=1, source_target_pairs={{0,1},{1,0},{2,3},{3,2},{4,5},{5,4},{6,7},{7,6},{8,9},{9,8},{10,11... | collective-permute-start | bytes 12296 | tf_op jit(solution)/shard_map/ppermute | solution.py:384
  26.9 5.5 %collective-permute-start.12 = (f32[8,128]{1,0:T(8,128)S(1)}, f32[8,128]{1,0:T(8,128)S(1)}, u32[]{:S(2)}, u32[]{:S(2)}) collective-permute-start(f32[8,128]{1,0:T(8,128)S(1)} %get-tuple-element.37), channel_id=1, source_target_pairs={{0,12},{4,8},{8,4},{12,0},{1,13},{5,9},{9,5},{13,1},{2,14},{6,10},... | collective-permute-start | bytes 12296 | tf_op jit(solution)/shard_map/ppermute | solution.py:384
  28.8 4.5 %collective-permute-start.13 = (f32[8,128]{1,0:T(8,128)S(1)}, f32[8,128]{1,0:T(8,128)S(1)}, u32[]{:S(2)}, u32[]{:S(2)}) collective-permute-start(f32[8,128]{1,0:T(8,128)S(1)} %get-tuple-element.38), channel_id=1, source_target_pairs={{0,8},{4,12},{8,0},{12,4},{1,9},{5,13},{9,1},{13,5},{2,10},{6,14},... | collective-permute-start | bytes 12296 | tf_op jit(solution)/shard_map/ppermute | solution.py:384
  29.9 3.6 %collective-permute-start.14 = (f32[8,128]{1,0:T(8,128)S(1)}, f32[8,128]{1,0:T(8,128)S(1)}, u32[]{:S(2)}, u32[]{:S(2)}) collective-permute-start(f32[8,128]{1,0:T(8,128)S(1)} %get-tuple-element.39), channel_id=1, source_target_pairs={{0,4},{4,0},{8,12},{12,8},{1,5},{5,1},{9,13},{13,9},{2,6},{6,2},{1... | collective-permute-start | bytes 12296 | tf_op jit(solution)/shard_map/ppermute | solution.py:384
